TPU v7x, 32 devices: a whole 2x2x4 slice. The times are simulated.
32 devices in a mesh: groups: 2 (over y), seg: 4 (over z), slab: 2 (over x), comp: 2 (over core).
Axes of the slice: x: 2, y: 2, z: 4, core: 2. Of those that a mesh axis runs over, the one named last changes fastest.
Arguments:
- base: float32 [8, 3, 64, 4096], P(('groups', 'seg'), None, 'slab'), parts along dimension 0, may hold values from -6 to 6
- state: float32 [8, 2, 3, 64, 4096], P(('groups', 'seg'), 'comp', None, 'slab'), parts along dimension 0, may hold values from -6 to 6
- wavenumber: int32 [2], P('groups'), parts along dimension 0, may hold values from 1 to 4
- cutoff: int32 [6], P('groups'), parts along dimension 0, may hold values from 18 to 21, as said below
Outputs:
- base_gap: float32 [8, 3, 64, 4096], P(('groups', 'seg'), None, ('slab', 'comp')), parts along dimension 0
- state_gap: float32 [8, 2, 3, 64, 4096], P(('groups', 'seg'), 'comp', None, 'slab'), parts along dimension 0
There are 2 independent parts, one for each index of `groups`. A program takes and returns all parts, laid end to end along the dimension named above; each array names one. Nothing has to cross between parts.
Inputs may be any that keep to these rules, and one draw needn't show every extreme that they name: `cutoff`: each entry is at most one third of 64, rounded down, and at least that minus three; one entry always equals it.
All inputs are finite; a program needn't handle non-finite values.
Results may differ from a plain program's by a relative error of at most 0.0001.
Values sent between devices are 32-bit elements; how exact they have to be, the bound alone decides.
No kernel may reach another device: no remote copies, remote signals or barrier semaphores. Data moves between devices by JAX's collectives and lax.ppermute only.
A program may use at most 128 MiB of HBM per device.

v0:
```python
import jax
import jax.numpy as jnp
from jax import lax
from jax.sharding import PartitionSpec as P

N = 64


viscosity = 0.025
time_step = 0.02
forcing_amp = 10.0
highest = lax.Precision.HIGHEST


def swapped(value, axis, apart):
    mask = 2**apart
    pairs = [(source, source ^ mask) for source in range(lax.axis_size(axis))]
    return lax.ppermute(value, axis, pairs)


def shifted(block, axis, distance):
    devices = range(lax.axis_size(axis))
    route = [((i - distance) % len(devices), i) for i in devices]
    return lax.ppermute(block, axis, route)


def wavenumbers(grid_points):
    position = jnp.arange(grid_points, dtype=jnp.int32)
    return jnp.where(position < grid_points // 2, position, position - grid_points)


def phases(first, second, grid_points):
    product = jnp.mod(first[:, None] * second[None, :], grid_points)
    return product.astype(jnp.float32) * (2.0 * jnp.pi / grid_points)


def combine(partial_value, columns):
    cosine_part = partial_value[0]
    sine_part = partial_value[1]
    real_part = cosine_part[..., :columns] - sine_part[..., columns:]
    imag_part = cosine_part[..., columns:] + sine_part[..., :columns]
    return jnp.concatenate([real_part, imag_part], axis=-1)


def times_unit(values, wave, columns):
    return jnp.concatenate([-wave * values[..., columns:], wave * values[..., :columns]], axis=-1)


def doubled(values):
    return jnp.concatenate([values, values], axis=-1)


def body(base, state, wavenumber, cutoff):
    grid_points = N
    base = base.reshape(base.shape[0], 3, base.shape[2], grid_points, grid_points)
    state = state.reshape(
        state.shape[0], state.shape[1], 3, state.shape[3], grid_points, grid_points
    )
    slab_rows = state.shape[3]
    half_rows = slab_rows // 2
    slab_count = lax.axis_size("slab")
    group_count = slab_count * lax.axis_size("comp")
    core_side = lax.axis_index("comp")
    block_number = lax.axis_index(("slab", "comp"))
    base_whole = base[0]
    base_half = lax.dynamic_slice_in_dim(base_whole, core_side * half_rows, half_rows, 1)
    own_state = state[0, 0]
    spectrum = wavenumbers(grid_points)
    one_third = grid_points // 3
    row_total = (2 * one_third + group_count) // group_count * group_count
    row_index = jnp.arange(row_total, dtype=jnp.int32)
    row_alive_mask = row_index <= 2 * one_third
    row_wave = jnp.where(row_index <= one_third, row_index, row_index - (2 * one_third + 1))
    row_wave = jnp.where(row_alive_mask, row_wave, 0)
    width = grid_points // 2
    rows_per_block = row_total // group_count
    alive_flags = row_alive_mask.astype(jnp.float32)
    grid_index = jnp.arange(grid_points, dtype=jnp.int32)
    column_index = grid_index[:width]
    angle_grid = phases(grid_index, grid_index, grid_points)
    angle_ahead = phases(grid_index, column_index, grid_points)
    angle_behind = phases(column_index, grid_index, grid_points)
    column_weight = jnp.where(column_index == 0, 1.0, 2.0).astype(jnp.float32)[:, None]
    forward_z = jnp.concatenate([jnp.cos(angle_ahead), -jnp.sin(angle_ahead)], axis=1)
    inverse_z = (
        jnp.concatenate(
            [jnp.cos(angle_behind) * column_weight, -jnp.sin(angle_behind) * column_weight], axis=0
        )
        / grid_points
    )
    phase_angle_rows = phases(row_wave, grid_index, grid_points)
    forward_transform_y = (
        jnp.stack([jnp.cos(phase_angle_rows), -jnp.sin(phase_angle_rows)])
        * alive_flags[None, :, None]
    )
    inverse_y = (
        jnp.stack([jnp.cos(phase_angle_rows).T, jnp.sin(phase_angle_rows).T])
        * alive_flags[None, None, :]
        / grid_points
    )
    forward_x = jnp.stack([jnp.cos(angle_grid), -jnp.sin(angle_grid)])
    inverse_x = jnp.stack([jnp.cos(angle_grid), jnp.sin(angle_grid)]) / grid_points
    table_ahead = forward_x.reshape(2, grid_points, slab_count, slab_rows)
    table_back = inverse_x.reshape(2, slab_count, slab_rows, grid_points)
    local_wave = lax.dynamic_slice_in_dim(row_wave, block_number * rows_per_block, rows_per_block)
    local_alive_mask = lax.dynamic_slice_in_dim(
        alive_flags, block_number * rows_per_block, rows_per_block
    )
    shape_local = (grid_points, rows_per_block, width)
    wave_x = jnp.broadcast_to(spectrum[:, None, None], shape_local)
    wave_y = jnp.broadcast_to(local_wave[None, :, None], shape_local)
    wave_z = jnp.broadcast_to(spectrum[:width][None, None, :], shape_local)
    inside = (
        (jnp.abs(wave_x) <= cutoff[0])
        & (jnp.abs(wave_y) <= cutoff[1])
        & (jnp.abs(wave_z) <= cutoff[2])
    )
    keep_mask = doubled(inside.astype(jnp.float32) * local_alive_mask[None, :, None])
    float_x = wave_x.astype(jnp.float32)
    float_y = wave_y.astype(jnp.float32)
    float_z = wave_z.astype(jnp.float32)
    ksquare = float_x * float_x + float_y * float_y + float_z * float_z
    safe_square = doubled(jnp.where(ksquare > 0, ksquare, jnp.ones_like(ksquare)))
    damping = doubled(1.0 / (1.0 + viscosity * time_step * ksquare))
    double_x = doubled(float_x)
    double_y = doubled(float_y)
    double_z = doubled(float_z)

    def project(field):
        divergence = (double_x * field[0] + double_y * field[1] + double_z * field[2]) / safe_square
        return jnp.stack(
            [
                field[0] - double_x * divergence,
                field[1] - double_y * divergence,
                field[2] - double_z * divergence,
            ]
        )

    def yz_forward(field):
        along_z = jnp.einsum("...z,zk->...k", field, forward_z, precision=highest)
        partial_value = jnp.einsum(
            "sry,...yk->s...rk", forward_transform_y, along_z, precision=highest
        )
        return combine(partial_value, width)

    def yz_inverse(modes):
        partial_value = jnp.einsum("syr,...rk->s...yk", inverse_y, modes, precision=highest)
        return jnp.einsum(
            "...k,kz->...z", combine(partial_value, width), inverse_z, precision=highest
        )

    def spectral(state_fields, base_fields):
        state_modes = yz_forward(state_fields)[:, :, None]
        base_modes = yz_forward(base_fields)[:, :, None]
        state_got = lax.all_to_all(
            state_modes, ("slab", "comp"), split_axis=4, concat_axis=2, tiled=True
        )
        base_got = lax.all_to_all(
            base_modes, ("slab", "comp"), split_axis=4, concat_axis=2, tiled=True
        )
        item_count = state_got.shape[0]
        part_count = state_got.shape[1]
        state_split = state_got.reshape(
            item_count, part_count, slab_count, 2, slab_rows, rows_per_block, 2 * width
        )
        state_partial = jnp.einsum(
            "srpx,ijpcxyk->sijcryk", table_ahead, state_split, precision=highest
        )
        base_lined = base_got.reshape(item_count, 1, grid_points, rows_per_block, 2 * width)
        base_partial = jnp.einsum("srx,ijxyk->sijryk", forward_x, base_lined, precision=highest)
        return (combine(state_partial, width), combine(base_partial, width))

    state_first, base_first = spectral(own_state[:, None], base_half[:, None])
    state_hat = state_first[:, 0] * keep_mask
    base_hat = base_first[:, 0] * keep_mask
    grad_hat = jnp.stack(
        [
            times_unit(base_hat, float_x, width),
            times_unit(base_hat, float_y, width),
            times_unit(base_hat, float_z, width),
        ],
        axis=1,
    )
    grad_hat = grad_hat.reshape(9, grid_points, rows_per_block, 2 * width)
    grad_partial = jnp.einsum("sxr,iryk->sixyk", inverse_x, grad_hat, precision=highest)
    grad_spread = combine(grad_partial, width).reshape(
        9, group_count, half_rows, rows_per_block, 2 * width
    )
    own_rows = yz_inverse(
        lax.all_to_all(grad_spread, ("slab", "comp"), split_axis=1, concat_axis=3, tiled=True)[:, 0]
    )
    other_rows = swapped(own_rows, "comp", 0)
    gradient = jnp.where(
        core_side == 0,
        jnp.concatenate([own_rows, other_rows], axis=1),
        jnp.concatenate([other_rows, own_rows], axis=1),
    )
    gradient = gradient.reshape(3, 3, slab_rows, grid_points, grid_points)
    gradient_half = lax.dynamic_slice_in_dim(gradient, core_side * half_rows, half_rows, 2)
    flux_terms = own_state[:, None] * base_whole[None, :]
    coupling_matrix = jnp.where(core_side == 0, gradient, jnp.swapaxes(gradient, 0, 1))
    coupling = jnp.sum(coupling_matrix * own_state[None, :], axis=1)
    forcing_phase = phases(wavenumber, grid_index, grid_points)[0]
    forcing = forcing_amp * jnp.sin(forcing_phase)[None, :, None]
    base_drive = jnp.sum(gradient_half * base_half[None, :], axis=1)
    base_drive = jnp.concatenate([base_drive[:1] - forcing[None], base_drive[1:]], axis=0)
    state_fields = jnp.concatenate([flux_terms, coupling[:, None]], axis=1)
    drive_modes, base_modes_two = spectral(state_fields, base_drive[:, None])
    orient = jnp.array([1.0, -1.0], dtype=jnp.float32)[None, :, None, None, None]
    divergence = (
        times_unit(drive_modes[:, 0], float_x, width)
        + times_unit(drive_modes[:, 1], float_y, width)
        + times_unit(drive_modes[:, 2], float_z, width)
    )
    state_drive = keep_mask * (orient * divergence + drive_modes[:, 3])
    new_hat = damping * project(state_hat - time_step * state_drive)
    base_new_hat = damping * project(base_hat - time_step * keep_mask * base_modes_two[:, 0])
    state_partial = jnp.einsum("spxr,icryk->sipcxyk", table_back, new_hat, precision=highest)
    state_back = combine(state_partial, width).reshape(
        3, group_count, slab_rows, rows_per_block, 2 * width
    )
    base_partial = jnp.einsum("sxr,iryk->sixyk", inverse_x, base_new_hat, precision=highest)
    base_back = combine(base_partial, width).reshape(
        3, group_count, half_rows, rows_per_block, 2 * width
    )
    state_got = lax.all_to_all(
        state_back, ("slab", "comp"), split_axis=1, concat_axis=3, tiled=True
    )
    base_got = lax.all_to_all(base_back, ("slab", "comp"), split_axis=1, concat_axis=3, tiled=True)
    state_new = yz_inverse(state_got[:, 0])
    base_new = yz_inverse(base_got[:, 0])
    base_later, later_state = shifted((base_half, own_state), "seg", -1)
    prior_state = shifted(own_state, "seg", 1)
    neighbour = jnp.where(core_side == 0, later_state, prior_state)
    base_gap = (base_new - base_later).reshape(1, 3, half_rows, grid_points * grid_points)
    state_gap = (state_new - neighbour).reshape(1, 1, 3, slab_rows, grid_points * grid_points)
    return (base_gap, state_gap)


def solution(mesh):
    return jax.shard_map(
        body,
        mesh=mesh,
        in_specs=(
            P(("groups", "seg"), None, "slab", None),
            P(("groups", "seg"), "comp", None, "slab", None),
            P("groups"),
            P("groups"),
        ),
        out_specs=(
            P(("groups", "seg"), None, ("slab", "comp"), None),
            P(("groups", "seg"), "comp", None, "slab", None),
        ),
        check_vma=False,
    )
```

profile of v0, /device:TPU:0, one launch (start us, length us, event | category | flops | bytes accessed | tf_op | source)
XLA Modules:
  0.0 482.5 jit_solution(9221279356138996617)
XLA Ops:
  10.7 4.4 all-to-all-start
  19.8 4.3 all-to-all-done
  34.8 7.3 %convolution_bitcast_fusion = f32[2,9,64,11,64]{2,4,0,3,1:T(8,128)S(1)} fusion(f32[9,64,11,64,1]{3,1,4,2,0:T(8,128)} %bitcast.400, f32[1,64,64]{2,1,0:T(8,128)S(1)} %get-tuple-element.106, f32[1,64,64]{2,1,0:T(8,128)S(1)} %copy-done.32), kind=kOutput, calls=%fused_computation.53 | convolution fusion | flops 622870528 | bytes 4898816 | tf_op jit(solution)/shard_map/sxr,iryk->sixyk/dot_general | solution.py:185
  52.4 4.4 all-to-all-start.1
  60.8 16.7 %all-to-all-done.1 = f32[4,1,101376]{2,1,0:T(1,128)} async-done(((f32[4,1,101376]{2,1,0:T(1,128)}), f32[4,1,101376]{2,1,0:T(1,128)}, u32[]{:S(2)}, u32[]{:S(2)}) %all-to-all-start.1) | async-done | bytes 1622048 | tf_op jit(solution)/shard_map/all_to_all | solution.py:190
  77.5 7.5 %reduce.1 = f32[4,101376]{1,0:T(4,128)} reduce(f32[4,1,101376]{2,1,0:T(1,128)} %all-to-all-done.1, f32[]{:T(128)} %broadcast.833), dimensions={1}, to_apply=%all_to_all.80.reduce_sub_computation | reduce | bytes 3244036 | tf_op jit(solution)/shard_map/all_to_all | solution.py:190
  85.0 4.3 reshape.640
  91.6 8.0 %fusion.22 = f32[2,9,16,64,64]{3,4,0,2,1:T(8,128)S(1)} fusion(f32[9,16,44,64,1]{3,1,2,0,4:T(8,128)S(1)} %bitcast.399, f32[1,64,44]{1,2,0:T(8,128)S(1)} %get-tuple-element.98, f32[1,64,44]{1,2,0:T(8,128)S(1)} %get-tuple-element.97, f32[44]{0:T(128)S(1)} %compare_convert_fusion), kind=kOutput, calls=%fused_computation.39 | convolution fusion | flops 622871040 | bytes 6363312 | tf_op jit(solution)/shard_map/syr,...rk->s...yk/dot_general | solution.py:147
  99.6 3.6 slice_bitcast_fusion.5
  103.2 3.6 slice_subtract_fusion.3
  106.8 9.4 %fusion.16 = f32[9,16,64,64]{3,2,1,0:T(8,128)} fusion(f32[9,16,64,32]{2,3,1,0:T(8,128)S(1)} %get-tuple-element.17, f32[9,16,64,32]{2,3,1,0:T(8,128)S(1)} %get-tuple-element.16, f32[32,64]{1,0:T(8,128)S(1)} %get-tuple-element.94, f32[32,64]{1,0:T(8,128)S(1)} %get-tuple-element.93), kind=kOutput, calls=%fused_computation.29 | convolution fusion | flops 453582848 | bytes 4734976 | tf_op jit(solution)/shard_map/...k,kz->...z/dot_general | solution.py:148
  116.3 9.1 %fusion.125 = f32[64,3,32,64]{3,0,2,1:T(8,128)S(1)} fusion(f32[3,32,64,64]{3,2,1,0:T(8,128)S(1)} %reshape.604, f32[64,64]{1,0:T(8,128)S(1)} %pad_maximum_fusion.21), kind=kOutput, calls=%fused_computation.263 | convolution fusion | flops 301989888 | bytes 3162112 | tf_op jit(solution)/shard_map/...z,zk->...k/dot_general | solution.py:140
  125.4 9.5 %fusion.32 = f32[2,3,1,32,44,64]{5,4,0,3,1,2:T(8,128)S(1)} fusion(f32[64,3,32,64]{3,0,2,1:T(8,128)S(1)} %fusion.125, f32[1,44,64]{2,1,0:T(8,128)S(1)} %get-tuple-element.103, f32[1,44,64]{2,1,0:T(8,128)S(1)} %get-tuple-element.102, f32[44]{0:T(128)S(1)} %compare_convert_fusion), kind=kOutput, calls=%fused_computation.63 | convolution fusion | flops 415247360 | bytes 3758256 | tf_op jit(solution)/shard_map/sry,...yk->s...rk/dot_general | solution.py:141
  143.0 9.2 %maximum_select_fusion = f32[3,3,32,64,64]{4,3,2,1,0:T(8,128)S(1)} fusion(f32[3,3,16,64,64]{4,3,2,1,0:T(8,128)} %bitcast.50, f32[3,3,16,64,64]{4,3,2,1,0:T(8,128)} %bitcast.49, pred[]{:T(512)S(6)} %eq.23), kind=kLoop, calls=%fused_computation.16 | loop fusion | flops 3538944 | bytes 9437185 | tf_op jit(solution)/shard_map/jit(_where)/select_n | solution.py:193
  154.3 9.4 %broadcast_multiply_fusion = (f32[3,3,32,64,64]{4,3,2,1,0:T(8,128)}, f32[3,32,64,64]{3,2,1,0:T(8,128)}) fusion(f32[3,32,64,64]{3,2,1,0:T(8,128)} %copy-done.2, f32[3,32,64,64]{3,2,1,0:T(8,128)} %copy-done, f32[3,3,32,64,64]{4,3,2,1,0:T(8,128)S(1)} %maximum_select_fusion, pred[]{:T(512)S(6)} %eq.23), kind=kLoop, calls=%fused_computation.33 | loop fusion | flops 4325376 | bytes 14155777 | tf_op jit(solution)/shard_map/mul | solution.py:200
  174.2 4.1 all-to-all-start.2
  178.4 13.1 %fusion = f32[3,4,32,64,64]{4,3,2,1,0:T(8,128)S(1)} fusion(f32[3,1,32,64,64]{4,3,2,1,0:T(8,128)S(1)} %bitcast.404, f32[3,3,32,64,64]{4,3,2,1,0:T(8,128)} %get-tuple-element.43, f32[64,64]{1,0:T(8,128)} %copy-done.19), kind=kOutput, calls=%fused_computation | convolution fusion | flops 1209532416 | bytes 12599296 | tf_op jit(solution)/shard_map/...z,zk->...k/dot_general | solution.py:140
  191.5 17.0 %fusion.10 = f32[2,3,4,32,44,64]{5,4,0,3,2,1:T(8,128)S(1)} fusion(f32[3,4,32,64,64]{4,3,2,1,0:T(8,128)S(1)} %fusion, f32[1,44,64]{2,1,0:T(8,128)S(1)} %copy-done.27, f32[1,44,64]{2,1,0:T(8,128)S(1)} %copy-done.24, f32[44]{0:T(128)S(1)} %compare_convert_fusion), kind=kOutput, calls=%fused_computation.25 | convolution fusion | flops 1660955648 | bytes 14964912 | tf_op jit(solution)/shard_map/sry,...yk->s...rk/dot_general | solution.py:141
  208.6 7.3 %slice_bitcast_fusion.1 = (f32[3,4,32,44,64]{4,3,2,1,0:T(8,128)}, f32[3,4,32,44,64]{4,3,2,1,0:T(8,128)}) fusion(f32[2,3,4,32,44,64]{5,4,0,3,2,1:T(8,128)S(1)} %fusion.10), kind=kLoop, calls=%fused_computation.15 | loop fusion | bytes 17301504 | tf_op jit(solution)/shard_map/squeeze | solution.py:38
  215.9 3.5 all-to-all-start.4
  235.1 4.3 all-to-all-start.3
  239.5 23.0 %slice_subtract_fusion = (f32[3,4,32,44,32]{4,3,2,1,0:T(8,128)}, f32[3,4,32,44,32]{4,3,2,1,0:T(8,128)}) fusion(f32[3,4,32,44,64]{4,3,2,1,0:T(8,128)} %get-tuple-element.11, f32[3,4,32,44,64]{4,3,2,1,0:T(8,128)} %get-tuple-element.10), kind=kLoop, calls=%fused_computation.13 | loop fusion | flops 1081344 | bytes 12976128 | tf_op jit(solution)/shard_map/sub | solution.py:40
  262.5 12.6 %maximum_bitcast_fusion = f32[3,4,1,32,44,64]{5,4,3,1,0,2:T(8,128)} fusion(f32[3,4,32,44,32]{4,3,2,1,0:T(8,128)} %get-tuple-element.9, f32[3,4,32,44,32]{4,3,2,1,0:T(8,128)} %get-tuple-element.8), kind=kLoop, calls=%fused_computation.17 | loop fusion | flops 1081344 | bytes 8650752 | tf_op jit(solution)/shard_map/broadcast_in_dim | solution.py:153
  275.0 9.9 %copy.208 = f32[3,4,1,32,44,64]{5,3,2,1,0,4:T(8,128)} copy(f32[3,4,1,32,44,64]{5,4,3,1,0,2:T(8,128)} %maximum_bitcast_fusion) | data formatting | bytes 8650752 | tf_op jit(solution)/shard_map/broadcast_in_dim | solution.py:153
  284.9 8.8 %reshape.645 = f32[4,1,270336]{2,1,0:T(1,128)} reshape(f32[44,3,4,1,32,64]{5,4,3,2,1,0:T(8,128)} %bitcast.397) | data formatting | bytes 8650752
  293.7 5.1 %all-to-all-start.5 = ((f32[4,1,270336]{2,1,0:T(1,128)}), f32[4,1,270336]{2,1,0:T(1,128)}, u32[]{:S(2)}, u32[]{:S(2)}) async-start(f32[4,1,270336]{2,1,0:T(1,128)} %reshape.645), calls=%async_computation.5 | async-start | bytes 8650752 | tf_op jit(solution)/shard_map/all_to_all | solution.py:155
  298.8 4.3 collective-permute-start.1
  309.0 5.7 %reduce.5 = f32[4,67584]{1,0:T(4,128)} reduce(f32[4,1,67584]{2,1,0:T(1,128)} %copy-done.11, f32[]{:T(128)} %broadcast.833), dimensions={1}, to_apply=%all_to_all.89.reduce_sub_computation | reduce | bytes 2162692 | tf_op jit(solution)/shard_map/all_to_all | solution.py:155
  314.6 3.6 reshape.648
  318.3 5.2 %convolution_bitcast_fusion.3 = f32[2,3,1,2,64,11,64]{4,6,0,5,3,1,2:T(8,128)S(1)} fusion(f32[3,2,2,32,11,64,1]{5,3,0,4,2,1,6:T(8,128)} %bitcast.405, f32[1,64,2,32]{1,3,2,0:T(8,128)} %get-tuple-element.92, f32[1,64,2,32]{1,3,2,0:T(8,128)S(1)} %get-tuple-element.91), kind=kOutput, calls=%fused_computation.65 | convolution fusion | flops 415244288 | bytes 3276800 | tf_op jit(solution)/shard_map/srpx,ijpcxyk->sijcryk/dot_general | solution.py:166
  325.9 3.9 reduce.3
  333.6 4.9 %convolution_bitcast_fusion.4 = f32[2,3,16,64,64]{3,4,0,2,1:T(8,128)} fusion(f32[3,16,44,64,1]{3,1,2,0,4:T(8,128)S(1)} %bitcast.410, f32[1,64,44]{1,2,0:T(8,128)S(1)} %copy-done.31, f32[1,64,44]{1,2,0:T(8,128)S(1)} %copy-done.29, f32[44]{0:T(128)S(1)} %copy-done.44), kind=kOutput, calls=%fused_computation.97 | convolution fusion | flops 207634944 | bytes 2136240 | tf_op jit(solution)/shard_map/syr,...rk->s...yk/dot_general | solution.py:147
  338.5 10.0 %all-to-all-done.5 = f32[4,1,270336]{2,1,0:T(1,128)} async-done(((f32[4,1,270336]{2,1,0:T(1,128)}), f32[4,1,270336]{2,1,0:T(1,128)}, u32[]{:S(2)}, u32[]{:S(2)}) %all-to-all-start.5) | async-done | bytes 4325408 | tf_op jit(solution)/shard_map/all_to_all | solution.py:155
  348.5 15.2 %reduce.4 = f32[4,270336]{1,0:T(4,128)} reduce(f32[4,1,270336]{2,1,0:T(1,128)} %all-to-all-done.5, f32[]{:T(128)} %broadcast.833), dimensions={1}, to_apply=%all_to_all.92.reduce_sub_computation | reduce | bytes 8650756 | tf_op jit(solution)/shard_map/all_to_all | solution.py:155
  363.6 9.6 %reshape.646 = f32[44,3,4,1,32,64]{5,4,3,2,1,0:T(8,128)} reshape(f32[4,270336]{1,0:T(4,128)} %reduce.4) | data formatting | bytes 8650752
  373.2 16.6 %fusion.13 = f32[2,3,4,2,64,11,64]{4,6,5,3,1,2,0:T(8,128)S(1)} fusion(f32[3,4,2,2,32,11,64,1]{6,4,1,0,5,3,2,7:T(8,128)} %bitcast.396, f32[1,64,2,32]{1,3,2,0:T(8,128)} %get-tuple-element.92, f32[1,64,2,32]{1,3,2,0:T(8,128)} %copy-done.36), kind=kOutput, calls=%fused_computation.26 | convolution fusion | flops 1660952576 | bytes 13008896 | tf_op jit(solution)/shard_map/srpx,ijpcxyk->sijcryk/dot_general | solution.py:166
  389.8 6.9 %slice_bitcast_fusion.3 = (f32[3,4,2,64,11,64]{3,5,4,2,0,1:T(8,128)}, f32[3,4,2,64,11,64]{3,5,4,2,0,1:T(8,128)}) fusion(f32[2,3,4,2,64,11,64]{4,6,5,3,1,2,0:T(8,128)S(1)} %fusion.13), kind=kLoop, calls=%fused_computation.22 | loop fusion | bytes 17301504 | tf_op jit(solution)/shard_map/squeeze | solution.py:38
  396.8 12.5 %slice_subtract_fusion.1 = (f32[3,4,2,64,11,32]{3,5,4,2,0,1:T(8,128)}, f32[3,4,2,64,11,32]{3,5,4,2,0,1:T(8,128)}) fusion(f32[3,4,2,64,11,64]{3,5,4,2,0,1:T(8,128)} %get-tuple-element.15, f32[3,4,2,64,11,64]{3,5,4,2,0,1:T(8,128)} %get-tuple-element.14), kind=kLoop, calls=%fused_computation.36 | loop fusion | flops 1081344 | bytes 12976128 | tf_op jit(solution)/shard_map/sub | solution.py:40
  409.3 3.6 fusion.36
  420.2 6.3 %convolution_bitcast_fusion.2 = f32[2,3,2,2,32,11,64]{6,4,2,0,5,3,1:T(8,128)S(1)} fusion(f32[1,2,64,11,64]{2,4,3,1,0:T(8,128)S(1)} %get-tuple-element.50, f32[1,2,64,11,64]{2,4,3,1,0:T(8,128)S(1)} %get-tuple-element.49, f32[1,2,64,11,64]{2,4,3,1,0:T(8,128)S(1)} %get-tuple-element.2, f32[64,11,64]{0,2,1:T(8,128)S(1)} %get-tuple-element.108, ...), kind=kOutput, calls=%fused_computation.64 | convolution fusion | flops 416063488 | bytes 3457024 | tf_op jit(solution)/shard_map/spxr,icryk->sipcxyk/dot_general | solution.py:218
  430.6 4.2 reshape.649
  434.8 4.5 all-to-all-start.6
  442.1 5.2 %fusion.66 = f32[3,16,64,64]{3,2,1,0:T(8,128)} fusion(f32[3,16,64,64]{3,2,1,0:T(8,128)} %collective-permute-done.1, f32[3,16,64,32]{2,3,1,0:T(8,128)S(1)} %get-tuple-element.46, f32[3,16,64,32]{2,3,1,0:T(8,128)S(1)} %get-tuple-element.45, f32[32,64]{1,0:T(8,128)S(1)} %copy-done.40, f32[32,64]{1,0:T(8,128)S(1)} %copy-done.38), kind=kOutput, calls=%fused_computation.119 | convolution fusion | flops 151396352 | bytes 2375680 | tf_op jit(solution)/shard_map/...k,kz->...z/dot_general | solution.py:148
  450.1 3.9 all-to-all-done.6
  453.9 5.6 %reduce.6 = f32[4,67584]{1,0:T(4,128)} reduce(f32[4,1,67584]{2,1,0:T(1,128)} %all-to-all-done.6, f32[]{:T(128)} %broadcast.833), dimensions={1}, to_apply=%all_to_all.95.reduce_sub_computation | reduce | bytes 2162692 | tf_op jit(solution)/shard_map/all_to_all | solution.py:226
  459.6 3.6 reshape.650
  464.9 6.4 %convolution_bitcast_fusion.1 = f32[2,3,32,64,64]{3,4,0,2,1:T(8,128)S(1)} fusion(f32[3,32,44,64,1]{3,1,2,0,4:T(8,128)S(1)} %bitcast.398, f32[1,64,44]{1,2,0:T(8,128)S(1)} %copy-done.31, f32[1,64,44]{1,2,0:T(8,128)S(1)} %copy-done.29, f32[44]{0:T(128)S(1)} %copy-done.45), kind=kOutput, calls=%fused_computation.54 | convolution fusion | flops 415252992 | bytes 4249776 | tf_op jit(solution)/shard_map/syr,...rk->s...yk/dot_general | solution.py:147
  473.5 6.7 %select_subtract_fusion = f32[3,32,64,64]{3,2,1,0:T(8,128)S(1)} fusion(f32[3,32,64,64]{3,2,1,0:T(8,128)} %collective-permute-done.2, f32[3,32,64,64]{3,2,1,0:T(8,128)} %collective-permute-done.3, pred[]{:T(512)S(6)} %eq.23, f32[32,64]{1,0:T(8,128)S(1)} %copy-done.40, f32[32,64]{1,0:T(8,128)S(1)} %copy-done.38, f32[3,32,64,32]{2,3,1,0:T(8,128)S(1)} %get-tuple-element.28, ...), kind=kOutput, calls=%fused_computation.52 | convolution fusion | flops 303177728 | bytes 6307841 | tf_op jit(solution)/shard_map/...k,kz->...z/dot_general | solution.py:148
  (280 shorter events, 111.5 us)
Async XLA Ops:
  0.6 16.8 %copy-start.52 = (s32[44]{0:T(128)}, s32[44]{0:T(128)S(1)}, u32[]{:S(2)}) copy-start(s32[44]{0:T(128)S(1)} %compare_select_fusion.7) | copy-start | bytes 532
  0.7 190.9 %copy-start.43 = (f32[44]{0:T(128)}, f32[44]{0:T(128)S(1)}, u32[]{:S(2)}) copy-start(f32[44]{0:T(128)S(1)} %compare_convert_fusion) | copy-start | bytes 532
  3.5 121.9 %copy-start.22 = (f32[1,44,64]{2,1,0:T(8,128)}, f32[1,44,64]{2,1,0:T(8,128)S(1)}, u32[]{:S(2)}) copy-start(f32[1,44,64]{2,1,0:T(8,128)S(1)} %get-tuple-element.102) | copy-start | bytes 33796
  3.5 121.9 %copy-start.25 = (f32[1,44,64]{2,1,0:T(8,128)}, f32[1,44,64]{2,1,0:T(8,128)S(1)}, u32[]{:S(2)}) copy-start(f32[1,44,64]{2,1,0:T(8,128)S(1)} %get-tuple-element.103) | copy-start | bytes 33796
  3.8 112.5 %copy-start.19 = (f32[64,64]{1,0:T(8,128)}, f32[64,64]{1,0:T(8,128)S(1)}, u32[]{:S(2)}) copy-start(f32[64,64]{1,0:T(8,128)S(1)} %pad_maximum_fusion.21) | copy-start | bytes 49156
  8.8 7.4 %copy-start.56 = (s32[3]{0:T(128)S(1)}, s32[3]{0:T(128)}, u32[]{:S(2)}) copy-start(s32[3]{0:T(128)} %param.8) | copy-start | bytes 40
  10.7 13.4 %all-to-all-start = ((f32[4,1,33792]{2,1,0:T(1,128)}), f32[4,1,33792]{2,1,0:T(1,128)S(1)}, u32[]{:S(2)}, u32[]{:S(2)}) async-start(f32[4,1,33792]{2,1,0:T(1,128)} %reshape.637), calls=%async_computation | async-start | bytes 1081344 | tf_op jit(solution)/shard_map/all_to_all | solution.py:158
  15.1 291.2 %copy-start.48 = (f32[64]{0:T(128)}, f32[64]{0:T(128)S(1)}, u32[]{:S(2)}) copy-start(f32[64]{0:T(128)S(1)} %fusion.194) | copy-start | bytes 772
  15.3 12.2 %copy-start.34 = (f32[1,64,64]{2,1,0:T(8,128)}, f32[1,64,64]{2,1,0:T(8,128)S(1)}, u32[]{:S(2)}) copy-start(f32[1,64,64]{2,1,0:T(8,128)S(1)} %get-tuple-element.107) | copy-start | bytes 49156
  15.3 14.8 %copy-start.57 = (f32[64]{0:T(128)}, f32[64]{0:T(128)S(1)}, u32[]{:S(2)}) copy-start(f32[64]{0:T(128)S(1)} %fusion.195) | copy-start | bytes 772
  15.5 14.6 %copy-start.54 = (f32[11]{0:T(128)}, f32[11]{0:T(128)S(1)}, u32[]{:S(2)}) copy-start(f32[11]{0:T(128)S(1)} %get-tuple-element.6) | copy-start | bytes 136
  15.5 290.8 %copy-start.46 = (f32[11]{0:T(128)}, f32[11]{0:T(128)S(1)}, u32[]{:S(2)}) copy-start(f32[11]{0:T(128)S(1)} %get-tuple-element.7) | copy-start | bytes 136
  19.7 10.2 %copy-start.14 = (f32[64,11,64]{0,2,1:T(8,128)}, f32[64,11,64]{0,2,1:T(8,128)S(1)}, u32[]{:S(2)}) copy-start(f32[64,11,64]{0,2,1:T(8,128)S(1)} %get-tuple-element.86) | copy-start | bytes 540676
  19.7 285.6 %copy-start.50 = (f32[32]{0:T(128)}, f32[32]{0:T(128)S(1)}, u32[]{:S(2)}) copy-start(f32[32]{0:T(128)S(1)} %slice_convert_fusion) | copy-start | bytes 388
  19.7 10.3 %copy-start.59 = (f32[32]{0:T(128)}, f32[32]{0:T(128)S(1)}, u32[]{:S(2)}) copy-start(f32[32]{0:T(128)S(1)} %get-tuple-element.96) | copy-start | bytes 388
  19.8 120.8 %copy-start.63 = (f32[32]{0:T(128)}, f32[32]{0:T(128)S(1)}, u32[]{:S(2)}) copy-start(f32[32]{0:T(128)S(1)} %get-tuple-element.95) | copy-start | bytes 388
  52.4 25.1 %all-to-all-start.1 = ((f32[4,1,101376]{2,1,0:T(1,128)}), f32[4,1,101376]{2,1,0:T(1,128)}, u32[]{:S(2)}, u32[]{:S(2)}) async-start(f32[4,1,101376]{2,1,0:T(1,128)} %reshape.639), calls=%async_computation.1 | async-start | bytes 3244032 | tf_op jit(solution)/shard_map/all_to_all | solution.py:190
  56.9 83.7 %copy-start.64 = (f32[11]{0:T(128)}, f32[11]{0:T(128)S(1)}, u32[]{:S(2)}) copy-start(f32[11]{0:T(128)S(1)} %mul.711) | copy-start | bytes 136
  60.4 55.8 %copy-start = (f32[3,32,64,64]{3,2,1,0:T(8,128)}, f32[3,32,64,64]{3,2,1,0:T(8,128)S(1)}, u32[]{:S(2)}) copy-start(f32[3,32,64,64]{3,2,1,0:T(8,128)S(1)} %reshape.604) | copy-start | bytes 4718596
  60.6 46.2 %copy-start.37 = (f32[32,64]{1,0:T(8,128)}, f32[32,64]{1,0:T(8,128)S(1)}, u32[]{:S(2)}) copy-start(f32[32,64]{1,0:T(8,128)S(1)} %get-tuple-element.93) | copy-start | bytes 24580
  60.6 46.2 %copy-start.39 = (f32[32,64]{1,0:T(8,128)}, f32[32,64]{1,0:T(8,128)S(1)}, u32[]{:S(2)}) copy-start(f32[32,64]{1,0:T(8,128)S(1)} %get-tuple-element.94) | copy-start | bytes 24580
  60.8 30.8 %copy-start.28 = (f32[1,64,44]{1,2,0:T(8,128)}, f32[1,64,44]{1,2,0:T(8,128)S(1)}, u32[]{:S(2)}) copy-start(f32[1,64,44]{1,2,0:T(8,128)S(1)} %get-tuple-element.97) | copy-start | bytes 33796
  60.8 30.8 %copy-start.30 = (f32[1,64,44]{1,2,0:T(8,128)}, f32[1,64,44]{1,2,0:T(8,128)S(1)}, u32[]{:S(2)}) copy-start(f32[1,64,44]{1,2,0:T(8,128)S(1)} %get-tuple-element.98) | copy-start | bytes 33796
  116.2 26.8 %collective-permute-start = (f32[9,16,64,64]{3,2,1,0:T(8,128)}, f32[9,16,64,64]{3,2,1,0:T(8,128)}, u32[]{:S(2)}, u32[]{:S(2)}) collective-permute-start(f32[9,16,64,64]{3,2,1,0:T(8,128)} %fusion.16), channel_id=1, source_target_pairs={{0,1},{1,0},{2,3},{3,2},{4,5},{5,4},{6,7},{7,6},{8,9},{9,8},{10,11... | collective-permute-start | bytes 7077896 | tf_op jit(solution)/shard_map/ppermute | solution.py:18
  143.0 9.2 %copy-start.4 = (f32[3,16,64,64]{3,2,1,0:T(8,128)S(1)}, f32[3,16,64,64]{3,2,1,0:T(8,128)}, u32[]{:S(2)}) copy-start(f32[3,16,64,64]{3,2,1,0:T(8,128)} %copy-done.3) | copy-start | bytes 2359300
  170.2 8.2 %copy-start.5 = (f32[3,32,64,64]{3,2,1,0:T(8,128)S(1)}, f32[3,32,64,64]{3,2,1,0:T(8,128)}, u32[]{:S(2)}) copy-start(f32[3,32,64,64]{3,2,1,0:T(8,128)} %get-tuple-element.44) | copy-start | bytes 4718596
  174.2 41.7 %all-to-all-start.2 = ((f32[4,1,33792]{2,1,0:T(1,128)}), f32[4,1,33792]{2,1,0:T(1,128)}, u32[]{:S(2)}, u32[]{:S(2)}) async-start(f32[4,1,33792]{2,1,0:T(1,128)} %reshape.641), calls=%async_computation.2 | async-start | bytes 1081344 | tf_op jit(solution)/shard_map/all_to_all | solution.py:158
  178.4 13.1 %copy-start.24 = (f32[1,44,64]{2,1,0:T(8,128)S(1)}, f32[1,44,64]{2,1,0:T(8,128)}, u32[]{:S(2)}) copy-start(f32[1,44,64]{2,1,0:T(8,128)} %copy-done.22) | copy-start | bytes 33796
  178.4 13.1 %copy-start.27 = (f32[1,44,64]{2,1,0:T(8,128)S(1)}, f32[1,44,64]{2,1,0:T(8,128)}, u32[]{:S(2)}) copy-start(f32[1,44,64]{2,1,0:T(8,128)} %copy-done.25) | copy-start | bytes 33796
  215.9 19.2 %all-to-all-start.4 = ((f32[4,1,67584]{2,1,0:T(1,128)}), f32[4,1,67584]{2,1,0:T(1,128)S(1)}, u32[]{:S(2)}, u32[]{:S(2)}) async-start(f32[4,1,67584]{2,1,0:T(1,128)} %reshape.647), calls=%async_computation.4 | async-start | bytes 2162688 | tf_op jit(solution)/shard_map/all_to_all | solution.py:155
  235.1 27.3 %copy-start.11 = (f32[4,1,67584]{2,1,0:T(1,128)}, f32[4,1,67584]{2,1,0:T(1,128)S(1)}, u32[]{:S(2)}) copy-start(f32[4,1,67584]{2,1,0:T(1,128)S(1)} %all-to-all-done.4) | copy-start | bytes 3244036
  235.1 58.5 %all-to-all-start.3 = ((f32[4,1,33792]{2,1,0:T(1,128)}), f32[4,1,33792]{2,1,0:T(1,128)}, u32[]{:S(2)}, u32[]{:S(2)}) async-start(f32[4,1,33792]{2,1,0:T(1,128)} %reshape.643), calls=%async_computation.3 | async-start | bytes 1081344 | tf_op jit(solution)/shard_map/all_to_all | solution.py:229
  293.7 9.5 %copy-start.1 = (f32[3,32,64,64]{3,2,1,0:T(8,128)S(1)}, f32[3,32,64,64]{3,2,1,0:T(8,128)}, u32[]{:S(2)}) copy-start(f32[3,32,64,64]{3,2,1,0:T(8,128)} %copy-done) | copy-start | bytes 4718596
  293.7 54.8 %all-to-all-start.5 = ((f32[4,1,270336]{2,1,0:T(1,128)}), f32[4,1,270336]{2,1,0:T(1,128)}, u32[]{:S(2)}, u32[]{:S(2)}) async-start(f32[4,1,270336]{2,1,0:T(1,128)} %reshape.645), calls=%async_computation.5 | async-start | bytes 8650752 | tf_op jit(solution)/shard_map/all_to_all | solution.py:155
  298.8 142.9 %collective-permute-start.1 = (f32[3,16,64,64]{3,2,1,0:T(8,128)}, f32[3,16,64,64]{3,2,1,0:T(8,128)}, u32[]{:S(2)}, u32[]{:S(2)}) collective-permute-start(f32[3,16,64,64]{3,2,1,0:T(8,128)} %copy-done.3), channel_id=1, source_target_pairs={{4,0},{8,4},{12,8},{0,12},{5,1},{9,5},{13,9},{1,13},{6,2},{10,6},{... | collective-permute-start | bytes 2359304 | tf_op jit(solution)/shard_map/ppermute | solution.py:24
  303.2 170.1 %collective-permute-start.2 = (f32[3,32,64,64]{3,2,1,0:T(8,128)S(1)}, f32[3,32,64,64]{3,2,1,0:T(8,128)}, u32[]{:S(2)}, u32[]{:S(2)}) collective-permute-start(f32[3,32,64,64]{3,2,1,0:T(8,128)S(1)} %copy-done.1), channel_id=1, source_target_pairs={{4,0},{8,4},{12,8},{0,12},{5,1},{9,5},{13,9},{1,13},{6,2},{10,6},{... | collective-permute-start | bytes 4718600 | tf_op jit(solution)/shard_map/ppermute | solution.py:24
  303.6 169.9 %collective-permute-start.3 = (f32[3,32,64,64]{3,2,1,0:T(8,128)S(1)}, f32[3,32,64,64]{3,2,1,0:T(8,128)}, u32[]{:S(2)}, u32[]{:S(2)}) collective-permute-start(f32[3,32,64,64]{3,2,1,0:T(8,128)S(1)} %copy-done.1), channel_id=1, source_target_pairs={{12,0},{0,4},{4,8},{8,12},{13,1},{1,5},{5,9},{9,13},{14,2},{2,6},{... | collective-permute-start | bytes 4718600 | tf_op jit(solution)/shard_map/ppermute | solution.py:24
  308.1 10.1 %copy-start.36 = (f32[1,64,2,32]{1,3,2,0:T(8,128)}, f32[1,64,2,32]{1,3,2,0:T(8,128)S(1)}, u32[]{:S(2)}) copy-start(f32[1,64,2,32]{1,3,2,0:T(8,128)S(1)} %get-tuple-element.91) | copy-start | bytes 49156
  329.8 3.8 copy-start.29
  329.8 3.9 copy-start.31
  409.3 3.7 copy-start.49
  409.3 3.7 copy-start.58
  409.3 4.0 copy-start.47
  409.3 4.0 copy-start.55
  413.0 3.5 slice-start.2
  414.2 3.1 copy-start.15
  414.2 3.1 copy-start.65
  434.8 19.1 %all-to-all-start.6 = ((f32[4,1,67584]{2,1,0:T(1,128)}), f32[4,1,67584]{2,1,0:T(1,128)}, u32[]{:S(2)}, u32[]{:S(2)}) async-start(f32[4,1,67584]{2,1,0:T(1,128)} %reshape.649), calls=%async_computation.6 | async-start | bytes 2162688 | tf_op jit(solution)/shard_map/all_to_all | solution.py:226
  (34 other events, 58.7 us)
where the time goes:
time: 490 us; the launch traced here: 483 us
  other arithmetic  145 us (30%)
  matrix products  137 us (28%)
  local copies, waits for them, and re-layouts  124 us (25%)
  starting transfers between devices  37 us (8%)
  waiting for transfers between devices  35 us (7%)
    unnamed x154, local copies, waits for them, and re-layouts  57.1 us
    sub x14, other arithmetic, combine(): real_part = cosine_part[..., :columns] - sine_part[..., columns:]  47.3 us
    dot_general x4, matrix products, yz_forward(): jnp.einsum('sry,...yk->s...rk', forward_transform_y, along_z, precision=h...  30.7 us
    squeeze x14, local copies, waits for them, and re-layouts, combine(): cosine_part = partial_value[0]  25 us
    dot_general x4, matrix products, yz_forward(): along_z = jnp.einsum('...z,zk->...k', field, forward_z, precision=highest)  25 us
    dot_general x2, matrix products, spectral(): jnp.einsum('srpx,ijpcxyk->sijcryk', table_ahead, state_split, precision=h...  21.8 us
    dot_general x3, matrix products, yz_inverse(): jnp.einsum('...k,kz->...z', combine(partial_value, width), inverse_z, pre...  21.2 us
    all_to_all x2, other arithmetic, spectral(): lax.all_to_all(state_modes, ('slab', 'comp'), split_axis=4, concat_axis=2...  20.8 us
  transfers between devices with their start and end apart: 11, of which 5 were waited for; matrix products, arithmetic and copies ran while one was open for 59% of the time, Pallas kernels for 0%

commit v1 on v0

--- a/solution.py
+++ b/solution.py
@@ -1,14 +1,31 @@
+import functools
+
 import jax
 import jax.numpy as jnp
+import ml_dtypes
+import numpy as np
 from jax import lax
+from jax.experimental import pallas as pl
+from jax.experimental.pallas import tpu as pltpu
 from jax.sharding import PartitionSpec as P
 
 N = 64
-
+HALF = 32
+KEEP = N // 3
+NKZ = KEEP + 1
+NKY = 44
+ROWS = 2 * NKY
+PACKED = NKZ + 3
+LANES = 128
 
 viscosity = 0.025
 time_step = 0.02
 forcing_amp = 10.0
+
+f32 = jnp.float32
+bf16 = jnp.bfloat16
+
+
 highest = lax.Precision.HIGHEST
 
 
@@ -50,7 +67,7 @@
     return jnp.concatenate([values, values], axis=-1)
 
 
-def body(base, state, wavenumber, cutoff):
+def general_body(base, state, wavenumber, cutoff):
     grid_points = N
     base = base.reshape(base.shape[0], 3, base.shape[2], grid_points, grid_points)
     state = state.reshape(
@@ -237,9 +254,500 @@
     return (base_gap, state_gap)
 
 
+def halves(table):
+    high = table.astype(np.float32).astype(ml_dtypes.bfloat16)
+    low = (table - high.astype(np.float64)).astype(ml_dtypes.bfloat16)
+    return high, low
+
+
+def left_table(table, depth):
+    padded = np.zeros((table.shape[0], depth))
+    padded[:, : table.shape[1]] = table
+    high, low = halves(padded)
+    return np.concatenate(
+        [np.concatenate([high, high], 1), np.concatenate([low, np.zeros_like(low)], 1)], 0
+    )
+
+
+def right_table(table, depth):
+    return np.ascontiguousarray(left_table(table.T, depth).T)
+
+
+def ky_values():
+    index = np.arange(NKY)
+    wave = np.where(index <= KEEP, index, index - (2 * KEEP + 1))
+    alive = (index <= 2 * KEEP).astype(np.float64)
+    return wave * alive, alive
+
+
+@functools.cache
+def tables():
+    out = {}
+    z = np.arange(N)
+    kz = np.arange(NKZ)
+    angle = 2 * np.pi * kz[:, None] * z[None, :] / N
+    weight = np.where(kz == 0, 1.0, 2.0)[:, None] / N
+    forward = np.zeros((2, 2, NKZ, 2, N))
+    inverse = np.zeros((NKZ, 2, 2, 2, N))
+    turned = np.zeros((NKZ, 2, 2, 2, N))
+    slope = np.zeros((NKZ, 2, 2, 2, N))
+    for y2 in range(2):
+        forward[y2, 0, :, y2] = np.cos(angle)
+        forward[y2, 1, :, y2] = -np.sin(angle)
+        inverse[:, y2, 0, y2] = weight * np.cos(angle)
+        inverse[:, y2, 1, y2] = -weight * np.sin(angle)
+        turned[:, y2, 0, y2] = weight * np.sin(angle)
+        turned[:, y2, 1, y2] = weight * np.cos(angle)
+        slope[:, y2, 0, y2] = -weight * kz[:, None] * np.sin(angle)
+        slope[:, y2, 1, y2] = -weight * kz[:, None] * np.cos(angle)
+    out["fz"] = left_table(forward.reshape(4 * NKZ, 2 * N), 128)
+    out["iz"] = right_table(inverse.reshape(4 * NKZ, 2 * N), 128)
+    out["izr"] = right_table(turned.reshape(4 * NKZ, 2 * N), 128)
+    out["izd"] = right_table(slope.reshape(4 * NKZ, 2 * N), 128)
+    ky, alive = ky_values()
+    y = 2 * np.arange(HALF)[None, :] + np.arange(2)[:, None]
+    phase = 2 * np.pi * ky[:, None, None] * y[None] / N
+    cosine = np.cos(phase) * alive[:, None, None]
+    sine = np.sin(phase) * alive[:, None, None]
+    plain = np.zeros((2, NKY, 2, 2, HALF))
+    plain[0, :, :, 0] = cosine
+    plain[0, :, :, 1] = sine
+    plain[1, :, :, 0] = -sine
+    plain[1, :, :, 1] = cosine
+    rotated = np.stack([-plain[1], plain[0]])
+    out["fy"] = left_table(plain.reshape(ROWS, 128), 128)
+    out["fyr"] = left_table(rotated.reshape(ROWS, 128), 128)
+    back = np.zeros((2, 2, HALF, 2, NKY))
+    cos_t = np.moveaxis(cosine, 0, -1) / N
+    sin_t = np.moveaxis(sine, 0, -1) / N
+    back[:, 0, :, 0] = cos_t
+    back[:, 0, :, 1] = -sin_t
+    back[:, 1, :, 0] = sin_t
+    back[:, 1, :, 1] = cos_t
+    back_slope = np.zeros_like(back)
+    back_slope[..., 0, :] = ky * back[..., 1, :]
+    back_slope[..., 1, :] = -ky * back[..., 0, :]
+    out["iy"] = left_table(back.reshape(128, ROWS), 128)
+    out["iyd"] = left_table(back_slope.reshape(128, ROWS), 128)
+    grad_high, grad_low = [], []
+    x = np.arange(N)
+    apart = x[:HALF, None] - x[None, :]
+    for cut in range(KEEP - 3, KEEP + 1):
+        k = np.arange(cut + 1)
+        wk = np.where(k == 0, 1.0, 2.0) / N
+        arg = 2 * np.pi * apart[..., None] * k / N
+        keep = (np.cos(arg) * wk).sum(-1)
+        derive = (-np.sin(arg) * wk * k).sum(-1)
+        table = np.zeros((2, 4, HALF, 2, 4, HALF))
+        for comp in range(3):
+            for side in range(2):
+                rows = slice(side * HALF, (side + 1) * HALF)
+                table[side, comp, :, 0, comp, :] = keep[:, rows].T
+                table[side, comp, :, 1, comp, :] = derive[:, rows].T
+        high, low = halves(table.reshape(256, 256))
+        grad_high.append(high)
+        grad_low.append(low)
+    out["gxh"] = np.stack(grad_high)
+    out["gxl"] = np.stack(grad_low)
+    kx = np.arange(HALF)
+    live = (kx <= KEEP).astype(np.float64)
+    xl = np.arange(HALF)
+    arg = 2 * np.pi * xl[:, None] * kx[None, :] / N
+    value = np.concatenate([np.cos(arg) * live, np.sin(arg) * live], 1)
+    change = np.concatenate([kx * np.sin(arg) * live, -kx * np.cos(arg) * live], 1)
+
+    def d_of(block):
+        return np.concatenate([kx * block[:, HALF:], -kx * block[:, :HALF]], 1)
+
+    fx = np.zeros((4, 4, HALF, 4, 2, 2 * HALF))
+
+    def put(tile, block, quantity, part, what):
+        fx[tile, block, :, quantity, part] += what
+        if quantity == 0:
+            fx[tile, block, :, 1, part] += -d_of(what)
+
+    put(0, 0, 2, 0, change)
+    put(0, 1, 3, 0, change)
+    put(0, 2, 0, 0, value)
+    put(0, 3, 0, 0, value)
+    put(1, 0, 2, 0, value)
+    put(1, 1, 3, 0, value)
+    put(1, 2, 2, 1, value)
+    put(1, 3, 3, 1, value)
+    put(2, 0, 0, 0, change)
+    put(2, 1, 2, 0, value)
+    put(2, 2, 3, 0, value)
+    put(2, 3, 0, 0, value)
+    put(3, 0, 2, 0, value)
+    put(3, 1, 3, 0, value)
+    put(3, 2, 0, 1, value)
+    out["fxh"], out["fxl"] = halves(fx.reshape(512, 512))
+    inv_high, inv_low = [], []
+    wx = np.where(kx == 0, 1.0, 2.0) * live / N
+    for core in range(2):
+        ix = np.zeros((4, 2, 2 * HALF, 3 * LANES))
+        for side in range(2):
+            xs = np.arange(HALF) + side * HALF
+            arg = 2 * np.pi * kx[:, None] * xs[None, :] / N
+            give = np.concatenate([np.cos(arg) * wx[:, None], np.sin(arg) * wx[:, None]], 0)
+            fall = np.concatenate(
+                [np.sin(arg) * (wx * kx)[:, None], -np.cos(arg) * (wx * kx)[:, None]], 0
+            )
+            own = slice(core * 16, core * 16 + 16)
+            at = side * LANES
+            ix[0, 0, :, at : at + 32] = give
+            ix[1, 0, :, at : at + 32] = fall
+            ix[0, 1, :, at + 32 : at + 48] = give[:, own]
+            ix[1, 1, :, at + 32 : at + 48] = fall[:, own]
+            ix[2, 1, :, at + 48 : at + 64] = give[:, own]
+            ix[2, 0, :, at + 64 : at + 96] = give
+            ix[3, 0, :, at + 96 : at + 128] = give
+            last = 2 * LANES + side * 16
+            ix[3, 1, :, last : last + 16] = give[:, own]
+        high, low = halves(ix.reshape(512, 3 * LANES))
+        inv_high.append(high)
+        inv_low.append(low)
+    out["ixh"] = np.stack(inv_high)
+    out["ixl"] = np.stack(inv_low)
+    ky_rows = np.tile(ky, 2)[:, None]
+    fixed = np.ones((3, ROWS, 4, HALF))
+    by_kz = np.zeros((3, ROWS, 4, HALF))
+    fixed[0, :, 2] = -ky_rows
+    fixed[0, :, 3] = 0
+    by_kz[0, :, 3] = -1
+    fixed[1, :, 1] = ky_rows
+    fixed[1, :, 2] = ky_rows
+    fixed[2, :, 0] = 0
+    fixed[2, :, 1] = 0
+    by_kz[2, :, 0] = 1
+    by_kz[2, :, 1] = 1
+    out["fixed"] = fixed.reshape(3, ROWS, LANES).astype(np.float32)
+    out["bykz"] = by_kz.reshape(3, ROWS, LANES).astype(np.float32)
+    out["kyrow"] = np.broadcast_to(ky_rows, (ROWS, LANES)).astype(np.float32).copy()
+    lane_kx = np.tile(kx * live, 4)
+    out["kxlane"] = np.broadcast_to(lane_kx, (8, LANES)).astype(np.float32).copy()
+    yy = np.arange(N)
+    force = [forcing_amp * np.sin(2 * np.pi * ((w * yy) % N) / N) for w in range(1, 5)]
+    force = np.repeat(np.stack(force).reshape(4, HALF, 2, 1), N, axis=3)
+    out["force"] = force.reshape(4, HALF, LANES).astype(np.float32)
+    return out
+
+
+def split(values):
+    high = values.astype(bf16)
+    low = (values - high.astype(f32)).astype(bf16)
+    return high, low
+
+
+def dot(a, b):
+    return jnp.dot(a, b, preferred_element_type=f32)
+
+
+def dot_nt(a, b):
+    return lax.dot_general(a, b, (((1,), (1,)), ((), ())), preferred_element_type=f32)
+
+
+def stacked(values):
+    high, low = split(values)
+    return jnp.concatenate([high, low], 0)
+
+
+def beside(values):
+    high, low = split(values)
+    return jnp.concatenate([high, low], 1)
+
+
+def folded(result):
+    rows = result.shape[0] // 2
+    return result[:rows] + result[rows:]
+
+
+def folded_lanes(result):
+    return result[:, :LANES] + result[:, LANES:]
+
+
+def padded(values, rows=128):
+    return jnp.concatenate([values, jnp.zeros((rows - values.shape[0], values.shape[1]), f32)], 0)
+
+
+def triple(values, high_ref, low_ref):
+    high, low = split(values)
+    return dot(high, high_ref) + dot(low, high_ref) + dot(high, low_ref)
+
+
+def columns(yh):
+    return pl.ds(pl.multiple_of(yh * LANES, LANES), LANES)
+
+
+def along_y(ref, tile, kz):
+    return jnp.concatenate(
+        [ref[tile, pl.ds(q * NKZ + kz, HALF, stride=ROWS), :] for q in range(4)], 0
+    )
+
+
+def base_kernel(base_ref, fz_ref, fy_ref, out_ref, lines):
+    def z_step(yh, _):
+        rows = jnp.concatenate(
+            [base_ref[i, :, columns(yh)] for i in range(3)] + [jnp.zeros((HALF, LANES), f32)], 0
+        )
+        got = folded(dot_nt(fz_ref[...], beside(rows)))
+        lines[0, pl.ds(pl.multiple_of(yh * ROWS, 8), ROWS), :] = got
+        return 0
+
+    lax.fori_loop(0, HALF, z_step, 0, unroll=2)
+
+    def y_step(kz, _):
+        out_ref[kz] = folded(dot(fy_ref[...], stacked(along_y(lines, 0, kz))))
+        return 0
+
+    lax.fori_loop(0, NKZ, y_step, 0, unroll=2)
+
+
+def main_kernel(
+    core_ref, cutoff_ref, wave_ref, base_ref, state_ref, here_ref, there_ref,
+    gxh_ref, gxl_ref, iy_ref, iyd_ref, iz_ref, izd_ref, fz_ref, fy_ref, fyr_ref,
+    fxh_ref, fxl_ref, ixh_ref, ixl_ref, fixed_ref, bykz_ref, kyrow_ref, kxlane_ref, force_ref,
+    near_ref, far_ref, planes, lines,
+):
+    core = core_ref[0]
+    cut_x, cut_y, cut_z = cutoff_ref[0], cutoff_ref[1], cutoff_ref[2]
+    which = jnp.clip(cut_x - (KEEP - 3), 0, 3)
+    ky = kyrow_ref[...]
+    keep_y = jnp.where(jnp.abs(ky) <= cut_y.astype(f32), 1.0, 0.0).astype(f32)
+    high_x = gxh_ref[which]
+    low_x = gxl_ref[which]
+
+    def gradient_step(pair, _):
+        kz = pair * 2
+        parts = []
+        for ref in (here_ref, there_ref):
+            both = []
+            for k in range(2):
+                keep_z = jnp.where(kz + k <= cut_z, 1.0, 0.0).astype(f32)
+                both.append(ref[kz + k] * (keep_y * keep_z))
+            parts.append(jnp.concatenate(both, 0))
+        got = triple(jnp.concatenate(parts, 1), high_x, low_x)
+        for k in range(2):
+            data = stacked(padded(got[k * ROWS : (k + 1) * ROWS]))
+            even = folded(dot(iy_ref[...], data))
+            odd = folded(dot(iyd_ref[...], data[:, :LANES]))
+            rows = pl.ds(pl.multiple_of((kz + k) * LANES, LANES), LANES)
+            planes[0, rows, :] = even[:, LANES:]
+            planes[1, rows, :] = odd
+            planes[2, rows, :] = even[:, :LANES]
+        return 0
+
+    lax.fori_loop(0, NKZ // 2, gradient_step, 0)
+    sigma = jnp.where(core == 0, -time_step, time_step).astype(f32)
+    force_at = jnp.clip(wave_ref[0] - 1, 0, 3)
+
+    def physical_step(yh, _):
+        grads = []
+        for d in range(3):
+            data = padded(planes[d, pl.ds(yh, ROWS, stride=HALF), :]).T
+            table = izd_ref if d == 2 else iz_ref
+            got = folded_lanes(dot(beside(data), table[...]))
+            grads.append([got[HALF * i : HALF * (i + 1)] for i in range(3)])
+        b = [base_ref[i, :, columns(yh)] for i in range(3)]
+        s = [state_ref[i, :, columns(yh)] for i in range(3)]
+        t = [sigma * v for v in s]
+        comb, comb_base = [], []
+        for i in range(3):
+            coupling = sum(jnp.where(core == 0, grads[j][i], grads[i][j]) * s[j] for j in range(3))
+            comb.append(s[i] - time_step * coupling)
+            drive = sum(grads[j][i] * b[j] for j in range(3))
+            if i == 0:
+                drive = drive - force_ref[force_at, pl.ds(yh, 1), :]
+            comb_base.append(b[i] - time_step * drive)
+        blocks = [
+            t[1] * b[0], t[2] * b[0], t[0] * b[1], t[0] * b[2],
+            comb[1], comb[2], comb_base[1], comb_base[2],
+            t[0] * b[0], t[1] * b[1], t[2] * b[1], comb[0],
+            t[1] * b[2], t[2] * b[2], comb_base[0], jnp.zeros((HALF, LANES), f32),
+        ]
+        got = folded(dot_nt(fz_ref[...], beside(jnp.concatenate(blocks, 0))))
+        rows = pl.ds(pl.multiple_of(yh * ROWS, 8), ROWS)
+        for tile in range(4):
+            lines[tile, rows, :] = got[:, tile * LANES : (tile + 1) * LANES]
+        return 0
+
+    lax.fori_loop(0, HALF, physical_step, 0)
+    kx = kxlane_ref[0:1, :]
+    keep_x = jnp.where(kx <= cut_x.astype(f32), 1.0, 0.0).astype(f32)
+    keep_xy = keep_y * keep_x
+    square_xy = ky * ky + kx * kx
+    lane = lax.broadcasted_iota(jnp.int32, (ROWS, LANES), 1)
+    for group in range(3):
+        near_ref[NKZ + group] = jnp.zeros((ROWS, LANES), f32)
+        far_ref[NKZ + group] = jnp.zeros((ROWS, LANES), f32)
+
+    def spectral_step(pair, _):
+        stack = []
+        for k in range(2):
+            kz = pair * 2 + k
+            kzf = kz.astype(f32)
+            first = jnp.concatenate([stacked(along_y(lines, t, kz)) for t in (0, 1)], 1)
+            second = jnp.concatenate([stacked(along_y(lines, t, kz)) for t in (2, 3)], 1)
+            even = folded(dot(fy_ref[...], first))
+            odd = folded(dot(fyr_ref[...], second))
+            factor = [fixed_ref[n] + kzf * bykz_ref[n] for n in range(3)]
+            stack.append(
+                jnp.concatenate(
+                    [
+                        even[:, :LANES] * factor[0],
+                        even[:, LANES:],
+                        odd[:, :LANES] * factor[1],
+                        odd[:, LANES:] * factor[2],
+                    ],
+                    1,
+                )
+            )
+        modes = triple(jnp.concatenate(stack, 0), fxh_ref[...], fxl_ref[...])
+        results = []
+        for k in range(2):
+            kz = pair * 2 + k
+            kzf = kz.astype(f32)
+            vx, slope, uy, uz = (
+                modes[k * ROWS : (k + 1) * ROWS, n * LANES : (n + 1) * LANES] for n in range(4)
+            )
+            square = square_xy + kzf * kzf
+            keep_z = jnp.where(kz <= cut_z, 1.0, 0.0).astype(f32)
+            factor = keep_xy * keep_z / (1.0 + viscosity * time_step * square)
+            share = (slope + ky * uy + kzf * uz) / jnp.where(square > 0, square, 1.0)
+            results.append(
+                jnp.concatenate(
+                    [
+                        factor * vx,
+                        factor * share,
+                        factor * (uy - ky * share),
+                        factor * (uz - kzf * share),
+                    ],
+                    1,
+                )
+            )
+        got = triple(jnp.concatenate(results, 0), ixh_ref[core], ixl_ref[core])
+        for k in range(2):
+            kz = pair * 2 + k
+            mine = got[k * ROWS : (k + 1) * ROWS]
+            near_ref[kz] = mine[:, :LANES]
+            far_ref[kz] = mine[:, LANES : 2 * LANES]
+            last = mine[:, 2 * LANES :]
+            group = NKZ + kz // 8
+            shift = (kz % 8) * 16
+            own = pltpu.roll(jnp.where(lane < 16, last, 0.0), shift, 1)
+            other = jnp.where((lane >= 16) & (lane < 32), last, 0.0)
+            other = pltpu.roll(other, (shift + LANES - 16) % LANES, 1)
+            near_ref[group] += own
+            far_ref[group] += other
+        return 0
+
+    lax.fori_loop(0, NKZ // 2, spectral_step, 0)
+
+
+def final_kernel(
+    near_ref, far_ref, state_ref, base_ref, iy_ref, iz_ref, izr_ref,
+    base_out, state_out, planes,
+):
+    def y_step(kz, _):
+        shift = (LANES - (kz % 8) * 16) % LANES
+        group = NKZ + kz // 8
+        rest = pltpu.roll(near_ref[group] + far_ref[group], shift, 1)
+        data = jnp.concatenate([near_ref[kz] + far_ref[kz], rest], 1)
+        got = folded(dot(iy_ref[...], stacked(padded(data))))
+        rows = pl.ds(pl.multiple_of(kz * LANES, LANES), LANES)
+        planes[0, rows, :] = got[:, :LANES]
+        planes[1, rows, :] = got[:, LANES:]
+        return 0
+
+    lax.fori_loop(0, NKZ, y_step, 0, unroll=2)
+
+    def z_step(yh, _):
+        data = padded(planes[0, pl.ds(yh, ROWS, stride=HALF), :]).T
+        last = padded(planes[1, pl.ds(yh, ROWS, stride=HALF), :]).T[:16]
+        turned = folded_lanes(dot(beside(data[:48]), izr_ref[...]))
+        plain = folded_lanes(dot(beside(jnp.concatenate([data[48:], last], 0)), iz_ref[...]))
+        at = columns(yh)
+        state_out[0, :, at] = turned[:32] - state_ref[0, :, at]
+        state_out[1, :, at] = plain[16:48] - state_ref[1, :, at]
+        state_out[2, :, at] = plain[48:80] - state_ref[2, :, at]
+        base_out[0, :, at] = turned[32:48] - base_ref[0, :, at]
+        base_out[1, :, at] = plain[:16] - base_ref[1, :, at]
+        base_out[2, :, at] = plain[80:96] - base_ref[2, :, at]
+        return 0
+
+    lax.fori_loop(0, HALF, z_step, 0, unroll=2)
+
+
+interpret = False
+
+
+def call(kernel, outs, scratch, inputs, flops, in_smem=0):
+    whole = pl.BlockSpec(memory_space=pltpu.VMEM)
+    small = pl.BlockSpec(memory_space=pltpu.SMEM)
+    return pl.pallas_call(
+        kernel,
+        out_shape=outs,
+        in_specs=[small] * in_smem + [whole] * (len(inputs) - in_smem),
+        out_specs=jax.tree.map(lambda _: whole, outs),
+        scratch_shapes=scratch,
+        compiler_params=pltpu.CompilerParams(vmem_limit_bytes=56 * 2**20),
+        cost_estimate=pl.CostEstimate(flops=flops, bytes_accessed=4 * 2**20, transcendentals=0),
+        interpret=interpret,
+    )(*inputs)
+
+
+def body(base, state, wavenumber, cutoff):
+    t = {name: jnp.asarray(value) for name, value in tables().items()}
+    core = lax.axis_index("comp")
+    seg_count = lax.axis_size("seg")
+    own_base = base[0]
+    own_state = state[0, 0]
+    base_half = lax.dynamic_slice_in_dim(own_base, core * 16, 16, 1)
+    back = [((s + 1) % seg_count, s) for s in range(seg_count)]
+    around = [(2 * i, 2 * o) for i, o in back] + [(2 * o + 1, 2 * i + 1) for i, o in back]
+    base_next = lax.ppermute(base_half, "seg", back)
+    state_next = lax.ppermute(own_state, ("seg", "comp"), around)
+    sds = jax.ShapeDtypeStruct
+    spectrum = call(
+        base_kernel,
+        sds((NKZ, ROWS, LANES), f32),
+        [pltpu.VMEM((1, HALF * ROWS, LANES), f32)],
+        [own_base, t["fz"], t["fy"]],
+        10**9,
+    )
+    swap = [(0, 1), (1, 0)]
+    there = lax.ppermute(spectrum, "slab", swap)
+    names = (
+        "gxh", "gxl", "iy", "iyd", "iz", "izd", "fz", "fy", "fyr", "fxh", "fxl", "ixh", "ixl",
+        "fixed", "bykz", "kyrow", "kxlane", "force",
+    )
+    near, far = call(
+        main_kernel,
+        [sds((PACKED, ROWS, LANES), f32)] * 2,
+        [
+            pltpu.VMEM((3, NKZ * LANES, LANES), f32),
+            pltpu.VMEM((4, HALF * ROWS, LANES), f32),
+        ],
+        [core.reshape(1), cutoff, wavenumber, own_base, own_state, spectrum, there]
+        + [t[name] for name in names],
+        10**10,
+        in_smem=3,
+    )
+    far = lax.ppermute(far, "slab", swap)
+    base_gap, state_gap = call(
+        final_kernel,
+        [sds((3, 16, N * N), f32), sds((3, HALF, N * N), f32)],
+        [pltpu.VMEM((2, NKZ * LANES, LANES), f32)],
+        [near, far, state_next, base_next, t["iy"], t["iz"], t["izr"]],
+        10**9,
+    )
+    return base_gap[None], state_gap[None, None]
+
+
 def solution(mesh):
+    paired = mesh.shape["slab"] == 2 and mesh.shape["comp"] == 2
     return jax.shard_map(
-        body,
+        body if paired else general_body,
         mesh=mesh,
         in_specs=(
             P(("groups", "seg"), None, "slab", None),

time: 490 us -> 118 us (0.24); the launches traced: 483 us -> 118 us
  other arithmetic: 145 us -> 0 us
  matrix products: 137 us -> 0 us
  local copies, waits for them, and re-layouts: 124 us -> 1.06 us
  Pallas kernels: 0 us -> 64.9 us
  starting transfers between devices: 37 us -> 11.9 us
    dot_general x21 -> x0, matrix products: 137 us -> none  [the longest x4 30.7 us: yz_forward(): jnp.einsum('sry,...yk->s...rk', forward_transform_y, along_z, precision=h...]
    pallas_call x0 -> x3, Pallas kernels: none -> 64.9 us  [call(): pl.pallas_call(kernel, out_shape=outs, in_specs=[small] * in_smem + [whol...]
    unnamed x154 -> x10, local copies, waits for them, and re-layouts: 57.1 us -> 1.01 us
    sub x21 -> x0, other arithmetic: 50.4 us -> none  [the longest x14 47.3 us: combine(): real_part = cosine_part[..., :columns] - sine_part[..., columns:]]
    all_to_all x7 -> x0, other arithmetic: 43 us -> none  [the longest x2 20.8 us: spectral(): lax.all_to_all(state_modes, ('slab', 'comp'), split_axis=4, concat_axis=2...]
    ppermute x4, waiting for transfers between devices: 0.23 us -> 38.8 us  [the longest x1 18 us: body(): there = lax.ppermute(spectrum, 'slab', swap)]
    all_to_all x7 -> x0, waiting for transfers between devices: 34.8 us -> none  [the longest x1 16.7 us: body(): lax.all_to_all(grad_spread, ('slab', 'comp'), split_axis=1, concat_axis=3...]
    all_to_all x7 -> x0, starting transfers between devices: 30.4 us -> none  [the longest x2 8.65 us: spectral(): lax.all_to_all(state_modes, ('slab', 'comp'), split_axis=4, concat_axis=2...]
  transfers between devices with their start and end apart: 11 -> 4, of which waited for: 5 -> 3; matrix products, arithmetic and copies ran while one was open for 59% -> 0% of each run, Pallas kernels for 0% -> 37%
where the time goes in v1:
time: 118 us
  Pallas kernels  64.9 us (55%)
  waiting for transfers between devices  38.8 us (33%)
  starting transfers between devices  11.9 us (10%)
  between operations  1.3 us (1%)
    pallas_call x3, Pallas kernels, call(): pl.pallas_call(kernel, out_shape=outs, in_specs=[small] * in_smem + [whol...  64.9 us
    ppermute x1, waiting for transfers between devices, body(): there = lax.ppermute(spectrum, 'slab', swap)  18 us
    ppermute x1, waiting for transfers between devices, body(): base_next = lax.ppermute(base_half, 'seg', back)  15.7 us
    ppermute x1, waiting for transfers between devices, body(): far = lax.ppermute(far, 'slab', swap)  5.11 us
    ppermute x1, starting transfers between devices, body(): base_next = lax.ppermute(base_half, 'seg', back)  3.65 us
    ppermute x1, starting transfers between devices, body(): state_next = lax.ppermute(own_state, ('seg', 'comp'), around)  3.6 us
    ppermute x1, starting transfers between devices, body(): there = lax.ppermute(spectrum, 'slab', swap)  2.94 us
  transfers between devices with their start and end apart: 4, of which 3 were waited for; matrix products, arithmetic and copies ran while one was open for 0% of the time, Pallas kernels for 37%

profile of v1, /device:TPU:0, one launch (start us, length us, event | category | flops | bytes accessed | tf_op | source)
XLA Modules:
  0.0 117.9 jit_solution(8459865253682554733)
XLA Ops:
  0.6 0.0 copy-start.4
  0.6 8.3 %shard_map.230.here_ref = f32[22,88,128]{2,1,0:T(8,128)} custom-call(f32[3,32,4096]{2,1,0:T(8,128)} %bitcast.7, bf16[176,256]{1,0:T(8,128)(2,1)} %constant.49.clone.fz_ref, bf16[176,256]{1,0:T(8,128)(2,1)} %constant.53.clone.fy_ref), custom_call_target="tpu_custom_call" | custom-call | flops 1000000000 | bytes 4194304 | tf_op jit(solution)/shard_map/pallas_call | solution.py:687
  8.9 2.9 %collective-permute-start = (f32[22,88,128]{2,1,0:T(8,128)}, f32[22,88,128]{2,1,0:T(8,128)}, u32[]{:S(2)}, u32[]{:S(2)}) collective-permute-start(f32[22,88,128]{2,1,0:T(8,128)} %shard_map.230.here_ref), channel_id=1, source_target_pairs={{0,2},{2,0},{1,3},{3,1},{4,6},{6,4},{5,7},{7,5},{8,10},{10,8},{9,1... | collective-permute-start | bytes 2973704 | tf_op jit(solution)/shard_map/ppermute | solution.py:719
  11.8 0.0 copy-done.4
  11.8 3.6 %collective-permute-start.2 = (f32[3,32,4096]{2,1,0:T(8,128)S(1)}, f32[3,32,4096]{2,1,0:T(8,128)S(1)}, u32[]{:S(2)}, u32[]{:S(2)}) collective-permute-start(f32[3,32,4096]{2,1,0:T(8,128)S(1)} %bitcast.10), channel_id=1, source_target_pairs={{4,0},{8,4},{12,8},{0,12},{1,5},{5,9},{9,13},{13,1},{6,2},{10,6},{... | collective-permute-start | bytes 4718600 | tf_op jit(solution)/shard_map/ppermute | solution.py:709
  16.1 18.0 %collective-permute-done.there_ref = f32[22,88,128]{2,1,0:T(8,128)} collective-permute-done((f32[22,88,128]{2,1,0:T(8,128)}, f32[22,88,128]{2,1,0:T(8,128)}, u32[]{:S(2)}, u32[]{:S(2)}) %collective-permute-start) | collective-permute-done | bytes 991264 | tf_op jit(solution)/shard_map/ppermute | solution.py:719
  34.1 0.0 copy-start.3
  34.1 44.0 %shard_map.231 = (f32[25,88,128]{2,1,0:T(8,128)}, f32[25,88,128]{2,1,0:T(8,128)}) custom-call(s32[1]{0:T(128)} %bitcast.core_ref, s32[3]{0:T(128)} %cutoff_ref.1, s32[1]{0:T(128)S(6)} %copy.25.wave_ref, f32[3,32,4096]{2,1,0:T(8,128)} %bitcast.8, f32[3,32,4096]{2,1,0:T(8,128)} %bitcast.9, f32[22,88,128]{2,1,0:T(8,128)} %shard_map.230.here_ref, ...), custom_call_target="tpu_custom_call" | custom-call | flops 10000000000 | bytes 4194304 | tf_op jit(solution)/shard_map/pallas_call | solution.py:687
  78.1 1.7 %collective-permute-start.1 = (f32[25,88,128]{2,1,0:T(8,128)}, f32[25,88,128]{2,1,0:T(8,128)S(1)}, u32[]{:S(2)}, u32[]{:S(2)}) collective-permute-start(f32[25,88,128]{2,1,0:T(8,128)} %get-tuple-element.7), channel_id=1, source_target_pairs={{0,2},{2,0},{1,3},{3,1},{4,6},{6,4},{5,7},{7,5},{8,10},{10,8},{9,1... | collective-permute-start | bytes 3379208 | tf_op jit(solution)/shard_map/ppermute | solution.py:736
  79.8 0.0 copy-done.3
  79.8 0.1 dynamic-slice_bitcast_fusion
  79.9 3.6 %collective-permute-start.3 = (f32[3,16,4096]{2,1,0:T(8,128)S(1)}, f32[3,16,4096]{2,1,0:T(8,128)S(1)}, u32[]{:S(2)}, u32[]{:S(2)}) collective-permute-start(f32[3,16,4096]{2,1,0:T(8,128)S(1)} %dynamic-slice_bitcast_fusion), channel_id=1, source_target_pairs={{4,0},{8,4},{12,8},{0,12},{5,1},{9,5},{13,9},{1,13},{6,2},{10,6},{... | collective-permute-start | bytes 2359304 | tf_op jit(solution)/shard_map/ppermute | solution.py:708
  83.5 15.7 %collective-permute-done.3.base_ref = f32[3,16,4096]{2,1,0:T(8,128)S(1)} collective-permute-done((f32[3,16,4096]{2,1,0:T(8,128)S(1)}, f32[3,16,4096]{2,1,0:T(8,128)S(1)}, u32[]{:S(2)}, u32[]{:S(2)}) %collective-permute-start.3) | collective-permute-done | bytes 786464 | tf_op jit(solution)/shard_map/ppermute | solution.py:708
  99.2 0.0 copy-start.2
  99.2 0.0 collective-permute-done.2.state_ref
  99.2 0.0 copy-start
  99.2 5.1 %collective-permute-done.1.far_ref = f32[25,88,128]{2,1,0:T(8,128)S(1)} collective-permute-done((f32[25,88,128]{2,1,0:T(8,128)}, f32[25,88,128]{2,1,0:T(8,128)S(1)}, u32[]{:S(2)}, u32[]{:S(2)}) %collective-permute-start.1) | collective-permute-done | bytes 1126432 | tf_op jit(solution)/shard_map/ppermute | solution.py:736
  104.3 0.0 copy-start.1
  104.3 0.0 copy-done.2
  104.3 0.0 copy-done
  104.3 1.0 copy-done.1
  105.3 12.6 %shard_map.232 = (f32[3,16,4096]{2,1,0:T(8,128)}, f32[3,32,4096]{2,1,0:T(8,128)}) custom-call(f32[25,88,128]{2,1,0:T(8,128)} %get-tuple-element.6.near_ref, f32[25,88,128]{2,1,0:T(8,128)} %copy-done.1, f32[3,32,4096]{2,1,0:T(8,128)} %copy-done, f32[3,16,4096]{2,1,0:T(8,128)} %copy-done.2, bf16[256,256]{1,0:T(8,128)(2,1)} %constant.55.clone.iy_ref, ...), custom_call_target="tpu_custom_call" | custom-call | flops 1000000000 | bytes 4194304 | tf_op jit(solution)/shard_map/pallas_call | solution.py:687
Async XLA Ops:
  0.6 11.2 %copy-start.4 = (f32[1,1,3,32,4096]{4,3,2,1,0:T(8,128)S(1)}, f32[1,1,3,32,4096]{4,3,2,1,0:T(8,128)}, u32[]{:S(2)}) copy-start(f32[1,1,3,32,4096]{4,3,2,1,0:T(8,128)} %param.24) | copy-start | bytes 4718596
  8.9 25.2 %collective-permute-start = (f32[22,88,128]{2,1,0:T(8,128)}, f32[22,88,128]{2,1,0:T(8,128)}, u32[]{:S(2)}, u32[]{:S(2)}) collective-permute-start(f32[22,88,128]{2,1,0:T(8,128)} %shard_map.230.here_ref), channel_id=1, source_target_pairs={{0,2},{2,0},{1,3},{3,1},{4,6},{6,4},{5,7},{7,5},{8,10},{10,8},{9,1... | collective-permute-start | bytes 2973704 | tf_op jit(solution)/shard_map/ppermute | solution.py:719
  11.8 87.4 %collective-permute-start.2 = (f32[3,32,4096]{2,1,0:T(8,128)S(1)}, f32[3,32,4096]{2,1,0:T(8,128)S(1)}, u32[]{:S(2)}, u32[]{:S(2)}) collective-permute-start(f32[3,32,4096]{2,1,0:T(8,128)S(1)} %bitcast.10), channel_id=1, source_target_pairs={{4,0},{8,4},{12,8},{0,12},{1,5},{5,9},{9,13},{13,1},{6,2},{10,6},{... | collective-permute-start | bytes 4718600 | tf_op jit(solution)/shard_map/ppermute | solution.py:709
  34.1 45.8 %copy-start.3 = (f32[1,3,32,4096]{3,2,1,0:T(8,128)S(1)}, f32[1,3,32,4096]{3,2,1,0:T(8,128)}, u32[]{:S(2)}) copy-start(f32[1,3,32,4096]{3,2,1,0:T(8,128)} %param.23) | copy-start | bytes 4718596
  78.1 26.2 %collective-permute-start.1 = (f32[25,88,128]{2,1,0:T(8,128)}, f32[25,88,128]{2,1,0:T(8,128)S(1)}, u32[]{:S(2)}, u32[]{:S(2)}) collective-permute-start(f32[25,88,128]{2,1,0:T(8,128)} %get-tuple-element.7), channel_id=1, source_target_pairs={{0,2},{2,0},{1,3},{3,1},{4,6},{6,4},{5,7},{7,5},{8,10},{10,8},{9,1... | collective-permute-start | bytes 3379208 | tf_op jit(solution)/shard_map/ppermute | solution.py:736
  79.9 19.3 %collective-permute-start.3 = (f32[3,16,4096]{2,1,0:T(8,128)S(1)}, f32[3,16,4096]{2,1,0:T(8,128)S(1)}, u32[]{:S(2)}, u32[]{:S(2)}) collective-permute-start(f32[3,16,4096]{2,1,0:T(8,128)S(1)} %dynamic-slice_bitcast_fusion), channel_id=1, source_target_pairs={{4,0},{8,4},{12,8},{0,12},{5,1},{9,5},{13,9},{1,13},{6,2},{10,6},{... | collective-permute-start | bytes 2359304 | tf_op jit(solution)/shard_map/ppermute | solution.py:708
  99.2 5.1 %copy-start.2 = (f32[3,16,4096]{2,1,0:T(8,128)}, f32[3,16,4096]{2,1,0:T(8,128)S(1)}, u32[]{:S(2)}) copy-start(f32[3,16,4096]{2,1,0:T(8,128)S(1)} %collective-permute-done.3.base_ref) | copy-start | bytes 2359300
  99.2 5.1 %copy-start = (f32[3,32,4096]{2,1,0:T(8,128)}, f32[3,32,4096]{2,1,0:T(8,128)S(1)}, u32[]{:S(2)}) copy-start(f32[3,32,4096]{2,1,0:T(8,128)S(1)} %collective-permute-done.2.state_ref) | copy-start | bytes 4718596
  104.3 1.0 copy-start.1

commit v2 on v1

--- a/solution.py
+++ b/solution.py
@@ -16,6 +16,7 @@
 NKY = 44
 ROWS = 2 * NKY
 PACKED = NKZ + 3
+HALF_KZ = NKZ // 2
 LANES = 128
 
 viscosity = 0.025
@@ -356,73 +357,46 @@
     value = np.concatenate([np.cos(arg) * live, np.sin(arg) * live], 1)
     change = np.concatenate([kx * np.sin(arg) * live, -kx * np.cos(arg) * live], 1)
 
-    def d_of(block):
-        return np.concatenate([kx * block[:, HALF:], -kx * block[:, :HALF]], 1)
-
-    fx = np.zeros((4, 4, HALF, 4, 2, 2 * HALF))
-
-    def put(tile, block, quantity, part, what):
-        fx[tile, block, :, quantity, part] += what
-        if quantity == 0:
-            fx[tile, block, :, 1, part] += -d_of(what)
-
-    put(0, 0, 2, 0, change)
-    put(0, 1, 3, 0, change)
-    put(0, 2, 0, 0, value)
-    put(0, 3, 0, 0, value)
-    put(1, 0, 2, 0, value)
-    put(1, 1, 3, 0, value)
-    put(1, 2, 2, 1, value)
-    put(1, 3, 3, 1, value)
-    put(2, 0, 0, 0, change)
-    put(2, 1, 2, 0, value)
-    put(2, 2, 3, 0, value)
-    put(2, 3, 0, 0, value)
-    put(3, 0, 2, 0, value)
-    put(3, 1, 3, 0, value)
-    put(3, 2, 0, 1, value)
-    out["fxh"], out["fxl"] = halves(fx.reshape(512, 512))
-    inv_high, inv_low = [], []
+    def coefficients(blocks):
+        table = np.zeros((4, HALF, 2, 2 * HALF))
+        for block, part, what in blocks:
+            table[block, :, part] = what
+        return table.reshape(LANES, LANES)
+
+    first = coefficients([(0, 0, value), (1, 1, value), (2, 0, change), (3, 0, value)])
+    last = coefficients([(0, 0, change), (1, 0, value), (2, 0, value), (3, 1, value)])
+    fall = first.reshape(LANES, 2, 2, HALF)
+    fall = np.stack([-kx * fall[:, :, 1], kx * fall[:, :, 0]], 2).reshape(LANES, LANES)
+    out["fx"] = np.stack([right_table(part, 128) for part in (first, fall, first, last)])
     wx = np.where(kx == 0, 1.0, 2.0) * live / N
     for core in range(2):
-        ix = np.zeros((4, 2, 2 * HALF, 3 * LANES))
+        ix = np.zeros((4, 2, 2 * HALF, LANES))
         for side in range(2):
             xs = np.arange(HALF) + side * HALF
             arg = 2 * np.pi * kx[:, None] * xs[None, :] / N
             give = np.concatenate([np.cos(arg) * wx[:, None], np.sin(arg) * wx[:, None]], 0)
-            fall = np.concatenate(
+            drop = np.concatenate(
                 [np.sin(arg) * (wx * kx)[:, None], -np.cos(arg) * (wx * kx)[:, None]], 0
             )
             own = slice(core * 16, core * 16 + 16)
-            at = side * LANES
-            ix[0, 0, :, at : at + 32] = give
-            ix[1, 0, :, at : at + 32] = fall
-            ix[0, 1, :, at + 32 : at + 48] = give[:, own]
-            ix[1, 1, :, at + 32 : at + 48] = fall[:, own]
-            ix[2, 1, :, at + 48 : at + 64] = give[:, own]
-            ix[2, 0, :, at + 64 : at + 96] = give
-            ix[3, 0, :, at + 96 : at + 128] = give
-            last = 2 * LANES + side * 16
-            ix[3, 1, :, last : last + 16] = give[:, own]
-        high, low = halves(ix.reshape(512, 3 * LANES))
-        inv_high.append(high)
-        inv_low.append(low)
-    out["ixh"] = np.stack(inv_high)
-    out["ixl"] = np.stack(inv_low)
+
+            def put(quantity, part, lane, what):
+                at = (lane + side * 64 + np.arange(what.shape[1])) % LANES
+                ix[quantity, part][:, at] = what
+
+            put(0, 0, 0, give)
+            put(1, 0, 0, drop)
+            put(0, 1, 32, give[:, own])
+            put(1, 1, 32, drop[:, own])
+            put(2, 1, 48, give[:, own])
+            put(2, 0, 64, give)
+            put(3, 0, 96, give)
+            put(3, 1, 0, give[:, own])
+        out["ix%d" % core] = np.stack(
+            [right_table(part, 128) for part in ix.reshape(4, LANES, LANES)]
+        )
+    out["ix"] = np.stack([out.pop("ix0"), out.pop("ix1")])
     ky_rows = np.tile(ky, 2)[:, None]
-    fixed = np.ones((3, ROWS, 4, HALF))
-    by_kz = np.zeros((3, ROWS, 4, HALF))
-    fixed[0, :, 2] = -ky_rows
-    fixed[0, :, 3] = 0
-    by_kz[0, :, 3] = -1
-    fixed[1, :, 1] = ky_rows
-    fixed[1, :, 2] = ky_rows
-    fixed[2, :, 0] = 0
-    fixed[2, :, 1] = 0
-    by_kz[2, :, 0] = 1
-    by_kz[2, :, 1] = 1
-    out["fixed"] = fixed.reshape(3, ROWS, LANES).astype(np.float32)
-    out["bykz"] = by_kz.reshape(3, ROWS, LANES).astype(np.float32)
     out["kyrow"] = np.broadcast_to(ky_rows, (ROWS, LANES)).astype(np.float32).copy()
     lane_kx = np.tile(kx * live, 4)
     out["kxlane"] = np.broadcast_to(lane_kx, (8, LANES)).astype(np.float32).copy()
@@ -485,28 +459,111 @@
     )
 
 
-def base_kernel(base_ref, fz_ref, fy_ref, out_ref, lines):
-    def z_step(yh, _):
-        rows = jnp.concatenate(
-            [base_ref[i, :, columns(yh)] for i in range(3)] + [jnp.zeros((HALF, LANES), f32)], 0
-        )
-        got = folded(dot_nt(fz_ref[...], beside(rows)))
-        lines[0, pl.ds(pl.multiple_of(yh * ROWS, 8), ROWS), :] = got
+def along_kz(ref, tile, yh):
+    return padded(ref[tile, pl.ds(yh, ROWS, stride=HALF), :]).T
+
+
+def line_rows(yh):
+    return pl.ds(pl.multiple_of(yh * ROWS, 8), ROWS)
+
+
+def plane_rows(kz):
+    return pl.ds(pl.multiple_of(kz * LANES, LANES), LANES)
+
+
+def lane_parts(values):
+    return [values[:, at : at + LANES] for at in range(0, values.shape[1], LANES)]
+
+
+def over_planes(step):
+    def four(index, _):
+        step([index * 4 + k for k in range(4)])
         return 0
 
-    lax.fori_loop(0, HALF, z_step, 0, unroll=2)
-
-    def y_step(kz, _):
-        out_ref[kz] = folded(dot(fy_ref[...], stacked(along_y(lines, 0, kz))))
+    lax.fori_loop(0, NKZ // 4, four, 0)
+    step([jnp.int32(kz) for kz in range(NKZ // 4 * 4, NKZ)])
+
+
+def over_lines(step, many):
+    def some(index, _):
+        step([index * many + k for k in range(many)])
         return 0
 
-    lax.fori_loop(0, NKZ, y_step, 0, unroll=2)
+    lax.fori_loop(0, HALF // many, some, 0)
+
+
+def base_kernel(core_ref, base_ref, fz_ref, fy_ref, out_ref, lines):
+    nothing = jnp.zeros((HALF, LANES), f32)
+
+    def z_step(yhs):
+        rows = []
+        for yh in yhs:
+            rows += [base_ref[i, :, columns(yh)] for i in range(3)] + [nothing]
+        got = folded(dot_nt(fz_ref[...], beside(jnp.concatenate(rows, 0))))
+        for yh, part in zip(yhs, lane_parts(got)):
+            lines[0, line_rows(yh), :] = part
+
+    over_lines(z_step, 4)
+    start = core_ref[0] * HALF_KZ
+    for pair in range(0, HALF_KZ, 2):
+        ks = range(pair, min(pair + 2, HALF_KZ))
+        data = jnp.concatenate([stacked(along_y(lines, 0, start + k)) for k in ks], 1)
+        got = folded(dot(fy_ref[...], data))
+        for k, part in zip(ks, lane_parts(got)):
+            out_ref[k] = part
+
+
+def flux_kernel(
+    core_ref, base_ref, state_ref, fz_ref, fy_ref, fyr_ref, kyrow_ref, out_ref, lines
+):
+    sigma = jnp.where(core_ref[0] == 0, -time_step, time_step).astype(f32)
+    nothing = jnp.zeros((HALF, LANES), f32)
+
+    def z_step(yhs):
+        rows = []
+        for yh in yhs:
+            b = [base_ref[i, :, columns(yh)] for i in range(3)]
+            t = [sigma * state_ref[i, :, columns(yh)] for i in range(3)]
+            rows += [t[2] * b[0], t[0] * b[1], t[1] * b[0], t[0] * b[2]]
+            rows += [t[2] * b[1], t[2] * b[2], t[1] * b[1], t[1] * b[2]]
+            rows += [nothing, nothing, t[0] * b[0], nothing]
+        got = lane_parts(folded(dot_nt(fz_ref[...], beside(jnp.concatenate(rows, 0)))))
+        for n, yh in enumerate(yhs):
+            for tile in range(3):
+                lines[tile, line_rows(yh), :] = got[3 * n + tile]
+
+    over_lines(z_step, 2)
+    ky = kyrow_ref[...]
+    lane = lax.broadcasted_iota(jnp.int32, (ROWS, LANES), 1)
+    odd_block = (lane // HALF) % 2 == 1
+
+    def y_step(kzs):
+        even = []
+        for pair in range(0, len(kzs), 2):
+            data = [stacked(along_y(lines, 0, kz)) for kz in kzs[pair : pair + 2]]
+            even += lane_parts(folded(dot(fy_ref[...], jnp.concatenate(data, 1))))
+        odd = []
+        for kz in kzs:
+            data = [stacked(along_y(lines, tile, kz)) for tile in (1, 2)]
+            odd.append(lane_parts(folded(dot(fyr_ref[...], jnp.concatenate(data, 1)))))
+        for n, kz in enumerate(kzs):
+            kzf = kz.astype(f32)
+            plain = even[n]
+            slopes = odd[n][0] * jnp.where(odd_block, kzf, ky)
+            slopes = slopes + pltpu.roll(slopes, 32, 1)
+            out_ref[0, kz] = jnp.where(odd_block, slopes, plain)
+            other = plain * jnp.where(lane >= 96, -kzf, -ky)
+            other = other + pltpu.roll(other, 64, 1)
+            out_ref[1, kz] = jnp.where(lane >= 96, other, odd[n][1])
+
+    over_planes(y_step)
 
 
 def main_kernel(
-    core_ref, cutoff_ref, wave_ref, base_ref, state_ref, here_ref, there_ref,
+    core_ref, cutoff_ref, wave_ref, base_ref, state_ref,
+    here_own, here_other, there_own, there_other, flux_ref,
     gxh_ref, gxl_ref, iy_ref, iyd_ref, iz_ref, izd_ref, fz_ref, fy_ref, fyr_ref,
-    fxh_ref, fxl_ref, ixh_ref, ixl_ref, fixed_ref, bykz_ref, kyrow_ref, kxlane_ref, force_ref,
+    fx_ref, ix_ref, kyrow_ref, kxlane_ref, force_ref,
     near_ref, far_ref, planes, lines,
 ):
     core = core_ref[0]
@@ -514,64 +571,63 @@
     which = jnp.clip(cut_x - (KEEP - 3), 0, 3)
     ky = kyrow_ref[...]
     keep_y = jnp.where(jnp.abs(ky) <= cut_y.astype(f32), 1.0, 0.0).astype(f32)
-    high_x = gxh_ref[which]
-    low_x = gxl_ref[which]
-
-    def gradient_step(pair, _):
-        kz = pair * 2
-        parts = []
-        for ref in (here_ref, there_ref):
-            both = []
-            for k in range(2):
-                keep_z = jnp.where(kz + k <= cut_z, 1.0, 0.0).astype(f32)
-                both.append(ref[kz + k] * (keep_y * keep_z))
-            parts.append(jnp.concatenate(both, 0))
-        got = triple(jnp.concatenate(parts, 1), high_x, low_x)
-        for k in range(2):
-            data = stacked(padded(got[k * ROWS : (k + 1) * ROWS]))
-            even = folded(dot(iy_ref[...], data))
-            odd = folded(dot(iyd_ref[...], data[:, :LANES]))
-            rows = pl.ds(pl.multiple_of((kz + k) * LANES, LANES), LANES)
-            planes[0, rows, :] = even[:, LANES:]
-            planes[1, rows, :] = odd
-            planes[2, rows, :] = even[:, :LANES]
-        return 0
-
-    lax.fori_loop(0, NKZ // 2, gradient_step, 0)
-    sigma = jnp.where(core == 0, -time_step, time_step).astype(f32)
+
+    def kept_z(kz):
+        return jnp.where(kz <= cut_z, 1.0, 0.0).astype(f32)
+
+    def gradient_step(kzs):
+        rows = []
+        for kz in kzs:
+            half = kz // HALF_KZ
+            at = kz - half * HALF_KZ
+            keep = keep_y * kept_z(kz)
+            here = jnp.where(half == core, here_own[at], here_other[at]) * keep
+            there = jnp.where(half == core, there_own[at], there_other[at]) * keep
+            rows.append(jnp.concatenate([here, there], 1))
+        got = triple(jnp.concatenate(rows, 0), gxh_ref[which], gxl_ref[which])
+        data = [stacked(padded(got[n * ROWS : (n + 1) * ROWS])) for n in range(len(kzs))]
+        for n, kz in enumerate(kzs):
+            even = lane_parts(folded(dot(iy_ref[...], data[n])))
+            planes[0, plane_rows(kz), :] = even[1]
+            planes[2, plane_rows(kz), :] = even[0]
+        for n in range(0, len(kzs), 2):
+            both = jnp.concatenate([data[n][:, :LANES], data[n + 1][:, :LANES]], 1)
+            odd = lane_parts(folded(dot(iyd_ref[...], both)))
+            planes[1, plane_rows(kzs[n]), :] = odd[0]
+            planes[1, plane_rows(kzs[n + 1]), :] = odd[1]
+
+    over_planes(gradient_step)
     force_at = jnp.clip(wave_ref[0] - 1, 0, 3)
-
-    def physical_step(yh, _):
-        grads = []
-        for d in range(3):
-            data = padded(planes[d, pl.ds(yh, ROWS, stride=HALF), :]).T
-            table = izd_ref if d == 2 else iz_ref
-            got = folded_lanes(dot(beside(data), table[...]))
-            grads.append([got[HALF * i : HALF * (i + 1)] for i in range(3)])
-        b = [base_ref[i, :, columns(yh)] for i in range(3)]
-        s = [state_ref[i, :, columns(yh)] for i in range(3)]
-        t = [sigma * v for v in s]
-        comb, comb_base = [], []
-        for i in range(3):
-            coupling = sum(jnp.where(core == 0, grads[j][i], grads[i][j]) * s[j] for j in range(3))
-            comb.append(s[i] - time_step * coupling)
-            drive = sum(grads[j][i] * b[j] for j in range(3))
-            if i == 0:
-                drive = drive - force_ref[force_at, pl.ds(yh, 1), :]
-            comb_base.append(b[i] - time_step * drive)
-        blocks = [
-            t[1] * b[0], t[2] * b[0], t[0] * b[1], t[0] * b[2],
-            comb[1], comb[2], comb_base[1], comb_base[2],
-            t[0] * b[0], t[1] * b[1], t[2] * b[1], comb[0],
-            t[1] * b[2], t[2] * b[2], comb_base[0], jnp.zeros((HALF, LANES), f32),
-        ]
-        got = folded(dot_nt(fz_ref[...], beside(jnp.concatenate(blocks, 0))))
-        rows = pl.ds(pl.multiple_of(yh * ROWS, 8), ROWS)
-        for tile in range(4):
-            lines[tile, rows, :] = got[:, tile * LANES : (tile + 1) * LANES]
-        return 0
-
-    lax.fori_loop(0, HALF, physical_step, 0)
+    nothing = jnp.zeros((HALF, LANES), f32)
+
+    def physical_step(yhs):
+        count = len(yhs)
+        flat = [along_kz(planes, d, yh)[:96] for d in range(2) for yh in yhs]
+        steep = [along_kz(planes, 2, yh)[:96] for yh in yhs]
+        flat = folded_lanes(dot(beside(jnp.concatenate(flat, 0)), iz_ref[...]))
+        steep = folded_lanes(dot(beside(jnp.concatenate(steep, 0)), izd_ref[...]))
+        for n, yh in enumerate(yhs):
+            sets = [flat[96 * n :], flat[96 * (count + n) :], steep[96 * n :]]
+            grads = [[one[HALF * i : HALF * (i + 1)] for i in range(3)] for one in sets]
+            b = [base_ref[i, :, columns(yh)] for i in range(3)]
+            s = [state_ref[i, :, columns(yh)] for i in range(3)]
+            comb, comb_base = [], []
+            for i in range(3):
+                coupling = sum(
+                    jnp.where(core == 0, grads[j][i], grads[i][j]) * s[j] for j in range(3)
+                )
+                comb.append(s[i] - time_step * coupling)
+                drive = sum(grads[j][i] * b[j] for j in range(3))
+                if i == 0:
+                    drive = drive - force_ref[force_at, pl.ds(yh, 1), :]
+                comb_base.append(b[i] - time_step * drive)
+            rows = [comb[1], comb_base[1], comb[2], comb_base[2]]
+            rows += [comb[0], comb_base[0], nothing, nothing]
+            got = folded(dot_nt(fz_ref[...], beside(jnp.concatenate(rows, 0))))
+            for tile, part in enumerate(lane_parts(got)):
+                lines[tile, line_rows(yh), :] = part
+
+    over_lines(physical_step, 4)
     kx = kxlane_ref[0:1, :]
     keep_x = jnp.where(kx <= cut_x.astype(f32), 1.0, 0.0).astype(f32)
     keep_xy = keep_y * keep_x
@@ -581,101 +637,88 @@
         near_ref[NKZ + group] = jnp.zeros((ROWS, LANES), f32)
         far_ref[NKZ + group] = jnp.zeros((ROWS, LANES), f32)
 
-    def spectral_step(pair, _):
-        stack = []
-        for k in range(2):
-            kz = pair * 2 + k
+    def spectral_step(kzs):
+        fields = [[], [], []]
+        for pair in range(0, len(kzs), 2):
+            ks = kzs[pair : pair + 2]
+            data = [jnp.concatenate([stacked(along_y(lines, t, kz)) for kz in ks], 1) for t in (0, 1)]
+            even = lane_parts(folded(dot(fy_ref[...], data[0])))
+            odd = lane_parts(folded(dot(fyr_ref[...], data[1])))
+            for n, kz in enumerate(ks):
+                flux = flux_ref[0, kz]
+                fields[0].append(odd[n] + flux_ref[1, kz])
+                fields[1].append(jnp.where(lane < 64, even[n], flux))
+                fields[2].append(jnp.where(lane < 64, flux, even[n]))
+        data = [beside(jnp.concatenate(field, 0)) for field in fields]
+        modes = [folded_lanes(dot(data[max(n - 1, 0)], fx_ref[n])) for n in range(4)]
+        results = [[], [], [], []]
+        for n, kz in enumerate(kzs):
             kzf = kz.astype(f32)
-            first = jnp.concatenate([stacked(along_y(lines, t, kz)) for t in (0, 1)], 1)
-            second = jnp.concatenate([stacked(along_y(lines, t, kz)) for t in (2, 3)], 1)
-            even = folded(dot(fy_ref[...], first))
-            odd = folded(dot(fyr_ref[...], second))
-            factor = [fixed_ref[n] + kzf * bykz_ref[n] for n in range(3)]
-            stack.append(
-                jnp.concatenate(
-                    [
-                        even[:, :LANES] * factor[0],
-                        even[:, LANES:],
-                        odd[:, :LANES] * factor[1],
-                        odd[:, LANES:] * factor[2],
-                    ],
-                    1,
-                )
+            vx, slope, uy, uz = (mode[n * ROWS : (n + 1) * ROWS] for mode in modes)
+            square = square_xy + kzf * kzf
+            factor = keep_xy * kept_z(kz) / (1.0 + viscosity * time_step * square)
+            share = (slope + ky * uy + kzf * uz) / jnp.where(square > 0, square, 1.0)
+            results[0].append(factor * vx)
+            results[1].append(factor * share)
+            results[2].append(factor * (uy - ky * share))
+            results[3].append(factor * (uz - kzf * share))
+        got = [
+            dot(beside(jnp.concatenate(result, 0)), ix_ref[core, n])
+            for n, result in enumerate(results)
+        ]
+        got = [folded_lanes(part) for part in (got[0] + got[1], got[2], got[3])]
+        for n, kz in enumerate(kzs):
+            x, y, z = (part[n * ROWS : (n + 1) * ROWS] for part in got)
+            near_ref[kz] = jnp.where(lane < 48, x, jnp.where(lane < 96, y, z))
+            away = jnp.where(
+                (lane >= 64) & (lane < 112), x, jnp.where((lane >= 32) & (lane < 64), z, y)
             )
-        modes = triple(jnp.concatenate(stack, 0), fxh_ref[...], fxl_ref[...])
-        results = []
-        for k in range(2):
-            kz = pair * 2 + k
-            kzf = kz.astype(f32)
-            vx, slope, uy, uz = (
-                modes[k * ROWS : (k + 1) * ROWS, n * LANES : (n + 1) * LANES] for n in range(4)
-            )
-            square = square_xy + kzf * kzf
-            keep_z = jnp.where(kz <= cut_z, 1.0, 0.0).astype(f32)
-            factor = keep_xy * keep_z / (1.0 + viscosity * time_step * square)
-            share = (slope + ky * uy + kzf * uz) / jnp.where(square > 0, square, 1.0)
-            results.append(
-                jnp.concatenate(
-                    [
-                        factor * vx,
-                        factor * share,
-                        factor * (uy - ky * share),
-                        factor * (uz - kzf * share),
-                    ],
-                    1,
-                )
-            )
-        got = triple(jnp.concatenate(results, 0), ixh_ref[core], ixl_ref[core])
-        for k in range(2):
-            kz = pair * 2 + k
-            mine = got[k * ROWS : (k + 1) * ROWS]
-            near_ref[kz] = mine[:, :LANES]
-            far_ref[kz] = mine[:, LANES : 2 * LANES]
-            last = mine[:, 2 * LANES :]
+            far_ref[kz] = pltpu.roll(away, 64, 1)
             group = NKZ + kz // 8
             shift = (kz % 8) * 16
-            own = pltpu.roll(jnp.where(lane < 16, last, 0.0), shift, 1)
-            other = jnp.where((lane >= 16) & (lane < 32), last, 0.0)
-            other = pltpu.roll(other, (shift + LANES - 16) % LANES, 1)
-            near_ref[group] += own
-            far_ref[group] += other
-        return 0
-
-    lax.fori_loop(0, NKZ // 2, spectral_step, 0)
+            near_ref[group] += pltpu.roll(jnp.where(lane < 16, z, 0.0), shift, 1)
+            rest = jnp.where((lane >= 64) & (lane < 80), z, 0.0)
+            far_ref[group] += pltpu.roll(rest, (shift + 64) % LANES, 1)
+
+    over_planes(spectral_step)
 
 
 def final_kernel(
     near_ref, far_ref, state_ref, base_ref, iy_ref, iz_ref, izr_ref,
     base_out, state_out, planes,
 ):
-    def y_step(kz, _):
-        shift = (LANES - (kz % 8) * 16) % LANES
-        group = NKZ + kz // 8
-        rest = pltpu.roll(near_ref[group] + far_ref[group], shift, 1)
-        data = jnp.concatenate([near_ref[kz] + far_ref[kz], rest], 1)
-        got = folded(dot(iy_ref[...], stacked(padded(data))))
-        rows = pl.ds(pl.multiple_of(kz * LANES, LANES), LANES)
-        planes[0, rows, :] = got[:, :LANES]
-        planes[1, rows, :] = got[:, LANES:]
-        return 0
-
-    lax.fori_loop(0, NKZ, y_step, 0, unroll=2)
-
-    def z_step(yh, _):
-        data = padded(planes[0, pl.ds(yh, ROWS, stride=HALF), :]).T
-        last = padded(planes[1, pl.ds(yh, ROWS, stride=HALF), :]).T[:16]
-        turned = folded_lanes(dot(beside(data[:48]), izr_ref[...]))
-        plain = folded_lanes(dot(beside(jnp.concatenate([data[48:], last], 0)), iz_ref[...]))
-        at = columns(yh)
-        state_out[0, :, at] = turned[:32] - state_ref[0, :, at]
-        state_out[1, :, at] = plain[16:48] - state_ref[1, :, at]
-        state_out[2, :, at] = plain[48:80] - state_ref[2, :, at]
-        base_out[0, :, at] = turned[32:48] - base_ref[0, :, at]
-        base_out[1, :, at] = plain[:16] - base_ref[1, :, at]
-        base_out[2, :, at] = plain[80:96] - base_ref[2, :, at]
-        return 0
-
-    lax.fori_loop(0, HALF, z_step, 0, unroll=2)
+    def y_step(kzs):
+        for kz in kzs:
+            shift = (LANES - (kz % 8) * 16) % LANES
+            group = NKZ + kz // 8
+            rest = pltpu.roll(near_ref[group] + far_ref[group], shift, 1)
+            data = jnp.concatenate([near_ref[kz] + far_ref[kz], rest], 1)
+            got = lane_parts(folded(dot(iy_ref[...], stacked(padded(data)))))
+            planes[0, plane_rows(kz), :] = got[0]
+            planes[1, plane_rows(kz), :] = got[1]
+
+    over_planes(y_step)
+
+    def z_step(yhs):
+        data = [along_kz(planes, 0, yh) for yh in yhs]
+        rest = [along_kz(planes, 1, yh)[:16] for yh in yhs]
+        turned = beside(jnp.concatenate([one[:48] for one in data], 0))
+        plain = beside(jnp.concatenate([one[48:] for one in data] + rest, 0))
+        turned = folded_lanes(dot(turned, izr_ref[...]))
+        plain = folded_lanes(dot(plain, iz_ref[...]))
+        for n, yh in enumerate(yhs):
+            at = columns(yh)
+            first = turned[48 * n : 48 * n + 48]
+            second = plain[80 * n : 80 * n + 80]
+            third = plain[80 * len(yhs) + 16 * n :][:16]
+            state_out[0, :, at] = first[:32] - state_ref[0, :, at]
+            state_out[1, :, at] = second[16:48] - state_ref[1, :, at]
+            state_out[2, :, at] = second[48:80] - state_ref[2, :, at]
+            base_out[0, :, at] = first[32:48] - base_ref[0, :, at]
+            base_out[1, :, at] = second[:16] - base_ref[1, :, at]
+            base_out[2, :, at] = third - base_ref[2, :, at]
+
+    over_lines(z_step, 4)
 
 
 interpret = False
@@ -708,27 +751,40 @@
     base_next = lax.ppermute(base_half, "seg", back)
     state_next = lax.ppermute(own_state, ("seg", "comp"), around)
     sds = jax.ShapeDtypeStruct
-    spectrum = call(
+    core_at = core.reshape(1)
+    swap = [(0, 1), (1, 0)]
+    here_own = call(
         base_kernel,
-        sds((NKZ, ROWS, LANES), f32),
+        sds((HALF_KZ, ROWS, LANES), f32),
         [pltpu.VMEM((1, HALF * ROWS, LANES), f32)],
-        [own_base, t["fz"], t["fy"]],
+        [core_at, own_base, t["fz"], t["fy"]],
         10**9,
-    )
-    swap = [(0, 1), (1, 0)]
-    there = lax.ppermute(spectrum, "slab", swap)
+        in_smem=1,
+    )
+    there_own = lax.ppermute(here_own, "slab", swap)
+    here_other = lax.ppermute(here_own, "comp", swap)
+    there_other = lax.ppermute(there_own, "comp", swap)
+    flux = call(
+        flux_kernel,
+        sds((2, NKZ, ROWS, LANES), f32),
+        [pltpu.VMEM((3, HALF * ROWS, LANES), f32)],
+        [core_at, own_base, own_state, t["fz"], t["fy"], t["fyr"], t["kyrow"]],
+        4 * 10**9,
+        in_smem=1,
+    )
     names = (
-        "gxh", "gxl", "iy", "iyd", "iz", "izd", "fz", "fy", "fyr", "fxh", "fxl", "ixh", "ixl",
-        "fixed", "bykz", "kyrow", "kxlane", "force",
+        "gxh", "gxl", "iy", "iyd", "iz", "izd", "fz", "fy", "fyr", "fx", "ix",
+        "kyrow", "kxlane", "force",
     )
     near, far = call(
         main_kernel,
         [sds((PACKED, ROWS, LANES), f32)] * 2,
         [
             pltpu.VMEM((3, NKZ * LANES, LANES), f32),
-            pltpu.VMEM((4, HALF * ROWS, LANES), f32),
+            pltpu.VMEM((2, HALF * ROWS, LANES), f32),
         ],
-        [core.reshape(1), cutoff, wavenumber, own_base, own_state, spectrum, there]
+        [core_at, cutoff, wavenumber, own_base, own_state]
+        + [here_own, here_other, there_own, there_other, flux]
         + [t[name] for name in names],
         10**10,
         in_smem=3,

time: 118 us -> 94.1 us (0.80)
  Pallas kernels: 64.9 us -> 48.1 us
  waiting for transfers between devices: 38.8 us -> 34.7 us
  starting transfers between devices: 11.9 us -> 8.8 us
    pallas_call x3 -> x4, Pallas kernels: 64.9 us -> 48.1 us  [call(): pl.pallas_call(kernel, out_shape=outs, in_specs=[small] * in_smem + [whol...]
    ppermute x1 -> x3, waiting for transfers between devices: 18 us -> 11.6 us  [the longest x1 11.6 us: body(): there_own = lax.ppermute(here_own, 'slab', swap)]
    ppermute x1, starting transfers between devices: 3.65 us -> 0.51 us  [body(): base_next = lax.ppermute(base_half, 'seg', back)]
    ppermute x1, waiting for transfers between devices: 15.7 us -> 16.9 us  [body(): base_next = lax.ppermute(base_half, 'seg', back)]
    ppermute x1 -> x3, starting transfers between devices: 2.94 us -> 2.94 us  [the longest x1 2.94 us: body(): there_own = lax.ppermute(here_own, 'slab', swap)]
  transfers between devices with their start and end apart: 4 -> 6, of which waited for: 3 -> 3; matrix products, arithmetic and copies ran while one was open for 0% -> 0% of each run, Pallas kernels for 37% -> 36%
where the time goes in v2:
time: 94.1 us; the launch traced here: 94 us
  Pallas kernels  48.1 us (51%)
  waiting for transfers between devices  34.7 us (37%)
  starting transfers between devices  8.8 us (9%)
  between operations  1.31 us (1%)
  local copies, waits for them, and re-layouts  1.05 us (1%)
    pallas_call x4, Pallas kernels, call(): pl.pallas_call(kernel, out_shape=outs, in_specs=[small] * in_smem + [whol...  48.1 us
    ppermute x1, waiting for transfers between devices, body(): base_next = lax.ppermute(base_half, 'seg', back)  16.9 us
    ppermute x1, waiting for transfers between devices, body(): there_own = lax.ppermute(here_own, 'slab', swap)  11.6 us
    ppermute x1, waiting for transfers between devices, body(): far = lax.ppermute(far, 'slab', swap)  6.17 us
    ppermute x1, starting transfers between devices, body(): state_next = lax.ppermute(own_state, ('seg', 'comp'), around)  3.86 us
    ppermute x1, starting transfers between devices, body(): there_own = lax.ppermute(here_own, 'slab', swap)  2.94 us
  transfers between devices with their start and end apart: 6, of which 3 were waited for; matrix products, arithmetic and copies ran while one was open for 0% of the time, Pallas kernels for 36%

profile of v2, /device:TPU:0, one launch (start us, length us, event | category | flops | bytes accessed | tf_op | source)
XLA Modules:
  0.0 94.0 jit_solution(9521244417493623393)
XLA Ops:
  0.6 0.0 copy-start.4
  0.6 4.7 %shard_map.194.here_own = f32[11,88,128]{2,1,0:T(8,128)} custom-call(s32[1]{0:T(128)} %bitcast.core_ref, f32[3,32,4096]{2,1,0:T(8,128)} %bitcast.7, bf16[176,256]{1,0:T(8,128)(2,1)} %constant.41.clone.fz_ref, bf16[176,256]{1,0:T(8,128)(2,1)} %constant.45.clone.fy_ref), custom_call_target="tpu_custom_call" | custom-call | flops 1000000000 | bytes 4194304 | tf_op jit(solution)/shard_map/pallas_call | solution.py:730
  5.4 2.9 %collective-permute-start.1 = (f32[11,88,128]{2,1,0:T(8,128)}, f32[11,88,128]{2,1,0:T(8,128)}, u32[]{:S(2)}, u32[]{:S(2)}) collective-permute-start(f32[11,88,128]{2,1,0:T(8,128)} %shard_map.194.here_own), channel_id=1, source_target_pairs={{0,2},{2,0},{1,3},{3,1},{4,6},{6,4},{5,7},{7,5},{8,10},{10,8},{9,1... | collective-permute-start | bytes 1486856 | tf_op jit(solution)/shard_map/ppermute | solution.py:764
  8.3 0.0 collective-permute-start
  8.3 11.6 %collective-permute-done.1.there_own = f32[11,88,128]{2,1,0:T(8,128)} collective-permute-done((f32[11,88,128]{2,1,0:T(8,128)}, f32[11,88,128]{2,1,0:T(8,128)}, u32[]{:S(2)}, u32[]{:S(2)}) %collective-permute-start.1) | collective-permute-done | bytes 495648 | tf_op jit(solution)/shard_map/ppermute | solution.py:764
  19.9 0.0 collective-permute-start.2
  19.9 0.0 copy-done.4
  19.9 3.9 %collective-permute-start.4 = (f32[3,32,4096]{2,1,0:T(8,128)S(1)}, f32[3,32,4096]{2,1,0:T(8,128)S(1)}, u32[]{:S(2)}, u32[]{:S(2)}) collective-permute-start(f32[3,32,4096]{2,1,0:T(8,128)S(1)} %bitcast.12), channel_id=1, source_target_pairs={{4,0},{8,4},{12,8},{0,12},{1,5},{5,9},{9,13},{13,1},{6,2},{10,6},{... | collective-permute-start | bytes 4718600 | tf_op jit(solution)/shard_map/ppermute | solution.py:752
  24.5 10.6 %shard_map.195.flux_ref = f32[2,22,88,128]{3,2,1,0:T(8,128)} custom-call(s32[1]{0:T(128)} %bitcast.core_ref, f32[3,32,4096]{2,1,0:T(8,128)} %bitcast.8, f32[3,32,4096]{2,1,0:T(8,128)} %bitcast.10, bf16[176,256]{1,0:T(8,128)(2,1)} %constant.41.clone.fz_ref, bf16[176,256]{1,0:T(8,128)(2,1)} %constant.45.clone.fy_ref, bf16[176,256]{1,0:T(8,128)(2,1)} %constant.46.clone.fyr_ref, ...), custom_call_target="tpu_custom_call" | custom-call | flops 4000000000 | bytes 4194304 | tf_op jit(solution)/shard_map/pallas_call | solution.py:730
  35.1 0.0 copy-start.3
  35.1 0.0 collective-permute-done.here_other
  35.1 0.0 collective-permute-done.2.there_other
  35.1 23.4 %shard_map.196 = (f32[25,88,128]{2,1,0:T(8,128)}, f32[25,88,128]{2,1,0:T(8,128)}) custom-call(s32[1]{0:T(128)} %bitcast.core_ref, s32[3]{0:T(128)} %cutoff_ref.1, s32[1]{0:T(128)S(6)} %copy.21.wave_ref, f32[3,32,4096]{2,1,0:T(8,128)} %bitcast.9, f32[3,32,4096]{2,1,0:T(8,128)} %bitcast.11, f32[11,88,128]{2,1,0:T(8,128)} %shard_map.194.here_own, ...), custom_call_target="tpu_custom_call" | custom-call | flops 10000000000 | bytes 4194304 | tf_op jit(solution)/shard_map/pallas_call | solution.py:730
  58.5 1.5 %collective-permute-start.3 = (f32[25,88,128]{2,1,0:T(8,128)}, f32[25,88,128]{2,1,0:T(8,128)S(1)}, u32[]{:S(2)}, u32[]{:S(2)}) collective-permute-start(f32[25,88,128]{2,1,0:T(8,128)} %get-tuple-element.7), channel_id=1, source_target_pairs={{0,2},{2,0},{1,3},{3,1},{4,6},{6,4},{5,7},{7,5},{8,10},{10,8},{9,1... | collective-permute-start | bytes 3379208 | tf_op jit(solution)/shard_map/ppermute | solution.py:792
  60.0 0.0 copy-done.3
  60.0 0.1 dynamic-slice_bitcast_fusion
  60.1 0.5 collective-permute-start.5
  60.6 16.9 %collective-permute-done.5.base_ref = f32[3,16,4096]{2,1,0:T(8,128)S(1)} collective-permute-done((f32[3,16,4096]{2,1,0:T(8,128)S(1)}, f32[3,16,4096]{2,1,0:T(8,128)S(1)}, u32[]{:S(2)}, u32[]{:S(2)}) %collective-permute-start.5) | collective-permute-done | bytes 786464 | tf_op jit(solution)/shard_map/ppermute | solution.py:751
  77.5 0.0 copy-start.2
  77.5 0.0 collective-permute-done.4.state_ref
  77.5 0.0 copy-start
  77.5 6.2 %collective-permute-done.3.far_ref = f32[25,88,128]{2,1,0:T(8,128)S(1)} collective-permute-done((f32[25,88,128]{2,1,0:T(8,128)}, f32[25,88,128]{2,1,0:T(8,128)S(1)}, u32[]{:S(2)}, u32[]{:S(2)}) %collective-permute-start.3) | collective-permute-done | bytes 1126432 | tf_op jit(solution)/shard_map/ppermute | solution.py:792
  83.7 0.0 copy-start.1
  83.7 0.0 copy-done.2
  83.7 0.0 copy-done
  83.7 1.0 %copy-done.1 = f32[25,88,128]{2,1,0:T(8,128)} copy-done((f32[25,88,128]{2,1,0:T(8,128)}, f32[25,88,128]{2,1,0:T(8,128)S(1)}, u32[]{:S(2)}) %copy-start.1) | copy-done | bytes 1126424
  84.7 9.3 %shard_map.197 = (f32[3,16,4096]{2,1,0:T(8,128)}, f32[3,32,4096]{2,1,0:T(8,128)}) custom-call(f32[25,88,128]{2,1,0:T(8,128)} %get-tuple-element.6.near_ref, f32[25,88,128]{2,1,0:T(8,128)} %copy-done.1, f32[3,32,4096]{2,1,0:T(8,128)} %copy-done, f32[3,16,4096]{2,1,0:T(8,128)} %copy-done.2, bf16[256,256]{1,0:T(8,128)(2,1)} %constant.47.clone.iy_ref, ...), custom_call_target="tpu_custom_call" | custom-call | flops 1000000000 | bytes 4194304 | tf_op jit(solution)/shard_map/pallas_call | solution.py:730
Async XLA Ops:
  0.6 19.3 %copy-start.4 = (f32[1,1,3,32,4096]{4,3,2,1,0:T(8,128)S(1)}, f32[1,1,3,32,4096]{4,3,2,1,0:T(8,128)}, u32[]{:S(2)}) copy-start(f32[1,1,3,32,4096]{4,3,2,1,0:T(8,128)} %param.20) | copy-start | bytes 4718596
  5.4 14.6 %collective-permute-start.1 = (f32[11,88,128]{2,1,0:T(8,128)}, f32[11,88,128]{2,1,0:T(8,128)}, u32[]{:S(2)}, u32[]{:S(2)}) collective-permute-start(f32[11,88,128]{2,1,0:T(8,128)} %shard_map.194.here_own), channel_id=1, source_target_pairs={{0,2},{2,0},{1,3},{3,1},{4,6},{6,4},{5,7},{7,5},{8,10},{10,8},{9,1... | collective-permute-start | bytes 1486856 | tf_op jit(solution)/shard_map/ppermute | solution.py:764
  8.3 26.8 %collective-permute-start = (f32[11,88,128]{2,1,0:T(8,128)}, f32[11,88,128]{2,1,0:T(8,128)}, u32[]{:S(2)}, u32[]{:S(2)}) collective-permute-start(f32[11,88,128]{2,1,0:T(8,128)} %shard_map.194.here_own), channel_id=1, source_target_pairs={{0,1},{1,0},{2,3},{3,2},{4,5},{5,4},{6,7},{7,6},{8,9},{9,8},{10,11... | collective-permute-start | bytes 1486856 | tf_op jit(solution)/shard_map/ppermute | solution.py:765
  19.9 15.2 %collective-permute-start.2 = (f32[11,88,128]{2,1,0:T(8,128)}, f32[11,88,128]{2,1,0:T(8,128)}, u32[]{:S(2)}, u32[]{:S(2)}) collective-permute-start(f32[11,88,128]{2,1,0:T(8,128)} %collective-permute-done.1.there_own), channel_id=1, source_target_pairs={{0,1},{1,0},{2,3},{3,2},{4,5},{5,4},{6,7},{7,6},{8,9},{9,8},{10,11... | collective-permute-start | bytes 1486856 | tf_op jit(solution)/shard_map/ppermute | solution.py:766
  19.9 57.6 %collective-permute-start.4 = (f32[3,32,4096]{2,1,0:T(8,128)S(1)}, f32[3,32,4096]{2,1,0:T(8,128)S(1)}, u32[]{:S(2)}, u32[]{:S(2)}) collective-permute-start(f32[3,32,4096]{2,1,0:T(8,128)S(1)} %bitcast.12), channel_id=1, source_target_pairs={{4,0},{8,4},{12,8},{0,12},{1,5},{5,9},{9,13},{13,1},{6,2},{10,6},{... | collective-permute-start | bytes 4718600 | tf_op jit(solution)/shard_map/ppermute | solution.py:752
  35.1 24.9 %copy-start.3 = (f32[1,3,32,4096]{3,2,1,0:T(8,128)S(1)}, f32[1,3,32,4096]{3,2,1,0:T(8,128)}, u32[]{:S(2)}) copy-start(f32[1,3,32,4096]{3,2,1,0:T(8,128)} %param.19) | copy-start | bytes 4718596
  58.5 25.1 %collective-permute-start.3 = (f32[25,88,128]{2,1,0:T(8,128)}, f32[25,88,128]{2,1,0:T(8,128)S(1)}, u32[]{:S(2)}, u32[]{:S(2)}) collective-permute-start(f32[25,88,128]{2,1,0:T(8,128)} %get-tuple-element.7), channel_id=1, source_target_pairs={{0,2},{2,0},{1,3},{3,1},{4,6},{6,4},{5,7},{7,5},{8,10},{10,8},{9,1... | collective-permute-start | bytes 3379208 | tf_op jit(solution)/shard_map/ppermute | solution.py:792
  60.1 17.4 %collective-permute-start.5 = (f32[3,16,4096]{2,1,0:T(8,128)S(1)}, f32[3,16,4096]{2,1,0:T(8,128)S(1)}, u32[]{:S(2)}, u32[]{:S(2)}) collective-permute-start(f32[3,16,4096]{2,1,0:T(8,128)S(1)} %dynamic-slice_bitcast_fusion), channel_id=1, source_target_pairs={{4,0},{8,4},{12,8},{0,12},{5,1},{9,5},{13,9},{1,13},{6,2},{10,6},{... | collective-permute-start | bytes 2359304 | tf_op jit(solution)/shard_map/ppermute | solution.py:751
  77.5 6.2 %copy-start.2 = (f32[3,16,4096]{2,1,0:T(8,128)}, f32[3,16,4096]{2,1,0:T(8,128)S(1)}, u32[]{:S(2)}) copy-start(f32[3,16,4096]{2,1,0:T(8,128)S(1)} %collective-permute-done.5.base_ref) | copy-start | bytes 2359300
  77.5 6.2 %copy-start = (f32[3,32,4096]{2,1,0:T(8,128)}, f32[3,32,4096]{2,1,0:T(8,128)S(1)}, u32[]{:S(2)}) copy-start(f32[3,32,4096]{2,1,0:T(8,128)S(1)} %collective-permute-done.4.state_ref) | copy-start | bytes 4718596
  83.7 1.0 %copy-start.1 = (f32[25,88,128]{2,1,0:T(8,128)}, f32[25,88,128]{2,1,0:T(8,128)S(1)}, u32[]{:S(2)}) copy-start(f32[25,88,128]{2,1,0:T(8,128)S(1)} %collective-permute-done.3.far_ref) | copy-start | bytes 3379204

commit v3 on v2

--- a/solution.py
+++ b/solution.py
@@ -503,7 +503,7 @@
         for yh, part in zip(yhs, lane_parts(got)):
             lines[0, line_rows(yh), :] = part
 
-    over_lines(z_step, 4)
+    over_lines(z_step, 8)
     start = core_ref[0] * HALF_KZ
     for pair in range(0, HALF_KZ, 2):
         ks = range(pair, min(pair + 2, HALF_KZ))
@@ -532,7 +532,7 @@
             for tile in range(3):
                 lines[tile, line_rows(yh), :] = got[3 * n + tile]
 
-    over_lines(z_step, 2)
+    over_lines(z_step, 4)
     ky = kyrow_ref[...]
     lane = lax.broadcasted_iota(jnp.int32, (ROWS, LANES), 1)
     odd_block = (lane // HALF) % 2 == 1
@@ -627,7 +627,7 @@
             for tile, part in enumerate(lane_parts(got)):
                 lines[tile, line_rows(yh), :] = part
 
-    over_lines(physical_step, 4)
+    over_lines(physical_step, 8)
     kx = kxlane_ref[0:1, :]
     keep_x = jnp.where(kx <= cut_x.astype(f32), 1.0, 0.0).astype(f32)
     keep_xy = keep_y * keep_x
@@ -718,7 +718,7 @@
             base_out[1, :, at] = second[:16] - base_ref[1, :, at]
             base_out[2, :, at] = third - base_ref[2, :, at]
 
-    over_lines(z_step, 4)
+    over_lines(z_step, 8)
 
 
 interpret = False
@@ -763,7 +763,6 @@
     )
     there_own = lax.ppermute(here_own, "slab", swap)
     here_other = lax.ppermute(here_own, "comp", swap)
-    there_other = lax.ppermute(there_own, "comp", swap)
     flux = call(
         flux_kernel,
         sds((2, NKZ, ROWS, LANES), f32),
@@ -772,6 +771,8 @@
         4 * 10**9,
         in_smem=1,
     )
+    there_own, flux = lax.optimization_barrier((there_own, flux))
+    there_other = lax.ppermute(there_own, "comp", swap)
     names = (
         "gxh", "gxl", "iy", "iyd", "iz", "izd", "fz", "fy", "fyr", "fx", "ix",
         "kyrow", "kxlane", "force",

time: 94.1 us -> 83.7 us (0.89)
  waiting for transfers between devices: 34.7 us -> 26.2 us
  Pallas kernels: 48.1 us -> 44.5 us
    ppermute x1, waiting for transfers between devices: 11.6 us -> 2.36 us  [body(): there_own = lax.ppermute(here_own, 'slab', swap)]
    ppermute x1, waiting for transfers between devices: 16.9 us -> 23.8 us  [body(): base_next = lax.ppermute(base_half, 'seg', back)]
    ppermute x1, waiting for transfers between devices: 6.17 us -> 0.01 us  [body(): far = lax.ppermute(far, 'slab', swap)]
    pallas_call x4, Pallas kernels: 48.1 us -> 44.5 us  [call(): pl.pallas_call(kernel, out_shape=outs, in_specs=[small] * in_smem + [whol...]
  transfers between devices with their start and end apart: 6 -> 6, of which waited for: 3 -> 2; matrix products, arithmetic and copies ran while one was open for 0% -> 0% of each run, Pallas kernels for 36% -> 38%
where the time goes in v3:
time: 83.7 us; the launch traced here: 83.6 us
  Pallas kernels  44.5 us (53%)
  waiting for transfers between devices  26.2 us (31%)
  starting transfers between devices  9.73 us (12%)
  local copies, waits for them, and re-layouts  1.8 us (2%)
  between operations  1.33 us (2%)
    pallas_call x4, Pallas kernels, call(): pl.pallas_call(kernel, out_shape=outs, in_specs=[small] * in_smem + [whol...  44.5 us
    ppermute x1, waiting for transfers between devices, body(): base_next = lax.ppermute(base_half, 'seg', back)  23.8 us
    ppermute x1, starting transfers between devices, body(): state_next = lax.ppermute(own_state, ('seg', 'comp'), around)  3.86 us
    ppermute x1, starting transfers between devices, body(): there_own = lax.ppermute(here_own, 'slab', swap)  2.94 us
    ppermute x1, waiting for transfers between devices, body(): there_own = lax.ppermute(here_own, 'slab', swap)  2.36 us
    unnamed x10, local copies, waits for them, and re-layouts  1.75 us
  transfers between devices with their start and end apart: 6, of which 2 were waited for; matrix products, arithmetic and copies ran while one was open for 0% of the time, Pallas kernels for 38%

profile of v3, /device:TPU:0, one launch (start us, length us, event | category | flops | bytes accessed | tf_op | source)
XLA Modules:
  0.0 83.6 jit_solution(11979407510263140547)
XLA Ops:
  0.6 4.0 %shard_map.194.here_own = f32[11,88,128]{2,1,0:T(8,128)} custom-call(s32[1]{0:T(128)} %bitcast.core_ref, f32[3,32,4096]{2,1,0:T(8,128)} %bitcast.7, bf16[176,256]{1,0:T(8,128)(2,1)} %constant.41.clone.fz_ref, bf16[176,256]{1,0:T(8,128)(2,1)} %constant.45.clone.fy_ref), custom_call_target="tpu_custom_call" | custom-call | flops 1000000000 | bytes 4194304 | tf_op jit(solution)/shard_map/pallas_call | solution.py:730
  4.6 2.9 %collective-permute-start.1 = (f32[11,88,128]{2,1,0:T(8,128)}, f32[11,88,128]{2,1,0:T(8,128)}, u32[]{:S(2)}, u32[]{:S(2)}) collective-permute-start(f32[11,88,128]{2,1,0:T(8,128)} %shard_map.194.here_own), channel_id=1, source_target_pairs={{0,2},{2,0},{1,3},{3,1},{4,6},{6,4},{5,7},{7,5},{8,10},{10,8},{9,1... | collective-permute-start | bytes 1486856 | tf_op jit(solution)/shard_map/ppermute | solution.py:764
  7.5 0.0 collective-permute-start
  7.5 0.0 copy-start.4
  7.5 9.3 %shard_map.195.flux_ref = f32[2,22,88,128]{3,2,1,0:T(8,128)} custom-call(s32[1]{0:T(128)} %bitcast.core_ref, f32[3,32,4096]{2,1,0:T(8,128)} %bitcast.8, f32[3,32,4096]{2,1,0:T(8,128)} %bitcast.10, bf16[176,256]{1,0:T(8,128)(2,1)} %constant.41.clone.fz_ref, bf16[176,256]{1,0:T(8,128)(2,1)} %constant.45.clone.fy_ref, bf16[176,256]{1,0:T(8,128)(2,1)} %constant.46.clone.fyr_ref, ...), custom_call_target="tpu_custom_call" | custom-call | flops 4000000000 | bytes 4194304 | tf_op jit(solution)/shard_map/pallas_call | solution.py:730
  16.8 2.4 %collective-permute-done.1.there_own = f32[11,88,128]{2,1,0:T(8,128)} collective-permute-done((f32[11,88,128]{2,1,0:T(8,128)}, f32[11,88,128]{2,1,0:T(8,128)}, u32[]{:S(2)}, u32[]{:S(2)}) %collective-permute-start.1) | collective-permute-done | bytes 495648 | tf_op jit(solution)/shard_map/ppermute | solution.py:764
  19.2 0.0 collective-permute-start.2
  19.2 0.0 copy-done.4
  19.2 3.9 %collective-permute-start.4 = (f32[3,32,4096]{2,1,0:T(8,128)S(1)}, f32[3,32,4096]{2,1,0:T(8,128)S(1)}, u32[]{:S(2)}, u32[]{:S(2)}) collective-permute-start(f32[3,32,4096]{2,1,0:T(8,128)S(1)} %bitcast.12), channel_id=1, source_target_pairs={{4,0},{8,4},{12,8},{0,12},{1,5},{5,9},{9,13},{13,1},{6,2},{10,6},{... | collective-permute-start | bytes 4718600 | tf_op jit(solution)/shard_map/ppermute | solution.py:752
  23.7 0.0 copy-start.3
  23.7 0.0 collective-permute-done.here_other
  23.7 0.0 collective-permute-done.2.there_other
  23.7 22.8 %shard_map.196 = (f32[25,88,128]{2,1,0:T(8,128)}, f32[25,88,128]{2,1,0:T(8,128)}) custom-call(s32[1]{0:T(128)} %bitcast.core_ref, s32[3]{0:T(128)} %cutoff_ref.1, s32[1]{0:T(128)S(6)} %copy.21.wave_ref, f32[3,32,4096]{2,1,0:T(8,128)} %bitcast.9, f32[3,32,4096]{2,1,0:T(8,128)} %bitcast.11, f32[11,88,128]{2,1,0:T(8,128)} %shard_map.194.here_own, ...), custom_call_target="tpu_custom_call" | custom-call | flops 10000000000 | bytes 4194304 | tf_op jit(solution)/shard_map/pallas_call | solution.py:730
  46.5 1.5 %collective-permute-start.3 = (f32[25,88,128]{2,1,0:T(8,128)}, f32[25,88,128]{2,1,0:T(8,128)S(1)}, u32[]{:S(2)}, u32[]{:S(2)}) collective-permute-start(f32[25,88,128]{2,1,0:T(8,128)} %get-tuple-element.11), channel_id=1, source_target_pairs={{0,2},{2,0},{1,3},{3,1},{4,6},{6,4},{5,7},{7,5},{8,10},{10,8},{9,1... | collective-permute-start | bytes 3379208 | tf_op jit(solution)/shard_map/ppermute | solution.py:793
  48.0 0.0 copy-done.3
  48.0 0.1 dynamic-slice_bitcast_fusion
  48.0 1.4 %collective-permute-start.5 = (f32[3,16,4096]{2,1,0:T(8,128)S(1)}, f32[3,16,4096]{2,1,0:T(8,128)S(1)}, u32[]{:S(2)}, u32[]{:S(2)}) collective-permute-start(f32[3,16,4096]{2,1,0:T(8,128)S(1)} %dynamic-slice_bitcast_fusion), channel_id=1, source_target_pairs={{4,0},{8,4},{12,8},{0,12},{5,1},{9,5},{13,9},{1,13},{6,2},{10,6},{... | collective-permute-start | bytes 2359304 | tf_op jit(solution)/shard_map/ppermute | solution.py:751
  49.5 23.8 %collective-permute-done.5.base_ref = f32[3,16,4096]{2,1,0:T(8,128)S(1)} collective-permute-done((f32[3,16,4096]{2,1,0:T(8,128)S(1)}, f32[3,16,4096]{2,1,0:T(8,128)S(1)}, u32[]{:S(2)}, u32[]{:S(2)}) %collective-permute-start.5) | collective-permute-done | bytes 786464 | tf_op jit(solution)/shard_map/ppermute | solution.py:751
  73.3 0.0 copy-start.2
  73.3 0.0 collective-permute-done.4.state_ref
  73.3 0.0 copy-start
  73.3 0.0 collective-permute-done.3.far_ref
  73.3 0.0 copy-start.1
  73.3 0.9 %copy-done.2 = f32[3,16,4096]{2,1,0:T(8,128)} copy-done((f32[3,16,4096]{2,1,0:T(8,128)}, f32[3,16,4096]{2,1,0:T(8,128)S(1)}, u32[]{:S(2)}) %copy-start.2) | copy-done | bytes 786456
  74.2 0.6 copy-done
  74.7 0.3 copy-done.1
  75.1 8.5 %shard_map.197 = (f32[3,16,4096]{2,1,0:T(8,128)}, f32[3,32,4096]{2,1,0:T(8,128)}) custom-call(f32[25,88,128]{2,1,0:T(8,128)} %get-tuple-element.10.near_ref, f32[25,88,128]{2,1,0:T(8,128)} %copy-done.1, f32[3,32,4096]{2,1,0:T(8,128)} %copy-done, f32[3,16,4096]{2,1,0:T(8,128)} %copy-done.2, bf16[256,256]{1,0:T(8,128)(2,1)} %constant.47.clone.iy_ref, ...), custom_call_target="tpu_custom_call" | custom-call | flops 1000000000 | bytes 4194304 | tf_op jit(solution)/shard_map/pallas_call | solution.py:730
Async XLA Ops:
  4.6 14.6 %collective-permute-start.1 = (f32[11,88,128]{2,1,0:T(8,128)}, f32[11,88,128]{2,1,0:T(8,128)}, u32[]{:S(2)}, u32[]{:S(2)}) collective-permute-start(f32[11,88,128]{2,1,0:T(8,128)} %shard_map.194.here_own), channel_id=1, source_target_pairs={{0,2},{2,0},{1,3},{3,1},{4,6},{6,4},{5,7},{7,5},{8,10},{10,8},{9,1... | collective-permute-start | bytes 1486856 | tf_op jit(solution)/shard_map/ppermute | solution.py:764
  7.5 16.2 %collective-permute-start = (f32[11,88,128]{2,1,0:T(8,128)}, f32[11,88,128]{2,1,0:T(8,128)}, u32[]{:S(2)}, u32[]{:S(2)}) collective-permute-start(f32[11,88,128]{2,1,0:T(8,128)} %shard_map.194.here_own), channel_id=1, source_target_pairs={{0,1},{1,0},{2,3},{3,2},{4,5},{5,4},{6,7},{7,6},{8,9},{9,8},{10,11... | collective-permute-start | bytes 1486856 | tf_op jit(solution)/shard_map/ppermute | solution.py:765
  7.5 11.6 %copy-start.4 = (f32[1,1,3,32,4096]{4,3,2,1,0:T(8,128)S(1)}, f32[1,1,3,32,4096]{4,3,2,1,0:T(8,128)}, u32[]{:S(2)}) copy-start(f32[1,1,3,32,4096]{4,3,2,1,0:T(8,128)} %param.20) | copy-start | bytes 4718596
  19.2 4.5 %collective-permute-start.2 = (f32[11,88,128]{2,1,0:T(8,128)}, f32[11,88,128]{2,1,0:T(8,128)}, u32[]{:S(2)}, u32[]{:S(2)}) collective-permute-start(f32[11,88,128]{2,1,0:T(8,128)} %collective-permute-done.1.there_own), channel_id=1, source_target_pairs={{0,1},{1,0},{2,3},{3,2},{4,5},{5,4},{6,7},{7,6},{8,9},{9,8},{10,11... | collective-permute-start | bytes 1486856 | tf_op jit(solution)/shard_map/ppermute | solution.py:775
  19.2 54.1 %collective-permute-start.4 = (f32[3,32,4096]{2,1,0:T(8,128)S(1)}, f32[3,32,4096]{2,1,0:T(8,128)S(1)}, u32[]{:S(2)}, u32[]{:S(2)}) collective-permute-start(f32[3,32,4096]{2,1,0:T(8,128)S(1)} %bitcast.12), channel_id=1, source_target_pairs={{4,0},{8,4},{12,8},{0,12},{1,5},{5,9},{9,13},{13,1},{6,2},{10,6},{... | collective-permute-start | bytes 4718600 | tf_op jit(solution)/shard_map/ppermute | solution.py:752
  23.7 24.3 %copy-start.3 = (f32[1,3,32,4096]{3,2,1,0:T(8,128)S(1)}, f32[1,3,32,4096]{3,2,1,0:T(8,128)}, u32[]{:S(2)}) copy-start(f32[1,3,32,4096]{3,2,1,0:T(8,128)} %param.19) | copy-start | bytes 4718596
  46.5 26.8 %collective-permute-start.3 = (f32[25,88,128]{2,1,0:T(8,128)}, f32[25,88,128]{2,1,0:T(8,128)S(1)}, u32[]{:S(2)}, u32[]{:S(2)}) collective-permute-start(f32[25,88,128]{2,1,0:T(8,128)} %get-tuple-element.11), channel_id=1, source_target_pairs={{0,2},{2,0},{1,3},{3,1},{4,6},{6,4},{5,7},{7,5},{8,10},{10,8},{9,1... | collective-permute-start | bytes 3379208 | tf_op jit(solution)/shard_map/ppermute | solution.py:793
  48.0 25.3 %collective-permute-start.5 = (f32[3,16,4096]{2,1,0:T(8,128)S(1)}, f32[3,16,4096]{2,1,0:T(8,128)S(1)}, u32[]{:S(2)}, u32[]{:S(2)}) collective-permute-start(f32[3,16,4096]{2,1,0:T(8,128)S(1)} %dynamic-slice_bitcast_fusion), channel_id=1, source_target_pairs={{4,0},{8,4},{12,8},{0,12},{5,1},{9,5},{13,9},{1,13},{6,2},{10,6},{... | collective-permute-start | bytes 2359304 | tf_op jit(solution)/shard_map/ppermute | solution.py:751
  73.3 0.9 %copy-start.2 = (f32[3,16,4096]{2,1,0:T(8,128)}, f32[3,16,4096]{2,1,0:T(8,128)S(1)}, u32[]{:S(2)}) copy-start(f32[3,16,4096]{2,1,0:T(8,128)S(1)} %collective-permute-done.5.base_ref) | copy-start | bytes 2359300
  73.3 1.4 %copy-start = (f32[3,32,4096]{2,1,0:T(8,128)}, f32[3,32,4096]{2,1,0:T(8,128)S(1)}, u32[]{:S(2)}) copy-start(f32[3,32,4096]{2,1,0:T(8,128)S(1)} %collective-permute-done.4.state_ref) | copy-start | bytes 4718596
  73.3 1.7 %copy-start.1 = (f32[25,88,128]{2,1,0:T(8,128)}, f32[25,88,128]{2,1,0:T(8,128)S(1)}, u32[]{:S(2)}) copy-start(f32[25,88,128]{2,1,0:T(8,128)S(1)} %collective-permute-done.3.far_ref) | copy-start | bytes 3379204

commit v4 on v3

--- a/solution.py
+++ b/solution.py
@@ -15,7 +15,9 @@
 NKZ = KEEP + 1
 NKY = 44
 ROWS = 2 * NKY
-PACKED = NKZ + 3
+CHUNK = 8
+CHUNKS = 3
+LINE = CHUNKS * CHUNK * 4
 HALF_KZ = NKZ // 2
 LANES = 128
 
@@ -288,20 +290,21 @@
     kz = np.arange(NKZ)
     angle = 2 * np.pi * kz[:, None] * z[None, :] / N
     weight = np.where(kz == 0, 1.0, 2.0)[:, None] / N
-    forward = np.zeros((2, 2, NKZ, 2, N))
+    forward = np.zeros((2, 2, CHUNKS * CHUNK, 2, N))
     inverse = np.zeros((NKZ, 2, 2, 2, N))
     turned = np.zeros((NKZ, 2, 2, 2, N))
     slope = np.zeros((NKZ, 2, 2, 2, N))
     for y2 in range(2):
-        forward[y2, 0, :, y2] = np.cos(angle)
-        forward[y2, 1, :, y2] = -np.sin(angle)
+        forward[y2, 0, :NKZ, y2] = np.cos(angle)
+        forward[y2, 1, :NKZ, y2] = -np.sin(angle)
         inverse[:, y2, 0, y2] = weight * np.cos(angle)
         inverse[:, y2, 1, y2] = -weight * np.sin(angle)
         turned[:, y2, 0, y2] = weight * np.sin(angle)
         turned[:, y2, 1, y2] = weight * np.cos(angle)
         slope[:, y2, 0, y2] = -weight * kz[:, None] * np.sin(angle)
         slope[:, y2, 1, y2] = -weight * kz[:, None] * np.cos(angle)
-    out["fz"] = left_table(forward.reshape(4 * NKZ, 2 * N), 128)
+    forward = np.moveaxis(forward.reshape(4, CHUNKS, CHUNK, 2 * N), 1, 0)
+    out["fz"] = left_table(forward.reshape(LINE, 2 * N), 128)
     out["iz"] = right_table(inverse.reshape(4 * NKZ, 2 * N), 128)
     out["izr"] = right_table(turned.reshape(4 * NKZ, 2 * N), 128)
     out["izd"] = right_table(slope.reshape(4 * NKZ, 2 * N), 128)
@@ -453,9 +456,10 @@
     return pl.ds(pl.multiple_of(yh * LANES, LANES), LANES)
 
 
-def along_y(ref, tile, kz):
+def along_y(ref, tile, kz, line=LINE):
+    at = kz % CHUNK + (0 if line == LINE // CHUNKS else kz // CHUNK * (4 * CHUNK))
     return jnp.concatenate(
-        [ref[tile, pl.ds(q * NKZ + kz, HALF, stride=ROWS), :] for q in range(4)], 0
+        [ref[tile, pl.ds(q * CHUNK + at, HALF, stride=line), :] for q in range(4)], 0
     )
 
 
@@ -464,7 +468,7 @@
 
 
 def line_rows(yh):
-    return pl.ds(pl.multiple_of(yh * ROWS, 8), ROWS)
+    return pl.ds(pl.multiple_of(yh * LINE, 8), LINE)
 
 
 def plane_rows(kz):
@@ -475,13 +479,19 @@
     return [values[:, at : at + LANES] for at in range(0, values.shape[1], LANES)]
 
 
-def over_planes(step):
+def over_planes(step, first=0, last=NKZ):
     def four(index, _):
-        step([index * 4 + k for k in range(4)])
+        step([first + index * 4 + k for k in range(4)])
         return 0
 
-    lax.fori_loop(0, NKZ // 4, four, 0)
-    step([jnp.int32(kz) for kz in range(NKZ // 4 * 4, NKZ)])
+    count = (last - first) // 4
+    lax.fori_loop(0, count, four, 0)
+    if first + count * 4 < last:
+        step([jnp.int32(kz) for kz in range(first + count * 4, last)])
+
+
+def planes_of(chunk):
+    return chunk * CHUNK, min((chunk + 1) * CHUNK, NKZ)
 
 
 def over_lines(step, many):
@@ -514,8 +524,9 @@
 
 
 def flux_kernel(
-    core_ref, base_ref, state_ref, fz_ref, fy_ref, fyr_ref, kyrow_ref, out_ref, lines
+    core_ref, base_ref, state_ref, fz_ref, fy_ref, fyr_ref, kyrow_ref, *refs
 ):
+    *out_refs, lines = refs
     sigma = jnp.where(core_ref[0] == 0, -time_step, time_step).astype(f32)
     nothing = jnp.zeros((HALF, LANES), f32)
 
@@ -537,7 +548,8 @@
     lane = lax.broadcasted_iota(jnp.int32, (ROWS, LANES), 1)
     odd_block = (lane // HALF) % 2 == 1
 
-    def y_step(kzs):
+    def y_step(chunk, kzs):
+        out_ref = out_refs[chunk]
         even = []
         for pair in range(0, len(kzs), 2):
             data = [stacked(along_y(lines, 0, kz)) for kz in kzs[pair : pair + 2]]
@@ -551,21 +563,22 @@
             plain = even[n]
             slopes = odd[n][0] * jnp.where(odd_block, kzf, ky)
             slopes = slopes + pltpu.roll(slopes, 32, 1)
-            out_ref[0, kz] = jnp.where(odd_block, slopes, plain)
+            at = kz - chunk * CHUNK
+            out_ref[0, at] = jnp.where(odd_block, slopes, plain)
             other = plain * jnp.where(lane >= 96, -kzf, -ky)
             other = other + pltpu.roll(other, 64, 1)
-            out_ref[1, kz] = jnp.where(lane >= 96, other, odd[n][1])
-
-    over_planes(y_step)
-
-
-def main_kernel(
+            out_ref[1, at] = jnp.where(lane >= 96, other, odd[n][1])
+
+    for chunk in range(CHUNKS):
+        over_planes(functools.partial(y_step, chunk), *planes_of(chunk))
+
+
+def gradient_kernel(
     core_ref, cutoff_ref, wave_ref, base_ref, state_ref,
-    here_own, here_other, there_own, there_other, flux_ref,
-    gxh_ref, gxl_ref, iy_ref, iyd_ref, iz_ref, izd_ref, fz_ref, fy_ref, fyr_ref,
-    fx_ref, ix_ref, kyrow_ref, kxlane_ref, force_ref,
-    near_ref, far_ref, planes, lines,
+    here_own, here_other, there_own, there_other,
+    gxh_ref, gxl_ref, iy_ref, iyd_ref, iz_ref, izd_ref, fz_ref, kyrow_ref, force_ref, *refs
 ):
+    *out_refs, planes = refs
     core = core_ref[0]
     cut_x, cut_y, cut_z = cutoff_ref[0], cutoff_ref[1], cutoff_ref[2]
     which = jnp.clip(cut_x - (KEEP - 3), 0, 3)
@@ -624,29 +637,51 @@
             rows = [comb[1], comb_base[1], comb[2], comb_base[2]]
             rows += [comb[0], comb_base[0], nothing, nothing]
             got = folded(dot_nt(fz_ref[...], beside(jnp.concatenate(rows, 0))))
+            depth = LINE // CHUNKS
+            rows = pl.ds(pl.multiple_of(yh * depth, 8), depth)
             for tile, part in enumerate(lane_parts(got)):
-                lines[tile, line_rows(yh), :] = part
+                for chunk in range(CHUNKS):
+                    out_refs[chunk][tile, rows, :] = part[chunk * depth : (chunk + 1) * depth]
 
     over_lines(physical_step, 8)
+
+
+def spectral_kernel(
+    chunk, core_ref, cutoff_ref, lines_ref, flux_ref,
+    fy_ref, fyr_ref, fx_ref, ix_ref, kyrow_ref, kxlane_ref, near_ref, far_ref,
+):
+    core = core_ref[0]
+    cut_x, cut_y, cut_z = cutoff_ref[0], cutoff_ref[1], cutoff_ref[2]
+    first, last = planes_of(chunk)
+    extra = last - first
+    ky = kyrow_ref[...]
     kx = kxlane_ref[0:1, :]
+    keep_y = jnp.where(jnp.abs(ky) <= cut_y.astype(f32), 1.0, 0.0).astype(f32)
     keep_x = jnp.where(kx <= cut_x.astype(f32), 1.0, 0.0).astype(f32)
     keep_xy = keep_y * keep_x
     square_xy = ky * ky + kx * kx
     lane = lax.broadcasted_iota(jnp.int32, (ROWS, LANES), 1)
-    for group in range(3):
-        near_ref[NKZ + group] = jnp.zeros((ROWS, LANES), f32)
-        far_ref[NKZ + group] = jnp.zeros((ROWS, LANES), f32)
+    near_ref[extra] = jnp.zeros((ROWS, LANES), f32)
+    far_ref[extra] = jnp.zeros((ROWS, LANES), f32)
+
+    def kept_z(kz):
+        return jnp.where(kz <= cut_z, 1.0, 0.0).astype(f32)
 
     def spectral_step(kzs):
         fields = [[], [], []]
         for pair in range(0, len(kzs), 2):
             ks = kzs[pair : pair + 2]
-            data = [jnp.concatenate([stacked(along_y(lines, t, kz)) for kz in ks], 1) for t in (0, 1)]
+            data = [
+                jnp.concatenate(
+                    [stacked(along_y(lines_ref, t, kz, LINE // CHUNKS)) for kz in ks], 1
+                )
+                for t in (0, 1)
+            ]
             even = lane_parts(folded(dot(fy_ref[...], data[0])))
             odd = lane_parts(folded(dot(fyr_ref[...], data[1])))
             for n, kz in enumerate(ks):
-                flux = flux_ref[0, kz]
-                fields[0].append(odd[n] + flux_ref[1, kz])
+                flux = flux_ref[0, kz - first]
+                fields[0].append(odd[n] + flux_ref[1, kz - first])
                 fields[1].append(jnp.where(lane < 64, even[n], flux))
                 fields[2].append(jnp.where(lane < 64, flux, even[n]))
         data = [beside(jnp.concatenate(field, 0)) for field in fields]
@@ -669,39 +704,55 @@
         got = [folded_lanes(part) for part in (got[0] + got[1], got[2], got[3])]
         for n, kz in enumerate(kzs):
             x, y, z = (part[n * ROWS : (n + 1) * ROWS] for part in got)
-            near_ref[kz] = jnp.where(lane < 48, x, jnp.where(lane < 96, y, z))
+            near_ref[kz - first] = jnp.where(lane < 48, x, jnp.where(lane < 96, y, z))
             away = jnp.where(
                 (lane >= 64) & (lane < 112), x, jnp.where((lane >= 32) & (lane < 64), z, y)
             )
-            far_ref[kz] = pltpu.roll(away, 64, 1)
-            group = NKZ + kz // 8
-            shift = (kz % 8) * 16
-            near_ref[group] += pltpu.roll(jnp.where(lane < 16, z, 0.0), shift, 1)
+            far_ref[kz - first] = pltpu.roll(away, 64, 1)
+            shift = (kz - first) * 16
+            near_ref[extra] += pltpu.roll(jnp.where(lane < 16, z, 0.0), shift, 1)
             rest = jnp.where((lane >= 64) & (lane < 80), z, 0.0)
-            far_ref[group] += pltpu.roll(rest, (shift + 64) % LANES, 1)
-
-    over_planes(spectral_step)
+            far_ref[extra] += pltpu.roll(rest, (shift + 64) % LANES, 1)
+
+    over_planes(spectral_step, first, last)
+
+
+def inverse_y(near_ref, far_ref, iy_ref, planes):
+    count = near_ref.shape[0] - 1
+    rest = near_ref[count] + far_ref[count]
+    for kz in range(count):
+        turned = pltpu.roll(rest, (LANES - kz * 16) % LANES, 1) if kz else rest
+        data = jnp.concatenate([near_ref[kz] + far_ref[kz], turned], 1)
+        got = lane_parts(folded(dot(iy_ref[...], stacked(padded(data)))))
+        for tile in range(2):
+            planes[tile, kz * LANES : (kz + 1) * LANES, :] = got[tile]
+    if count < CHUNK:
+        blank = jnp.zeros(((CHUNK - count) * LANES, LANES), f32)
+        for tile in range(2):
+            planes[tile, count * LANES :, :] = blank
+
+
+def inverse_kernel(near_a, far_a, near_b, far_b, iy_ref, planes_a, planes_b):
+    inverse_y(near_a, far_a, iy_ref, planes_a)
+    inverse_y(near_b, far_b, iy_ref, planes_b)
 
 
 def final_kernel(
-    near_ref, far_ref, state_ref, base_ref, iy_ref, iz_ref, izr_ref,
-    base_out, state_out, planes,
+    near_ref, far_ref, planes_a, planes_b, state_ref, base_ref, iy_ref, iz_ref, izr_ref,
+    base_out, state_out, planes_c,
 ):
-    def y_step(kzs):
-        for kz in kzs:
-            shift = (LANES - (kz % 8) * 16) % LANES
-            group = NKZ + kz // 8
-            rest = pltpu.roll(near_ref[group] + far_ref[group], shift, 1)
-            data = jnp.concatenate([near_ref[kz] + far_ref[kz], rest], 1)
-            got = lane_parts(folded(dot(iy_ref[...], stacked(padded(data)))))
-            planes[0, plane_rows(kz), :] = got[0]
-            planes[1, plane_rows(kz), :] = got[1]
-
-    over_planes(y_step)
+    inverse_y(near_ref, far_ref, iy_ref, planes_c)
+
+    def along_chunks(tile, yh):
+        parts = [
+            ref[tile, pl.ds(yh, 4 * CHUNK, stride=HALF), :]
+            for ref in (planes_a, planes_b, planes_c)
+        ]
+        return padded(jnp.concatenate(parts, 0)).T
 
     def z_step(yhs):
-        data = [along_kz(planes, 0, yh) for yh in yhs]
-        rest = [along_kz(planes, 1, yh)[:16] for yh in yhs]
+        data = [along_chunks(0, yh) for yh in yhs]
+        rest = [along_chunks(1, yh)[:16] for yh in yhs]
         turned = beside(jnp.concatenate([one[:48] for one in data], 0))
         plain = beside(jnp.concatenate([one[48:] for one in data] + rest, 0))
         turned = folded_lanes(dot(turned, izr_ref[...]))
@@ -724,7 +775,7 @@
 interpret = False
 
 
-def call(kernel, outs, scratch, inputs, flops, in_smem=0):
+def call(kernel, outs, scratch, inputs, in_smem=0, room=24):
     whole = pl.BlockSpec(memory_space=pltpu.VMEM)
     small = pl.BlockSpec(memory_space=pltpu.SMEM)
     return pl.pallas_call(
@@ -733,8 +784,8 @@
         in_specs=[small] * in_smem + [whole] * (len(inputs) - in_smem),
         out_specs=jax.tree.map(lambda _: whole, outs),
         scratch_shapes=scratch,
-        compiler_params=pltpu.CompilerParams(vmem_limit_bytes=56 * 2**20),
-        cost_estimate=pl.CostEstimate(flops=flops, bytes_accessed=4 * 2**20, transcendentals=0),
+        compiler_params=pltpu.CompilerParams(vmem_limit_bytes=room * 2**20),
+        cost_estimate=pl.CostEstimate(flops=1000, bytes_accessed=1000, transcendentals=0),
         interpret=interpret,
     )(*inputs)
 
@@ -756,47 +807,54 @@
     here_own = call(
         base_kernel,
         sds((HALF_KZ, ROWS, LANES), f32),
-        [pltpu.VMEM((1, HALF * ROWS, LANES), f32)],
+        [pltpu.VMEM((1, HALF * LINE, LANES), f32)],
         [core_at, own_base, t["fz"], t["fy"]],
-        10**9,
         in_smem=1,
     )
     there_own = lax.ppermute(here_own, "slab", swap)
     here_other = lax.ppermute(here_own, "comp", swap)
+    counts = [planes_of(chunk)[1] - planes_of(chunk)[0] for chunk in range(CHUNKS)]
     flux = call(
         flux_kernel,
-        sds((2, NKZ, ROWS, LANES), f32),
-        [pltpu.VMEM((3, HALF * ROWS, LANES), f32)],
+        [sds((2, count, ROWS, LANES), f32) for count in counts],
+        [pltpu.VMEM((3, HALF * LINE, LANES), f32)],
         [core_at, own_base, own_state, t["fz"], t["fy"], t["fyr"], t["kyrow"]],
-        4 * 10**9,
         in_smem=1,
     )
     there_own, flux = lax.optimization_barrier((there_own, flux))
     there_other = lax.ppermute(there_own, "comp", swap)
-    names = (
-        "gxh", "gxl", "iy", "iyd", "iz", "izd", "fz", "fy", "fyr", "fx", "ix",
-        "kyrow", "kxlane", "force",
-    )
-    near, far = call(
-        main_kernel,
-        [sds((PACKED, ROWS, LANES), f32)] * 2,
-        [
-            pltpu.VMEM((3, NKZ * LANES, LANES), f32),
-            pltpu.VMEM((2, HALF * ROWS, LANES), f32),
-        ],
+    names = ("gxh", "gxl", "iy", "iyd", "iz", "izd", "fz", "kyrow", "force")
+    lines = call(
+        gradient_kernel,
+        [sds((2, HALF * 4 * CHUNK, LANES), f32)] * CHUNKS,
+        [pltpu.VMEM((3, NKZ * LANES, LANES), f32)],
         [core_at, cutoff, wavenumber, own_base, own_state]
-        + [here_own, here_other, there_own, there_other, flux]
+        + [here_own, here_other, there_own, there_other]
         + [t[name] for name in names],
-        10**10,
         in_smem=3,
     )
-    far = lax.ppermute(far, "slab", swap)
+    names = ("fy", "fyr", "fx", "ix", "kyrow", "kxlane")
+    near, far = [], []
+    for chunk in range(CHUNKS):
+        near_part, far_part = call(
+            functools.partial(spectral_kernel, chunk),
+            [sds((counts[chunk] + 1, ROWS, LANES), f32)] * 2,
+            [],
+            [core_at, cutoff, lines[chunk], flux[chunk]] + [t[name] for name in names],
+            in_smem=2,
+        )
+        near.append(near_part)
+        far.append(lax.ppermute(far_part, "slab", swap))
+    planes = sds((2, CHUNK * LANES, LANES), f32)
+    planes_a, planes_b = call(
+        inverse_kernel, [planes] * 2, [], [near[0], far[0], near[1], far[1], t["iy"]]
+    )
     base_gap, state_gap = call(
         final_kernel,
         [sds((3, 16, N * N), f32), sds((3, HALF, N * N), f32)],
-        [pltpu.VMEM((2, NKZ * LANES, LANES), f32)],
-        [near, far, state_next, base_next, t["iy"], t["iz"], t["izr"]],
-        10**9,
+        [pltpu.VMEM((2, CHUNK * LANES, LANES), f32)],
+        [near[2], far[2], planes_a, planes_b, state_next, base_next]
+        + [t["iy"], t["iz"], t["izr"]],
     )
     return base_gap[None], state_gap[None, None]
 

time: 83.7 us -> 78 us (0.932)
  waiting for transfers between devices: 26.2 us -> 17.9 us
  local copies, waits for them, and re-layouts: 1.8 us -> 7.76 us
  Pallas kernels: 44.5 us -> 39.4 us
  starting transfers between devices: 9.73 us -> 11.1 us
    ppermute x1, waiting for transfers between devices: 23.8 us -> 0.01 us  [body(): base_next = lax.ppermute(base_half, 'seg', back)]
    ppermute x1 -> x3, waiting for transfers between devices: 0.01 us -> 17.6 us  [body(): far.append(lax.ppermute(far_part, 'slab', swap))]
    unnamed x10 -> x54, local copies, waits for them, and re-layouts: 1.75 us -> 7.71 us
    pallas_call x4 -> x8, Pallas kernels: 44.5 us -> 39.4 us  [call(): pl.pallas_call(kernel, out_shape=outs, in_specs=[small] * in_smem + [whol...]
    ppermute x1, waiting for transfers between devices: 2.36 us -> 0.01 us  [body(): there_own = lax.ppermute(here_own, 'slab', swap)]
    ppermute x1 -> x3, starting transfers between devices: 1.49 us -> 3.27 us  [body(): far.append(lax.ppermute(far_part, 'slab', swap))]
  transfers between devices with their start and end apart: 6 -> 8, of which waited for: 2 -> 4; matrix products, arithmetic and copies ran while one was open for 0% -> 0% of each run, Pallas kernels for 38% -> 39%
where the time goes in v4:
time: 78 us; the launch traced here: 77.7 us
  Pallas kernels  39.4 us (51%)
  waiting for transfers between devices  17.9 us (23%)
  starting transfers between devices  11.1 us (14%)
  local copies, waits for them, and re-layouts  7.76 us (10%)
  between operations  1.53 us (2%)
    pallas_call x8, Pallas kernels, call(): pl.pallas_call(kernel, out_shape=outs, in_specs=[small] * in_smem + [whol...  39.4 us
    ppermute x3, waiting for transfers between devices, body(): far.append(lax.ppermute(far_part, 'slab', swap))  17.6 us
    unnamed x54, local copies, waits for them, and re-layouts  7.71 us
    ppermute x1, starting transfers between devices, body(): state_next = lax.ppermute(own_state, ('seg', 'comp'), around)  3.6 us
    ppermute x3, starting transfers between devices, body(): far.append(lax.ppermute(far_part, 'slab', swap))  3.27 us
    ppermute x1, starting transfers between devices, body(): there_own = lax.ppermute(here_own, 'slab', swap)  2.94 us
  transfers between devices with their start and end apart: 8, of which 4 were waited for; matrix products, arithmetic and copies ran while one was open for 0% of the time, Pallas kernels for 39%

profile of v4, /device:TPU:0, one launch (start us, length us, event | category | flops | bytes accessed | tf_op | source)
XLA Modules:
  0.0 77.7 jit_solution(557801455889308837)
XLA Ops:
  0.6 0.0 copy-start
  0.6 1.4 %copy-done = f32[1,3,32,4096]{3,2,1,0:T(8,128)S(1)} copy-done((f32[1,3,32,4096]{3,2,1,0:T(8,128)S(1)}, f32[1,3,32,4096]{3,2,1,0:T(8,128)}, u32[]{:S(2)}) %copy-start) | copy-done | bytes 1572888
  2.0 0.9 %copy-done.5 = bf16[176,256]{1,0:T(8,128)(2,1)S(1)} copy-done((bf16[176,256]{1,0:T(8,128)(2,1)S(1)}, bf16[176,256]{1,0:T(8,128)(2,1)}, u32[]{:S(2)}) %copy-start.5) | copy-done | bytes 90136
  2.9 0.9 %copy-done.10 = bf16[192,256]{1,0:T(8,128)(2,1)S(1)} copy-done((bf16[192,256]{1,0:T(8,128)(2,1)S(1)}, bf16[192,256]{1,0:T(8,128)(2,1)}, u32[]{:S(2)}) %copy-start.10) | copy-done | bytes 98328
  3.8 3.0 %shard_map.194.here_own = f32[11,88,128]{2,1,0:T(8,128)} custom-call(s32[1]{0:T(128)} %bitcast.core_ref, f32[3,32,4096]{2,1,0:T(8,128)S(1)} %bitcast.7, bf16[192,256]{1,0:T(8,128)(2,1)S(1)} %copy-done.10, bf16[176,256]{1,0:T(8,128)(2,1)S(1)} %copy-done.5), custom_call_target="tpu_custom_call" | custom-call | flops 1000 | bytes 1000 | tf_op jit(solution)/shard_map/pallas_call | solution.py:781
  6.9 2.9 %collective-permute-start.1 = (f32[11,88,128]{2,1,0:T(8,128)}, f32[11,88,128]{2,1,0:T(8,128)}, u32[]{:S(2)}, u32[]{:S(2)}) collective-permute-start(f32[11,88,128]{2,1,0:T(8,128)} %shard_map.194.here_own), channel_id=1, source_target_pairs={{0,2},{2,0},{1,3},{3,1},{4,6},{6,4},{5,7},{7,5},{8,10},{10,8},{9,1... | collective-permute-start | bytes 1486856 | tf_op jit(solution)/shard_map/ppermute | solution.py:814
  9.8 3.6 %collective-permute-start.6 = (f32[3,32,4096]{2,1,0:T(8,128)S(1)}, f32[3,32,4096]{2,1,0:T(8,128)}, u32[]{:S(2)}, u32[]{:S(2)}) collective-permute-start(f32[3,32,4096]{2,1,0:T(8,128)S(1)} %bitcast.10), channel_id=1, source_target_pairs={{4,0},{8,4},{12,8},{0,12},{1,5},{5,9},{9,13},{13,1},{6,2},{10,6},{... | collective-permute-start | bytes 4718600 | tf_op jit(solution)/shard_map/ppermute | solution.py:803
  13.4 0.0 collective-permute-start
  13.4 0.0 copy-done.9
  13.4 8.4 %shard_map.195 = (f32[2,8,88,128]{3,2,1,0:T(8,128)S(1)}, f32[2,8,88,128]{3,2,1,0:T(8,128)S(1)}, f32[2,6,88,128]{3,2,1,0:T(8,128)S(1)}) custom-call(s32[1]{0:T(128)} %bitcast.core_ref, f32[3,32,4096]{2,1,0:T(8,128)S(1)} %bitcast.8, f32[3,32,4096]{2,1,0:T(8,128)S(1)} %bitcast.11, bf16[192,256]{1,0:T(8,128)(2,1)S(1)} %copy-done.10, ...), custom_call_target="tpu_custom_call" | custom-call | flops 1000 | bytes 1000 | tf_op jit(solution)/shard_map/pallas_call | solution.py:781
  21.8 0.0 copy-start.12
  21.9 0.8 %copy-done.12 = f32[2,8,88,128]{3,2,1,0:T(8,128)} copy-done((f32[2,8,88,128]{3,2,1,0:T(8,128)}, f32[2,8,88,128]{3,2,1,0:T(8,128)S(1)}, u32[]{:S(2)}) %copy-start.12) | copy-done | bytes 720920
  22.7 0.9 %copy-done.14 = f32[2,8,88,128]{3,2,1,0:T(8,128)} copy-done((f32[2,8,88,128]{3,2,1,0:T(8,128)}, f32[2,8,88,128]{3,2,1,0:T(8,128)S(1)}, u32[]{:S(2)}) %copy-start.14) | copy-done | bytes 720920
  23.6 0.8 %copy-done.16 = f32[2,6,88,128]{3,2,1,0:T(8,128)} copy-done((f32[2,6,88,128]{3,2,1,0:T(8,128)}, f32[2,6,88,128]{3,2,1,0:T(8,128)S(1)}, u32[]{:S(2)}) %copy-start.16) | copy-done | bytes 540696
  24.4 0.0 copy-start.19
  24.4 0.0 copy-start.20
  24.4 0.0 copy-start.22
  24.4 0.0 collective-permute-done.1.there_own
  24.4 0.6 collective-permute-start.2
  25.0 0.0 copy-done.1
  25.0 0.1 dynamic-slice_bitcast_fusion
  25.1 0.7 collective-permute-start.7
  26.4 0.0 copy-start.2
  26.4 0.0 copy-start.4
  26.4 0.0 copy-start.6
  26.4 0.0 copy-start.15
  26.4 0.0 collective-permute-done.here_other
  26.5 0.3 collective-permute-done.2.there_other
  26.7 0.0 copy-done.8
  26.7 0.0 copy-done.19
  26.7 0.0 copy-start.23
  26.8 1.1 %copy-done.23 = bf16[256,256]{1,0:T(8,128)(2,1)S(1)} copy-done((bf16[256,256]{1,0:T(8,128)(2,1)S(1)}, bf16[256,256]{1,0:T(8,128)(2,1)}, u32[]{:S(2)}) %copy-start.23) | copy-done | bytes 131096
  27.8 0.8 %copy-done.24 = f32[4,32,128]{2,1,0:T(8,128)S(1)} copy-done((f32[4,32,128]{2,1,0:T(8,128)S(1)}, f32[4,32,128]{2,1,0:T(8,128)}, u32[]{:S(2)}) %copy-start.24) | copy-done | bytes 65560
  28.7 12.9 %shard_map.196 = (f32[2,1024,128]{2,1,0:T(8,128)S(1)}, f32[2,1024,128]{2,1,0:T(8,128)S(1)}, f32[2,1024,128]{2,1,0:T(8,128)S(1)}) custom-call(s32[1]{0:T(128)} %bitcast.core_ref, s32[3]{0:T(128)S(1)} %copy-done.26, s32[1]{0:T(128)S(6)} %copy.21.wave_ref, f32[3,32,4096]{2,1,0:T(8,128)S(1)} %bitcast.9, f32[3,32,4096]{2,1,0:T(8,128)S(1)} %bitcast.12, ...), custom_call_target="tpu_custom_call" | custom-call | flops 1000 | bytes 1000 | tf_op jit(solution)/shard_map/pallas_call | solution.py:781
  41.6 0.0 copy-start.13
  41.6 3.1 %shard_map.199 = (f32[9,88,128]{2,1,0:T(8,128)S(1)}, f32[9,88,128]{2,1,0:T(8,128)S(1)}) custom-call(s32[1]{0:T(128)} %bitcast.core_ref, s32[3]{0:T(128)S(1)} %copy-done.26, f32[2,1024,128]{2,1,0:T(8,128)S(1)} %get-tuple-element.34.lines_ref, f32[2,8,88,128]{3,2,1,0:T(8,128)S(1)} %copy-done.15, bf16[176,256]{1,0:T(8,128)(2,1)S(1)} %copy-done.6, ...), custom_call_target="tpu_custom_call" | custom-call | flops 1000 | bytes 1000 | tf_op jit(solution)/shard_map/pallas_call | solution.py:781
  44.7 1.1 %collective-permute-start.5 = (f32[9,88,128]{2,1,0:T(8,128)S(1)}, f32[9,88,128]{2,1,0:T(8,128)S(1)}, u32[]{:S(2)}, u32[]{:S(2)}) collective-permute-start(f32[9,88,128]{2,1,0:T(8,128)S(1)} %get-tuple-element.37), channel_id=1, source_target_pairs={{0,2},{2,0},{1,3},{3,1},{4,6},{6,4},{5,7},{7,5},{8,10},{10,8},{9,1... | collective-permute-start | bytes 1216520 | tf_op jit(solution)/shard_map/ppermute | solution.py:847
  45.8 3.1 %shard_map.198 = (f32[9,88,128]{2,1,0:T(8,128)S(1)}, f32[9,88,128]{2,1,0:T(8,128)S(1)}) custom-call(s32[1]{0:T(128)} %bitcast.core_ref, s32[3]{0:T(128)S(1)} %copy-done.26, f32[2,1024,128]{2,1,0:T(8,128)S(1)} %get-tuple-element.30.lines_ref, f32[2,8,88,128]{3,2,1,0:T(8,128)S(1)} %copy-done.13, bf16[176,256]{1,0:T(8,128)(2,1)S(1)} %copy-done.6, ...), custom_call_target="tpu_custom_call" | custom-call | flops 1000 | bytes 1000 | tf_op jit(solution)/shard_map/pallas_call | solution.py:781
  48.9 1.0 %collective-permute-start.4 = (f32[9,88,128]{2,1,0:T(8,128)S(1)}, f32[9,88,128]{2,1,0:T(8,128)S(1)}, u32[]{:S(2)}, u32[]{:S(2)}) collective-permute-start(f32[9,88,128]{2,1,0:T(8,128)S(1)} %get-tuple-element.33), channel_id=1, source_target_pairs={{0,2},{2,0},{1,3},{3,1},{4,6},{6,4},{5,7},{7,5},{8,10},{10,8},{9,1... | collective-permute-start | bytes 1216520 | tf_op jit(solution)/shard_map/ppermute | solution.py:847
  50.0 2.2 %shard_map.197 = (f32[7,88,128]{2,1,0:T(8,128)S(1)}, f32[7,88,128]{2,1,0:T(8,128)S(1)}) custom-call(s32[1]{0:T(128)} %bitcast.core_ref, s32[3]{0:T(128)S(1)} %copy-done.26, f32[2,1024,128]{2,1,0:T(8,128)S(1)} %get-tuple-element.26.lines_ref, f32[2,6,88,128]{3,2,1,0:T(8,128)S(1)} %copy-done.17, bf16[176,256]{1,0:T(8,128)(2,1)S(1)} %copy-done.6, ...), custom_call_target="tpu_custom_call" | custom-call | flops 1000 | bytes 1000 | tf_op jit(solution)/shard_map/pallas_call | solution.py:781
  52.2 1.1 %collective-permute-start.3 = (f32[7,88,128]{2,1,0:T(8,128)S(1)}, f32[7,88,128]{2,1,0:T(8,128)S(1)}, u32[]{:S(2)}, u32[]{:S(2)}) collective-permute-start(f32[7,88,128]{2,1,0:T(8,128)S(1)} %get-tuple-element.29), channel_id=1, source_target_pairs={{0,2},{2,0},{1,3},{3,1},{4,6},{6,4},{5,7},{7,5},{8,10},{10,8},{9,1... | collective-permute-start | bytes 946184 | tf_op jit(solution)/shard_map/ppermute | solution.py:847
  53.3 3.7 %collective-permute-done.5.far_b = f32[9,88,128]{2,1,0:T(8,128)S(1)} collective-permute-done((f32[9,88,128]{2,1,0:T(8,128)S(1)}, f32[9,88,128]{2,1,0:T(8,128)S(1)}, u32[]{:S(2)}, u32[]{:S(2)}) %collective-permute-start.5) | collective-permute-done | bytes 405536 | tf_op jit(solution)/shard_map/ppermute | solution.py:847
  57.0 8.7 %collective-permute-done.4.far_a = f32[9,88,128]{2,1,0:T(8,128)S(1)} collective-permute-done((f32[9,88,128]{2,1,0:T(8,128)S(1)}, f32[9,88,128]{2,1,0:T(8,128)S(1)}, u32[]{:S(2)}, u32[]{:S(2)}) %collective-permute-start.4) | collective-permute-done | bytes 405536 | tf_op jit(solution)/shard_map/ppermute | solution.py:847
  65.7 0.8 %shard_map.200 = (f32[2,1024,128]{2,1,0:T(8,128)S(1)}, f32[2,1024,128]{2,1,0:T(8,128)S(1)}) custom-call(f32[9,88,128]{2,1,0:T(8,128)S(1)} %get-tuple-element.32.near_a, f32[9,88,128]{2,1,0:T(8,128)S(1)} %collective-permute-done.4.far_a, f32[9,88,128]{2,1,0:T(8,128)S(1)} %get-tuple-element.36.near_b, f32[9,88,128]{2,1,0:T(8,128)S(1)} %collective-permute-done.5.far_b, ...), custom_call_target="tpu_custom_call" | custom-call | flops 1000 | bytes 1000 | tf_op jit(solution)/shard_map/pallas_call | solution.py:781
  66.5 0.0 collective-permute-done.7.base_ref
  66.5 5.3 %collective-permute-done.3.far_ref = f32[7,88,128]{2,1,0:T(8,128)S(1)} collective-permute-done((f32[7,88,128]{2,1,0:T(8,128)S(1)}, f32[7,88,128]{2,1,0:T(8,128)S(1)}, u32[]{:S(2)}, u32[]{:S(2)}) %collective-permute-start.3) | collective-permute-done | bytes 315424 | tf_op jit(solution)/shard_map/ppermute | solution.py:847
  71.7 0.0 collective-permute-done.6.state_ref
  71.7 5.9 %shard_map.201 = (f32[3,16,4096]{2,1,0:T(8,128)}, f32[3,32,4096]{2,1,0:T(8,128)}) custom-call(f32[7,88,128]{2,1,0:T(8,128)S(1)} %get-tuple-element.28.near_ref, f32[7,88,128]{2,1,0:T(8,128)S(1)} %collective-permute-done.3.far_ref, f32[2,1024,128]{2,1,0:T(8,128)S(1)} %get-tuple-element.38.planes_a, f32[2,1024,128]{2,1,0:T(8,128)S(1)} %get-tuple-element.39.planes_b, ...), custom_call_target="tpu_custom_call" | custom-call | flops 1000 | bytes 1000 | tf_op jit(solution)/shard_map/pallas_call | solution.py:781
  (31 shorter events, 0.1 us)
Async XLA Ops:
  0.6 1.4 %copy-start = (f32[1,3,32,4096]{3,2,1,0:T(8,128)S(1)}, f32[1,3,32,4096]{3,2,1,0:T(8,128)}, u32[]{:S(2)}) copy-start(f32[1,3,32,4096]{3,2,1,0:T(8,128)} %param.19) | copy-start | bytes 4718596
  2.0 0.9 %copy-start.5 = (bf16[176,256]{1,0:T(8,128)(2,1)S(1)}, bf16[176,256]{1,0:T(8,128)(2,1)}, u32[]{:S(2)}) copy-start(bf16[176,256]{1,0:T(8,128)(2,1)} %constant.45.clone.fy_ref) | copy-start | bytes 270340
  2.9 0.9 %copy-start.10 = (bf16[192,256]{1,0:T(8,128)(2,1)S(1)}, bf16[192,256]{1,0:T(8,128)(2,1)}, u32[]{:S(2)}) copy-start(bf16[192,256]{1,0:T(8,128)(2,1)} %constant.41.clone.fz_ref) | copy-start | bytes 294916
  3.8 6.0 %copy-start.3 = (f32[1,1,3,32,4096]{4,3,2,1,0:T(8,128)S(1)}, f32[1,1,3,32,4096]{4,3,2,1,0:T(8,128)}, u32[]{:S(2)}) copy-start(f32[1,1,3,32,4096]{4,3,2,1,0:T(8,128)} %param.20) | copy-start | bytes 4718596
  3.8 9.6 %copy-start.7 = (bf16[176,256]{1,0:T(8,128)(2,1)S(1)}, bf16[176,256]{1,0:T(8,128)(2,1)}, u32[]{:S(2)}) copy-start(bf16[176,256]{1,0:T(8,128)(2,1)} %constant.46.clone.fyr_ref) | copy-start | bytes 270340
  3.8 9.6 %copy-start.9 = (f32[88,128]{1,0:T(8,128)S(1)}, f32[88,128]{1,0:T(8,128)}, u32[]{:S(2)}) copy-start(f32[88,128]{1,0:T(8,128)} %constant.53.clone.kyrow_ref) | copy-start | bytes 135172
  6.9 17.6 %collective-permute-start.1 = (f32[11,88,128]{2,1,0:T(8,128)}, f32[11,88,128]{2,1,0:T(8,128)}, u32[]{:S(2)}, u32[]{:S(2)}) collective-permute-start(f32[11,88,128]{2,1,0:T(8,128)} %shard_map.194.here_own), channel_id=1, source_target_pairs={{0,2},{2,0},{1,3},{3,1},{4,6},{6,4},{5,7},{7,5},{8,10},{10,8},{9,1... | collective-permute-start | bytes 1486856 | tf_op jit(solution)/shard_map/ppermute | solution.py:814
  9.8 15.2 %copy-start.1 = (f32[1,3,32,4096]{3,2,1,0:T(8,128)S(1)}, f32[1,3,32,4096]{3,2,1,0:T(8,128)}, u32[]{:S(2)}) copy-start(f32[1,3,32,4096]{3,2,1,0:T(8,128)} %param.19) | copy-start | bytes 4718596
  9.8 61.9 %collective-permute-start.6 = (f32[3,32,4096]{2,1,0:T(8,128)S(1)}, f32[3,32,4096]{2,1,0:T(8,128)}, u32[]{:S(2)}, u32[]{:S(2)}) collective-permute-start(f32[3,32,4096]{2,1,0:T(8,128)S(1)} %bitcast.10), channel_id=1, source_target_pairs={{4,0},{8,4},{12,8},{0,12},{1,5},{5,9},{9,13},{13,1},{6,2},{10,6},{... | collective-permute-start | bytes 4718600 | tf_op jit(solution)/shard_map/ppermute | solution.py:803
  13.4 13.1 %collective-permute-start = (f32[11,88,128]{2,1,0:T(8,128)}, f32[11,88,128]{2,1,0:T(8,128)}, u32[]{:S(2)}, u32[]{:S(2)}) collective-permute-start(f32[11,88,128]{2,1,0:T(8,128)} %shard_map.194.here_own), channel_id=1, source_target_pairs={{0,1},{1,0},{2,3},{3,2},{4,5},{5,4},{6,7},{7,6},{8,9},{9,8},{10,11... | collective-permute-start | bytes 1486856 | tf_op jit(solution)/shard_map/ppermute | solution.py:815
  21.8 0.9 %copy-start.12 = (f32[2,8,88,128]{3,2,1,0:T(8,128)}, f32[2,8,88,128]{3,2,1,0:T(8,128)S(1)}, u32[]{:S(2)}) copy-start(f32[2,8,88,128]{3,2,1,0:T(8,128)S(1)} %get-tuple-element.31.flux_ref) | copy-start | bytes 2162692
  22.7 0.9 %copy-start.14 = (f32[2,8,88,128]{3,2,1,0:T(8,128)}, f32[2,8,88,128]{3,2,1,0:T(8,128)S(1)}, u32[]{:S(2)}) copy-start(f32[2,8,88,128]{3,2,1,0:T(8,128)S(1)} %get-tuple-element.35.flux_ref) | copy-start | bytes 2162692
  23.6 0.8 %copy-start.16 = (f32[2,6,88,128]{3,2,1,0:T(8,128)}, f32[2,6,88,128]{3,2,1,0:T(8,128)S(1)}, u32[]{:S(2)}) copy-start(f32[2,6,88,128]{3,2,1,0:T(8,128)S(1)} %get-tuple-element.27.flux_ref) | copy-start | bytes 1622020
  24.4 2.3 %copy-start.8 = (bf16[256,256]{1,0:T(8,128)(2,1)S(1)}, bf16[256,256]{1,0:T(8,128)(2,1)}, u32[]{:S(2)}) copy-start(bf16[256,256]{1,0:T(8,128)(2,1)} %constant.47.clone.iy_ref) | copy-start | bytes 393220
  24.4 2.3 %copy-start.11 = (bf16[192,256]{1,0:T(8,128)(2,1)S(1)}, bf16[192,256]{1,0:T(8,128)(2,1)}, u32[]{:S(2)}) copy-start(bf16[192,256]{1,0:T(8,128)(2,1)} %constant.41.clone.fz_ref) | copy-start | bytes 294916
  24.4 2.3 %copy-start.26 = (s32[3]{0:T(128)S(1)}, s32[3]{0:T(128)}, u32[]{:S(2)}) copy-start(s32[3]{0:T(128)} %cutoff_ref.7) | copy-start | bytes 40
  24.4 2.3 %copy-start.18 = (bf16[256,256]{1,0:T(8,128)(2,1)S(1)}, bf16[256,256]{1,0:T(8,128)(2,1)}, u32[]{:S(2)}) copy-start(bf16[256,256]{1,0:T(8,128)(2,1)} %constant.42.clone.iz_ref) | copy-start | bytes 393220
  24.4 2.3 %copy-start.19 = (bf16[4,256,256]{2,1,0:T(8,128)(2,1)S(1)}, bf16[4,256,256]{2,1,0:T(8,128)(2,1)}, u32[]{:S(2)}) copy-start(bf16[4,256,256]{2,1,0:T(8,128)(2,1)} %constant.49.clone.gxh_ref) | copy-start | bytes 1572868
  24.4 2.3 %copy-start.20 = (bf16[4,256,256]{2,1,0:T(8,128)(2,1)S(1)}, bf16[4,256,256]{2,1,0:T(8,128)(2,1)}, u32[]{:S(2)}) copy-start(bf16[4,256,256]{2,1,0:T(8,128)(2,1)} %constant.50.clone.gxl_ref) | copy-start | bytes 1572868
  24.4 2.3 %copy-start.22 = (bf16[256,256]{1,0:T(8,128)(2,1)S(1)}, bf16[256,256]{1,0:T(8,128)(2,1)}, u32[]{:S(2)}) copy-start(bf16[256,256]{1,0:T(8,128)(2,1)} %constant.44.clone.izd_ref) | copy-start | bytes 393220
  24.4 2.3 %collective-permute-start.2 = (f32[11,88,128]{2,1,0:T(8,128)}, f32[11,88,128]{2,1,0:T(8,128)S(1)}, u32[]{:S(2)}, u32[]{:S(2)}) collective-permute-start(f32[11,88,128]{2,1,0:T(8,128)} %collective-permute-done.1.there_own), channel_id=1, source_target_pairs={{0,1},{1,0},{2,3},{3,2},{4,5},{5,4},{6,7},{7,6},{8,9},{9,8},{10,11... | collective-permute-start | bytes 1486856 | tf_op jit(solution)/shard_map/ppermute | solution.py:825
  25.1 41.4 %collective-permute-start.7 = (f32[3,16,4096]{2,1,0:T(8,128)S(1)}, f32[3,16,4096]{2,1,0:T(8,128)S(1)}, u32[]{:S(2)}, u32[]{:S(2)}) collective-permute-start(f32[3,16,4096]{2,1,0:T(8,128)S(1)} %dynamic-slice_bitcast_fusion), channel_id=1, source_target_pairs={{4,0},{8,4},{12,8},{0,12},{5,1},{9,5},{13,9},{1,13},{6,2},{10,6},{... | collective-permute-start | bytes 2359304 | tf_op jit(solution)/shard_map/ppermute | solution.py:802
  26.4 15.1 %copy-start.2 = (bf16[2,4,256,256]{3,2,1,0:T(8,128)(2,1)S(1)}, bf16[2,4,256,256]{3,2,1,0:T(8,128)(2,1)}, u32[]{:S(2)}) copy-start(bf16[2,4,256,256]{3,2,1,0:T(8,128)(2,1)} %constant.52.clone.ix_ref) | copy-start | bytes 3145732
  26.4 15.1 %copy-start.4 = (bf16[4,256,256]{2,1,0:T(8,128)(2,1)S(1)}, bf16[4,256,256]{2,1,0:T(8,128)(2,1)}, u32[]{:S(2)}) copy-start(bf16[4,256,256]{2,1,0:T(8,128)(2,1)} %constant.51.clone.fx_ref) | copy-start | bytes 1572868
  26.4 15.1 %copy-start.6 = (bf16[176,256]{1,0:T(8,128)(2,1)S(1)}, bf16[176,256]{1,0:T(8,128)(2,1)}, u32[]{:S(2)}) copy-start(bf16[176,256]{1,0:T(8,128)(2,1)} %constant.45.clone.fy_ref) | copy-start | bytes 270340
  26.4 15.1 %copy-start.15 = (f32[2,8,88,128]{3,2,1,0:T(8,128)S(1)}, f32[2,8,88,128]{3,2,1,0:T(8,128)}, u32[]{:S(2)}) copy-start(f32[2,8,88,128]{3,2,1,0:T(8,128)} %copy-done.14) | copy-start | bytes 2162692
  26.7 1.1 %copy-start.23 = (bf16[256,256]{1,0:T(8,128)(2,1)S(1)}, bf16[256,256]{1,0:T(8,128)(2,1)}, u32[]{:S(2)}) copy-start(bf16[256,256]{1,0:T(8,128)(2,1)} %constant.48.clone.iyd_ref) | copy-start | bytes 393220
  27.8 0.8 %copy-start.24 = (f32[4,32,128]{2,1,0:T(8,128)S(1)}, f32[4,32,128]{2,1,0:T(8,128)}, u32[]{:S(2)}) copy-start(f32[4,32,128]{2,1,0:T(8,128)} %constant.55.clone.force_ref) | copy-start | bytes 196612
  28.7 12.9 %copy-start.25 = (f32[8,128]{1,0:T(8,128)S(1)}, f32[8,128]{1,0:T(8,128)}, u32[]{:S(2)}) copy-start(f32[8,128]{1,0:T(8,128)} %constant.54.clone.kxlane_ref) | copy-start | bytes 12292
  41.6 4.2 %copy-start.13 = (f32[2,8,88,128]{3,2,1,0:T(8,128)S(1)}, f32[2,8,88,128]{3,2,1,0:T(8,128)}, u32[]{:S(2)}) copy-start(f32[2,8,88,128]{3,2,1,0:T(8,128)} %copy-done.12) | copy-start | bytes 2162692
  44.7 12.3 %collective-permute-start.5 = (f32[9,88,128]{2,1,0:T(8,128)S(1)}, f32[9,88,128]{2,1,0:T(8,128)S(1)}, u32[]{:S(2)}, u32[]{:S(2)}) collective-permute-start(f32[9,88,128]{2,1,0:T(8,128)S(1)} %get-tuple-element.37), channel_id=1, source_target_pairs={{0,2},{2,0},{1,3},{3,1},{4,6},{6,4},{5,7},{7,5},{8,10},{10,8},{9,1... | collective-permute-start | bytes 1216520 | tf_op jit(solution)/shard_map/ppermute | solution.py:847
  45.8 4.1 %copy-start.17 = (f32[2,6,88,128]{3,2,1,0:T(8,128)S(1)}, f32[2,6,88,128]{3,2,1,0:T(8,128)}, u32[]{:S(2)}) copy-start(f32[2,6,88,128]{3,2,1,0:T(8,128)} %copy-done.16) | copy-start | bytes 1622020
  48.9 16.8 %collective-permute-start.4 = (f32[9,88,128]{2,1,0:T(8,128)S(1)}, f32[9,88,128]{2,1,0:T(8,128)S(1)}, u32[]{:S(2)}, u32[]{:S(2)}) collective-permute-start(f32[9,88,128]{2,1,0:T(8,128)S(1)} %get-tuple-element.33), channel_id=1, source_target_pairs={{0,2},{2,0},{1,3},{3,1},{4,6},{6,4},{5,7},{7,5},{8,10},{10,8},{9,1... | collective-permute-start | bytes 1216520 | tf_op jit(solution)/shard_map/ppermute | solution.py:847
  52.2 19.6 %copy-start.21 = (bf16[256,256]{1,0:T(8,128)(2,1)S(1)}, bf16[256,256]{1,0:T(8,128)(2,1)}, u32[]{:S(2)}) copy-start(bf16[256,256]{1,0:T(8,128)(2,1)} %constant.43.clone.izr_ref) | copy-start | bytes 393220
  52.2 19.6 %collective-permute-start.3 = (f32[7,88,128]{2,1,0:T(8,128)S(1)}, f32[7,88,128]{2,1,0:T(8,128)S(1)}, u32[]{:S(2)}, u32[]{:S(2)}) collective-permute-start(f32[7,88,128]{2,1,0:T(8,128)S(1)} %get-tuple-element.29), channel_id=1, source_target_pairs={{0,2},{2,0},{1,3},{3,1},{4,6},{6,4},{5,7},{7,5},{8,10},{10,8},{9,1... | collective-permute-start | bytes 946184 | tf_op jit(solution)/shard_map/ppermute | solution.py:847

commit v5 on v4

--- a/solution.py
+++ b/solution.py
@@ -407,7 +407,24 @@
     force = [forcing_amp * np.sin(2 * np.pi * ((w * yy) % N) / N) for w in range(1, 5)]
     force = np.repeat(np.stack(force).reshape(4, HALF, 2, 1), N, axis=3)
     out["force"] = force.reshape(4, HALF, LANES).astype(np.float32)
-    return out
+    merged = {}
+    merged["ahead"] = np.concatenate([out["fz"], out["fy"], out["fyr"]], 0)
+    gx = [out["gxh"].reshape(-1, 256), out["gxl"].reshape(-1, 256)]
+    square = [out[name] for name in ("iy", "iyd", "iz", "izd", "izr")]
+    merged["back"] = np.concatenate(square + gx, 0)
+    merged["along"] = np.concatenate([out["fx"].reshape(-1, 256), out["ix"].reshape(-1, 256)], 0)
+    merged["waves"] = np.concatenate(
+        [out["kyrow"], out["kxlane"], out["force"].reshape(-1, LANES)], 0
+    )
+    return merged
+
+
+def view(ref, index, rows=256, start=0):
+    return ref.at[pl.ds(start + index * rows, rows), :]
+
+
+def ahead_tables(ref):
+    return view(ref, 0, 2 * LINE), view(ref, 0, 2 * ROWS, 2 * LINE), view(ref, 1, 2 * ROWS, 2 * LINE)
 
 
 def split(values):
@@ -502,18 +519,38 @@
     lax.fori_loop(0, HALF // many, some, 0)
 
 
-def base_kernel(core_ref, base_ref, fz_ref, fy_ref, out_ref, lines):
+PIECES = 4
+
+
+def base_kernel(core_ref, base_hbm, ahead_hbm, out_ref, lines, base_ref, ahead_ref, arrived):
     nothing = jnp.zeros((HALF, LANES), f32)
-
-    def z_step(yhs):
+    wide = N * N // PIECES
+    table = pltpu.make_async_copy(ahead_hbm, ahead_ref, arrived.at[PIECES])
+    pieces = [
+        pltpu.make_async_copy(
+            base_hbm.at[:, :, pl.ds(n * wide, wide)],
+            base_ref.at[:, :, pl.ds(n * wide, wide)],
+            arrived.at[n],
+        )
+        for n in range(PIECES)
+    ]
+    pieces[0].start()
+    table.start()
+    for piece in pieces[1:]:
+        piece.start()
+    fz_ref, fy_ref, _ = ahead_tables(ahead_ref)
+    table.wait()
+    many = HALF // PIECES
+    for n, piece in enumerate(pieces):
+        piece.wait()
+        yhs = range(n * many, (n + 1) * many)
         rows = []
         for yh in yhs:
-            rows += [base_ref[i, :, columns(yh)] for i in range(3)] + [nothing]
+            at = slice(yh * LANES, (yh + 1) * LANES)
+            rows += [base_ref[i, :, at] for i in range(3)] + [nothing]
         got = folded(dot_nt(fz_ref[...], beside(jnp.concatenate(rows, 0))))
         for yh, part in zip(yhs, lane_parts(got)):
-            lines[0, line_rows(yh), :] = part
-
-    over_lines(z_step, 8)
+            lines[0, yh * LINE : (yh + 1) * LINE, :] = part
     start = core_ref[0] * HALF_KZ
     for pair in range(0, HALF_KZ, 2):
         ks = range(pair, min(pair + 2, HALF_KZ))
@@ -523,10 +560,9 @@
             out_ref[k] = part
 
 
-def flux_kernel(
-    core_ref, base_ref, state_ref, fz_ref, fy_ref, fyr_ref, kyrow_ref, *refs
-):
+def flux_kernel(core_ref, base_ref, state_ref, ahead_ref, waves_ref, *refs):
     *out_refs, lines = refs
+    fz_ref, fy_ref, fyr_ref = ahead_tables(ahead_ref)
     sigma = jnp.where(core_ref[0] == 0, -time_step, time_step).astype(f32)
     nothing = jnp.zeros((HALF, LANES), f32)
 
@@ -544,7 +580,7 @@
                 lines[tile, line_rows(yh), :] = got[3 * n + tile]
 
     over_lines(z_step, 4)
-    ky = kyrow_ref[...]
+    ky = waves_ref[:ROWS]
     lane = lax.broadcasted_iota(jnp.int32, (ROWS, LANES), 1)
     odd_block = (lane // HALF) % 2 == 1
 
@@ -576,13 +612,15 @@
 def gradient_kernel(
     core_ref, cutoff_ref, wave_ref, base_ref, state_ref,
     here_own, here_other, there_own, there_other,
-    gxh_ref, gxl_ref, iy_ref, iyd_ref, iz_ref, izd_ref, fz_ref, kyrow_ref, force_ref, *refs
+    ahead_ref, back_ref, waves_ref, *refs
 ):
     *out_refs, planes = refs
+    fz_ref = ahead_tables(ahead_ref)[0]
+    iy_ref, iyd_ref, iz_ref, izd_ref = (view(back_ref, n) for n in range(4))
     core = core_ref[0]
     cut_x, cut_y, cut_z = cutoff_ref[0], cutoff_ref[1], cutoff_ref[2]
     which = jnp.clip(cut_x - (KEEP - 3), 0, 3)
-    ky = kyrow_ref[...]
+    ky = waves_ref[:ROWS]
     keep_y = jnp.where(jnp.abs(ky) <= cut_y.astype(f32), 1.0, 0.0).astype(f32)
 
     def kept_z(kz):
@@ -597,7 +635,9 @@
             here = jnp.where(half == core, here_own[at], here_other[at]) * keep
             there = jnp.where(half == core, there_own[at], there_other[at]) * keep
             rows.append(jnp.concatenate([here, there], 1))
-        got = triple(jnp.concatenate(rows, 0), gxh_ref[which], gxl_ref[which])
+        high = back_ref[pl.ds(pl.multiple_of((5 + which) * 256, 256), 256), :]
+        low = back_ref[pl.ds(pl.multiple_of((9 + which) * 256, 256), 256), :]
+        got = triple(jnp.concatenate(rows, 0), high, low)
         data = [stacked(padded(got[n * ROWS : (n + 1) * ROWS])) for n in range(len(kzs))]
         for n, kz in enumerate(kzs):
             even = lane_parts(folded(dot(iy_ref[...], data[n])))
@@ -632,7 +672,7 @@
                 comb.append(s[i] - time_step * coupling)
                 drive = sum(grads[j][i] * b[j] for j in range(3))
                 if i == 0:
-                    drive = drive - force_ref[force_at, pl.ds(yh, 1), :]
+                    drive = drive - waves_ref[pl.ds(ROWS + 8 + force_at * HALF + yh, 1), :]
                 comb_base.append(b[i] - time_step * drive)
             rows = [comb[1], comb_base[1], comb[2], comb_base[2]]
             rows += [comb[0], comb_base[0], nothing, nothing]
@@ -648,14 +688,15 @@
 
 def spectral_kernel(
     chunk, core_ref, cutoff_ref, lines_ref, flux_ref,
-    fy_ref, fyr_ref, fx_ref, ix_ref, kyrow_ref, kxlane_ref, near_ref, far_ref,
+    ahead_ref, along_ref, waves_ref, near_ref, far_ref,
 ):
+    _, fy_ref, fyr_ref = ahead_tables(ahead_ref)
     core = core_ref[0]
     cut_x, cut_y, cut_z = cutoff_ref[0], cutoff_ref[1], cutoff_ref[2]
     first, last = planes_of(chunk)
     extra = last - first
-    ky = kyrow_ref[...]
-    kx = kxlane_ref[0:1, :]
+    ky = waves_ref[:ROWS]
+    kx = waves_ref[ROWS : ROWS + 1]
     keep_y = jnp.where(jnp.abs(ky) <= cut_y.astype(f32), 1.0, 0.0).astype(f32)
     keep_x = jnp.where(kx <= cut_x.astype(f32), 1.0, 0.0).astype(f32)
     keep_xy = keep_y * keep_x
@@ -685,7 +726,7 @@
                 fields[1].append(jnp.where(lane < 64, even[n], flux))
                 fields[2].append(jnp.where(lane < 64, flux, even[n]))
         data = [beside(jnp.concatenate(field, 0)) for field in fields]
-        modes = [folded_lanes(dot(data[max(n - 1, 0)], fx_ref[n])) for n in range(4)]
+        modes = [folded_lanes(dot(data[max(n - 1, 0)], view(along_ref, n)[...])) for n in range(4)]
         results = [[], [], [], []]
         for n, kz in enumerate(kzs):
             kzf = kz.astype(f32)
@@ -698,7 +739,10 @@
             results[2].append(factor * (uy - ky * share))
             results[3].append(factor * (uz - kzf * share))
         got = [
-            dot(beside(jnp.concatenate(result, 0)), ix_ref[core, n])
+            dot(
+                beside(jnp.concatenate(result, 0)),
+                along_ref[pl.ds(pl.multiple_of((4 + core * 4 + n) * 256, 256), 256), :],
+            )
             for n, result in enumerate(results)
         ]
         got = [folded_lanes(part) for part in (got[0] + got[1], got[2], got[3])]
@@ -732,15 +776,17 @@
             planes[tile, count * LANES :, :] = blank
 
 
-def inverse_kernel(near_a, far_a, near_b, far_b, iy_ref, planes_a, planes_b):
+def inverse_kernel(near_a, far_a, near_b, far_b, back_ref, planes_a, planes_b):
+    iy_ref = view(back_ref, 0)
     inverse_y(near_a, far_a, iy_ref, planes_a)
     inverse_y(near_b, far_b, iy_ref, planes_b)
 
 
 def final_kernel(
-    near_ref, far_ref, planes_a, planes_b, state_ref, base_ref, iy_ref, iz_ref, izr_ref,
+    near_ref, far_ref, planes_a, planes_b, state_ref, base_ref, back_ref,
     base_out, state_out, planes_c,
 ):
+    iy_ref, iz_ref, izr_ref = (view(back_ref, n) for n in (0, 2, 4))
     inverse_y(near_ref, far_ref, iy_ref, planes_c)
 
     def along_chunks(tile, yh):
@@ -775,13 +821,15 @@
 interpret = False
 
 
-def call(kernel, outs, scratch, inputs, in_smem=0, room=24):
+def call(kernel, outs, scratch, inputs, room, in_smem=0, in_hbm=0):
     whole = pl.BlockSpec(memory_space=pltpu.VMEM)
     small = pl.BlockSpec(memory_space=pltpu.SMEM)
     return pl.pallas_call(
         kernel,
         out_shape=outs,
-        in_specs=[small] * in_smem + [whole] * (len(inputs) - in_smem),
+        in_specs=[small] * in_smem
+        + [pl.BlockSpec(memory_space=pltpu.HBM)] * in_hbm
+        + [whole] * (len(inputs) - in_smem - in_hbm),
         out_specs=jax.tree.map(lambda _: whole, outs),
         scratch_shapes=scratch,
         compiler_params=pltpu.CompilerParams(vmem_limit_bytes=room * 2**20),
@@ -807,9 +855,16 @@
     here_own = call(
         base_kernel,
         sds((HALF_KZ, ROWS, LANES), f32),
-        [pltpu.VMEM((1, HALF * LINE, LANES), f32)],
-        [core_at, own_base, t["fz"], t["fy"]],
+        [
+            pltpu.VMEM((1, HALF * LINE, LANES), f32),
+            pltpu.VMEM(own_base.shape, f32),
+            pltpu.VMEM(t["ahead"].shape, bf16),
+            pltpu.SemaphoreType.DMA((PIECES + 1,)),
+        ],
+        [core_at, own_base, t["ahead"]],
+        room=56,
         in_smem=1,
+        in_hbm=2,
     )
     there_own = lax.ppermute(here_own, "slab", swap)
     here_other = lax.ppermute(here_own, "comp", swap)
@@ -818,43 +873,43 @@
         flux_kernel,
         [sds((2, count, ROWS, LANES), f32) for count in counts],
         [pltpu.VMEM((3, HALF * LINE, LANES), f32)],
-        [core_at, own_base, own_state, t["fz"], t["fy"], t["fyr"], t["kyrow"]],
+        [core_at, own_base, own_state, t["ahead"], t["waves"]],
+        room=16,
         in_smem=1,
     )
     there_own, flux = lax.optimization_barrier((there_own, flux))
     there_other = lax.ppermute(there_own, "comp", swap)
-    names = ("gxh", "gxl", "iy", "iyd", "iz", "izd", "fz", "kyrow", "force")
     lines = call(
         gradient_kernel,
         [sds((2, HALF * 4 * CHUNK, LANES), f32)] * CHUNKS,
         [pltpu.VMEM((3, NKZ * LANES, LANES), f32)],
         [core_at, cutoff, wavenumber, own_base, own_state]
-        + [here_own, here_other, there_own, there_other]
-        + [t[name] for name in names],
+        + [here_own, here_other, there_own, there_other, t["ahead"], t["back"], t["waves"]],
+        room=20,
         in_smem=3,
     )
-    names = ("fy", "fyr", "fx", "ix", "kyrow", "kxlane")
     near, far = [], []
     for chunk in range(CHUNKS):
         near_part, far_part = call(
             functools.partial(spectral_kernel, chunk),
             [sds((counts[chunk] + 1, ROWS, LANES), f32)] * 2,
             [],
-            [core_at, cutoff, lines[chunk], flux[chunk]] + [t[name] for name in names],
+            [core_at, cutoff, lines[chunk], flux[chunk], t["ahead"], t["along"], t["waves"]],
+            room=10,
             in_smem=2,
         )
         near.append(near_part)
         far.append(lax.ppermute(far_part, "slab", swap))
     planes = sds((2, CHUNK * LANES, LANES), f32)
     planes_a, planes_b = call(
-        inverse_kernel, [planes] * 2, [], [near[0], far[0], near[1], far[1], t["iy"]]
+        inverse_kernel, [planes] * 2, [], [near[0], far[0], near[1], far[1], t["back"]], room=10
     )
     base_gap, state_gap = call(
         final_kernel,
         [sds((3, 16, N * N), f32), sds((3, HALF, N * N), f32)],
         [pltpu.VMEM((2, CHUNK * LANES, LANES), f32)],
-        [near[2], far[2], planes_a, planes_b, state_next, base_next]
-        + [t["iy"], t["iz"], t["izr"]],
+        [near[2], far[2], planes_a, planes_b, state_next, base_next, t["back"]],
+        room=16,
     )
     return base_gap[None], state_gap[None, None]
 

time: 78 us -> 77.3 us (level)
  local copies, waits for them, and re-layouts: 7.76 us -> 6.11 us
  Pallas kernels: 39.4 us -> 40.4 us
    unnamed x54 -> x32, local copies, waits for them, and re-layouts: 7.71 us -> 6.06 us
    pallas_call x8, Pallas kernels: 39.4 us -> 40.4 us  [call(): pl.pallas_call(kernel, out_shape=outs, in_specs=[small] * in_smem + [pl.B...]
where the time goes in v5:
time: 77.3 us; the launch traced here: 77 us
  Pallas kernels  40.4 us (52%)
  waiting for transfers between devices  18.5 us (24%)
  starting transfers between devices  10.5 us (14%)
  local copies, waits for them, and re-layouts  6.11 us (8%)
  between operations  1.45 us (2%)
    pallas_call x8, Pallas kernels, call(): pl.pallas_call(kernel, out_shape=outs, in_specs=[small] * in_smem + [pl.B...  40.4 us
    ppermute x3, waiting for transfers between devices, body(): far.append(lax.ppermute(far_part, 'slab', swap))  18.2 us
    unnamed x32, local copies, waits for them, and re-layouts  6.06 us
    ppermute x1, starting transfers between devices, body(): state_next = lax.ppermute(own_state, ('seg', 'comp'), around)  3.6 us
    ppermute x1, starting transfers between devices, body(): there_own = lax.ppermute(here_own, 'slab', swap)  3 us
    ppermute x3, starting transfers between devices, body(): far.append(lax.ppermute(far_part, 'slab', swap))  2.76 us
  transfers between devices with their start and end apart: 8, of which 4 were waited for; matrix products, arithmetic and copies ran while one was open for 0% of the time, Pallas kernels for 39%

profile of v5, /device:TPU:0, one launch (start us, length us, event | category | flops | bytes accessed | tf_op | source)
XLA Modules:
  0.0 77.0 jit_solution(15067784587913325505)
XLA Ops:
  0.6 0.0 copy-start.3
  0.6 0.0 copy-start
  0.7 0.0 copy-start.6
  0.7 4.3 %shard_map.95.here_own = f32[11,88,128]{2,1,0:T(8,128)} custom-call(s32[1]{0:T(128)} %bitcast.core_ref, f32[3,32,4096]{2,1,0:T(8,128)} %bitcast.7, bf16[544,256]{1,0:T(8,128)(2,1)} %constant.19.clone.ahead_hbm.ahead_ref), custom_call_target="tpu_custom_call" | custom-call | flops 1000 | bytes 1000 | tf_op jit(solution)/shard_map/pallas_call | solution.py:827
  4.9 3.0 %collective-permute-start.1 = (f32[11,88,128]{2,1,0:T(8,128)}, f32[11,88,128]{2,1,0:T(8,128)}, u32[]{:S(2)}, u32[]{:S(2)}) collective-permute-start(f32[11,88,128]{2,1,0:T(8,128)} %shard_map.95.here_own), channel_id=1, source_target_pairs={{0,2},{2,0},{1,3},{3,1},{4,6},{6,4},{5,7},{7,5},{8,10},{10,8},{9,1... | collective-permute-start | bytes 1486856 | tf_op jit(solution)/shard_map/ppermute | solution.py:869
  8.0 3.6 %collective-permute-start.6 = (f32[3,32,4096]{2,1,0:T(8,128)}, f32[3,32,4096]{2,1,0:T(8,128)}, u32[]{:S(2)}, u32[]{:S(2)}) collective-permute-start(f32[3,32,4096]{2,1,0:T(8,128)} %bitcast.10), channel_id=1, source_target_pairs={{4,0},{8,4},{12,8},{0,12},{1,5},{5,9},{9,13},{13,1},{6,2},{10,6},{... | collective-permute-start | bytes 4718600 | tf_op jit(solution)/shard_map/ppermute | solution.py:851
  11.6 0.0 collective-permute-start
  11.6 0.0 copy-done.3
  11.6 0.0 copy-done
  11.6 0.0 copy-done.6
  11.6 0.0 copy-start.4
  11.6 1.4 %copy-done.4 = f32[1,1,3,32,4096]{4,3,2,1,0:T(8,128)S(1)} copy-done((f32[1,1,3,32,4096]{4,3,2,1,0:T(8,128)S(1)}, f32[1,1,3,32,4096]{4,3,2,1,0:T(8,128)}, u32[]{:S(2)}) %copy-start.4) | copy-done | bytes 1572888
  13.0 8.4 %shard_map.96 = (f32[2,8,88,128]{3,2,1,0:T(8,128)S(1)}, f32[2,8,88,128]{3,2,1,0:T(8,128)S(1)}, f32[2,6,88,128]{3,2,1,0:T(8,128)S(1)}) custom-call(s32[1]{0:T(128)} %bitcast.core_ref, f32[3,32,4096]{2,1,0:T(8,128)S(1)} %bitcast.8, f32[3,32,4096]{2,1,0:T(8,128)S(1)} %bitcast.11, bf16[544,256]{1,0:T(8,128)(2,1)S(1)} %copy-done.3, f32[224,128]{1,0:T(8,128)S(1)} %copy-done.6), custom_call_target="tpu_custom_call" | custom-call | flops 1000 | bytes 1000 | tf_op jit(solution)/shard_map/pallas_call | solution.py:827
  21.4 0.0 copy-start.9
  21.4 0.8 %copy-done.9 = f32[2,8,88,128]{3,2,1,0:T(8,128)} copy-done((f32[2,8,88,128]{3,2,1,0:T(8,128)}, f32[2,8,88,128]{3,2,1,0:T(8,128)S(1)}, u32[]{:S(2)}) %copy-start.9) | copy-done | bytes 720920
  22.3 0.9 %copy-done.11 = f32[2,8,88,128]{3,2,1,0:T(8,128)} copy-done((f32[2,8,88,128]{3,2,1,0:T(8,128)}, f32[2,8,88,128]{3,2,1,0:T(8,128)S(1)}, u32[]{:S(2)}) %copy-start.11) | copy-done | bytes 720920
  23.1 0.8 %copy-done.13 = f32[2,6,88,128]{3,2,1,0:T(8,128)} copy-done((f32[2,6,88,128]{3,2,1,0:T(8,128)}, f32[2,6,88,128]{3,2,1,0:T(8,128)S(1)}, u32[]{:S(2)}) %copy-start.13) | copy-done | bytes 540696
  23.9 0.0 collective-permute-done.1.there_own
  24.0 0.5 collective-permute-start.2
  24.4 0.1 dynamic-slice_bitcast_fusion
  24.5 0.7 collective-permute-start.7
  25.8 0.0 copy-start.2
  25.8 0.0 collective-permute-done.here_other
  25.9 0.3 collective-permute-done.2.there_other
  26.2 0.0 copy-done.1
  26.2 0.0 copy-done.5
  26.2 0.0 copy-done.15
  26.2 1.0 %copy-done.7 = f32[224,128]{1,0:T(8,128)S(1)} copy-done((f32[224,128]{1,0:T(8,128)S(1)}, f32[224,128]{1,0:T(8,128)}, u32[]{:S(2)}) %copy-start.7) | copy-done | bytes 114712
  27.2 1.0 %copy-done.8 = f32[11,88,128]{2,1,0:T(8,128)S(1)} copy-done((f32[11,88,128]{2,1,0:T(8,128)S(1)}, f32[11,88,128]{2,1,0:T(8,128)}, u32[]{:S(2)}) %copy-start.8) | copy-done | bytes 495640
  28.2 12.7 %shard_map.97 = (f32[2,1024,128]{2,1,0:T(8,128)S(1)}, f32[2,1024,128]{2,1,0:T(8,128)S(1)}, f32[2,1024,128]{2,1,0:T(8,128)S(1)}) custom-call(s32[1]{0:T(128)} %bitcast.core_ref, s32[3]{0:T(128)S(1)} %copy-done.15, s32[1]{0:T(128)S(6)} %copy.10.wave_ref, f32[3,32,4096]{2,1,0:T(8,128)S(1)} %bitcast.9, f32[3,32,4096]{2,1,0:T(8,128)S(1)} %bitcast.12, ...), custom_call_target="tpu_custom_call" | custom-call | flops 1000 | bytes 1000 | tf_op jit(solution)/shard_map/pallas_call | solution.py:827
  40.9 0.0 copy-done.2
  40.9 0.0 copy-done.12
  41.0 0.0 copy-start.10
  41.0 3.1 %shard_map.100 = (f32[9,88,128]{2,1,0:T(8,128)S(1)}, f32[9,88,128]{2,1,0:T(8,128)S(1)}) custom-call(s32[1]{0:T(128)} %bitcast.core_ref, s32[3]{0:T(128)S(1)} %copy-done.15, f32[2,1024,128]{2,1,0:T(8,128)S(1)} %get-tuple-element.34.lines_ref, f32[2,8,88,128]{3,2,1,0:T(8,128)S(1)} %copy-done.12, bf16[544,256]{1,0:T(8,128)(2,1)S(1)} %copy-done.3, ...), custom_call_target="tpu_custom_call" | custom-call | flops 1000 | bytes 1000 | tf_op jit(solution)/shard_map/pallas_call | solution.py:827
  44.1 0.6 collective-permute-start.5
  44.7 0.0 copy-done.10
  44.7 3.1 %shard_map.99 = (f32[9,88,128]{2,1,0:T(8,128)S(1)}, f32[9,88,128]{2,1,0:T(8,128)S(1)}) custom-call(s32[1]{0:T(128)} %bitcast.core_ref, s32[3]{0:T(128)S(1)} %copy-done.15, f32[2,1024,128]{2,1,0:T(8,128)S(1)} %get-tuple-element.30.lines_ref, f32[2,8,88,128]{3,2,1,0:T(8,128)S(1)} %copy-done.10, bf16[544,256]{1,0:T(8,128)(2,1)S(1)} %copy-done.3, ...), custom_call_target="tpu_custom_call" | custom-call | flops 1000 | bytes 1000 | tf_op jit(solution)/shard_map/pallas_call | solution.py:827
  47.7 1.6 %collective-permute-start.4 = (f32[9,88,128]{2,1,0:T(8,128)S(1)}, f32[9,88,128]{2,1,0:T(8,128)S(1)}, u32[]{:S(2)}, u32[]{:S(2)}) collective-permute-start(f32[9,88,128]{2,1,0:T(8,128)S(1)} %get-tuple-element.33), channel_id=1, source_target_pairs={{0,2},{2,0},{1,3},{3,1},{4,6},{6,4},{5,7},{7,5},{8,10},{10,8},{9,1... | collective-permute-start | bytes 1216520 | tf_op jit(solution)/shard_map/ppermute | solution.py:902
  49.3 0.0 copy-done.14
  49.3 2.2 %shard_map.98 = (f32[7,88,128]{2,1,0:T(8,128)S(1)}, f32[7,88,128]{2,1,0:T(8,128)S(1)}) custom-call(s32[1]{0:T(128)} %bitcast.core_ref, s32[3]{0:T(128)S(1)} %copy-done.15, f32[2,1024,128]{2,1,0:T(8,128)S(1)} %get-tuple-element.26.lines_ref, f32[2,6,88,128]{3,2,1,0:T(8,128)S(1)} %copy-done.14, bf16[544,256]{1,0:T(8,128)(2,1)S(1)} %copy-done.3, ...), custom_call_target="tpu_custom_call" | custom-call | flops 1000 | bytes 1000 | tf_op jit(solution)/shard_map/pallas_call | solution.py:827
  51.5 0.6 collective-permute-start.3
  52.1 4.3 %collective-permute-done.5.far_b = f32[9,88,128]{2,1,0:T(8,128)S(1)} collective-permute-done((f32[9,88,128]{2,1,0:T(8,128)S(1)}, f32[9,88,128]{2,1,0:T(8,128)S(1)}, u32[]{:S(2)}, u32[]{:S(2)}) %collective-permute-start.5) | collective-permute-done | bytes 405536 | tf_op jit(solution)/shard_map/ppermute | solution.py:902
  56.3 8.7 %collective-permute-done.4.far_a = f32[9,88,128]{2,1,0:T(8,128)S(1)} collective-permute-done((f32[9,88,128]{2,1,0:T(8,128)S(1)}, f32[9,88,128]{2,1,0:T(8,128)S(1)}, u32[]{:S(2)}, u32[]{:S(2)}) %collective-permute-start.4) | collective-permute-done | bytes 405536 | tf_op jit(solution)/shard_map/ppermute | solution.py:902
  65.0 0.8 %shard_map.101 = (f32[2,1024,128]{2,1,0:T(8,128)S(1)}, f32[2,1024,128]{2,1,0:T(8,128)S(1)}) custom-call(f32[9,88,128]{2,1,0:T(8,128)S(1)} %get-tuple-element.32.near_a, f32[9,88,128]{2,1,0:T(8,128)S(1)} %collective-permute-done.4.far_a, f32[9,88,128]{2,1,0:T(8,128)S(1)} %get-tuple-element.36.near_b, f32[9,88,128]{2,1,0:T(8,128)S(1)} %collective-permute-done.5.far_b, ...), custom_call_target="tpu_custom_call" | custom-call | flops 1000 | bytes 1000 | tf_op jit(solution)/shard_map/pallas_call | solution.py:827
  65.8 0.0 collective-permute-done.7.base_ref
  65.8 5.3 %collective-permute-done.3.far_ref = f32[7,88,128]{2,1,0:T(8,128)S(1)} collective-permute-done((f32[7,88,128]{2,1,0:T(8,128)S(1)}, f32[7,88,128]{2,1,0:T(8,128)S(1)}, u32[]{:S(2)}, u32[]{:S(2)}) %collective-permute-start.3) | collective-permute-done | bytes 315424 | tf_op jit(solution)/shard_map/ppermute | solution.py:902
  71.1 0.0 collective-permute-done.6.state_ref
  71.1 5.9 %shard_map.102 = (f32[3,16,4096]{2,1,0:T(8,128)}, f32[3,32,4096]{2,1,0:T(8,128)}) custom-call(f32[7,88,128]{2,1,0:T(8,128)S(1)} %get-tuple-element.28.near_ref, f32[7,88,128]{2,1,0:T(8,128)S(1)} %collective-permute-done.3.far_ref, f32[2,1024,128]{2,1,0:T(8,128)S(1)} %get-tuple-element.38.planes_a, f32[2,1024,128]{2,1,0:T(8,128)S(1)} %get-tuple-element.39.planes_b, ...), custom_call_target="tpu_custom_call" | custom-call | flops 1000 | bytes 1000 | tf_op jit(solution)/shard_map/pallas_call | solution.py:827
  (9 shorter events, 0.0 us)
Async XLA Ops:
  0.6 10.9 %copy-start.3 = (bf16[544,256]{1,0:T(8,128)(2,1)S(1)}, bf16[544,256]{1,0:T(8,128)(2,1)}, u32[]{:S(2)}) copy-start(bf16[544,256]{1,0:T(8,128)(2,1)} %constant.19.clone.ahead_hbm.ahead_ref) | copy-start | bytes 835588
  0.6 10.9 %copy-start = (f32[1,3,32,4096]{3,2,1,0:T(8,128)S(1)}, f32[1,3,32,4096]{3,2,1,0:T(8,128)}, u32[]{:S(2)}) copy-start(f32[1,3,32,4096]{3,2,1,0:T(8,128)} %param.8) | copy-start | bytes 4718596
  0.7 10.9 %copy-start.6 = (f32[224,128]{1,0:T(8,128)S(1)}, f32[224,128]{1,0:T(8,128)}, u32[]{:S(2)}) copy-start(f32[224,128]{1,0:T(8,128)} %constant.22.clone.waves_ref) | copy-start | bytes 344068
  4.9 19.0 %collective-permute-start.1 = (f32[11,88,128]{2,1,0:T(8,128)}, f32[11,88,128]{2,1,0:T(8,128)}, u32[]{:S(2)}, u32[]{:S(2)}) collective-permute-start(f32[11,88,128]{2,1,0:T(8,128)} %shard_map.95.here_own), channel_id=1, source_target_pairs={{0,2},{2,0},{1,3},{3,1},{4,6},{6,4},{5,7},{7,5},{8,10},{10,8},{9,1... | collective-permute-start | bytes 1486856 | tf_op jit(solution)/shard_map/ppermute | solution.py:869
  8.0 63.1 %collective-permute-start.6 = (f32[3,32,4096]{2,1,0:T(8,128)}, f32[3,32,4096]{2,1,0:T(8,128)}, u32[]{:S(2)}, u32[]{:S(2)}) collective-permute-start(f32[3,32,4096]{2,1,0:T(8,128)} %bitcast.10), channel_id=1, source_target_pairs={{4,0},{8,4},{12,8},{0,12},{1,5},{5,9},{9,13},{13,1},{6,2},{10,6},{... | collective-permute-start | bytes 4718600 | tf_op jit(solution)/shard_map/ppermute | solution.py:851
  11.6 14.3 %collective-permute-start = (f32[11,88,128]{2,1,0:T(8,128)}, f32[11,88,128]{2,1,0:T(8,128)}, u32[]{:S(2)}, u32[]{:S(2)}) collective-permute-start(f32[11,88,128]{2,1,0:T(8,128)} %shard_map.95.here_own), channel_id=1, source_target_pairs={{0,1},{1,0},{2,3},{3,2},{4,5},{5,4},{6,7},{7,6},{8,9},{9,8},{10,11... | collective-permute-start | bytes 1486856 | tf_op jit(solution)/shard_map/ppermute | solution.py:870
  11.6 1.4 %copy-start.4 = (f32[1,1,3,32,4096]{4,3,2,1,0:T(8,128)S(1)}, f32[1,1,3,32,4096]{4,3,2,1,0:T(8,128)}, u32[]{:S(2)}) copy-start(f32[1,1,3,32,4096]{4,3,2,1,0:T(8,128)} %param.9) | copy-start | bytes 4718596
  13.0 13.2 %copy-start.1 = (bf16[3328,256]{1,0:T(8,128)(2,1)S(1)}, bf16[3328,256]{1,0:T(8,128)(2,1)}, u32[]{:S(2)}) copy-start(bf16[3328,256]{1,0:T(8,128)(2,1)} %constant.20.clone.back_ref) | copy-start | bytes 5111812
  21.4 0.9 %copy-start.9 = (f32[2,8,88,128]{3,2,1,0:T(8,128)}, f32[2,8,88,128]{3,2,1,0:T(8,128)S(1)}, u32[]{:S(2)}) copy-start(f32[2,8,88,128]{3,2,1,0:T(8,128)S(1)} %get-tuple-element.31.flux_ref) | copy-start | bytes 2162692
  22.3 0.9 %copy-start.11 = (f32[2,8,88,128]{3,2,1,0:T(8,128)}, f32[2,8,88,128]{3,2,1,0:T(8,128)S(1)}, u32[]{:S(2)}) copy-start(f32[2,8,88,128]{3,2,1,0:T(8,128)S(1)} %get-tuple-element.35.flux_ref) | copy-start | bytes 2162692
  23.1 0.8 %copy-start.13 = (f32[2,6,88,128]{3,2,1,0:T(8,128)}, f32[2,6,88,128]{3,2,1,0:T(8,128)S(1)}, u32[]{:S(2)}) copy-start(f32[2,6,88,128]{3,2,1,0:T(8,128)S(1)} %get-tuple-element.27.flux_ref) | copy-start | bytes 1622020
  23.9 2.2 %copy-start.5 = (f32[1,1,3,32,4096]{4,3,2,1,0:T(8,128)S(1)}, f32[1,1,3,32,4096]{4,3,2,1,0:T(8,128)}, u32[]{:S(2)}) copy-start(f32[1,1,3,32,4096]{4,3,2,1,0:T(8,128)} %param.9) | copy-start | bytes 4718596
  23.9 2.2 %copy-start.15 = (s32[3]{0:T(128)S(1)}, s32[3]{0:T(128)}, u32[]{:S(2)}) copy-start(s32[3]{0:T(128)} %cutoff_ref.7) | copy-start | bytes 40
  24.0 2.2 %collective-permute-start.2 = (f32[11,88,128]{2,1,0:T(8,128)}, f32[11,88,128]{2,1,0:T(8,128)S(1)}, u32[]{:S(2)}, u32[]{:S(2)}) collective-permute-start(f32[11,88,128]{2,1,0:T(8,128)} %collective-permute-done.1.there_own), channel_id=1, source_target_pairs={{0,1},{1,0},{2,3},{3,2},{4,5},{5,4},{6,7},{7,6},{8,9},{9,8},{10,11... | collective-permute-start | bytes 1486856 | tf_op jit(solution)/shard_map/ppermute | solution.py:881
  24.5 41.3 %collective-permute-start.7 = (f32[3,16,4096]{2,1,0:T(8,128)S(1)}, f32[3,16,4096]{2,1,0:T(8,128)S(1)}, u32[]{:S(2)}, u32[]{:S(2)}) collective-permute-start(f32[3,16,4096]{2,1,0:T(8,128)S(1)} %dynamic-slice_bitcast_fusion), channel_id=1, source_target_pairs={{4,0},{8,4},{12,8},{0,12},{5,1},{9,5},{13,9},{1,13},{6,2},{10,6},{... | collective-permute-start | bytes 2359304 | tf_op jit(solution)/shard_map/ppermute | solution.py:850
  25.8 15.1 %copy-start.2 = (bf16[3072,256]{1,0:T(8,128)(2,1)S(1)}, bf16[3072,256]{1,0:T(8,128)(2,1)}, u32[]{:S(2)}) copy-start(bf16[3072,256]{1,0:T(8,128)(2,1)} %constant.21.clone.along_ref) | copy-start | bytes 4718596
  26.2 1.0 %copy-start.7 = (f32[224,128]{1,0:T(8,128)S(1)}, f32[224,128]{1,0:T(8,128)}, u32[]{:S(2)}) copy-start(f32[224,128]{1,0:T(8,128)} %constant.22.clone.waves_ref) | copy-start | bytes 344068
  27.2 1.0 %copy-start.8 = (f32[11,88,128]{2,1,0:T(8,128)S(1)}, f32[11,88,128]{2,1,0:T(8,128)}, u32[]{:S(2)}) copy-start(f32[11,88,128]{2,1,0:T(8,128)} %shard_map.95.here_own) | copy-start | bytes 1486852
  28.2 12.7 %copy-start.12 = (f32[2,8,88,128]{3,2,1,0:T(8,128)S(1)}, f32[2,8,88,128]{3,2,1,0:T(8,128)}, u32[]{:S(2)}) copy-start(f32[2,8,88,128]{3,2,1,0:T(8,128)} %copy-done.11) | copy-start | bytes 2162692
  41.0 3.7 %copy-start.10 = (f32[2,8,88,128]{3,2,1,0:T(8,128)S(1)}, f32[2,8,88,128]{3,2,1,0:T(8,128)}, u32[]{:S(2)}) copy-start(f32[2,8,88,128]{3,2,1,0:T(8,128)} %copy-done.9) | copy-start | bytes 2162692
  44.1 12.3 %collective-permute-start.5 = (f32[9,88,128]{2,1,0:T(8,128)S(1)}, f32[9,88,128]{2,1,0:T(8,128)S(1)}, u32[]{:S(2)}, u32[]{:S(2)}) collective-permute-start(f32[9,88,128]{2,1,0:T(8,128)S(1)} %get-tuple-element.37), channel_id=1, source_target_pairs={{0,2},{2,0},{1,3},{3,1},{4,6},{6,4},{5,7},{7,5},{8,10},{10,8},{9,1... | collective-permute-start | bytes 1216520 | tf_op jit(solution)/shard_map/ppermute | solution.py:902
  44.7 4.6 %copy-start.14 = (f32[2,6,88,128]{3,2,1,0:T(8,128)S(1)}, f32[2,6,88,128]{3,2,1,0:T(8,128)}, u32[]{:S(2)}) copy-start(f32[2,6,88,128]{3,2,1,0:T(8,128)} %copy-done.13) | copy-start | bytes 1622020
  47.7 17.3 %collective-permute-start.4 = (f32[9,88,128]{2,1,0:T(8,128)S(1)}, f32[9,88,128]{2,1,0:T(8,128)S(1)}, u32[]{:S(2)}, u32[]{:S(2)}) collective-permute-start(f32[9,88,128]{2,1,0:T(8,128)S(1)} %get-tuple-element.33), channel_id=1, source_target_pairs={{0,2},{2,0},{1,3},{3,1},{4,6},{6,4},{5,7},{7,5},{8,10},{10,8},{9,1... | collective-permute-start | bytes 1216520 | tf_op jit(solution)/shard_map/ppermute | solution.py:902
  51.5 19.6 %collective-permute-start.3 = (f32[7,88,128]{2,1,0:T(8,128)S(1)}, f32[7,88,128]{2,1,0:T(8,128)S(1)}, u32[]{:S(2)}, u32[]{:S(2)}) collective-permute-start(f32[7,88,128]{2,1,0:T(8,128)S(1)} %get-tuple-element.29), channel_id=1, source_target_pairs={{0,2},{2,0},{1,3},{3,1},{4,6},{6,4},{5,7},{7,5},{8,10},{10,8},{9,1... | collective-permute-start | bytes 946184 | tf_op jit(solution)/shard_map/ppermute | solution.py:902

commit v6 on v5

--- a/solution.py
+++ b/solution.py
@@ -307,7 +307,14 @@
     out["fz"] = left_table(forward.reshape(LINE, 2 * N), 128)
     out["iz"] = right_table(inverse.reshape(4 * NKZ, 2 * N), 128)
     out["izr"] = right_table(turned.reshape(4 * NKZ, 2 * N), 128)
-    out["izd"] = right_table(slope.reshape(4 * NKZ, 2 * N), 128)
+
+    def by_half(table):
+        wide = np.zeros((2, HALF_KZ + 1, 4, 2 * N))
+        wide[:, :HALF_KZ] = table.reshape(2, HALF_KZ, 4, 2 * N)
+        return right_table(wide.reshape(8 * HALF_KZ + 8, 2 * N), 128)
+
+    out["izg"] = by_half(inverse)
+    out["izd"] = by_half(slope)
     ky, alive = ky_values()
     y = 2 * np.arange(HALF)[None, :] + np.arange(2)[:, None]
     phase = 2 * np.pi * ky[:, None, None] * y[None] / N
@@ -399,23 +406,12 @@
             [right_table(part, 128) for part in ix.reshape(4, LANES, LANES)]
         )
     out["ix"] = np.stack([out.pop("ix0"), out.pop("ix1")])
-    ky_rows = np.tile(ky, 2)[:, None]
-    out["kyrow"] = np.broadcast_to(ky_rows, (ROWS, LANES)).astype(np.float32).copy()
-    lane_kx = np.tile(kx * live, 4)
-    out["kxlane"] = np.broadcast_to(lane_kx, (8, LANES)).astype(np.float32).copy()
-    yy = np.arange(N)
-    force = [forcing_amp * np.sin(2 * np.pi * ((w * yy) % N) / N) for w in range(1, 5)]
-    force = np.repeat(np.stack(force).reshape(4, HALF, 2, 1), N, axis=3)
-    out["force"] = force.reshape(4, HALF, LANES).astype(np.float32)
     merged = {}
     merged["ahead"] = np.concatenate([out["fz"], out["fy"], out["fyr"]], 0)
     gx = [out["gxh"].reshape(-1, 256), out["gxl"].reshape(-1, 256)]
-    square = [out[name] for name in ("iy", "iyd", "iz", "izd", "izr")]
+    square = [out[name] for name in ("iy", "iyd", "izg", "izd", "iz", "izr")]
     merged["back"] = np.concatenate(square + gx, 0)
     merged["along"] = np.concatenate([out["fx"].reshape(-1, 256), out["ix"].reshape(-1, 256)], 0)
-    merged["waves"] = np.concatenate(
-        [out["kyrow"], out["kxlane"], out["force"].reshape(-1, LANES)], 0
-    )
     return merged
 
 
@@ -425,6 +421,18 @@
 
 def ahead_tables(ref):
     return view(ref, 0, 2 * LINE), view(ref, 0, 2 * ROWS, 2 * LINE), view(ref, 1, 2 * ROWS, 2 * LINE)
+
+
+def ky_rows():
+    row = lax.broadcasted_iota(jnp.int32, (ROWS, LANES), 0)
+    index = jnp.where(row < NKY, row, row - NKY)
+    wave = jnp.where(index <= KEEP, index, index - (2 * KEEP + 1))
+    return jnp.where(index <= 2 * KEEP, wave, 0).astype(f32)
+
+
+def kx_lanes():
+    lane = lax.broadcasted_iota(jnp.int32, (1, LANES), 1) % HALF
+    return jnp.where(lane <= KEEP, lane, 0).astype(f32)
 
 
 def split(values):
@@ -480,16 +488,8 @@
     )
 
 
-def along_kz(ref, tile, yh):
-    return padded(ref[tile, pl.ds(yh, ROWS, stride=HALF), :]).T
-
-
 def line_rows(yh):
     return pl.ds(pl.multiple_of(yh * LINE, 8), LINE)
-
-
-def plane_rows(kz):
-    return pl.ds(pl.multiple_of(kz * LANES, LANES), LANES)
 
 
 def lane_parts(values):
@@ -511,12 +511,12 @@
     return chunk * CHUNK, min((chunk + 1) * CHUNK, NKZ)
 
 
-def over_lines(step, many):
+def over_lines(step, many, first=0, last=HALF):
     def some(index, _):
-        step([index * many + k for k in range(many)])
+        step([first + index * many + k for k in range(many)])
         return 0
 
-    lax.fori_loop(0, HALF // many, some, 0)
+    lax.fori_loop(0, (last - first) // many, some, 0)
 
 
 PIECES = 4
@@ -560,8 +560,20 @@
             out_ref[k] = part
 
 
-def flux_kernel(core_ref, base_ref, state_ref, ahead_ref, waves_ref, *refs):
-    *out_refs, lines = refs
+def flux_kernel(core_ref, base_hbm, state_hbm, ahead_hbm, *refs):
+    *out_refs, lines, base_ref, state_ref, ahead_ref, result, arrived, left = refs
+    wide = N * N // PIECES
+    pieces = [pltpu.make_async_copy(ahead_hbm, ahead_ref, arrived.at[2 * PIECES])]
+    for n in range(PIECES):
+        for k, (source, target) in enumerate(((base_hbm, base_ref), (state_hbm, state_ref))):
+            at = pl.ds(n * wide, wide)
+            pieces.append(
+                pltpu.make_async_copy(
+                    source.at[:, :, at], target.at[:, :, at], arrived.at[2 * n + k]
+                )
+            )
+    for piece in pieces:
+        piece.start()
     fz_ref, fy_ref, fyr_ref = ahead_tables(ahead_ref)
     sigma = jnp.where(core_ref[0] == 0, -time_step, time_step).astype(f32)
     nothing = jnp.zeros((HALF, LANES), f32)
@@ -579,13 +591,16 @@
             for tile in range(3):
                 lines[tile, line_rows(yh), :] = got[3 * n + tile]
 
-    over_lines(z_step, 4)
-    ky = waves_ref[:ROWS]
+    pieces[0].wait()
+    for n in range(PIECES):
+        pieces[2 * n + 1].wait()
+        pieces[2 * n + 2].wait()
+        over_lines(z_step, 4, n * HALF // PIECES, (n + 1) * HALF // PIECES)
+    ky = ky_rows()
     lane = lax.broadcasted_iota(jnp.int32, (ROWS, LANES), 1)
     odd_block = (lane // HALF) % 2 == 1
 
-    def y_step(chunk, kzs):
-        out_ref = out_refs[chunk]
+    def y_step(kzs):
         even = []
         for pair in range(0, len(kzs), 2):
             data = [stacked(along_y(lines, 0, kz)) for kz in kzs[pair : pair + 2]]
@@ -599,64 +614,82 @@
             plain = even[n]
             slopes = odd[n][0] * jnp.where(odd_block, kzf, ky)
             slopes = slopes + pltpu.roll(slopes, 32, 1)
-            at = kz - chunk * CHUNK
-            out_ref[0, at] = jnp.where(odd_block, slopes, plain)
+            result[0, kz] = jnp.where(odd_block, slopes, plain)
             other = plain * jnp.where(lane >= 96, -kzf, -ky)
             other = other + pltpu.roll(other, 64, 1)
-            out_ref[1, at] = jnp.where(lane >= 96, other, odd[n][1])
-
+            result[1, kz] = jnp.where(lane >= 96, other, odd[n][1])
+
+    sends = []
     for chunk in range(CHUNKS):
-        over_planes(functools.partial(y_step, chunk), *planes_of(chunk))
-
-
-def gradient_kernel(
-    core_ref, cutoff_ref, wave_ref, base_ref, state_ref,
-    here_own, here_other, there_own, there_other,
-    ahead_ref, back_ref, waves_ref, *refs
-):
-    *out_refs, planes = refs
-    fz_ref = ahead_tables(ahead_ref)[0]
-    iy_ref, iyd_ref, iz_ref, izd_ref = (view(back_ref, n) for n in range(4))
-    core = core_ref[0]
+        first, last = planes_of(chunk)
+        over_planes(y_step, first, last)
+        source = result.at[:, pl.ds(first, last - first)]
+        sends.append(pltpu.make_async_copy(source, out_refs[chunk], left.at[chunk]))
+        sends[-1].start()
+    for send in sends:
+        send.wait()
+
+
+def gradient_planes(cutoff_ref, here_ref, there_ref, back_ref, planes, start):
     cut_x, cut_y, cut_z = cutoff_ref[0], cutoff_ref[1], cutoff_ref[2]
     which = jnp.clip(cut_x - (KEEP - 3), 0, 3)
-    ky = waves_ref[:ROWS]
-    keep_y = jnp.where(jnp.abs(ky) <= cut_y.astype(f32), 1.0, 0.0).astype(f32)
-
-    def kept_z(kz):
-        return jnp.where(kz <= cut_z, 1.0, 0.0).astype(f32)
-
-    def gradient_step(kzs):
+    keep_y = jnp.where(jnp.abs(ky_rows()) <= cut_y.astype(f32), 1.0, 0.0).astype(f32)
+    iy_ref, iyd_ref = (view(back_ref, n) for n in range(2))
+    for d in range(3):
+        planes[d, HALF_KZ * LANES :, :] = jnp.zeros((LANES, LANES), f32)
+    for first in range(0, HALF_KZ, 4):
+        kzs = range(first, min(first + 4, HALF_KZ))
         rows = []
         for kz in kzs:
-            half = kz // HALF_KZ
-            at = kz - half * HALF_KZ
-            keep = keep_y * kept_z(kz)
-            here = jnp.where(half == core, here_own[at], here_other[at]) * keep
-            there = jnp.where(half == core, there_own[at], there_other[at]) * keep
-            rows.append(jnp.concatenate([here, there], 1))
-        high = back_ref[pl.ds(pl.multiple_of((5 + which) * 256, 256), 256), :]
-        low = back_ref[pl.ds(pl.multiple_of((9 + which) * 256, 256), 256), :]
+            keep = keep_y * jnp.where(start + kz <= cut_z, 1.0, 0.0).astype(f32)
+            rows.append(jnp.concatenate([here_ref[kz] * keep, there_ref[kz] * keep], 1))
+        high = back_ref[pl.ds(pl.multiple_of((6 + which) * 256, 256), 256), :]
+        low = back_ref[pl.ds(pl.multiple_of((10 + which) * 256, 256), 256), :]
         got = triple(jnp.concatenate(rows, 0), high, low)
         data = [stacked(padded(got[n * ROWS : (n + 1) * ROWS])) for n in range(len(kzs))]
         for n, kz in enumerate(kzs):
             even = lane_parts(folded(dot(iy_ref[...], data[n])))
-            planes[0, plane_rows(kz), :] = even[1]
-            planes[2, plane_rows(kz), :] = even[0]
+            planes[0, kz * LANES : (kz + 1) * LANES, :] = even[1]
+            planes[2, kz * LANES : (kz + 1) * LANES, :] = even[0]
         for n in range(0, len(kzs), 2):
-            both = jnp.concatenate([data[n][:, :LANES], data[n + 1][:, :LANES]], 1)
-            odd = lane_parts(folded(dot(iyd_ref[...], both)))
-            planes[1, plane_rows(kzs[n]), :] = odd[0]
-            planes[1, plane_rows(kzs[n + 1]), :] = odd[1]
-
-    over_planes(gradient_step)
-    force_at = jnp.clip(wave_ref[0] - 1, 0, 3)
+            both = jnp.concatenate([one[:, :LANES] for one in data[n : n + 2]], 1)
+            for k, part in enumerate(lane_parts(folded(dot(iyd_ref[...], both)))):
+                kz = kzs[n + k]
+                planes[1, kz * LANES : (kz + 1) * LANES, :] = part
+
+
+def half_kernel(core_ref, cutoff_ref, here_ref, there_ref, back_ref, planes):
+    start = core_ref[0] * HALF_KZ
+    gradient_planes(cutoff_ref, here_ref, there_ref, back_ref, planes, start)
+
+
+def gradient_kernel(
+    core_ref, cutoff_ref, wave_ref, base_ref, state_ref, own_ref, here_ref, there_ref,
+    ahead_ref, back_ref, *refs
+):
+    *out_refs, planes, force_ref = refs
+    core = core_ref[0]
+    start = (1 - core) * HALF_KZ
+    gradient_planes(cutoff_ref, here_ref, there_ref, back_ref, planes, start)
+    fz_ref = ahead_tables(ahead_ref)[0]
+    iz_ref, izd_ref = view(back_ref, 2), view(back_ref, 3)
+    y = lax.broadcasted_iota(jnp.int32, (HALF, LANES), 0) * 2
+    y = y + lax.broadcasted_iota(jnp.int32, (HALF, LANES), 1) // N
+    phase = ((wave_ref[0] * y) % N).astype(f32) * (2.0 * np.pi / N)
+    force_ref[...] = forcing_amp * jnp.sin(phase)
     nothing = jnp.zeros((HALF, LANES), f32)
+
+    def along_halves(d, yh):
+        at = pl.ds(yh, 4 * (HALF_KZ + 1), stride=HALF)
+        own, other = own_ref[d, at, :], planes[d, at, :]
+        low = jnp.where(core == 0, own, other)
+        high = jnp.where(core == 0, other, own)
+        return padded(jnp.concatenate([low, high], 0)).T
 
     def physical_step(yhs):
         count = len(yhs)
-        flat = [along_kz(planes, d, yh)[:96] for d in range(2) for yh in yhs]
-        steep = [along_kz(planes, 2, yh)[:96] for yh in yhs]
+        flat = [along_halves(d, yh)[:96] for d in range(2) for yh in yhs]
+        steep = [along_halves(2, yh)[:96] for yh in yhs]
         flat = folded_lanes(dot(beside(jnp.concatenate(flat, 0)), iz_ref[...]))
         steep = folded_lanes(dot(beside(jnp.concatenate(steep, 0)), izd_ref[...]))
         for n, yh in enumerate(yhs):
@@ -672,7 +705,7 @@
                 comb.append(s[i] - time_step * coupling)
                 drive = sum(grads[j][i] * b[j] for j in range(3))
                 if i == 0:
-                    drive = drive - waves_ref[pl.ds(ROWS + 8 + force_at * HALF + yh, 1), :]
+                    drive = drive - force_ref[pl.ds(yh, 1), :]
                 comb_base.append(b[i] - time_step * drive)
             rows = [comb[1], comb_base[1], comb[2], comb_base[2]]
             rows += [comb[0], comb_base[0], nothing, nothing]
@@ -688,15 +721,15 @@
 
 def spectral_kernel(
     chunk, core_ref, cutoff_ref, lines_ref, flux_ref,
-    ahead_ref, along_ref, waves_ref, near_ref, far_ref,
+    ahead_ref, along_ref, near_ref, far_ref,
 ):
     _, fy_ref, fyr_ref = ahead_tables(ahead_ref)
     core = core_ref[0]
     cut_x, cut_y, cut_z = cutoff_ref[0], cutoff_ref[1], cutoff_ref[2]
     first, last = planes_of(chunk)
     extra = last - first
-    ky = waves_ref[:ROWS]
-    kx = waves_ref[ROWS : ROWS + 1]
+    ky = ky_rows()
+    kx = kx_lanes()
     keep_y = jnp.where(jnp.abs(ky) <= cut_y.astype(f32), 1.0, 0.0).astype(f32)
     keep_x = jnp.where(kx <= cut_x.astype(f32), 1.0, 0.0).astype(f32)
     keep_xy = keep_y * keep_x
@@ -786,7 +819,7 @@
     near_ref, far_ref, planes_a, planes_b, state_ref, base_ref, back_ref,
     base_out, state_out, planes_c,
 ):
-    iy_ref, iz_ref, izr_ref = (view(back_ref, n) for n in (0, 2, 4))
+    iy_ref, iz_ref, izr_ref = (view(back_ref, n) for n in (0, 4, 5))
     inverse_y(near_ref, far_ref, iy_ref, planes_c)
 
     def along_chunks(tile, yh):
@@ -821,16 +854,17 @@
 interpret = False
 
 
-def call(kernel, outs, scratch, inputs, room, in_smem=0, in_hbm=0):
+def call(kernel, outs, scratch, inputs, room, in_smem=0, in_hbm=0, out_hbm=False):
     whole = pl.BlockSpec(memory_space=pltpu.VMEM)
     small = pl.BlockSpec(memory_space=pltpu.SMEM)
+    far = pl.BlockSpec(memory_space=pltpu.HBM)
     return pl.pallas_call(
         kernel,
         out_shape=outs,
         in_specs=[small] * in_smem
-        + [pl.BlockSpec(memory_space=pltpu.HBM)] * in_hbm
+        + [far] * in_hbm
         + [whole] * (len(inputs) - in_smem - in_hbm),
-        out_specs=jax.tree.map(lambda _: whole, outs),
+        out_specs=jax.tree.map(lambda _: far if out_hbm else whole, outs),
         scratch_shapes=scratch,
         compiler_params=pltpu.CompilerParams(vmem_limit_bytes=room * 2**20),
         cost_estimate=pl.CostEstimate(flops=1000, bytes_accessed=1000, transcendentals=0),
@@ -872,19 +906,38 @@
     flux = call(
         flux_kernel,
         [sds((2, count, ROWS, LANES), f32) for count in counts],
-        [pltpu.VMEM((3, HALF * LINE, LANES), f32)],
-        [core_at, own_base, own_state, t["ahead"], t["waves"]],
-        room=16,
+        [
+            pltpu.VMEM((3, HALF * LINE, LANES), f32),
+            pltpu.VMEM(own_base.shape, f32),
+            pltpu.VMEM(own_state.shape, f32),
+            pltpu.VMEM(t["ahead"].shape, bf16),
+            pltpu.VMEM((2, NKZ, ROWS, LANES), f32),
+            pltpu.SemaphoreType.DMA((2 * PIECES + 1,)),
+            pltpu.SemaphoreType.DMA((CHUNKS,)),
+        ],
+        [core_at, own_base, own_state, t["ahead"]],
+        room=56,
         in_smem=1,
+        in_hbm=3,
+        out_hbm=True,
     )
     there_own, flux = lax.optimization_barrier((there_own, flux))
     there_other = lax.ppermute(there_own, "comp", swap)
+    half_planes = sds((3, (HALF_KZ + 1) * LANES, LANES), f32)
+    own_planes = call(
+        half_kernel,
+        half_planes,
+        [],
+        [core_at, cutoff, here_own, there_own, t["back"]],
+        room=12,
+        in_smem=2,
+    )
     lines = call(
         gradient_kernel,
         [sds((2, HALF * 4 * CHUNK, LANES), f32)] * CHUNKS,
-        [pltpu.VMEM((3, NKZ * LANES, LANES), f32)],
-        [core_at, cutoff, wavenumber, own_base, own_state]
-        + [here_own, here_other, there_own, there_other, t["ahead"], t["back"], t["waves"]],
+        [pltpu.VMEM(half_planes.shape, f32), pltpu.VMEM((HALF, LANES), f32)],
+        [core_at, cutoff, wavenumber, own_base, own_state, own_planes, here_other, there_other]
+        + [t["ahead"], t["back"]],
         room=20,
         in_smem=3,
     )
@@ -894,7 +947,7 @@
             functools.partial(spectral_kernel, chunk),
             [sds((counts[chunk] + 1, ROWS, LANES), f32)] * 2,
             [],
-            [core_at, cutoff, lines[chunk], flux[chunk], t["ahead"], t["along"], t["waves"]],
+            [core_at, cutoff, lines[chunk], flux[chunk], t["ahead"], t["along"]],
             room=10,
             in_smem=2,
         )

time: 77.3 us -> 74.6 us (0.965)
  local copies, waits for them, and re-layouts: 6.11 us -> 0.1 us
  Pallas kernels: 40.4 us -> 43.8 us
  starting transfers between devices: 10.5 us -> 11.8 us
  waiting for transfers between devices: 18.5 us -> 17.3 us
    unnamed x32 -> x18, local copies, waits for them, and re-layouts: 6.06 us -> 0.05 us
    pallas_call x8 -> x9, Pallas kernels: 40.4 us -> 43.8 us  [call(): pl.pallas_call(kernel, out_shape=outs, in_specs=[small] * in_smem + [far]...]
    ppermute x3, waiting for transfers between devices: 18.2 us -> 17.3 us  [body(): far.append(lax.ppermute(far_part, 'slab', swap))]
    ppermute x3, starting transfers between devices: 2.76 us -> 3.71 us  [body(): far.append(lax.ppermute(far_part, 'slab', swap))]
  transfers between devices with their start and end apart: 8 -> 8, of which waited for: 4 -> 3; matrix products, arithmetic and copies ran while one was open for 0% -> 0% of each run, Pallas kernels for 39% -> 45%
where the time goes in v6:
time: 74.6 us; the launch traced here: 74.4 us
  Pallas kernels  43.8 us (59%)
  waiting for transfers between devices  17.3 us (23%)
  starting transfers between devices  11.8 us (16%)
  between operations  1.47 us (2%)
    pallas_call x9, Pallas kernels, call(): pl.pallas_call(kernel, out_shape=outs, in_specs=[small] * in_smem + [far]...  43.8 us
    ppermute x3, waiting for transfers between devices, body(): far.append(lax.ppermute(far_part, 'slab', swap))  17.3 us
    ppermute x3, starting transfers between devices, body(): far.append(lax.ppermute(far_part, 'slab', swap))  3.71 us
    ppermute x1, starting transfers between devices, body(): state_next = lax.ppermute(own_state, ('seg', 'comp'), around)  3.6 us
    ppermute x1, starting transfers between devices, body(): there_own = lax.ppermute(here_own, 'slab', swap)  3 us
  transfers between devices with their start and end apart: 8, of which 3 were waited for; matrix products, arithmetic and copies ran while one was open for 0% of the time, Pallas kernels for 45%

profile of v6, /device:TPU:0, one launch (start us, length us, event | category | flops | bytes accessed | tf_op | source)
XLA Modules:
  0.0 74.4 jit_solution(243549537164738590)
XLA Ops:
  0.6 4.1 %shard_map.86.here_ref = f32[11,88,128]{2,1,0:T(8,128)} custom-call(s32[1]{0:T(128)} %bitcast.core_ref, f32[3,32,4096]{2,1,0:T(8,128)} %bitcast.7, bf16[544,256]{1,0:T(8,128)(2,1)} %constant.17.clone.ahead_hbm.ahead_ref), custom_call_target="tpu_custom_call" | custom-call | flops 1000 | bytes 1000 | tf_op jit(solution)/shard_map/pallas_call | solution.py:861
  4.8 3.0 %collective-permute-start = (f32[11,88,128]{2,1,0:T(8,128)}, f32[11,88,128]{2,1,0:T(8,128)}, u32[]{:S(2)}, u32[]{:S(2)}) collective-permute-start(f32[11,88,128]{2,1,0:T(8,128)} %shard_map.86.here_ref), channel_id=1, source_target_pairs={{0,2},{2,0},{1,3},{3,1},{4,6},{6,4},{5,7},{7,5},{8,10},{10,8},{9,1... | collective-permute-start | bytes 1486856 | tf_op jit(solution)/shard_map/ppermute | solution.py:903
  7.8 0.0 copy-start.1
  7.8 3.6 %collective-permute-start.6 = (f32[3,32,4096]{2,1,0:T(8,128)}, f32[3,32,4096]{2,1,0:T(8,128)}, u32[]{:S(2)}, u32[]{:S(2)}) collective-permute-start(f32[3,32,4096]{2,1,0:T(8,128)} %bitcast.2.state_hbm.state_ref), channel_id=1, source_target_pairs={{4,0},{8,4},{12,8},{0,12},{1,5},{5,9},{9,13},{13,1},{6,2},{10,6},{... | collective-permute-start | bytes 4718600 | tf_op jit(solution)/shard_map/ppermute | solution.py:885
  11.4 0.0 collective-permute-start.1
  11.4 0.0 copy-start
  11.4 10.6 %shard_map.87 = (f32[2,8,88,128]{3,2,1,0:T(8,128)}, f32[2,8,88,128]{3,2,1,0:T(8,128)}, f32[2,6,88,128]{3,2,1,0:T(8,128)}) custom-call(s32[1]{0:T(128)} %bitcast.core_ref, f32[3,32,4096]{2,1,0:T(8,128)} %bitcast.8, f32[3,32,4096]{2,1,0:T(8,128)} %bitcast.2.state_hbm.state_ref, bf16[544,256]{1,0:T(8,128)(2,1)} %constant.17.clone.ahead_hbm.ahead_ref), custom_call_target="tpu_custom_call" | custom-call | flops 1000 | bytes 1000 | tf_op jit(solution)/shard_map/pallas_call | solution.py:861
  22.0 0.0 copy-start.8
  22.0 0.0 copy-start.4
  22.0 0.0 collective-permute-done.there_ref
  22.0 0.6 collective-permute-start.2
  22.6 0.0 copy-done.1
  22.6 0.1 dynamic-slice_bitcast_fusion
  22.6 0.9 %collective-permute-start.7 = (f32[3,16,4096]{2,1,0:T(8,128)S(1)}, f32[3,16,4096]{2,1,0:T(8,128)S(1)}, u32[]{:S(2)}, u32[]{:S(2)}) collective-permute-start(f32[3,16,4096]{2,1,0:T(8,128)S(1)} %dynamic-slice_bitcast_fusion), channel_id=1, source_target_pairs={{4,0},{8,4},{12,8},{0,12},{5,1},{9,5},{13,9},{1,13},{6,2},{10,6},{... | collective-permute-start | bytes 2359304 | tf_op jit(solution)/shard_map/ppermute | solution.py:884
  24.2 0.0 copy-done
  24.2 0.0 copy-done.8
  24.2 0.0 copy-done.4
  24.2 0.0 copy-start.3
  24.2 3.2 %shard_map.88.own_ref = f32[3,1536,128]{2,1,0:T(8,128)S(1)} custom-call(s32[1]{0:T(128)} %bitcast.core_ref, s32[3]{0:T(128)S(1)} %copy-done.8, f32[11,88,128]{2,1,0:T(8,128)S(1)} %copy-done.4, f32[11,88,128]{2,1,0:T(8,128)} %collective-permute-done.there_ref, bf16[3584,256]{1,0:T(8,128)(2,1)S(1)} %copy-done), custom_call_target="tpu_custom_call" | custom-call | flops 1000 | bytes 1000 | tf_op jit(solution)/shard_map/pallas_call | solution.py:861
  27.4 0.0 copy-start.2
  27.5 0.0 copy-start.6
  27.5 0.0 collective-permute-done.1.here_ref
  27.5 0.0 collective-permute-done.2.there_ref
  27.5 0.0 copy-done.3
  27.5 10.8 %shard_map.89 = (f32[2,1024,128]{2,1,0:T(8,128)S(1)}, f32[2,1024,128]{2,1,0:T(8,128)S(1)}, f32[2,1024,128]{2,1,0:T(8,128)S(1)}) custom-call(s32[1]{0:T(128)} %bitcast.core_ref, s32[3]{0:T(128)S(1)} %copy-done.8, s32[1]{0:T(128)S(6)} %copy.9.wave_ref, f32[3,32,4096]{2,1,0:T(8,128)S(1)} %bitcast.9, f32[3,32,4096]{2,1,0:T(8,128)} %bitcast.2.state_hbm.state_ref, ...), custom_call_target="tpu_custom_call" | custom-call | flops 1000 | bytes 1000 | tf_op jit(solution)/shard_map/pallas_call | solution.py:861
  38.3 0.0 copy-done.2
  38.3 0.0 copy-done.6
  38.3 0.0 copy-start.5
  38.4 3.1 %shard_map.92 = (f32[9,88,128]{2,1,0:T(8,128)S(1)}, f32[9,88,128]{2,1,0:T(8,128)S(1)}) custom-call(s32[1]{0:T(128)} %bitcast.core_ref, s32[3]{0:T(128)S(1)} %copy-done.8, f32[2,1024,128]{2,1,0:T(8,128)S(1)} %get-tuple-element.34.lines_ref, f32[2,8,88,128]{3,2,1,0:T(8,128)S(1)} %copy-done.6, bf16[544,256]{1,0:T(8,128)(2,1)S(1)} %copy-done.3, ...), custom_call_target="tpu_custom_call" | custom-call | flops 1000 | bytes 1000 | tf_op jit(solution)/shard_map/pallas_call | solution.py:861
  41.4 1.6 %collective-permute-start.5 = (f32[9,88,128]{2,1,0:T(8,128)S(1)}, f32[9,88,128]{2,1,0:T(8,128)S(1)}, u32[]{:S(2)}, u32[]{:S(2)}) collective-permute-start(f32[9,88,128]{2,1,0:T(8,128)S(1)} %get-tuple-element.37), channel_id=1, source_target_pairs={{0,2},{2,0},{1,3},{3,1},{4,6},{6,4},{5,7},{7,5},{8,10},{10,8},{9,1... | collective-permute-start | bytes 1216520 | tf_op jit(solution)/shard_map/ppermute | solution.py:955
  43.0 0.0 copy-done.5
  43.0 0.0 copy-start.7
  43.0 3.1 %shard_map.91 = (f32[9,88,128]{2,1,0:T(8,128)S(1)}, f32[9,88,128]{2,1,0:T(8,128)S(1)}) custom-call(s32[1]{0:T(128)} %bitcast.core_ref, s32[3]{0:T(128)S(1)} %copy-done.8, f32[2,1024,128]{2,1,0:T(8,128)S(1)} %get-tuple-element.30.lines_ref, f32[2,8,88,128]{3,2,1,0:T(8,128)S(1)} %copy-done.5, bf16[544,256]{1,0:T(8,128)(2,1)S(1)} %copy-done.3, ...), custom_call_target="tpu_custom_call" | custom-call | flops 1000 | bytes 1000 | tf_op jit(solution)/shard_map/pallas_call | solution.py:861
  46.1 0.6 collective-permute-start.4
  46.7 0.0 copy-done.7
  46.7 2.2 %shard_map.90 = (f32[7,88,128]{2,1,0:T(8,128)S(1)}, f32[7,88,128]{2,1,0:T(8,128)S(1)}) custom-call(s32[1]{0:T(128)} %bitcast.core_ref, s32[3]{0:T(128)S(1)} %copy-done.8, f32[2,1024,128]{2,1,0:T(8,128)S(1)} %get-tuple-element.26.lines_ref, f32[2,6,88,128]{3,2,1,0:T(8,128)S(1)} %copy-done.7, bf16[544,256]{1,0:T(8,128)(2,1)S(1)} %copy-done.3, ...), custom_call_target="tpu_custom_call" | custom-call | flops 1000 | bytes 1000 | tf_op jit(solution)/shard_map/pallas_call | solution.py:861
  48.9 1.6 %collective-permute-start.3 = (f32[7,88,128]{2,1,0:T(8,128)S(1)}, f32[7,88,128]{2,1,0:T(8,128)S(1)}, u32[]{:S(2)}, u32[]{:S(2)}) collective-permute-start(f32[7,88,128]{2,1,0:T(8,128)S(1)} %get-tuple-element.29), channel_id=1, source_target_pairs={{0,2},{2,0},{1,3},{3,1},{4,6},{6,4},{5,7},{7,5},{8,10},{10,8},{9,1... | collective-permute-start | bytes 946184 | tf_op jit(solution)/shard_map/ppermute | solution.py:955
  50.4 3.3 %collective-permute-done.5.far_b = f32[9,88,128]{2,1,0:T(8,128)S(1)} collective-permute-done((f32[9,88,128]{2,1,0:T(8,128)S(1)}, f32[9,88,128]{2,1,0:T(8,128)S(1)}, u32[]{:S(2)}, u32[]{:S(2)}) %collective-permute-start.5) | collective-permute-done | bytes 405536 | tf_op jit(solution)/shard_map/ppermute | solution.py:955
  53.7 8.7 %collective-permute-done.4.far_a = f32[9,88,128]{2,1,0:T(8,128)S(1)} collective-permute-done((f32[9,88,128]{2,1,0:T(8,128)S(1)}, f32[9,88,128]{2,1,0:T(8,128)S(1)}, u32[]{:S(2)}, u32[]{:S(2)}) %collective-permute-start.4) | collective-permute-done | bytes 405536 | tf_op jit(solution)/shard_map/ppermute | solution.py:955
  62.4 0.8 %shard_map.93 = (f32[2,1024,128]{2,1,0:T(8,128)S(1)}, f32[2,1024,128]{2,1,0:T(8,128)S(1)}) custom-call(f32[9,88,128]{2,1,0:T(8,128)S(1)} %get-tuple-element.32.near_a, f32[9,88,128]{2,1,0:T(8,128)S(1)} %collective-permute-done.4.far_a, f32[9,88,128]{2,1,0:T(8,128)S(1)} %get-tuple-element.36.near_b, f32[9,88,128]{2,1,0:T(8,128)S(1)} %collective-permute-done.5.far_b, ...), custom_call_target="tpu_custom_call" | custom-call | flops 1000 | bytes 1000 | tf_op jit(solution)/shard_map/pallas_call | solution.py:861
  63.2 0.0 collective-permute-done.7.base_ref
  63.2 5.3 %collective-permute-done.3.far_ref = f32[7,88,128]{2,1,0:T(8,128)S(1)} collective-permute-done((f32[7,88,128]{2,1,0:T(8,128)S(1)}, f32[7,88,128]{2,1,0:T(8,128)S(1)}, u32[]{:S(2)}, u32[]{:S(2)}) %collective-permute-start.3) | collective-permute-done | bytes 315424 | tf_op jit(solution)/shard_map/ppermute | solution.py:955
  68.5 0.0 collective-permute-done.6.state_ref
  68.5 5.9 %shard_map.94 = (f32[3,16,4096]{2,1,0:T(8,128)}, f32[3,32,4096]{2,1,0:T(8,128)}) custom-call(f32[7,88,128]{2,1,0:T(8,128)S(1)} %get-tuple-element.28.near_ref, f32[7,88,128]{2,1,0:T(8,128)S(1)} %collective-permute-done.3.far_ref, f32[2,1024,128]{2,1,0:T(8,128)S(1)} %get-tuple-element.38.planes_a, f32[2,1024,128]{2,1,0:T(8,128)S(1)} %get-tuple-element.39.planes_b, ...), custom_call_target="tpu_custom_call" | custom-call | flops 1000 | bytes 1000 | tf_op jit(solution)/shard_map/pallas_call | solution.py:861
Async XLA Ops:
  4.8 17.2 %collective-permute-start = (f32[11,88,128]{2,1,0:T(8,128)}, f32[11,88,128]{2,1,0:T(8,128)}, u32[]{:S(2)}, u32[]{:S(2)}) collective-permute-start(f32[11,88,128]{2,1,0:T(8,128)} %shard_map.86.here_ref), channel_id=1, source_target_pairs={{0,2},{2,0},{1,3},{3,1},{4,6},{6,4},{5,7},{7,5},{8,10},{10,8},{9,1... | collective-permute-start | bytes 1486856 | tf_op jit(solution)/shard_map/ppermute | solution.py:903
  7.8 14.8 %copy-start.1 = (f32[1,3,32,4096]{3,2,1,0:T(8,128)S(1)}, f32[1,3,32,4096]{3,2,1,0:T(8,128)}, u32[]{:S(2)}) copy-start(f32[1,3,32,4096]{3,2,1,0:T(8,128)} %param.7) | copy-start | bytes 4718596
  7.8 60.7 %collective-permute-start.6 = (f32[3,32,4096]{2,1,0:T(8,128)}, f32[3,32,4096]{2,1,0:T(8,128)}, u32[]{:S(2)}, u32[]{:S(2)}) collective-permute-start(f32[3,32,4096]{2,1,0:T(8,128)} %bitcast.2.state_hbm.state_ref), channel_id=1, source_target_pairs={{4,0},{8,4},{12,8},{0,12},{1,5},{5,9},{9,13},{13,1},{6,2},{10,6},{... | collective-permute-start | bytes 4718600 | tf_op jit(solution)/shard_map/ppermute | solution.py:885
  11.4 16.1 %collective-permute-start.1 = (f32[11,88,128]{2,1,0:T(8,128)}, f32[11,88,128]{2,1,0:T(8,128)}, u32[]{:S(2)}, u32[]{:S(2)}) collective-permute-start(f32[11,88,128]{2,1,0:T(8,128)} %shard_map.86.here_ref), channel_id=1, source_target_pairs={{0,1},{1,0},{2,3},{3,2},{4,5},{5,4},{6,7},{7,6},{8,9},{9,8},{10,11... | collective-permute-start | bytes 1486856 | tf_op jit(solution)/shard_map/ppermute | solution.py:904
  11.4 12.8 %copy-start = (bf16[3584,256]{1,0:T(8,128)(2,1)S(1)}, bf16[3584,256]{1,0:T(8,128)(2,1)}, u32[]{:S(2)}) copy-start(bf16[3584,256]{1,0:T(8,128)(2,1)} %constant.18.clone.back_ref) | copy-start | bytes 5505028
  22.0 2.2 %copy-start.8 = (s32[3]{0:T(128)S(1)}, s32[3]{0:T(128)}, u32[]{:S(2)}) copy-start(s32[3]{0:T(128)} %cutoff_ref.9) | copy-start | bytes 40
  22.0 2.2 %copy-start.4 = (f32[11,88,128]{2,1,0:T(8,128)S(1)}, f32[11,88,128]{2,1,0:T(8,128)}, u32[]{:S(2)}) copy-start(f32[11,88,128]{2,1,0:T(8,128)} %shard_map.86.here_ref) | copy-start | bytes 1486852
  22.0 5.5 %collective-permute-start.2 = (f32[11,88,128]{2,1,0:T(8,128)}, f32[11,88,128]{2,1,0:T(8,128)S(1)}, u32[]{:S(2)}, u32[]{:S(2)}) collective-permute-start(f32[11,88,128]{2,1,0:T(8,128)} %collective-permute-done.there_ref), channel_id=1, source_target_pairs={{0,1},{1,0},{2,3},{3,2},{4,5},{5,4},{6,7},{7,6},{8,9},{9,8},{10,11... | collective-permute-start | bytes 1486856 | tf_op jit(solution)/shard_map/ppermute | solution.py:925
  22.6 40.5 %collective-permute-start.7 = (f32[3,16,4096]{2,1,0:T(8,128)S(1)}, f32[3,16,4096]{2,1,0:T(8,128)S(1)}, u32[]{:S(2)}, u32[]{:S(2)}) collective-permute-start(f32[3,16,4096]{2,1,0:T(8,128)S(1)} %dynamic-slice_bitcast_fusion), channel_id=1, source_target_pairs={{4,0},{8,4},{12,8},{0,12},{5,1},{9,5},{13,9},{1,13},{6,2},{10,6},{... | collective-permute-start | bytes 2359304 | tf_op jit(solution)/shard_map/ppermute | solution.py:884
  24.2 3.3 %copy-start.3 = (bf16[544,256]{1,0:T(8,128)(2,1)S(1)}, bf16[544,256]{1,0:T(8,128)(2,1)}, u32[]{:S(2)}) copy-start(bf16[544,256]{1,0:T(8,128)(2,1)} %constant.17.clone.ahead_hbm.ahead_ref) | copy-start | bytes 835588
  27.4 10.9 %copy-start.2 = (bf16[3072,256]{1,0:T(8,128)(2,1)S(1)}, bf16[3072,256]{1,0:T(8,128)(2,1)}, u32[]{:S(2)}) copy-start(bf16[3072,256]{1,0:T(8,128)(2,1)} %constant.19.clone.along_ref) | copy-start | bytes 4718596
  27.5 10.9 %copy-start.6 = (f32[2,8,88,128]{3,2,1,0:T(8,128)S(1)}, f32[2,8,88,128]{3,2,1,0:T(8,128)}, u32[]{:S(2)}) copy-start(f32[2,8,88,128]{3,2,1,0:T(8,128)} %get-tuple-element.35.flux_ref) | copy-start | bytes 2162692
  38.3 4.7 %copy-start.5 = (f32[2,8,88,128]{3,2,1,0:T(8,128)S(1)}, f32[2,8,88,128]{3,2,1,0:T(8,128)}, u32[]{:S(2)}) copy-start(f32[2,8,88,128]{3,2,1,0:T(8,128)} %get-tuple-element.31.flux_ref) | copy-start | bytes 2162692
  41.4 12.3 %collective-permute-start.5 = (f32[9,88,128]{2,1,0:T(8,128)S(1)}, f32[9,88,128]{2,1,0:T(8,128)S(1)}, u32[]{:S(2)}, u32[]{:S(2)}) collective-permute-start(f32[9,88,128]{2,1,0:T(8,128)S(1)} %get-tuple-element.37), channel_id=1, source_target_pairs={{0,2},{2,0},{1,3},{3,1},{4,6},{6,4},{5,7},{7,5},{8,10},{10,8},{9,1... | collective-permute-start | bytes 1216520 | tf_op jit(solution)/shard_map/ppermute | solution.py:955
  43.0 3.7 %copy-start.7 = (f32[2,6,88,128]{3,2,1,0:T(8,128)S(1)}, f32[2,6,88,128]{3,2,1,0:T(8,128)}, u32[]{:S(2)}) copy-start(f32[2,6,88,128]{3,2,1,0:T(8,128)} %get-tuple-element.27.flux_ref) | copy-start | bytes 1622020
  46.1 16.3 %collective-permute-start.4 = (f32[9,88,128]{2,1,0:T(8,128)S(1)}, f32[9,88,128]{2,1,0:T(8,128)S(1)}, u32[]{:S(2)}, u32[]{:S(2)}) collective-permute-start(f32[9,88,128]{2,1,0:T(8,128)S(1)} %get-tuple-element.33), channel_id=1, source_target_pairs={{0,2},{2,0},{1,3},{3,1},{4,6},{6,4},{5,7},{7,5},{8,10},{10,8},{9,1... | collective-permute-start | bytes 1216520 | tf_op jit(solution)/shard_map/ppermute | solution.py:955
  48.9 19.6 %collective-permute-start.3 = (f32[7,88,128]{2,1,0:T(8,128)S(1)}, f32[7,88,128]{2,1,0:T(8,128)S(1)}, u32[]{:S(2)}, u32[]{:S(2)}) collective-permute-start(f32[7,88,128]{2,1,0:T(8,128)S(1)} %get-tuple-element.29), channel_id=1, source_target_pairs={{0,2},{2,0},{1,3},{3,1},{4,6},{6,4},{5,7},{7,5},{8,10},{10,8},{9,1... | collective-permute-start | bytes 946184 | tf_op jit(solution)/shard_map/ppermute | solution.py:955

commit v7 on v6

--- a/solution.py
+++ b/solution.py
@@ -267,13 +267,16 @@
     padded = np.zeros((table.shape[0], depth))
     padded[:, : table.shape[1]] = table
     high, low = halves(padded)
+    return np.concatenate([high, high, low], 1)
+
+
+def right_table(table, depth):
+    padded = np.zeros((depth, table.shape[1]))
+    padded[: table.shape[0]] = table
+    high, low = halves(padded)
     return np.concatenate(
-        [np.concatenate([high, high], 1), np.concatenate([low, np.zeros_like(low)], 1)], 0
-    )
-
-
-def right_table(table, depth):
-    return np.ascontiguousarray(left_table(table.T, depth).T)
+        [np.concatenate([high, low], 1), np.concatenate([high, np.zeros_like(low)], 1)], 0
+    )
 
 
 def ky_values():
@@ -326,8 +329,10 @@
     plain[1, :, :, 0] = -sine
     plain[1, :, :, 1] = cosine
     rotated = np.stack([-plain[1], plain[0]])
-    out["fy"] = left_table(plain.reshape(ROWS, 128), 128)
-    out["fyr"] = left_table(rotated.reshape(ROWS, 128), 128)
+    for name, table in (("fy", plain), ("fyr", rotated)):
+        tall = np.zeros((LINE, 128))
+        tall[:ROWS] = table.reshape(ROWS, 128)
+        out[name] = left_table(tall, 128)
     back = np.zeros((2, 2, HALF, 2, NKY))
     cos_t = np.moveaxis(cosine, 0, -1) / N
     sin_t = np.moveaxis(sine, 0, -1) / N
@@ -408,8 +413,9 @@
     out["ix"] = np.stack([out.pop("ix0"), out.pop("ix1")])
     merged = {}
     merged["ahead"] = np.concatenate([out["fz"], out["fy"], out["fyr"]], 0)
+    merged["height"] = np.concatenate([out["iy"], out["iyd"]], 0)
     gx = [out["gxh"].reshape(-1, 256), out["gxl"].reshape(-1, 256)]
-    square = [out[name] for name in ("iy", "iyd", "izg", "izd", "iz", "izr")]
+    square = [out[name] for name in ("izg", "izd", "iz", "izr")]
     merged["back"] = np.concatenate(square + gx, 0)
     merged["along"] = np.concatenate([out["fx"].reshape(-1, 256), out["ix"].reshape(-1, 256)], 0)
     return merged
@@ -420,7 +426,7 @@
 
 
 def ahead_tables(ref):
-    return view(ref, 0, 2 * LINE), view(ref, 0, 2 * ROWS, 2 * LINE), view(ref, 1, 2 * ROWS, 2 * LINE)
+    return [view(ref, n, LINE) for n in range(3)]
 
 
 def ky_rows():
@@ -451,17 +457,17 @@
 
 def stacked(values):
     high, low = split(values)
-    return jnp.concatenate([high, low], 0)
+    return jnp.concatenate([high, low, high], 0)
+
+
+def beside_thrice(values):
+    high, low = split(values)
+    return jnp.concatenate([high, low, high], 1)
 
 
 def beside(values):
     high, low = split(values)
     return jnp.concatenate([high, low], 1)
-
-
-def folded(result):
-    rows = result.shape[0] // 2
-    return result[:rows] + result[rows:]
 
 
 def folded_lanes(result):
@@ -548,14 +554,14 @@
         for yh in yhs:
             at = slice(yh * LANES, (yh + 1) * LANES)
             rows += [base_ref[i, :, at] for i in range(3)] + [nothing]
-        got = folded(dot_nt(fz_ref[...], beside(jnp.concatenate(rows, 0))))
+        got = dot_nt(fz_ref[...], beside_thrice(jnp.concatenate(rows, 0)))
         for yh, part in zip(yhs, lane_parts(got)):
             lines[0, yh * LINE : (yh + 1) * LINE, :] = part
     start = core_ref[0] * HALF_KZ
     for pair in range(0, HALF_KZ, 2):
         ks = range(pair, min(pair + 2, HALF_KZ))
         data = jnp.concatenate([stacked(along_y(lines, 0, start + k)) for k in ks], 1)
-        got = folded(dot(fy_ref[...], data))
+        got = dot(fy_ref[...], data)[:ROWS]
         for k, part in zip(ks, lane_parts(got)):
             out_ref[k] = part
 
@@ -586,7 +592,7 @@
             rows += [t[2] * b[0], t[0] * b[1], t[1] * b[0], t[0] * b[2]]
             rows += [t[2] * b[1], t[2] * b[2], t[1] * b[1], t[1] * b[2]]
             rows += [nothing, nothing, t[0] * b[0], nothing]
-        got = lane_parts(folded(dot_nt(fz_ref[...], beside(jnp.concatenate(rows, 0)))))
+        got = lane_parts(dot_nt(fz_ref[...], beside_thrice(jnp.concatenate(rows, 0))))
         for n, yh in enumerate(yhs):
             for tile in range(3):
                 lines[tile, line_rows(yh), :] = got[3 * n + tile]
@@ -604,11 +610,11 @@
         even = []
         for pair in range(0, len(kzs), 2):
             data = [stacked(along_y(lines, 0, kz)) for kz in kzs[pair : pair + 2]]
-            even += lane_parts(folded(dot(fy_ref[...], jnp.concatenate(data, 1))))
+            even += lane_parts(dot(fy_ref[...], jnp.concatenate(data, 1))[:ROWS])
         odd = []
         for kz in kzs:
             data = [stacked(along_y(lines, tile, kz)) for tile in (1, 2)]
-            odd.append(lane_parts(folded(dot(fyr_ref[...], jnp.concatenate(data, 1)))))
+            odd.append(lane_parts(dot(fyr_ref[...], jnp.concatenate(data, 1))[:ROWS]))
         for n, kz in enumerate(kzs):
             kzf = kz.astype(f32)
             plain = even[n]
@@ -630,11 +636,11 @@
         send.wait()
 
 
-def gradient_planes(cutoff_ref, here_ref, there_ref, back_ref, planes, start):
+def gradient_planes(cutoff_ref, here_ref, there_ref, height_ref, back_ref, planes, start):
     cut_x, cut_y, cut_z = cutoff_ref[0], cutoff_ref[1], cutoff_ref[2]
     which = jnp.clip(cut_x - (KEEP - 3), 0, 3)
     keep_y = jnp.where(jnp.abs(ky_rows()) <= cut_y.astype(f32), 1.0, 0.0).astype(f32)
-    iy_ref, iyd_ref = (view(back_ref, n) for n in range(2))
+    iy_ref, iyd_ref = (view(height_ref, n, 128) for n in range(2))
     for d in range(3):
         planes[d, HALF_KZ * LANES :, :] = jnp.zeros((LANES, LANES), f32)
     for first in range(0, HALF_KZ, 4):
@@ -643,36 +649,36 @@
         for kz in kzs:
             keep = keep_y * jnp.where(start + kz <= cut_z, 1.0, 0.0).astype(f32)
             rows.append(jnp.concatenate([here_ref[kz] * keep, there_ref[kz] * keep], 1))
-        high = back_ref[pl.ds(pl.multiple_of((6 + which) * 256, 256), 256), :]
-        low = back_ref[pl.ds(pl.multiple_of((10 + which) * 256, 256), 256), :]
+        high = back_ref[pl.ds(pl.multiple_of((4 + which) * 256, 256), 256), :]
+        low = back_ref[pl.ds(pl.multiple_of((8 + which) * 256, 256), 256), :]
         got = triple(jnp.concatenate(rows, 0), high, low)
         data = [stacked(padded(got[n * ROWS : (n + 1) * ROWS])) for n in range(len(kzs))]
         for n, kz in enumerate(kzs):
-            even = lane_parts(folded(dot(iy_ref[...], data[n])))
+            even = lane_parts(dot(iy_ref[...], data[n]))
             planes[0, kz * LANES : (kz + 1) * LANES, :] = even[1]
             planes[2, kz * LANES : (kz + 1) * LANES, :] = even[0]
         for n in range(0, len(kzs), 2):
             both = jnp.concatenate([one[:, :LANES] for one in data[n : n + 2]], 1)
-            for k, part in enumerate(lane_parts(folded(dot(iyd_ref[...], both)))):
+            for k, part in enumerate(lane_parts(dot(iyd_ref[...], both))):
                 kz = kzs[n + k]
                 planes[1, kz * LANES : (kz + 1) * LANES, :] = part
 
 
-def half_kernel(core_ref, cutoff_ref, here_ref, there_ref, back_ref, planes):
+def half_kernel(core_ref, cutoff_ref, here_ref, there_ref, height_ref, back_ref, planes):
     start = core_ref[0] * HALF_KZ
-    gradient_planes(cutoff_ref, here_ref, there_ref, back_ref, planes, start)
+    gradient_planes(cutoff_ref, here_ref, there_ref, height_ref, back_ref, planes, start)
 
 
 def gradient_kernel(
     core_ref, cutoff_ref, wave_ref, base_ref, state_ref, own_ref, here_ref, there_ref,
-    ahead_ref, back_ref, *refs
+    ahead_ref, height_ref, back_ref, *refs
 ):
     *out_refs, planes, force_ref = refs
     core = core_ref[0]
     start = (1 - core) * HALF_KZ
-    gradient_planes(cutoff_ref, here_ref, there_ref, back_ref, planes, start)
+    gradient_planes(cutoff_ref, here_ref, there_ref, height_ref, back_ref, planes, start)
     fz_ref = ahead_tables(ahead_ref)[0]
-    iz_ref, izd_ref = view(back_ref, 2), view(back_ref, 3)
+    iz_ref, izd_ref = view(back_ref, 0), view(back_ref, 1)
     y = lax.broadcasted_iota(jnp.int32, (HALF, LANES), 0) * 2
     y = y + lax.broadcasted_iota(jnp.int32, (HALF, LANES), 1) // N
     phase = ((wave_ref[0] * y) % N).astype(f32) * (2.0 * np.pi / N)
@@ -709,7 +715,7 @@
                 comb_base.append(b[i] - time_step * drive)
             rows = [comb[1], comb_base[1], comb[2], comb_base[2]]
             rows += [comb[0], comb_base[0], nothing, nothing]
-            got = folded(dot_nt(fz_ref[...], beside(jnp.concatenate(rows, 0))))
+            got = dot_nt(fz_ref[...], beside_thrice(jnp.concatenate(rows, 0)))
             depth = LINE // CHUNKS
             rows = pl.ds(pl.multiple_of(yh * depth, 8), depth)
             for tile, part in enumerate(lane_parts(got)):
@@ -751,8 +757,8 @@
                 )
                 for t in (0, 1)
             ]
-            even = lane_parts(folded(dot(fy_ref[...], data[0])))
-            odd = lane_parts(folded(dot(fyr_ref[...], data[1])))
+            even = lane_parts(dot(fy_ref[...], data[0])[:ROWS])
+            odd = lane_parts(dot(fyr_ref[...], data[1])[:ROWS])
             for n, kz in enumerate(ks):
                 flux = flux_ref[0, kz - first]
                 fields[0].append(odd[n] + flux_ref[1, kz - first])
@@ -800,7 +806,7 @@
     for kz in range(count):
         turned = pltpu.roll(rest, (LANES - kz * 16) % LANES, 1) if kz else rest
         data = jnp.concatenate([near_ref[kz] + far_ref[kz], turned], 1)
-        got = lane_parts(folded(dot(iy_ref[...], stacked(padded(data)))))
+        got = lane_parts(dot(iy_ref[...], stacked(padded(data))))
         for tile in range(2):
             planes[tile, kz * LANES : (kz + 1) * LANES, :] = got[tile]
     if count < CHUNK:
@@ -809,17 +815,18 @@
             planes[tile, count * LANES :, :] = blank
 
 
-def inverse_kernel(near_a, far_a, near_b, far_b, back_ref, planes_a, planes_b):
-    iy_ref = view(back_ref, 0)
+def inverse_kernel(near_a, far_a, near_b, far_b, height_ref, planes_a, planes_b):
+    iy_ref = view(height_ref, 0, 128)
     inverse_y(near_a, far_a, iy_ref, planes_a)
     inverse_y(near_b, far_b, iy_ref, planes_b)
 
 
 def final_kernel(
-    near_ref, far_ref, planes_a, planes_b, state_ref, base_ref, back_ref,
+    near_ref, far_ref, planes_a, planes_b, state_ref, base_ref, height_ref, back_ref,
     base_out, state_out, planes_c,
 ):
-    iy_ref, iz_ref, izr_ref = (view(back_ref, n) for n in (0, 4, 5))
+    iy_ref = view(height_ref, 0, 128)
+    iz_ref, izr_ref = view(back_ref, 2), view(back_ref, 3)
     inverse_y(near_ref, far_ref, iy_ref, planes_c)
 
     def along_chunks(tile, yh):
@@ -928,7 +935,7 @@
         half_kernel,
         half_planes,
         [],
-        [core_at, cutoff, here_own, there_own, t["back"]],
+        [core_at, cutoff, here_own, there_own, t["height"], t["back"]],
         room=12,
         in_smem=2,
     )
@@ -937,7 +944,7 @@
         [sds((2, HALF * 4 * CHUNK, LANES), f32)] * CHUNKS,
         [pltpu.VMEM(half_planes.shape, f32), pltpu.VMEM((HALF, LANES), f32)],
         [core_at, cutoff, wavenumber, own_base, own_state, own_planes, here_other, there_other]
-        + [t["ahead"], t["back"]],
+        + [t["ahead"], t["height"], t["back"]],
         room=20,
         in_smem=3,
     )
@@ -955,13 +962,13 @@
         far.append(lax.ppermute(far_part, "slab", swap))
     planes = sds((2, CHUNK * LANES, LANES), f32)
     planes_a, planes_b = call(
-        inverse_kernel, [planes] * 2, [], [near[0], far[0], near[1], far[1], t["back"]], room=10
+        inverse_kernel, [planes] * 2, [], [near[0], far[0], near[1], far[1], t["height"]], room=10
     )
     base_gap, state_gap = call(
         final_kernel,
         [sds((3, 16, N * N), f32), sds((3, HALF, N * N), f32)],
         [pltpu.VMEM((2, CHUNK * LANES, LANES), f32)],
-        [near[2], far[2], planes_a, planes_b, state_next, base_next, t["back"]],
+        [near[2], far[2], planes_a, planes_b, state_next, base_next, t["height"], t["back"]],
         room=16,
     )
     return base_gap[None], state_gap[None, None]

time: 74.6 us -> 77.2 us (1.035)
  Pallas kernels: 43.8 us -> 46 us
  local copies, waits for them, and re-layouts: 0.1 us -> 1.12 us
  starting transfers between devices: 11.8 us -> 10.8 us
    pallas_call x9, Pallas kernels: 43.8 us -> 46 us  [call(): pl.pallas_call(kernel, out_shape=outs, in_specs=[small] * in_smem + [far]...]
    unnamed x18 -> x20, local copies, waits for them, and re-layouts: 0.05 us -> 1.07 us
    ppermute x3, starting transfers between devices: 3.71 us -> 2.93 us  [body(): far.append(lax.ppermute(far_part, 'slab', swap))]
  transfers between devices with their start and end apart: 8 -> 8, of which waited for: 3 -> 3; matrix products, arithmetic and copies ran while one was open for 0% -> 0% of each run, Pallas kernels for 45% -> 46%
where the time goes in v7:
time: 77.2 us; the launch traced here: 76.9 us
  Pallas kernels  46 us (60%)
  waiting for transfers between devices  17.6 us (23%)
  starting transfers between devices  10.8 us (14%)
  between operations  1.47 us (2%)
  local copies, waits for them, and re-layouts  1.12 us (1%)
    pallas_call x9, Pallas kernels, call(): pl.pallas_call(kernel, out_shape=outs, in_specs=[small] * in_smem + [far]...  46 us
    ppermute x3, waiting for transfers between devices, body(): far.append(lax.ppermute(far_part, 'slab', swap))  17.6 us
    ppermute x1, starting transfers between devices, body(): state_next = lax.ppermute(own_state, ('seg', 'comp'), around)  3.6 us
    ppermute x1, starting transfers between devices, body(): there_own = lax.ppermute(here_own, 'slab', swap)  3 us
    ppermute x3, starting transfers between devices, body(): far.append(lax.ppermute(far_part, 'slab', swap))  2.93 us
  transfers between devices with their start and end apart: 8, of which 3 were waited for; matrix products, arithmetic and copies ran while one was open for 0% of the time, Pallas kernels for 46%

profile of v7, /device:TPU:0, one launch (start us, length us, event | category | flops | bytes accessed | tf_op | source)
XLA Modules:
  0.0 76.9 jit_solution(10023349028684754991)
XLA Ops:
  0.6 4.6 %shard_map.95.here_ref = f32[11,88,128]{2,1,0:T(8,128)} custom-call(s32[1]{0:T(128)} %bitcast.core_ref, f32[3,32,4096]{2,1,0:T(8,128)} %bitcast.7, bf16[288,384]{1,0:T(8,128)(2,1)} %constant.19.clone.ahead_hbm.ahead_ref), custom_call_target="tpu_custom_call" | custom-call | flops 1000 | bytes 1000 | tf_op jit(solution)/shard_map/pallas_call | solution.py:868
  5.2 3.0 %collective-permute-start = (f32[11,88,128]{2,1,0:T(8,128)}, f32[11,88,128]{2,1,0:T(8,128)}, u32[]{:S(2)}, u32[]{:S(2)}) collective-permute-start(f32[11,88,128]{2,1,0:T(8,128)} %shard_map.95.here_ref), channel_id=1, source_target_pairs={{0,2},{2,0},{1,3},{3,1},{4,6},{6,4},{5,7},{7,5},{8,10},{10,8},{9,1... | collective-permute-start | bytes 1486856 | tf_op jit(solution)/shard_map/ppermute | solution.py:910
  8.2 0.0 copy-start
  8.2 3.6 %collective-permute-start.6 = (f32[3,32,4096]{2,1,0:T(8,128)}, f32[3,32,4096]{2,1,0:T(8,128)}, u32[]{:S(2)}, u32[]{:S(2)}) collective-permute-start(f32[3,32,4096]{2,1,0:T(8,128)} %bitcast.2.state_hbm.state_ref), channel_id=1, source_target_pairs={{4,0},{8,4},{12,8},{0,12},{1,5},{5,9},{9,13},{13,1},{6,2},{10,6},{... | collective-permute-start | bytes 4718600 | tf_op jit(solution)/shard_map/ppermute | solution.py:892
  11.8 0.0 collective-permute-start.1
  11.8 0.0 copy-start.4
  11.8 11.6 %shard_map.96 = (f32[2,8,88,128]{3,2,1,0:T(8,128)}, f32[2,8,88,128]{3,2,1,0:T(8,128)}, f32[2,6,88,128]{3,2,1,0:T(8,128)}) custom-call(s32[1]{0:T(128)} %bitcast.core_ref, f32[3,32,4096]{2,1,0:T(8,128)} %bitcast.8, f32[3,32,4096]{2,1,0:T(8,128)} %bitcast.2.state_hbm.state_ref, bf16[288,384]{1,0:T(8,128)(2,1)} %constant.19.clone.ahead_hbm.ahead_ref), custom_call_target="tpu_custom_call" | custom-call | flops 1000 | bytes 1000 | tf_op jit(solution)/shard_map/pallas_call | solution.py:868
  23.4 0.0 copy-start.2
  23.4 0.0 copy-start.9
  23.4 0.0 collective-permute-done.there_ref
  23.4 0.6 collective-permute-start.2
  24.0 0.0 copy-done
  24.0 0.1 dynamic-slice_bitcast_fusion
  24.1 0.7 collective-permute-start.7
  25.4 0.0 copy-done.4
  25.4 0.0 copy-done.2
  25.4 0.0 copy-done.9
  25.4 0.0 copy-start.5
  25.4 1.0 %copy-done.5 = f32[11,88,128]{2,1,0:T(8,128)S(1)} copy-done((f32[11,88,128]{2,1,0:T(8,128)S(1)}, f32[11,88,128]{2,1,0:T(8,128)}, u32[]{:S(2)}) %copy-start.5) | copy-done | bytes 495640
  26.5 0.0 copy-start.3
  26.5 3.2 %shard_map.97.own_ref = f32[3,1536,128]{2,1,0:T(8,128)S(1)} custom-call(s32[1]{0:T(128)} %bitcast.core_ref, s32[3]{0:T(128)S(1)} %copy-done.9, f32[11,88,128]{2,1,0:T(8,128)S(1)} %copy-done.5, f32[11,88,128]{2,1,0:T(8,128)} %collective-permute-done.there_ref, bf16[256,384]{1,0:T(8,128)(2,1)S(1)} %copy-done.4, bf16[3072,256]{1,0:T(8,128)(2,1)S(1)} %copy-done.2), custom_call_target="tpu_custom_call" | custom-call | flops 1000 | bytes 1000 | tf_op jit(solution)/shard_map/pallas_call | solution.py:868
  29.7 0.0 copy-start.1
  29.7 0.0 copy-start.7
  29.7 0.0 collective-permute-done.1.here_ref
  29.7 0.0 collective-permute-done.2.there_ref
  29.7 0.0 copy-done.3
  29.7 11.4 %shard_map.98 = (f32[2,1024,128]{2,1,0:T(8,128)S(1)}, f32[2,1024,128]{2,1,0:T(8,128)S(1)}, f32[2,1024,128]{2,1,0:T(8,128)S(1)}) custom-call(s32[1]{0:T(128)} %bitcast.core_ref, s32[3]{0:T(128)S(1)} %copy-done.9, s32[1]{0:T(128)S(6)} %copy.10.wave_ref, f32[3,32,4096]{2,1,0:T(8,128)S(1)} %bitcast.9, f32[3,32,4096]{2,1,0:T(8,128)} %bitcast.2.state_hbm.state_ref, ...), custom_call_target="tpu_custom_call" | custom-call | flops 1000 | bytes 1000 | tf_op jit(solution)/shard_map/pallas_call | solution.py:868
  41.2 0.0 copy-done.1
  41.2 0.0 copy-done.7
  41.2 0.0 copy-start.6
  41.2 3.1 %shard_map.101 = (f32[9,88,128]{2,1,0:T(8,128)S(1)}, f32[9,88,128]{2,1,0:T(8,128)S(1)}) custom-call(s32[1]{0:T(128)} %bitcast.core_ref, s32[3]{0:T(128)S(1)} %copy-done.9, f32[2,1024,128]{2,1,0:T(8,128)S(1)} %get-tuple-element.34.lines_ref, f32[2,8,88,128]{3,2,1,0:T(8,128)S(1)} %copy-done.7, bf16[288,384]{1,0:T(8,128)(2,1)S(1)} %copy-done.3, ...), custom_call_target="tpu_custom_call" | custom-call | flops 1000 | bytes 1000 | tf_op jit(solution)/shard_map/pallas_call | solution.py:868
  44.3 0.8 %collective-permute-start.5 = (f32[9,88,128]{2,1,0:T(8,128)S(1)}, f32[9,88,128]{2,1,0:T(8,128)S(1)}, u32[]{:S(2)}, u32[]{:S(2)}) collective-permute-start(f32[9,88,128]{2,1,0:T(8,128)S(1)} %get-tuple-element.37), channel_id=1, source_target_pairs={{0,2},{2,0},{1,3},{3,1},{4,6},{6,4},{5,7},{7,5},{8,10},{10,8},{9,1... | collective-permute-start | bytes 1216520 | tf_op jit(solution)/shard_map/ppermute | solution.py:962
  45.1 0.0 copy-done.6
  45.1 0.0 copy-start.8
  45.1 3.1 %shard_map.100 = (f32[9,88,128]{2,1,0:T(8,128)S(1)}, f32[9,88,128]{2,1,0:T(8,128)S(1)}) custom-call(s32[1]{0:T(128)} %bitcast.core_ref, s32[3]{0:T(128)S(1)} %copy-done.9, f32[2,1024,128]{2,1,0:T(8,128)S(1)} %get-tuple-element.30.lines_ref, f32[2,8,88,128]{3,2,1,0:T(8,128)S(1)} %copy-done.6, bf16[288,384]{1,0:T(8,128)(2,1)S(1)} %copy-done.3, ...), custom_call_target="tpu_custom_call" | custom-call | flops 1000 | bytes 1000 | tf_op jit(solution)/shard_map/pallas_call | solution.py:868
  48.2 1.4 %collective-permute-start.4 = (f32[9,88,128]{2,1,0:T(8,128)S(1)}, f32[9,88,128]{2,1,0:T(8,128)S(1)}, u32[]{:S(2)}, u32[]{:S(2)}) collective-permute-start(f32[9,88,128]{2,1,0:T(8,128)S(1)} %get-tuple-element.33), channel_id=1, source_target_pairs={{0,2},{2,0},{1,3},{3,1},{4,6},{6,4},{5,7},{7,5},{8,10},{10,8},{9,1... | collective-permute-start | bytes 1216520 | tf_op jit(solution)/shard_map/ppermute | solution.py:962
  49.6 0.0 copy-done.8
  49.6 2.3 %shard_map.99 = (f32[7,88,128]{2,1,0:T(8,128)S(1)}, f32[7,88,128]{2,1,0:T(8,128)S(1)}) custom-call(s32[1]{0:T(128)} %bitcast.core_ref, s32[3]{0:T(128)S(1)} %copy-done.9, f32[2,1024,128]{2,1,0:T(8,128)S(1)} %get-tuple-element.26.lines_ref, f32[2,6,88,128]{3,2,1,0:T(8,128)S(1)} %copy-done.8, bf16[288,384]{1,0:T(8,128)(2,1)S(1)} %copy-done.3, ...), custom_call_target="tpu_custom_call" | custom-call | flops 1000 | bytes 1000 | tf_op jit(solution)/shard_map/pallas_call | solution.py:868
  51.9 0.8 %collective-permute-start.3 = (f32[7,88,128]{2,1,0:T(8,128)S(1)}, f32[7,88,128]{2,1,0:T(8,128)S(1)}, u32[]{:S(2)}, u32[]{:S(2)}) collective-permute-start(f32[7,88,128]{2,1,0:T(8,128)S(1)} %get-tuple-element.29), channel_id=1, source_target_pairs={{0,2},{2,0},{1,3},{3,1},{4,6},{6,4},{5,7},{7,5},{8,10},{10,8},{9,1... | collective-permute-start | bytes 946184 | tf_op jit(solution)/shard_map/ppermute | solution.py:962
  52.6 4.0 %collective-permute-done.5.far_b = f32[9,88,128]{2,1,0:T(8,128)S(1)} collective-permute-done((f32[9,88,128]{2,1,0:T(8,128)S(1)}, f32[9,88,128]{2,1,0:T(8,128)S(1)}, u32[]{:S(2)}, u32[]{:S(2)}) %collective-permute-start.5) | collective-permute-done | bytes 405536 | tf_op jit(solution)/shard_map/ppermute | solution.py:962
  56.6 8.7 %collective-permute-done.4.far_a = f32[9,88,128]{2,1,0:T(8,128)S(1)} collective-permute-done((f32[9,88,128]{2,1,0:T(8,128)S(1)}, f32[9,88,128]{2,1,0:T(8,128)S(1)}, u32[]{:S(2)}, u32[]{:S(2)}) %collective-permute-start.4) | collective-permute-done | bytes 405536 | tf_op jit(solution)/shard_map/ppermute | solution.py:962
  65.3 0.8 %shard_map.102 = (f32[2,1024,128]{2,1,0:T(8,128)S(1)}, f32[2,1024,128]{2,1,0:T(8,128)S(1)}) custom-call(f32[9,88,128]{2,1,0:T(8,128)S(1)} %get-tuple-element.32.near_a, f32[9,88,128]{2,1,0:T(8,128)S(1)} %collective-permute-done.4.far_a, f32[9,88,128]{2,1,0:T(8,128)S(1)} %get-tuple-element.36.near_b, f32[9,88,128]{2,1,0:T(8,128)S(1)} %collective-permute-done.5.far_b, ...), custom_call_target="tpu_custom_call" | custom-call | flops 1000 | bytes 1000 | tf_op jit(solution)/shard_map/pallas_call | solution.py:868
  66.1 0.0 collective-permute-done.7.base_ref
  66.1 4.9 %collective-permute-done.3.far_ref = f32[7,88,128]{2,1,0:T(8,128)S(1)} collective-permute-done((f32[7,88,128]{2,1,0:T(8,128)S(1)}, f32[7,88,128]{2,1,0:T(8,128)S(1)}, u32[]{:S(2)}, u32[]{:S(2)}) %collective-permute-start.3) | collective-permute-done | bytes 315424 | tf_op jit(solution)/shard_map/ppermute | solution.py:962
  71.0 0.0 collective-permute-done.6.state_ref
  71.0 5.9 %shard_map.103 = (f32[3,16,4096]{2,1,0:T(8,128)}, f32[3,32,4096]{2,1,0:T(8,128)}) custom-call(f32[7,88,128]{2,1,0:T(8,128)S(1)} %get-tuple-element.28.near_ref, f32[7,88,128]{2,1,0:T(8,128)S(1)} %collective-permute-done.3.far_ref, f32[2,1024,128]{2,1,0:T(8,128)S(1)} %get-tuple-element.38.planes_a, f32[2,1024,128]{2,1,0:T(8,128)S(1)} %get-tuple-element.39.planes_b, ...), custom_call_target="tpu_custom_call" | custom-call | flops 1000 | bytes 1000 | tf_op jit(solution)/shard_map/pallas_call | solution.py:868
Async XLA Ops:
  5.2 18.2 %collective-permute-start = (f32[11,88,128]{2,1,0:T(8,128)}, f32[11,88,128]{2,1,0:T(8,128)}, u32[]{:S(2)}, u32[]{:S(2)}) collective-permute-start(f32[11,88,128]{2,1,0:T(8,128)} %shard_map.95.here_ref), channel_id=1, source_target_pairs={{0,2},{2,0},{1,3},{3,1},{4,6},{6,4},{5,7},{7,5},{8,10},{10,8},{9,1... | collective-permute-start | bytes 1486856 | tf_op jit(solution)/shard_map/ppermute | solution.py:910
  8.2 15.8 %copy-start = (f32[1,3,32,4096]{3,2,1,0:T(8,128)S(1)}, f32[1,3,32,4096]{3,2,1,0:T(8,128)}, u32[]{:S(2)}) copy-start(f32[1,3,32,4096]{3,2,1,0:T(8,128)} %param.8) | copy-start | bytes 4718596
  8.2 62.8 %collective-permute-start.6 = (f32[3,32,4096]{2,1,0:T(8,128)}, f32[3,32,4096]{2,1,0:T(8,128)}, u32[]{:S(2)}, u32[]{:S(2)}) collective-permute-start(f32[3,32,4096]{2,1,0:T(8,128)} %bitcast.2.state_hbm.state_ref), channel_id=1, source_target_pairs={{4,0},{8,4},{12,8},{0,12},{1,5},{5,9},{9,13},{13,1},{6,2},{10,6},{... | collective-permute-start | bytes 4718600 | tf_op jit(solution)/shard_map/ppermute | solution.py:892
  11.8 17.9 %collective-permute-start.1 = (f32[11,88,128]{2,1,0:T(8,128)}, f32[11,88,128]{2,1,0:T(8,128)}, u32[]{:S(2)}, u32[]{:S(2)}) collective-permute-start(f32[11,88,128]{2,1,0:T(8,128)} %shard_map.95.here_ref), channel_id=1, source_target_pairs={{0,1},{1,0},{2,3},{3,2},{4,5},{5,4},{6,7},{7,6},{8,9},{9,8},{10,11... | collective-permute-start | bytes 1486856 | tf_op jit(solution)/shard_map/ppermute | solution.py:911
  11.8 13.6 %copy-start.4 = (bf16[256,384]{1,0:T(8,128)(2,1)S(1)}, bf16[256,384]{1,0:T(8,128)(2,1)}, u32[]{:S(2)}) copy-start(bf16[256,384]{1,0:T(8,128)(2,1)} %constant.20.clone.height_ref) | copy-start | bytes 589828
  23.4 2.0 %copy-start.2 = (bf16[3072,256]{1,0:T(8,128)(2,1)S(1)}, bf16[3072,256]{1,0:T(8,128)(2,1)}, u32[]{:S(2)}) copy-start(bf16[3072,256]{1,0:T(8,128)(2,1)} %constant.21.clone.back_ref) | copy-start | bytes 4718596
  23.4 2.0 %copy-start.9 = (s32[3]{0:T(128)S(1)}, s32[3]{0:T(128)}, u32[]{:S(2)}) copy-start(s32[3]{0:T(128)} %cutoff_ref.9) | copy-start | bytes 40
  23.4 6.3 %collective-permute-start.2 = (f32[11,88,128]{2,1,0:T(8,128)}, f32[11,88,128]{2,1,0:T(8,128)S(1)}, u32[]{:S(2)}, u32[]{:S(2)}) collective-permute-start(f32[11,88,128]{2,1,0:T(8,128)} %collective-permute-done.there_ref), channel_id=1, source_target_pairs={{0,1},{1,0},{2,3},{3,2},{4,5},{5,4},{6,7},{7,6},{8,9},{9,8},{10,11... | collective-permute-start | bytes 1486856 | tf_op jit(solution)/shard_map/ppermute | solution.py:932
  24.1 42.0 %collective-permute-start.7 = (f32[3,16,4096]{2,1,0:T(8,128)S(1)}, f32[3,16,4096]{2,1,0:T(8,128)S(1)}, u32[]{:S(2)}, u32[]{:S(2)}) collective-permute-start(f32[3,16,4096]{2,1,0:T(8,128)S(1)} %dynamic-slice_bitcast_fusion), channel_id=1, source_target_pairs={{4,0},{8,4},{12,8},{0,12},{5,1},{9,5},{13,9},{1,13},{6,2},{10,6},{... | collective-permute-start | bytes 2359304 | tf_op jit(solution)/shard_map/ppermute | solution.py:891
  25.4 1.0 %copy-start.5 = (f32[11,88,128]{2,1,0:T(8,128)S(1)}, f32[11,88,128]{2,1,0:T(8,128)}, u32[]{:S(2)}) copy-start(f32[11,88,128]{2,1,0:T(8,128)} %shard_map.95.here_ref) | copy-start | bytes 1486852
  26.5 3.3 %copy-start.3 = (bf16[288,384]{1,0:T(8,128)(2,1)S(1)}, bf16[288,384]{1,0:T(8,128)(2,1)}, u32[]{:S(2)}) copy-start(bf16[288,384]{1,0:T(8,128)(2,1)} %constant.19.clone.ahead_hbm.ahead_ref) | copy-start | bytes 663556
  29.7 11.5 %copy-start.1 = (bf16[3072,256]{1,0:T(8,128)(2,1)S(1)}, bf16[3072,256]{1,0:T(8,128)(2,1)}, u32[]{:S(2)}) copy-start(bf16[3072,256]{1,0:T(8,128)(2,1)} %constant.22.clone.along_ref) | copy-start | bytes 4718596
  29.7 11.5 %copy-start.7 = (f32[2,8,88,128]{3,2,1,0:T(8,128)S(1)}, f32[2,8,88,128]{3,2,1,0:T(8,128)}, u32[]{:S(2)}) copy-start(f32[2,8,88,128]{3,2,1,0:T(8,128)} %get-tuple-element.35.flux_ref) | copy-start | bytes 2162692
  41.2 3.9 %copy-start.6 = (f32[2,8,88,128]{3,2,1,0:T(8,128)S(1)}, f32[2,8,88,128]{3,2,1,0:T(8,128)}, u32[]{:S(2)}) copy-start(f32[2,8,88,128]{3,2,1,0:T(8,128)} %get-tuple-element.31.flux_ref) | copy-start | bytes 2162692
  44.3 12.3 %collective-permute-start.5 = (f32[9,88,128]{2,1,0:T(8,128)S(1)}, f32[9,88,128]{2,1,0:T(8,128)S(1)}, u32[]{:S(2)}, u32[]{:S(2)}) collective-permute-start(f32[9,88,128]{2,1,0:T(8,128)S(1)} %get-tuple-element.37), channel_id=1, source_target_pairs={{0,2},{2,0},{1,3},{3,1},{4,6},{6,4},{5,7},{7,5},{8,10},{10,8},{9,1... | collective-permute-start | bytes 1216520 | tf_op jit(solution)/shard_map/ppermute | solution.py:962
  45.1 4.5 %copy-start.8 = (f32[2,6,88,128]{3,2,1,0:T(8,128)S(1)}, f32[2,6,88,128]{3,2,1,0:T(8,128)}, u32[]{:S(2)}) copy-start(f32[2,6,88,128]{3,2,1,0:T(8,128)} %get-tuple-element.27.flux_ref) | copy-start | bytes 1622020
  48.2 17.1 %collective-permute-start.4 = (f32[9,88,128]{2,1,0:T(8,128)S(1)}, f32[9,88,128]{2,1,0:T(8,128)S(1)}, u32[]{:S(2)}, u32[]{:S(2)}) collective-permute-start(f32[9,88,128]{2,1,0:T(8,128)S(1)} %get-tuple-element.33), channel_id=1, source_target_pairs={{0,2},{2,0},{1,3},{3,1},{4,6},{6,4},{5,7},{7,5},{8,10},{10,8},{9,1... | collective-permute-start | bytes 1216520 | tf_op jit(solution)/shard_map/ppermute | solution.py:962
  51.9 19.1 %collective-permute-start.3 = (f32[7,88,128]{2,1,0:T(8,128)S(1)}, f32[7,88,128]{2,1,0:T(8,128)S(1)}, u32[]{:S(2)}, u32[]{:S(2)}) collective-permute-start(f32[7,88,128]{2,1,0:T(8,128)S(1)} %get-tuple-element.29), channel_id=1, source_target_pairs={{0,2},{2,0},{1,3},{3,1},{4,6},{6,4},{5,7},{7,5},{8,10},{10,8},{9,1... | collective-permute-start | bytes 946184 | tf_op jit(solution)/shard_map/ppermute | solution.py:962

commit v8 on v6

--- a/solution.py
+++ b/solution.py
@@ -276,6 +276,10 @@
     return np.ascontiguousarray(left_table(table.T, depth).T)
 
 
+def planes_of(chunk):
+    return chunk * CHUNK, min((chunk + 1) * CHUNK, NKZ)
+
+
 def ky_values():
     index = np.arange(NKY)
     wave = np.where(index <= KEEP, index, index - (2 * KEEP + 1))
@@ -305,8 +309,16 @@
         slope[:, y2, 1, y2] = -weight * kz[:, None] * np.cos(angle)
     forward = np.moveaxis(forward.reshape(4, CHUNKS, CHUNK, 2 * N), 1, 0)
     out["fz"] = left_table(forward.reshape(LINE, 2 * N), 128)
-    out["iz"] = right_table(inverse.reshape(4 * NKZ, 2 * N), 128)
-    out["izr"] = right_table(turned.reshape(4 * NKZ, 2 * N), 128)
+
+    def by_chunk(table):
+        wide = np.zeros((CHUNKS, CHUNK, 4, 2 * N))
+        for chunk in range(CHUNKS):
+            first, last = planes_of(chunk)
+            wide[chunk, : last - first] = table.reshape(NKZ, 4, 2 * N)[first:last]
+        return right_table(wide.reshape(LINE, 2 * N), 128)
+
+    out["iz"] = by_chunk(inverse)
+    out["izr"] = by_chunk(turned)
 
     def by_half(table):
         wide = np.zeros((2, HALF_KZ + 1, 4, 2 * N))
@@ -507,10 +519,6 @@
         step([jnp.int32(kz) for kz in range(first + count * 4, last)])
 
 
-def planes_of(chunk):
-    return chunk * CHUNK, min((chunk + 1) * CHUNK, NKZ)
-
-
 def over_lines(step, many, first=0, last=HALF):
     def some(index, _):
         step([first + index * many + k for k in range(many)])
@@ -560,8 +568,36 @@
             out_ref[k] = part
 
 
-def flux_kernel(core_ref, base_hbm, state_hbm, ahead_hbm, *refs):
-    *out_refs, lines, base_ref, state_ref, ahead_ref, result, arrived, left = refs
+def flux_modes(lines_ref, fy_ref, fyr_ref, kzs):
+    ky = ky_rows()
+    lane = lax.broadcasted_iota(jnp.int32, (ROWS, LANES), 1)
+    odd_block = (lane // HALF) % 2 == 1
+    depth = LINE // CHUNKS
+    even = []
+    for pair in range(0, len(kzs), 2):
+        data = [stacked(along_y(lines_ref, 0, kz, depth)) for kz in kzs[pair : pair + 2]]
+        even += lane_parts(folded(dot(fy_ref[...], jnp.concatenate(data, 1))))
+    odd = []
+    for kz in kzs:
+        data = [stacked(along_y(lines_ref, tile, kz, depth)) for tile in (1, 2)]
+        odd.append(lane_parts(folded(dot(fyr_ref[...], jnp.concatenate(data, 1)))))
+    first, second = [], []
+    for n, kz in enumerate(kzs):
+        kzf = kz.astype(f32)
+        plain = even[n]
+        slopes = odd[n][0] * jnp.where(odd_block, kzf, ky)
+        slopes = slopes + pltpu.roll(slopes, 32, 1)
+        first.append(jnp.where(odd_block, slopes, plain))
+        other = plain * jnp.where(lane >= 96, -kzf, -ky)
+        other = other + pltpu.roll(other, 64, 1)
+        second.append(jnp.where(lane >= 96, other, jnp.where(lane >= 64, odd[n][1], 0.0)))
+    return first, second
+
+
+def flux_kernel(
+    core_ref, base_hbm, state_hbm, ahead_hbm, out_ref, out_b, out_c,
+    lines_a, lines_b, lines_c, base_ref, state_ref, ahead_ref, result, arrived, left,
+):
     wide = N * N // PIECES
     pieces = [pltpu.make_async_copy(ahead_hbm, ahead_ref, arrived.at[2 * PIECES])]
     for n in range(PIECES):
@@ -576,56 +612,45 @@
         piece.start()
     fz_ref, fy_ref, fyr_ref = ahead_tables(ahead_ref)
     sigma = jnp.where(core_ref[0] == 0, -time_step, time_step).astype(f32)
-    nothing = jnp.zeros((HALF, LANES), f32)
+    depth = LINE // CHUNKS
 
     def z_step(yhs):
-        rows = []
+        rows, lone = [], []
         for yh in yhs:
             b = [base_ref[i, :, columns(yh)] for i in range(3)]
             t = [sigma * state_ref[i, :, columns(yh)] for i in range(3)]
             rows += [t[2] * b[0], t[0] * b[1], t[1] * b[0], t[0] * b[2]]
             rows += [t[2] * b[1], t[2] * b[2], t[1] * b[1], t[1] * b[2]]
-            rows += [nothing, nothing, t[0] * b[0], nothing]
-        got = lane_parts(folded(dot_nt(fz_ref[...], beside(jnp.concatenate(rows, 0)))))
+            lone.append(t[0] * b[0])
+        got = lane_parts(folded(dot_nt(fz_ref[...], beside(jnp.concatenate(rows + lone, 0)))))
         for n, yh in enumerate(yhs):
-            for tile in range(3):
-                lines[tile, line_rows(yh), :] = got[3 * n + tile]
+            third = got[-1] if n == 2 else pltpu.roll(got[-1], (2 - n) % 4 * HALF, 1)
+            at = pl.ds(pl.multiple_of(yh * depth, 8), depth)
+            for tile, part in enumerate((got[2 * n], got[2 * n + 1], third)):
+                for chunk, lines in enumerate((lines_a, lines_b, lines_c)):
+                    lines[tile, at, :] = part[chunk * depth : (chunk + 1) * depth]
 
     pieces[0].wait()
     for n in range(PIECES):
         pieces[2 * n + 1].wait()
         pieces[2 * n + 2].wait()
         over_lines(z_step, 4, n * HALF // PIECES, (n + 1) * HALF // PIECES)
-    ky = ky_rows()
-    lane = lax.broadcasted_iota(jnp.int32, (ROWS, LANES), 1)
-    odd_block = (lane // HALF) % 2 == 1
+    sends = [
+        pltpu.make_async_copy(lines_b, out_b, left.at[1]),
+        pltpu.make_async_copy(lines_c, out_c, left.at[2]),
+        pltpu.make_async_copy(result, out_ref, left.at[0]),
+    ]
+    sends[0].start()
+    sends[1].start()
 
     def y_step(kzs):
-        even = []
-        for pair in range(0, len(kzs), 2):
-            data = [stacked(along_y(lines, 0, kz)) for kz in kzs[pair : pair + 2]]
-            even += lane_parts(folded(dot(fy_ref[...], jnp.concatenate(data, 1))))
-        odd = []
-        for kz in kzs:
-            data = [stacked(along_y(lines, tile, kz)) for tile in (1, 2)]
-            odd.append(lane_parts(folded(dot(fyr_ref[...], jnp.concatenate(data, 1)))))
+        first, second = flux_modes(lines_a, fy_ref, fyr_ref, kzs)
         for n, kz in enumerate(kzs):
-            kzf = kz.astype(f32)
-            plain = even[n]
-            slopes = odd[n][0] * jnp.where(odd_block, kzf, ky)
-            slopes = slopes + pltpu.roll(slopes, 32, 1)
-            result[0, kz] = jnp.where(odd_block, slopes, plain)
-            other = plain * jnp.where(lane >= 96, -kzf, -ky)
-            other = other + pltpu.roll(other, 64, 1)
-            result[1, kz] = jnp.where(lane >= 96, other, odd[n][1])
-
-    sends = []
-    for chunk in range(CHUNKS):
-        first, last = planes_of(chunk)
-        over_planes(y_step, first, last)
-        source = result.at[:, pl.ds(first, last - first)]
-        sends.append(pltpu.make_async_copy(source, out_refs[chunk], left.at[chunk]))
-        sends[-1].start()
+            result[0, kz] = first[n]
+            result[1, kz] = second[n]
+
+    over_planes(y_step, *planes_of(0))
+    sends[2].start()
     for send in sends:
         send.wait()
 
@@ -743,6 +768,11 @@
 
     def spectral_step(kzs):
         fields = [[], [], []]
+        if chunk == 0:
+            first_flux = [flux_ref[0, kz] for kz in kzs]
+            second_flux = [flux_ref[1, kz] for kz in kzs]
+        else:
+            first_flux, second_flux = flux_modes(flux_ref, fy_ref, fyr_ref, kzs)
         for pair in range(0, len(kzs), 2):
             ks = kzs[pair : pair + 2]
             data = [
@@ -754,8 +784,8 @@
             even = lane_parts(folded(dot(fy_ref[...], data[0])))
             odd = lane_parts(folded(dot(fyr_ref[...], data[1])))
             for n, kz in enumerate(ks):
-                flux = flux_ref[0, kz - first]
-                fields[0].append(odd[n] + flux_ref[1, kz - first])
+                flux = first_flux[pair + n]
+                fields[0].append(odd[n] + second_flux[pair + n])
                 fields[1].append(jnp.where(lane < 64, even[n], flux))
                 fields[2].append(jnp.where(lane < 64, flux, even[n]))
         data = [beside(jnp.concatenate(field, 0)) for field in fields]
@@ -809,16 +839,33 @@
             planes[tile, count * LANES :, :] = blank
 
 
-def inverse_kernel(near_a, far_a, near_b, far_b, back_ref, planes_a, planes_b):
-    iy_ref = view(back_ref, 0)
-    inverse_y(near_a, far_a, iy_ref, planes_a)
-    inverse_y(near_b, far_b, iy_ref, planes_b)
+def inverse_kernel(near_ref, far_ref, back_ref, planes):
+    inverse_y(near_ref, far_ref, view(back_ref, 0), planes)
 
 
 def final_kernel(
-    near_ref, far_ref, planes_a, planes_b, state_ref, base_ref, back_ref,
-    base_out, state_out, planes_c,
+    near_ref, far_ref, planes_a, planes_b, state_hbm, base_hbm, back_ref, base_out, state_out,
+    planes_c, state_ref, base_ref, state_gap, base_gap, arrived, left,
 ):
+    wide = N * N // PIECES
+    cuts = [pl.ds(n * wide, wide) for n in range(PIECES)]
+
+    def copies(pairs, flags):
+        return [
+            [
+                pltpu.make_async_copy(
+                    source.at[:, :, cut], target.at[:, :, cut], flags.at[2 * n + k]
+                )
+                for k, (source, target) in enumerate(pairs)
+            ]
+            for n, cut in enumerate(cuts)
+        ]
+
+    reads = copies(((state_hbm, state_ref), (base_hbm, base_ref)), arrived)
+    writes = copies(((state_gap, state_out), (base_gap, base_out)), left)
+    for piece in reads:
+        for copy in piece:
+            copy.start()
     iy_ref, iz_ref, izr_ref = (view(back_ref, n) for n in (0, 4, 5))
     inverse_y(near_ref, far_ref, iy_ref, planes_c)
 
@@ -829,41 +876,48 @@
         ]
         return padded(jnp.concatenate(parts, 0)).T
 
-    def z_step(yhs):
+    many = HALF // PIECES
+    for piece in range(PIECES):
+        yhs = range(piece * many, (piece + 1) * many)
         data = [along_chunks(0, yh) for yh in yhs]
         rest = [along_chunks(1, yh)[:16] for yh in yhs]
         turned = beside(jnp.concatenate([one[:48] for one in data], 0))
         plain = beside(jnp.concatenate([one[48:] for one in data] + rest, 0))
         turned = folded_lanes(dot(turned, izr_ref[...]))
         plain = folded_lanes(dot(plain, iz_ref[...]))
+        for copy in reads[piece]:
+            copy.wait()
         for n, yh in enumerate(yhs):
-            at = columns(yh)
+            at = slice(yh * LANES, (yh + 1) * LANES)
             first = turned[48 * n : 48 * n + 48]
             second = plain[80 * n : 80 * n + 80]
-            third = plain[80 * len(yhs) + 16 * n :][:16]
-            state_out[0, :, at] = first[:32] - state_ref[0, :, at]
-            state_out[1, :, at] = second[16:48] - state_ref[1, :, at]
-            state_out[2, :, at] = second[48:80] - state_ref[2, :, at]
-            base_out[0, :, at] = first[32:48] - base_ref[0, :, at]
-            base_out[1, :, at] = second[:16] - base_ref[1, :, at]
-            base_out[2, :, at] = third - base_ref[2, :, at]
-
-    over_lines(z_step, 8)
+            third = plain[80 * many + 16 * n :][:16]
+            state_gap[0, :, at] = first[:32] - state_ref[0, :, at]
+            state_gap[1, :, at] = second[16:48] - state_ref[1, :, at]
+            state_gap[2, :, at] = second[48:80] - state_ref[2, :, at]
+            base_gap[0, :, at] = first[32:48] - base_ref[0, :, at]
+            base_gap[1, :, at] = second[:16] - base_ref[1, :, at]
+            base_gap[2, :, at] = third - base_ref[2, :, at]
+        for copy in writes[piece]:
+            copy.start()
+    for piece in writes:
+        for copy in piece:
+            copy.wait()
 
 
 interpret = False
 
 
-def call(kernel, outs, scratch, inputs, room, in_smem=0, in_hbm=0, out_hbm=False):
+def call(kernel, outs, scratch, inputs, room, in_smem=0, in_hbm=(), out_hbm=False):
     whole = pl.BlockSpec(memory_space=pltpu.VMEM)
     small = pl.BlockSpec(memory_space=pltpu.SMEM)
     far = pl.BlockSpec(memory_space=pltpu.HBM)
     return pl.pallas_call(
         kernel,
         out_shape=outs,
-        in_specs=[small] * in_smem
-        + [far] * in_hbm
-        + [whole] * (len(inputs) - in_smem - in_hbm),
+        in_specs=[
+            small if n < in_smem else far if n in in_hbm else whole for n in range(len(inputs))
+        ],
         out_specs=jax.tree.map(lambda _: far if out_hbm else whole, outs),
         scratch_shapes=scratch,
         compiler_params=pltpu.CompilerParams(vmem_limit_bytes=room * 2**20),
@@ -898,27 +952,30 @@
         [core_at, own_base, t["ahead"]],
         room=56,
         in_smem=1,
-        in_hbm=2,
+        in_hbm=(1, 2),
     )
     there_own = lax.ppermute(here_own, "slab", swap)
     here_other = lax.ppermute(here_own, "comp", swap)
     counts = [planes_of(chunk)[1] - planes_of(chunk)[0] for chunk in range(CHUNKS)]
+    flux_lines = sds((3, HALF * 4 * CHUNK, LANES), f32)
     flux = call(
         flux_kernel,
-        [sds((2, count, ROWS, LANES), f32) for count in counts],
+        [sds((2, counts[0], ROWS, LANES), f32)] + [flux_lines] * 2,
         [
-            pltpu.VMEM((3, HALF * LINE, LANES), f32),
+            pltpu.VMEM(flux_lines.shape, f32),
+            pltpu.VMEM(flux_lines.shape, f32),
+            pltpu.VMEM(flux_lines.shape, f32),
             pltpu.VMEM(own_base.shape, f32),
             pltpu.VMEM(own_state.shape, f32),
             pltpu.VMEM(t["ahead"].shape, bf16),
-            pltpu.VMEM((2, NKZ, ROWS, LANES), f32),
+            pltpu.VMEM((2, counts[0], ROWS, LANES), f32),
             pltpu.SemaphoreType.DMA((2 * PIECES + 1,)),
             pltpu.SemaphoreType.DMA((CHUNKS,)),
         ],
         [core_at, own_base, own_state, t["ahead"]],
         room=56,
         in_smem=1,
-        in_hbm=3,
+        in_hbm=(1, 2, 3),
         out_hbm=True,
     )
     there_own, flux = lax.optimization_barrier((there_own, flux))
@@ -942,27 +999,40 @@
         in_smem=3,
     )
     near, far = [], []
+    lines = list(lines)
     for chunk in range(CHUNKS):
+        if chunk:
+            near[-1], lines[chunk] = lax.optimization_barrier((near[-1], lines[chunk]))
         near_part, far_part = call(
             functools.partial(spectral_kernel, chunk),
             [sds((counts[chunk] + 1, ROWS, LANES), f32)] * 2,
             [],
             [core_at, cutoff, lines[chunk], flux[chunk], t["ahead"], t["along"]],
-            room=10,
+            room=12,
             in_smem=2,
         )
         near.append(near_part)
         far.append(lax.ppermute(far_part, "slab", swap))
     planes = sds((2, CHUNK * LANES, LANES), f32)
-    planes_a, planes_b = call(
-        inverse_kernel, [planes] * 2, [], [near[0], far[0], near[1], far[1], t["back"]], room=10
-    )
+    planes_a = call(inverse_kernel, planes, [], [near[0], far[0], t["back"]], room=8)
+    near[1], planes_a = lax.optimization_barrier((near[1], planes_a))
+    planes_b = call(inverse_kernel, planes, [], [near[1], far[1], t["back"]], room=8)
     base_gap, state_gap = call(
         final_kernel,
-        [sds((3, 16, N * N), f32), sds((3, HALF, N * N), f32)],
-        [pltpu.VMEM((2, CHUNK * LANES, LANES), f32)],
+        [sds(base_next.shape, f32), sds(state_next.shape, f32)],
+        [
+            pltpu.VMEM((2, CHUNK * LANES, LANES), f32),
+            pltpu.VMEM(state_next.shape, f32),
+            pltpu.VMEM(base_next.shape, f32),
+            pltpu.VMEM(state_next.shape, f32),
+            pltpu.VMEM(base_next.shape, f32),
+            pltpu.SemaphoreType.DMA((2 * PIECES,)),
+            pltpu.SemaphoreType.DMA((2 * PIECES,)),
+        ],
         [near[2], far[2], planes_a, planes_b, state_next, base_next, t["back"]],
         room=16,
+        in_hbm=(4, 5),
+        out_hbm=True,
     )
     return base_gap[None], state_gap[None, None]
 

time: 74.6 us -> 73.2 us (0.981)
  waiting for transfers between devices: 17.3 us -> 14.7 us
  starting transfers between devices: 11.8 us -> 14.2 us
  Pallas kernels: 43.8 us -> 42.4 us
    ppermute x3, waiting for transfers between devices: 17.3 us -> 14.6 us  [body(): far.append(lax.ppermute(far_part, 'slab', swap))]
    ppermute x1, starting transfers between devices: 0.89 us -> 3.41 us  [body(): base_next = lax.ppermute(base_half, 'seg', back)]
    pallas_call x9 -> x10, Pallas kernels: 43.8 us -> 42.4 us  [call(): pl.pallas_call(kernel, out_shape=outs, in_specs=[small if n < in_smem els...]
  transfers between devices with their start and end apart: 8 -> 8, of which waited for: 3 -> 4; matrix products, arithmetic and copies ran while one was open for 0% -> 0% of each run, Pallas kernels for 45% -> 46%
where the time goes in v8:
time: 73.2 us; the launch traced here: 73.1 us
  Pallas kernels  42.4 us (58%)
  waiting for transfers between devices  14.7 us (20%)
  starting transfers between devices  14.2 us (19%)
  between operations  1.63 us (2%)
    pallas_call x10, Pallas kernels, call(): pl.pallas_call(kernel, out_shape=outs, in_specs=[small if n < in_smem els...  42.4 us
    ppermute x3, waiting for transfers between devices, body(): far.append(lax.ppermute(far_part, 'slab', swap))  14.6 us
    ppermute x3, starting transfers between devices, body(): far.append(lax.ppermute(far_part, 'slab', swap))  3.72 us
    ppermute x1, starting transfers between devices, body(): state_next = lax.ppermute(own_state, ('seg', 'comp'), around)  3.6 us
    ppermute x1, starting transfers between devices, body(): base_next = lax.ppermute(base_half, 'seg', back)  3.41 us
    ppermute x1, starting transfers between devices, body(): there_own = lax.ppermute(here_own, 'slab', swap)  3 us
  transfers between devices with their start and end apart: 8, of which 4 were waited for; matrix products, arithmetic and copies ran while one was open for 0% of the time, Pallas kernels for 46%

profile of v8, /device:TPU:0, one launch (start us, length us, event | category | flops | bytes accessed | tf_op | source)
XLA Modules:
  0.0 73.1 jit_solution(5379539281939635747)
XLA Ops:
  0.6 4.1 %shard_map.86.here_ref = f32[11,88,128]{2,1,0:T(8,128)} custom-call(s32[1]{0:T(128)} %bitcast.core_ref, f32[3,32,4096]{2,1,0:T(8,128)} %bitcast.7, bf16[544,256]{1,0:T(8,128)(2,1)} %constant.17.clone.ahead_hbm.ahead_ref), custom_call_target="tpu_custom_call" | custom-call | flops 1000 | bytes 1000 | tf_op jit(solution)/shard_map/pallas_call | solution.py:915
  4.8 3.0 %collective-permute-start = (f32[11,88,128]{2,1,0:T(8,128)}, f32[11,88,128]{2,1,0:T(8,128)}, u32[]{:S(2)}, u32[]{:S(2)}) collective-permute-start(f32[11,88,128]{2,1,0:T(8,128)} %shard_map.86.here_ref), channel_id=1, source_target_pairs={{0,2},{2,0},{1,3},{3,1},{4,6},{6,4},{5,7},{7,5},{8,10},{10,8},{9,1... | collective-permute-start | bytes 1486856 | tf_op jit(solution)/shard_map/ppermute | solution.py:957
  7.8 0.0 copy-start.1
  7.8 3.6 %collective-permute-start.6 = (f32[3,32,4096]{2,1,0:T(8,128)}, f32[3,32,4096]{2,1,0:T(8,128)}, u32[]{:S(2)}, u32[]{:S(2)}) collective-permute-start(f32[3,32,4096]{2,1,0:T(8,128)} %bitcast.2.state_hbm.state_ref), channel_id=1, source_target_pairs={{4,0},{8,4},{12,8},{0,12},{1,5},{5,9},{9,13},{13,1},{6,2},{10,6},{... | collective-permute-start | bytes 4718600 | tf_op jit(solution)/shard_map/ppermute | solution.py:939
  11.4 0.0 collective-permute-start.1
  11.4 0.0 copy-start
  11.4 7.9 %shard_map.87 = (f32[2,8,88,128]{3,2,1,0:T(8,128)}, f32[3,1024,128]{2,1,0:T(8,128)}, f32[3,1024,128]{2,1,0:T(8,128)}) custom-call(s32[1]{0:T(128)} %bitcast.core_ref, f32[3,32,4096]{2,1,0:T(8,128)} %bitcast.8, f32[3,32,4096]{2,1,0:T(8,128)} %bitcast.2.state_hbm.state_ref, bf16[544,256]{1,0:T(8,128)(2,1)} %constant.17.clone.ahead_hbm.ahead_ref), custom_call_target="tpu_custom_call" | custom-call | flops 1000 | bytes 1000 | tf_op jit(solution)/shard_map/pallas_call | solution.py:915
  19.3 0.0 copy-start.8
  19.3 0.0 copy-start.4
  19.3 0.1 collective-permute-done.there_ref
  19.4 0.5 collective-permute-start.2
  19.9 0.0 copy-done.1
  19.9 0.1 dynamic-slice_bitcast_fusion
  19.9 3.4 %collective-permute-start.7 = (f32[3,16,4096]{2,1,0:T(8,128)S(1)}, f32[3,16,4096]{2,1,0:T(8,128)S(1)}, u32[]{:S(2)}, u32[]{:S(2)}) collective-permute-start(f32[3,16,4096]{2,1,0:T(8,128)S(1)} %dynamic-slice_bitcast_fusion), channel_id=1, source_target_pairs={{4,0},{8,4},{12,8},{0,12},{5,1},{9,5},{13,9},{1,13},{6,2},{10,6},{... | collective-permute-start | bytes 2359304 | tf_op jit(solution)/shard_map/ppermute | solution.py:938
  24.0 0.0 copy-done
  24.0 0.0 copy-done.8
  24.0 0.0 copy-done.4
  24.0 0.0 copy-start.3
  24.1 3.2 %shard_map.88.own_ref = f32[3,1536,128]{2,1,0:T(8,128)S(1)} custom-call(s32[1]{0:T(128)} %bitcast.core_ref, s32[3]{0:T(128)S(1)} %copy-done.8, f32[11,88,128]{2,1,0:T(8,128)S(1)} %copy-done.4, f32[11,88,128]{2,1,0:T(8,128)} %collective-permute-done.there_ref, bf16[3584,256]{1,0:T(8,128)(2,1)S(1)} %copy-done), custom_call_target="tpu_custom_call" | custom-call | flops 1000 | bytes 1000 | tf_op jit(solution)/shard_map/pallas_call | solution.py:915
  27.3 0.0 copy-start.2
  27.3 0.0 copy-start.7
  27.3 0.0 collective-permute-done.1.here_ref
  27.3 0.0 collective-permute-done.2.there_ref
  27.3 0.0 copy-done.3
  27.3 11.0 %shard_map.89 = (f32[2,1024,128]{2,1,0:T(8,128)S(1)}, f32[2,1024,128]{2,1,0:T(8,128)S(1)}, f32[2,1024,128]{2,1,0:T(8,128)S(1)}) custom-call(s32[1]{0:T(128)} %bitcast.core_ref, s32[3]{0:T(128)S(1)} %copy-done.8, s32[1]{0:T(128)S(6)} %copy.9.wave_ref, f32[3,32,4096]{2,1,0:T(8,128)S(1)} %bitcast.9, f32[3,32,4096]{2,1,0:T(8,128)} %bitcast.2.state_hbm.state_ref, ...), custom_call_target="tpu_custom_call" | custom-call | flops 1000 | bytes 1000 | tf_op jit(solution)/shard_map/pallas_call | solution.py:915
  38.3 0.0 copy-done.2
  38.3 0.0 copy-done.7
  38.3 0.0 copy-start.6
  38.4 3.1 %shard_map.90 = (f32[9,88,128]{2,1,0:T(8,128)S(1)}, f32[9,88,128]{2,1,0:T(8,128)S(1)}) custom-call(s32[1]{0:T(128)} %bitcast.core_ref, s32[3]{0:T(128)S(1)} %copy-done.8, f32[2,1024,128]{2,1,0:T(8,128)S(1)} %get-tuple-element.30.lines_ref, f32[2,8,88,128]{3,2,1,0:T(8,128)S(1)} %copy-done.7, bf16[544,256]{1,0:T(8,128)(2,1)S(1)} %copy-done.3, ...), custom_call_target="tpu_custom_call" | custom-call | flops 1000 | bytes 1000 | tf_op jit(solution)/shard_map/pallas_call | solution.py:915
  41.4 1.6 %collective-permute-start.4 = (f32[9,88,128]{2,1,0:T(8,128)S(1)}, f32[9,88,128]{2,1,0:T(8,128)S(1)}, u32[]{:S(2)}, u32[]{:S(2)}) collective-permute-start(f32[9,88,128]{2,1,0:T(8,128)S(1)} %get-tuple-element.44), channel_id=1, source_target_pairs={{0,2},{2,0},{1,3},{3,1},{4,6},{6,4},{5,7},{7,5},{8,10},{10,8},{9,1... | collective-permute-start | bytes 1216520 | tf_op jit(solution)/shard_map/ppermute | solution.py:1015
  43.0 0.0 copy-done.6
  43.0 0.0 copy-start.5
  43.0 4.5 %shard_map.91 = (f32[9,88,128]{2,1,0:T(8,128)S(1)}, f32[9,88,128]{2,1,0:T(8,128)S(1)}) custom-call(s32[1]{0:T(128)} %bitcast.core_ref, s32[3]{0:T(128)S(1)} %copy-done.8, f32[2,1024,128]{2,1,0:T(8,128)S(1)} %get-tuple-element.34.lines_ref, f32[3,1024,128]{2,1,0:T(8,128)S(1)} %copy-done.6, bf16[544,256]{1,0:T(8,128)(2,1)S(1)} %copy-done.3, ...), custom_call_target="tpu_custom_call" | custom-call | flops 1000 | bytes 1000 | tf_op jit(solution)/shard_map/pallas_call | solution.py:915
  47.5 0.6 collective-permute-start.5
  48.1 0.0 copy-done.5
  48.1 3.1 %shard_map.92 = (f32[7,88,128]{2,1,0:T(8,128)S(1)}, f32[7,88,128]{2,1,0:T(8,128)S(1)}) custom-call(s32[1]{0:T(128)} %bitcast.core_ref, s32[3]{0:T(128)S(1)} %copy-done.8, f32[2,1024,128]{2,1,0:T(8,128)S(1)} %get-tuple-element.38.lines_ref, f32[3,1024,128]{2,1,0:T(8,128)S(1)} %copy-done.5, bf16[544,256]{1,0:T(8,128)(2,1)S(1)} %copy-done.3, ...), custom_call_target="tpu_custom_call" | custom-call | flops 1000 | bytes 1000 | tf_op jit(solution)/shard_map/pallas_call | solution.py:915
  51.3 1.6 %collective-permute-start.3 = (f32[7,88,128]{2,1,0:T(8,128)S(1)}, f32[7,88,128]{2,1,0:T(8,128)S(1)}, u32[]{:S(2)}, u32[]{:S(2)}) collective-permute-start(f32[7,88,128]{2,1,0:T(8,128)S(1)} %get-tuple-element.41), channel_id=1, source_target_pairs={{0,2},{2,0},{1,3},{3,1},{4,6},{6,4},{5,7},{7,5},{8,10},{10,8},{9,1... | collective-permute-start | bytes 946184 | tf_op jit(solution)/shard_map/ppermute | solution.py:1015
  52.8 0.9 %collective-permute-done.4.far_ref = f32[9,88,128]{2,1,0:T(8,128)S(1)} collective-permute-done((f32[9,88,128]{2,1,0:T(8,128)S(1)}, f32[9,88,128]{2,1,0:T(8,128)S(1)}, u32[]{:S(2)}, u32[]{:S(2)}) %collective-permute-start.4) | collective-permute-done | bytes 405536 | tf_op jit(solution)/shard_map/ppermute | solution.py:1015
  53.7 0.5 shard_map.93.planes_a
  54.2 8.2 %collective-permute-done.5.far_ref = f32[9,88,128]{2,1,0:T(8,128)S(1)} collective-permute-done((f32[9,88,128]{2,1,0:T(8,128)S(1)}, f32[9,88,128]{2,1,0:T(8,128)S(1)}, u32[]{:S(2)}, u32[]{:S(2)}) %collective-permute-start.5) | collective-permute-done | bytes 405536 | tf_op jit(solution)/shard_map/ppermute | solution.py:1015
  62.4 0.5 shard_map.94.planes_b
  62.9 0.0 collective-permute-done.7.base_hbm
  62.9 5.5 %collective-permute-done.3.far_ref = f32[7,88,128]{2,1,0:T(8,128)S(1)} collective-permute-done((f32[7,88,128]{2,1,0:T(8,128)S(1)}, f32[7,88,128]{2,1,0:T(8,128)S(1)}, u32[]{:S(2)}, u32[]{:S(2)}) %collective-permute-start.3) | collective-permute-done | bytes 315424 | tf_op jit(solution)/shard_map/ppermute | solution.py:1015
  68.5 0.0 collective-permute-done.6.state_hbm
  68.5 4.4 %shard_map.95 = (f32[3,16,4096]{2,1,0:T(8,128)}, f32[3,32,4096]{2,1,0:T(8,128)}) custom-call(f32[7,88,128]{2,1,0:T(8,128)S(1)} %get-tuple-element.40.near_ref, f32[7,88,128]{2,1,0:T(8,128)S(1)} %collective-permute-done.3.far_ref, f32[2,1024,128]{2,1,0:T(8,128)S(1)} %shard_map.93.planes_a, f32[2,1024,128]{2,1,0:T(8,128)S(1)} %shard_map.94.planes_b, ...), custom_call_target="tpu_custom_call" | custom-call | flops 1000 | bytes 1000 | tf_op jit(solution)/shard_map/pallas_call | solution.py:915
Async XLA Ops:
  4.8 14.6 %collective-permute-start = (f32[11,88,128]{2,1,0:T(8,128)}, f32[11,88,128]{2,1,0:T(8,128)}, u32[]{:S(2)}, u32[]{:S(2)}) collective-permute-start(f32[11,88,128]{2,1,0:T(8,128)} %shard_map.86.here_ref), channel_id=1, source_target_pairs={{0,2},{2,0},{1,3},{3,1},{4,6},{6,4},{5,7},{7,5},{8,10},{10,8},{9,1... | collective-permute-start | bytes 1486856 | tf_op jit(solution)/shard_map/ppermute | solution.py:957
  7.8 12.1 %copy-start.1 = (f32[1,3,32,4096]{3,2,1,0:T(8,128)S(1)}, f32[1,3,32,4096]{3,2,1,0:T(8,128)}, u32[]{:S(2)}) copy-start(f32[1,3,32,4096]{3,2,1,0:T(8,128)} %param.7) | copy-start | bytes 4718596
  7.8 60.7 %collective-permute-start.6 = (f32[3,32,4096]{2,1,0:T(8,128)}, f32[3,32,4096]{2,1,0:T(8,128)}, u32[]{:S(2)}, u32[]{:S(2)}) collective-permute-start(f32[3,32,4096]{2,1,0:T(8,128)} %bitcast.2.state_hbm.state_ref), channel_id=1, source_target_pairs={{4,0},{8,4},{12,8},{0,12},{1,5},{5,9},{9,13},{13,1},{6,2},{10,6},{... | collective-permute-start | bytes 4718600 | tf_op jit(solution)/shard_map/ppermute | solution.py:939
  11.4 15.9 %collective-permute-start.1 = (f32[11,88,128]{2,1,0:T(8,128)}, f32[11,88,128]{2,1,0:T(8,128)}, u32[]{:S(2)}, u32[]{:S(2)}) collective-permute-start(f32[11,88,128]{2,1,0:T(8,128)} %shard_map.86.here_ref), channel_id=1, source_target_pairs={{0,1},{1,0},{2,3},{3,2},{4,5},{5,4},{6,7},{7,6},{8,9},{9,8},{10,11... | collective-permute-start | bytes 1486856 | tf_op jit(solution)/shard_map/ppermute | solution.py:958
  11.4 12.6 %copy-start = (bf16[3584,256]{1,0:T(8,128)(2,1)S(1)}, bf16[3584,256]{1,0:T(8,128)(2,1)}, u32[]{:S(2)}) copy-start(bf16[3584,256]{1,0:T(8,128)(2,1)} %constant.18.clone.back_ref) | copy-start | bytes 5505028
  19.3 4.7 %copy-start.8 = (s32[3]{0:T(128)S(1)}, s32[3]{0:T(128)}, u32[]{:S(2)}) copy-start(s32[3]{0:T(128)} %cutoff_ref.9) | copy-start | bytes 40
  19.3 4.7 %copy-start.4 = (f32[11,88,128]{2,1,0:T(8,128)S(1)}, f32[11,88,128]{2,1,0:T(8,128)}, u32[]{:S(2)}) copy-start(f32[11,88,128]{2,1,0:T(8,128)} %shard_map.86.here_ref) | copy-start | bytes 1486852
  19.4 7.9 %collective-permute-start.2 = (f32[11,88,128]{2,1,0:T(8,128)}, f32[11,88,128]{2,1,0:T(8,128)S(1)}, u32[]{:S(2)}, u32[]{:S(2)}) collective-permute-start(f32[11,88,128]{2,1,0:T(8,128)} %collective-permute-done.there_ref), channel_id=1, source_target_pairs={{0,1},{1,0},{2,3},{3,2},{4,5},{5,4},{6,7},{7,6},{8,9},{9,8},{10,11... | collective-permute-start | bytes 1486856 | tf_op jit(solution)/shard_map/ppermute | solution.py:982
  19.9 43.0 %collective-permute-start.7 = (f32[3,16,4096]{2,1,0:T(8,128)S(1)}, f32[3,16,4096]{2,1,0:T(8,128)S(1)}, u32[]{:S(2)}, u32[]{:S(2)}) collective-permute-start(f32[3,16,4096]{2,1,0:T(8,128)S(1)} %dynamic-slice_bitcast_fusion), channel_id=1, source_target_pairs={{4,0},{8,4},{12,8},{0,12},{5,1},{9,5},{13,9},{1,13},{6,2},{10,6},{... | collective-permute-start | bytes 2359304 | tf_op jit(solution)/shard_map/ppermute | solution.py:938
  24.0 3.3 %copy-start.3 = (bf16[544,256]{1,0:T(8,128)(2,1)S(1)}, bf16[544,256]{1,0:T(8,128)(2,1)}, u32[]{:S(2)}) copy-start(bf16[544,256]{1,0:T(8,128)(2,1)} %constant.17.clone.ahead_hbm.ahead_ref) | copy-start | bytes 835588
  27.3 11.1 %copy-start.2 = (bf16[3072,256]{1,0:T(8,128)(2,1)S(1)}, bf16[3072,256]{1,0:T(8,128)(2,1)}, u32[]{:S(2)}) copy-start(bf16[3072,256]{1,0:T(8,128)(2,1)} %constant.19.clone.along_ref) | copy-start | bytes 4718596
  27.3 11.0 %copy-start.7 = (f32[2,8,88,128]{3,2,1,0:T(8,128)S(1)}, f32[2,8,88,128]{3,2,1,0:T(8,128)}, u32[]{:S(2)}) copy-start(f32[2,8,88,128]{3,2,1,0:T(8,128)} %get-tuple-element.31.flux_ref) | copy-start | bytes 2162692
  38.3 4.7 %copy-start.6 = (f32[3,1024,128]{2,1,0:T(8,128)S(1)}, f32[3,1024,128]{2,1,0:T(8,128)}, u32[]{:S(2)}) copy-start(f32[3,1024,128]{2,1,0:T(8,128)} %get-tuple-element.35.flux_ref) | copy-start | bytes 4718596
  41.4 12.3 %collective-permute-start.4 = (f32[9,88,128]{2,1,0:T(8,128)S(1)}, f32[9,88,128]{2,1,0:T(8,128)S(1)}, u32[]{:S(2)}, u32[]{:S(2)}) collective-permute-start(f32[9,88,128]{2,1,0:T(8,128)S(1)} %get-tuple-element.44), channel_id=1, source_target_pairs={{0,2},{2,0},{1,3},{3,1},{4,6},{6,4},{5,7},{7,5},{8,10},{10,8},{9,1... | collective-permute-start | bytes 1216520 | tf_op jit(solution)/shard_map/ppermute | solution.py:1015
  43.0 5.1 %copy-start.5 = (f32[3,1024,128]{2,1,0:T(8,128)S(1)}, f32[3,1024,128]{2,1,0:T(8,128)}, u32[]{:S(2)}) copy-start(f32[3,1024,128]{2,1,0:T(8,128)} %get-tuple-element.39.flux_ref) | copy-start | bytes 4718596
  47.5 14.9 %collective-permute-start.5 = (f32[9,88,128]{2,1,0:T(8,128)S(1)}, f32[9,88,128]{2,1,0:T(8,128)S(1)}, u32[]{:S(2)}, u32[]{:S(2)}) collective-permute-start(f32[9,88,128]{2,1,0:T(8,128)S(1)} %get-tuple-element.47), channel_id=1, source_target_pairs={{0,2},{2,0},{1,3},{3,1},{4,6},{6,4},{5,7},{7,5},{8,10},{10,8},{9,1... | collective-permute-start | bytes 1216520 | tf_op jit(solution)/shard_map/ppermute | solution.py:1015
  51.3 17.2 %collective-permute-start.3 = (f32[7,88,128]{2,1,0:T(8,128)S(1)}, f32[7,88,128]{2,1,0:T(8,128)S(1)}, u32[]{:S(2)}, u32[]{:S(2)}) collective-permute-start(f32[7,88,128]{2,1,0:T(8,128)S(1)} %get-tuple-element.41), channel_id=1, source_target_pairs={{0,2},{2,0},{1,3},{3,1},{4,6},{6,4},{5,7},{7,5},{8,10},{10,8},{9,1... | collective-permute-start | bytes 946184 | tf_op jit(solution)/shard_map/ppermute | solution.py:1015

commit v9 on v8

--- a/solution.py
+++ b/solution.py
@@ -19,6 +19,7 @@
 CHUNKS = 3
 LINE = CHUNKS * CHUNK * 4
 HALF_KZ = NKZ // 2
+SENT = 9
 LANES = 128
 
 viscosity = 0.025
@@ -560,12 +561,28 @@
         for yh, part in zip(yhs, lane_parts(got)):
             lines[0, yh * LINE : (yh + 1) * LINE, :] = part
     start = core_ref[0] * HALF_KZ
+    planes = []
     for pair in range(0, HALF_KZ, 2):
         ks = range(pair, min(pair + 2, HALF_KZ))
         data = jnp.concatenate([stacked(along_y(lines, 0, start + k)) for k in ks], 1)
-        got = folded(dot(fy_ref[...], data))
-        for k, part in zip(ks, lane_parts(got)):
-            out_ref[k] = part
+        planes += lane_parts(folded(dot(fy_ref[...], data)))
+    lane = lax.broadcasted_iota(jnp.int32, (ROWS, LANES), 1)
+    for k in range(SENT):
+        part = planes[k]
+        if k < 3 * (HALF_KZ - SENT):
+            guest = pltpu.roll(planes[SENT + k // 3], (3 - k % 3) * HALF, 1)
+            part = jnp.where(lane < 96, part, guest)
+        out_ref[k] = part
+
+
+def received(ref, k):
+    if k < SENT:
+        return ref[k]
+    lane = lax.broadcasted_iota(jnp.int32, (ROWS, LANES), 1)
+    blocks = [
+        pltpu.roll(ref[3 * (k - SENT) + j], LANES - (3 - j) * HALF, 1) for j in range(3)
+    ]
+    return jnp.where(lane < 32, blocks[0], jnp.where(lane < 64, blocks[1], blocks[2]))
 
 
 def flux_modes(lines_ref, fy_ref, fyr_ref, kzs):
@@ -667,7 +684,9 @@
         rows = []
         for kz in kzs:
             keep = keep_y * jnp.where(start + kz <= cut_z, 1.0, 0.0).astype(f32)
-            rows.append(jnp.concatenate([here_ref[kz] * keep, there_ref[kz] * keep], 1))
+            rows.append(
+                jnp.concatenate([received(ref, kz) * keep for ref in (here_ref, there_ref)], 1)
+            )
         high = back_ref[pl.ds(pl.multiple_of((6 + which) * 256, 256), 256), :]
         low = back_ref[pl.ds(pl.multiple_of((10 + which) * 256, 256), 256), :]
         got = triple(jnp.concatenate(rows, 0), high, low)
@@ -702,7 +721,6 @@
     y = y + lax.broadcasted_iota(jnp.int32, (HALF, LANES), 1) // N
     phase = ((wave_ref[0] * y) % N).astype(f32) * (2.0 * np.pi / N)
     force_ref[...] = forcing_amp * jnp.sin(phase)
-    nothing = jnp.zeros((HALF, LANES), f32)
 
     def along_halves(d, yh):
         at = pl.ds(yh, 4 * (HALF_KZ + 1), stride=HALF)
@@ -717,6 +735,7 @@
         steep = [along_halves(2, yh)[:96] for yh in yhs]
         flat = folded_lanes(dot(beside(jnp.concatenate(flat, 0)), iz_ref[...]))
         steep = folded_lanes(dot(beside(jnp.concatenate(steep, 0)), izd_ref[...]))
+        rows, lone = [], []
         for n, yh in enumerate(yhs):
             sets = [flat[96 * n :], flat[96 * (count + n) :], steep[96 * n :]]
             grads = [[one[HALF * i : HALF * (i + 1)] for i in range(3)] for one in sets]
@@ -732,14 +751,18 @@
                 if i == 0:
                     drive = drive - force_ref[pl.ds(yh, 1), :]
                 comb_base.append(b[i] - time_step * drive)
-            rows = [comb[1], comb_base[1], comb[2], comb_base[2]]
-            rows += [comb[0], comb_base[0], nothing, nothing]
-            got = folded(dot_nt(fz_ref[...], beside(jnp.concatenate(rows, 0))))
-            depth = LINE // CHUNKS
-            rows = pl.ds(pl.multiple_of(yh * depth, 8), depth)
-            for tile, part in enumerate(lane_parts(got)):
+            rows += [comb[1], comb_base[1], comb[2], comb_base[2]]
+            lone += [comb[0], comb_base[0]]
+        got = lane_parts(folded(dot_nt(fz_ref[...], beside(jnp.concatenate(rows + lone, 0)))))
+        depth = LINE // CHUNKS
+        for n, yh in enumerate(yhs):
+            second = got[count + n // 2]
+            if n % 2:
+                second = pltpu.roll(second, 64, 1)
+            at = pl.ds(pl.multiple_of(yh * depth, 8), depth)
+            for tile, part in enumerate((got[n], second)):
                 for chunk in range(CHUNKS):
-                    out_refs[chunk][tile, rows, :] = part[chunk * depth : (chunk + 1) * depth]
+                    out_refs[chunk][tile, at, :] = part[chunk * depth : (chunk + 1) * depth]
 
     over_lines(physical_step, 8)
 
@@ -785,7 +808,7 @@
             odd = lane_parts(folded(dot(fyr_ref[...], data[1])))
             for n, kz in enumerate(ks):
                 flux = first_flux[pair + n]
-                fields[0].append(odd[n] + second_flux[pair + n])
+                fields[0].append(jnp.where(lane < 64, odd[n], second_flux[pair + n]))
                 fields[1].append(jnp.where(lane < 64, even[n], flux))
                 fields[2].append(jnp.where(lane < 64, flux, even[n]))
         data = [beside(jnp.concatenate(field, 0)) for field in fields]
@@ -942,7 +965,7 @@
     swap = [(0, 1), (1, 0)]
     here_own = call(
         base_kernel,
-        sds((HALF_KZ, ROWS, LANES), f32),
+        sds((SENT, ROWS, LANES), f32),
         [
             pltpu.VMEM((1, HALF * LINE, LANES), f32),
             pltpu.VMEM(own_base.shape, f32),

time: 73.2 us -> 71.9 us (0.982)
  starting transfers between devices: 14.2 us -> 12.4 us
    ppermute x1, starting transfers between devices: 3.41 us -> 1.48 us  [body(): base_next = lax.ppermute(base_half, 'seg', back)]
  transfers between devices with their start and end apart: 8 -> 8, of which waited for: 4 -> 4; matrix products, arithmetic and copies ran while one was open for 0% -> 0% of each run, Pallas kernels for 46% -> 48%
where the time goes in v9:
time: 71.9 us; the launch traced here: 71.7 us
  Pallas kernels  43 us (60%)
  waiting for transfers between devices  14.6 us (20%)
  starting transfers between devices  12.4 us (17%)
  between operations  1.63 us (2%)
    pallas_call x10, Pallas kernels, call(): pl.pallas_call(kernel, out_shape=outs, in_specs=[small if n < in_smem els...  43 us
    ppermute x3, waiting for transfers between devices, body(): far.append(lax.ppermute(far_part, 'slab', swap))  14 us
    ppermute x3, starting transfers between devices, body(): far.append(lax.ppermute(far_part, 'slab', swap))  3.72 us
    ppermute x1, starting transfers between devices, body(): state_next = lax.ppermute(own_state, ('seg', 'comp'), around)  3.6 us
    ppermute x1, starting transfers between devices, body(): there_own = lax.ppermute(here_own, 'slab', swap)  3 us
    ppermute x1, starting transfers between devices, body(): base_next = lax.ppermute(base_half, 'seg', back)  1.48 us
  transfers between devices with their start and end apart: 8, of which 4 were waited for; matrix products, arithmetic and copies ran while one was open for 0% of the time, Pallas kernels for 48%

profile of v9, /device:TPU:0, one launch (start us, length us, event | category | flops | bytes accessed | tf_op | source)
XLA Modules:
  0.0 71.7 jit_solution(10651709468295706682)
XLA Ops:
  0.6 4.2 %shard_map.86.here_ref = f32[9,88,128]{2,1,0:T(8,128)} custom-call(s32[1]{0:T(128)} %bitcast.core_ref, f32[3,32,4096]{2,1,0:T(8,128)} %bitcast.7, bf16[544,256]{1,0:T(8,128)(2,1)} %constant.17.clone.ahead_hbm.ahead_ref), custom_call_target="tpu_custom_call" | custom-call | flops 1000 | bytes 1000 | tf_op jit(solution)/shard_map/pallas_call | solution.py:938
  4.9 3.0 %collective-permute-start = (f32[9,88,128]{2,1,0:T(8,128)}, f32[9,88,128]{2,1,0:T(8,128)}, u32[]{:S(2)}, u32[]{:S(2)}) collective-permute-start(f32[9,88,128]{2,1,0:T(8,128)} %shard_map.86.here_ref), channel_id=1, source_target_pairs={{0,2},{2,0},{1,3},{3,1},{4,6},{6,4},{5,7},{7,5},{8,10},{10,8},{9,1... | collective-permute-start | bytes 1216520 | tf_op jit(solution)/shard_map/ppermute | solution.py:980
  7.9 0.0 copy-start.1
  7.9 3.6 %collective-permute-start.6 = (f32[3,32,4096]{2,1,0:T(8,128)}, f32[3,32,4096]{2,1,0:T(8,128)}, u32[]{:S(2)}, u32[]{:S(2)}) collective-permute-start(f32[3,32,4096]{2,1,0:T(8,128)} %bitcast.2.state_hbm.state_ref), channel_id=1, source_target_pairs={{4,0},{8,4},{12,8},{0,12},{1,5},{5,9},{9,13},{13,1},{6,2},{10,6},{... | collective-permute-start | bytes 4718600 | tf_op jit(solution)/shard_map/ppermute | solution.py:962
  11.5 0.0 collective-permute-start.1
  11.5 0.0 copy-start
  11.5 7.9 %shard_map.87 = (f32[2,8,88,128]{3,2,1,0:T(8,128)}, f32[3,1024,128]{2,1,0:T(8,128)}, f32[3,1024,128]{2,1,0:T(8,128)}) custom-call(s32[1]{0:T(128)} %bitcast.core_ref, f32[3,32,4096]{2,1,0:T(8,128)} %bitcast.8, f32[3,32,4096]{2,1,0:T(8,128)} %bitcast.2.state_hbm.state_ref, bf16[544,256]{1,0:T(8,128)(2,1)} %constant.17.clone.ahead_hbm.ahead_ref), custom_call_target="tpu_custom_call" | custom-call | flops 1000 | bytes 1000 | tf_op jit(solution)/shard_map/pallas_call | solution.py:938
  19.4 0.0 copy-start.8
  19.4 0.0 copy-start.4
  19.4 0.0 collective-permute-done.there_ref
  19.4 0.6 collective-permute-start.2
  20.0 0.0 copy-done.1
  20.0 0.1 dynamic-slice_bitcast_fusion
  20.0 1.5 %collective-permute-start.7 = (f32[3,16,4096]{2,1,0:T(8,128)S(1)}, f32[3,16,4096]{2,1,0:T(8,128)S(1)}, u32[]{:S(2)}, u32[]{:S(2)}) collective-permute-start(f32[3,16,4096]{2,1,0:T(8,128)S(1)} %dynamic-slice_bitcast_fusion), channel_id=1, source_target_pairs={{4,0},{8,4},{12,8},{0,12},{5,1},{9,5},{13,9},{1,13},{6,2},{10,6},{... | collective-permute-start | bytes 2359304 | tf_op jit(solution)/shard_map/ppermute | solution.py:961
  22.2 0.0 copy-done
  22.2 0.0 copy-done.8
  22.2 0.0 copy-done.4
  22.2 0.0 copy-start.3
  22.2 3.2 %shard_map.88.own_ref = f32[3,1536,128]{2,1,0:T(8,128)S(1)} custom-call(s32[1]{0:T(128)} %bitcast.core_ref, s32[3]{0:T(128)S(1)} %copy-done.8, f32[9,88,128]{2,1,0:T(8,128)S(1)} %copy-done.4, f32[9,88,128]{2,1,0:T(8,128)} %collective-permute-done.there_ref, bf16[3584,256]{1,0:T(8,128)(2,1)S(1)} %copy-done), custom_call_target="tpu_custom_call" | custom-call | flops 1000 | bytes 1000 | tf_op jit(solution)/shard_map/pallas_call | solution.py:938
  25.4 0.0 copy-start.2
  25.4 0.0 copy-start.7
  25.4 0.0 collective-permute-done.1.here_ref
  25.4 0.0 collective-permute-done.2.there_ref
  25.5 0.0 copy-done.3
  25.5 11.5 %shard_map.89 = (f32[2,1024,128]{2,1,0:T(8,128)S(1)}, f32[2,1024,128]{2,1,0:T(8,128)S(1)}, f32[2,1024,128]{2,1,0:T(8,128)S(1)}) custom-call(s32[1]{0:T(128)} %bitcast.core_ref, s32[3]{0:T(128)S(1)} %copy-done.8, s32[1]{0:T(128)S(6)} %copy.9.wave_ref, f32[3,32,4096]{2,1,0:T(8,128)S(1)} %bitcast.9, f32[3,32,4096]{2,1,0:T(8,128)} %bitcast.2.state_hbm.state_ref, ...), custom_call_target="tpu_custom_call" | custom-call | flops 1000 | bytes 1000 | tf_op jit(solution)/shard_map/pallas_call | solution.py:938
  37.0 0.0 copy-done.2
  37.0 0.0 copy-done.7
  37.0 0.0 copy-start.6
  37.0 3.1 %shard_map.90 = (f32[9,88,128]{2,1,0:T(8,128)S(1)}, f32[9,88,128]{2,1,0:T(8,128)S(1)}) custom-call(s32[1]{0:T(128)} %bitcast.core_ref, s32[3]{0:T(128)S(1)} %copy-done.8, f32[2,1024,128]{2,1,0:T(8,128)S(1)} %get-tuple-element.30.lines_ref, f32[2,8,88,128]{3,2,1,0:T(8,128)S(1)} %copy-done.7, bf16[544,256]{1,0:T(8,128)(2,1)S(1)} %copy-done.3, ...), custom_call_target="tpu_custom_call" | custom-call | flops 1000 | bytes 1000 | tf_op jit(solution)/shard_map/pallas_call | solution.py:938
  40.1 1.6 %collective-permute-start.4 = (f32[9,88,128]{2,1,0:T(8,128)S(1)}, f32[9,88,128]{2,1,0:T(8,128)S(1)}, u32[]{:S(2)}, u32[]{:S(2)}) collective-permute-start(f32[9,88,128]{2,1,0:T(8,128)S(1)} %get-tuple-element.44), channel_id=1, source_target_pairs={{0,2},{2,0},{1,3},{3,1},{4,6},{6,4},{5,7},{7,5},{8,10},{10,8},{9,1... | collective-permute-start | bytes 1216520 | tf_op jit(solution)/shard_map/ppermute | solution.py:1038
  41.7 0.0 copy-done.6
  41.7 0.0 copy-start.5
  41.7 4.5 %shard_map.91 = (f32[9,88,128]{2,1,0:T(8,128)S(1)}, f32[9,88,128]{2,1,0:T(8,128)S(1)}) custom-call(s32[1]{0:T(128)} %bitcast.core_ref, s32[3]{0:T(128)S(1)} %copy-done.8, f32[2,1024,128]{2,1,0:T(8,128)S(1)} %get-tuple-element.34.lines_ref, f32[3,1024,128]{2,1,0:T(8,128)S(1)} %copy-done.6, bf16[544,256]{1,0:T(8,128)(2,1)S(1)} %copy-done.3, ...), custom_call_target="tpu_custom_call" | custom-call | flops 1000 | bytes 1000 | tf_op jit(solution)/shard_map/pallas_call | solution.py:938
  46.2 0.6 collective-permute-start.5
  46.8 0.0 copy-done.5
  46.8 3.2 %shard_map.92 = (f32[7,88,128]{2,1,0:T(8,128)S(1)}, f32[7,88,128]{2,1,0:T(8,128)S(1)}) custom-call(s32[1]{0:T(128)} %bitcast.core_ref, s32[3]{0:T(128)S(1)} %copy-done.8, f32[2,1024,128]{2,1,0:T(8,128)S(1)} %get-tuple-element.38.lines_ref, f32[3,1024,128]{2,1,0:T(8,128)S(1)} %copy-done.5, bf16[544,256]{1,0:T(8,128)(2,1)S(1)} %copy-done.3, ...), custom_call_target="tpu_custom_call" | custom-call | flops 1000 | bytes 1000 | tf_op jit(solution)/shard_map/pallas_call | solution.py:938
  49.9 1.6 %collective-permute-start.3 = (f32[7,88,128]{2,1,0:T(8,128)S(1)}, f32[7,88,128]{2,1,0:T(8,128)S(1)}, u32[]{:S(2)}, u32[]{:S(2)}) collective-permute-start(f32[7,88,128]{2,1,0:T(8,128)S(1)} %get-tuple-element.41), channel_id=1, source_target_pairs={{0,2},{2,0},{1,3},{3,1},{4,6},{6,4},{5,7},{7,5},{8,10},{10,8},{9,1... | collective-permute-start | bytes 946184 | tf_op jit(solution)/shard_map/ppermute | solution.py:1038
  51.5 0.9 %collective-permute-done.4.far_ref = f32[9,88,128]{2,1,0:T(8,128)S(1)} collective-permute-done((f32[9,88,128]{2,1,0:T(8,128)S(1)}, f32[9,88,128]{2,1,0:T(8,128)S(1)}, u32[]{:S(2)}, u32[]{:S(2)}) %collective-permute-start.4) | collective-permute-done | bytes 405536 | tf_op jit(solution)/shard_map/ppermute | solution.py:1038
  52.4 0.5 shard_map.93.planes_a
  52.9 8.2 %collective-permute-done.5.far_ref = f32[9,88,128]{2,1,0:T(8,128)S(1)} collective-permute-done((f32[9,88,128]{2,1,0:T(8,128)S(1)}, f32[9,88,128]{2,1,0:T(8,128)S(1)}, u32[]{:S(2)}, u32[]{:S(2)}) %collective-permute-start.5) | collective-permute-done | bytes 405536 | tf_op jit(solution)/shard_map/ppermute | solution.py:1038
  61.1 0.5 shard_map.94.planes_b
  61.6 0.6 collective-permute-done.7.base_hbm
  62.2 4.9 %collective-permute-done.3.far_ref = f32[7,88,128]{2,1,0:T(8,128)S(1)} collective-permute-done((f32[7,88,128]{2,1,0:T(8,128)S(1)}, f32[7,88,128]{2,1,0:T(8,128)S(1)}, u32[]{:S(2)}, u32[]{:S(2)}) %collective-permute-start.3) | collective-permute-done | bytes 315424 | tf_op jit(solution)/shard_map/ppermute | solution.py:1038
  67.1 0.0 collective-permute-done.6.state_hbm
  67.1 4.4 %shard_map.95 = (f32[3,16,4096]{2,1,0:T(8,128)}, f32[3,32,4096]{2,1,0:T(8,128)}) custom-call(f32[7,88,128]{2,1,0:T(8,128)S(1)} %get-tuple-element.40.near_ref, f32[7,88,128]{2,1,0:T(8,128)S(1)} %collective-permute-done.3.far_ref, f32[2,1024,128]{2,1,0:T(8,128)S(1)} %shard_map.93.planes_a, f32[2,1024,128]{2,1,0:T(8,128)S(1)} %shard_map.94.planes_b, ...), custom_call_target="tpu_custom_call" | custom-call | flops 1000 | bytes 1000 | tf_op jit(solution)/shard_map/pallas_call | solution.py:938
Async XLA Ops:
  4.9 14.5 %collective-permute-start = (f32[9,88,128]{2,1,0:T(8,128)}, f32[9,88,128]{2,1,0:T(8,128)}, u32[]{:S(2)}, u32[]{:S(2)}) collective-permute-start(f32[9,88,128]{2,1,0:T(8,128)} %shard_map.86.here_ref), channel_id=1, source_target_pairs={{0,2},{2,0},{1,3},{3,1},{4,6},{6,4},{5,7},{7,5},{8,10},{10,8},{9,1... | collective-permute-start | bytes 1216520 | tf_op jit(solution)/shard_map/ppermute | solution.py:980
  7.9 12.1 %copy-start.1 = (f32[1,3,32,4096]{3,2,1,0:T(8,128)S(1)}, f32[1,3,32,4096]{3,2,1,0:T(8,128)}, u32[]{:S(2)}) copy-start(f32[1,3,32,4096]{3,2,1,0:T(8,128)} %param.7) | copy-start | bytes 4718596
  7.9 59.3 %collective-permute-start.6 = (f32[3,32,4096]{2,1,0:T(8,128)}, f32[3,32,4096]{2,1,0:T(8,128)}, u32[]{:S(2)}, u32[]{:S(2)}) collective-permute-start(f32[3,32,4096]{2,1,0:T(8,128)} %bitcast.2.state_hbm.state_ref), channel_id=1, source_target_pairs={{4,0},{8,4},{12,8},{0,12},{1,5},{5,9},{9,13},{13,1},{6,2},{10,6},{... | collective-permute-start | bytes 4718600 | tf_op jit(solution)/shard_map/ppermute | solution.py:962
  11.5 14.0 %collective-permute-start.1 = (f32[9,88,128]{2,1,0:T(8,128)}, f32[9,88,128]{2,1,0:T(8,128)}, u32[]{:S(2)}, u32[]{:S(2)}) collective-permute-start(f32[9,88,128]{2,1,0:T(8,128)} %shard_map.86.here_ref), channel_id=1, source_target_pairs={{0,1},{1,0},{2,3},{3,2},{4,5},{5,4},{6,7},{7,6},{8,9},{9,8},{10,11... | collective-permute-start | bytes 1216520 | tf_op jit(solution)/shard_map/ppermute | solution.py:981
  11.5 10.7 %copy-start = (bf16[3584,256]{1,0:T(8,128)(2,1)S(1)}, bf16[3584,256]{1,0:T(8,128)(2,1)}, u32[]{:S(2)}) copy-start(bf16[3584,256]{1,0:T(8,128)(2,1)} %constant.18.clone.back_ref) | copy-start | bytes 5505028
  19.4 2.8 %copy-start.8 = (s32[3]{0:T(128)S(1)}, s32[3]{0:T(128)}, u32[]{:S(2)}) copy-start(s32[3]{0:T(128)} %cutoff_ref.9) | copy-start | bytes 40
  19.4 2.8 %copy-start.4 = (f32[9,88,128]{2,1,0:T(8,128)S(1)}, f32[9,88,128]{2,1,0:T(8,128)}, u32[]{:S(2)}) copy-start(f32[9,88,128]{2,1,0:T(8,128)} %shard_map.86.here_ref) | copy-start | bytes 1216516
  19.4 6.0 %collective-permute-start.2 = (f32[9,88,128]{2,1,0:T(8,128)}, f32[9,88,128]{2,1,0:T(8,128)S(1)}, u32[]{:S(2)}, u32[]{:S(2)}) collective-permute-start(f32[9,88,128]{2,1,0:T(8,128)} %collective-permute-done.there_ref), channel_id=1, source_target_pairs={{0,1},{1,0},{2,3},{3,2},{4,5},{5,4},{6,7},{7,6},{8,9},{9,8},{10,11... | collective-permute-start | bytes 1216520 | tf_op jit(solution)/shard_map/ppermute | solution.py:1005
  20.0 42.2 %collective-permute-start.7 = (f32[3,16,4096]{2,1,0:T(8,128)S(1)}, f32[3,16,4096]{2,1,0:T(8,128)S(1)}, u32[]{:S(2)}, u32[]{:S(2)}) collective-permute-start(f32[3,16,4096]{2,1,0:T(8,128)S(1)} %dynamic-slice_bitcast_fusion), channel_id=1, source_target_pairs={{4,0},{8,4},{12,8},{0,12},{5,1},{9,5},{13,9},{1,13},{6,2},{10,6},{... | collective-permute-start | bytes 2359304 | tf_op jit(solution)/shard_map/ppermute | solution.py:961
  22.2 3.3 %copy-start.3 = (bf16[544,256]{1,0:T(8,128)(2,1)S(1)}, bf16[544,256]{1,0:T(8,128)(2,1)}, u32[]{:S(2)}) copy-start(bf16[544,256]{1,0:T(8,128)(2,1)} %constant.17.clone.ahead_hbm.ahead_ref) | copy-start | bytes 835588
  25.4 11.6 %copy-start.2 = (bf16[3072,256]{1,0:T(8,128)(2,1)S(1)}, bf16[3072,256]{1,0:T(8,128)(2,1)}, u32[]{:S(2)}) copy-start(bf16[3072,256]{1,0:T(8,128)(2,1)} %constant.19.clone.along_ref) | copy-start | bytes 4718596
  25.4 11.6 %copy-start.7 = (f32[2,8,88,128]{3,2,1,0:T(8,128)S(1)}, f32[2,8,88,128]{3,2,1,0:T(8,128)}, u32[]{:S(2)}) copy-start(f32[2,8,88,128]{3,2,1,0:T(8,128)} %get-tuple-element.31.flux_ref) | copy-start | bytes 2162692
  37.0 4.7 %copy-start.6 = (f32[3,1024,128]{2,1,0:T(8,128)S(1)}, f32[3,1024,128]{2,1,0:T(8,128)}, u32[]{:S(2)}) copy-start(f32[3,1024,128]{2,1,0:T(8,128)} %get-tuple-element.35.flux_ref) | copy-start | bytes 4718596
  40.1 12.3 %collective-permute-start.4 = (f32[9,88,128]{2,1,0:T(8,128)S(1)}, f32[9,88,128]{2,1,0:T(8,128)S(1)}, u32[]{:S(2)}, u32[]{:S(2)}) collective-permute-start(f32[9,88,128]{2,1,0:T(8,128)S(1)} %get-tuple-element.44), channel_id=1, source_target_pairs={{0,2},{2,0},{1,3},{3,1},{4,6},{6,4},{5,7},{7,5},{8,10},{10,8},{9,1... | collective-permute-start | bytes 1216520 | tf_op jit(solution)/shard_map/ppermute | solution.py:1038
  41.7 5.1 %copy-start.5 = (f32[3,1024,128]{2,1,0:T(8,128)S(1)}, f32[3,1024,128]{2,1,0:T(8,128)}, u32[]{:S(2)}) copy-start(f32[3,1024,128]{2,1,0:T(8,128)} %get-tuple-element.39.flux_ref) | copy-start | bytes 4718596
  46.2 14.9 %collective-permute-start.5 = (f32[9,88,128]{2,1,0:T(8,128)S(1)}, f32[9,88,128]{2,1,0:T(8,128)S(1)}, u32[]{:S(2)}, u32[]{:S(2)}) collective-permute-start(f32[9,88,128]{2,1,0:T(8,128)S(1)} %get-tuple-element.47), channel_id=1, source_target_pairs={{0,2},{2,0},{1,3},{3,1},{4,6},{6,4},{5,7},{7,5},{8,10},{10,8},{9,1... | collective-permute-start | bytes 1216520 | tf_op jit(solution)/shard_map/ppermute | solution.py:1038
  49.9 17.2 %collective-permute-start.3 = (f32[7,88,128]{2,1,0:T(8,128)S(1)}, f32[7,88,128]{2,1,0:T(8,128)S(1)}, u32[]{:S(2)}, u32[]{:S(2)}) collective-permute-start(f32[7,88,128]{2,1,0:T(8,128)S(1)} %get-tuple-element.41), channel_id=1, source_target_pairs={{0,2},{2,0},{1,3},{3,1},{4,6},{6,4},{5,7},{7,5},{8,10},{10,8},{9,1... | collective-permute-start | bytes 946184 | tf_op jit(solution)/shard_map/ppermute | solution.py:1038

commit v10 on v9

--- a/solution.py
+++ b/solution.py
@@ -19,6 +19,7 @@
 CHUNKS = 3
 LINE = CHUNKS * CHUNK * 4
 HALF_KZ = NKZ // 2
+HALF_LINE = 4 * (HALF_KZ + 1)
 SENT = 9
 LANES = 128
 
@@ -310,6 +311,13 @@
         slope[:, y2, 1, y2] = -weight * kz[:, None] * np.cos(angle)
     forward = np.moveaxis(forward.reshape(4, CHUNKS, CHUNK, 2 * N), 1, 0)
     out["fz"] = left_table(forward.reshape(LINE, 2 * N), 128)
+    by_kz = np.moveaxis(forward.reshape(CHUNKS, 4, CHUNK, 2 * N), 1, 0).reshape(4, -1, 2 * N)
+    halved = []
+    for core in range(2):
+        wide = np.zeros((4, HALF_KZ + 1, 2 * N))
+        wide[:, :HALF_KZ] = by_kz[:, core * HALF_KZ : (core + 1) * HALF_KZ]
+        halved.append(left_table(wide.reshape(HALF_LINE, 2 * N), 128))
+    out["fzh"] = np.concatenate(halved, 0)
 
     def by_chunk(table):
         wide = np.zeros((CHUNKS, CHUNK, 4, 2 * N))
@@ -420,7 +428,7 @@
         )
     out["ix"] = np.stack([out.pop("ix0"), out.pop("ix1")])
     merged = {}
-    merged["ahead"] = np.concatenate([out["fz"], out["fy"], out["fyr"]], 0)
+    merged["ahead"] = np.concatenate([out["fz"], out["fy"], out["fyr"], out["fzh"]], 0)
     gx = [out["gxh"].reshape(-1, 256), out["gxl"].reshape(-1, 256)]
     square = [out[name] for name in ("iy", "iyd", "izg", "izd", "iz", "izr")]
     merged["back"] = np.concatenate(square + gx, 0)
@@ -433,7 +441,11 @@
 
 
 def ahead_tables(ref):
-    return view(ref, 0, 2 * LINE), view(ref, 0, 2 * ROWS, 2 * LINE), view(ref, 1, 2 * ROWS, 2 * LINE)
+    return (
+        view(ref, 0, 2 * LINE),
+        view(ref, 0, 2 * ROWS, 2 * LINE),
+        view(ref, 1, 2 * ROWS, 2 * LINE),
+    )
 
 
 def ky_rows():
@@ -494,10 +506,10 @@
     return pl.ds(pl.multiple_of(yh * LANES, LANES), LANES)
 
 
-def along_y(ref, tile, kz, line=LINE):
-    at = kz % CHUNK + (0 if line == LINE // CHUNKS else kz // CHUNK * (4 * CHUNK))
+def along_y(ref, tile, kz):
+    at = kz % CHUNK
     return jnp.concatenate(
-        [ref[tile, pl.ds(q * CHUNK + at, HALF, stride=line), :] for q in range(4)], 0
+        [ref[tile, pl.ds(q * CHUNK + at, HALF, stride=4 * CHUNK), :] for q in range(4)], 0
     )
 
 
@@ -547,8 +559,10 @@
     table.start()
     for piece in pieces[1:]:
         piece.start()
-    fz_ref, fy_ref, _ = ahead_tables(ahead_ref)
+    fy_ref = ahead_tables(ahead_ref)[1]
     table.wait()
+    first = 2 * LINE + 4 * ROWS + core_ref[0] * 2 * HALF_LINE
+    fz = ahead_ref[pl.ds(pl.multiple_of(first, 32), 2 * HALF_LINE), :]
     many = HALF // PIECES
     for n, piece in enumerate(pieces):
         piece.wait()
@@ -557,14 +571,18 @@
         for yh in yhs:
             at = slice(yh * LANES, (yh + 1) * LANES)
             rows += [base_ref[i, :, at] for i in range(3)] + [nothing]
-        got = folded(dot_nt(fz_ref[...], beside(jnp.concatenate(rows, 0))))
+        got = folded(dot_nt(fz, beside(jnp.concatenate(rows, 0))))
         for yh, part in zip(yhs, lane_parts(got)):
-            lines[0, yh * LINE : (yh + 1) * LINE, :] = part
-    start = core_ref[0] * HALF_KZ
+            lines[yh * HALF_LINE : (yh + 1) * HALF_LINE, :] = part
     planes = []
     for pair in range(0, HALF_KZ, 2):
         ks = range(pair, min(pair + 2, HALF_KZ))
-        data = jnp.concatenate([stacked(along_y(lines, 0, start + k)) for k in ks], 1)
+        data = []
+        for k in ks:
+            starts = [q * (HALF_KZ + 1) + k for q in range(4)]
+            picked = [lines[pl.ds(at, HALF, stride=HALF_LINE), :] for at in starts]
+            data.append(stacked(jnp.concatenate(picked, 0)))
+        data = jnp.concatenate(data, 1)
         planes += lane_parts(folded(dot(fy_ref[...], data)))
     lane = lax.broadcasted_iota(jnp.int32, (ROWS, LANES), 1)
     for k in range(SENT):
@@ -589,14 +607,13 @@
     ky = ky_rows()
     lane = lax.broadcasted_iota(jnp.int32, (ROWS, LANES), 1)
     odd_block = (lane // HALF) % 2 == 1
-    depth = LINE // CHUNKS
     even = []
     for pair in range(0, len(kzs), 2):
-        data = [stacked(along_y(lines_ref, 0, kz, depth)) for kz in kzs[pair : pair + 2]]
+        data = [stacked(along_y(lines_ref, 0, kz)) for kz in kzs[pair : pair + 2]]
         even += lane_parts(folded(dot(fy_ref[...], jnp.concatenate(data, 1))))
     odd = []
     for kz in kzs:
-        data = [stacked(along_y(lines_ref, tile, kz, depth)) for tile in (1, 2)]
+        data = [stacked(along_y(lines_ref, tile, kz)) for tile in (1, 2)]
         odd.append(lane_parts(folded(dot(fyr_ref[...], jnp.concatenate(data, 1)))))
     first, second = [], []
     for n, kz in enumerate(kzs):
@@ -721,6 +738,7 @@
     y = y + lax.broadcasted_iota(jnp.int32, (HALF, LANES), 1) // N
     phase = ((wave_ref[0] * y) % N).astype(f32) * (2.0 * np.pi / N)
     force_ref[...] = forcing_amp * jnp.sin(phase)
+    nothing = jnp.zeros((HALF, LANES), f32)
 
     def along_halves(d, yh):
         at = pl.ds(yh, 4 * (HALF_KZ + 1), stride=HALF)
@@ -735,7 +753,6 @@
         steep = [along_halves(2, yh)[:96] for yh in yhs]
         flat = folded_lanes(dot(beside(jnp.concatenate(flat, 0)), iz_ref[...]))
         steep = folded_lanes(dot(beside(jnp.concatenate(steep, 0)), izd_ref[...]))
-        rows, lone = [], []
         for n, yh in enumerate(yhs):
             sets = [flat[96 * n :], flat[96 * (count + n) :], steep[96 * n :]]
             grads = [[one[HALF * i : HALF * (i + 1)] for i in range(3)] for one in sets]
@@ -751,16 +768,12 @@
                 if i == 0:
                     drive = drive - force_ref[pl.ds(yh, 1), :]
                 comb_base.append(b[i] - time_step * drive)
-            rows += [comb[1], comb_base[1], comb[2], comb_base[2]]
-            lone += [comb[0], comb_base[0]]
-        got = lane_parts(folded(dot_nt(fz_ref[...], beside(jnp.concatenate(rows + lone, 0)))))
-        depth = LINE // CHUNKS
-        for n, yh in enumerate(yhs):
-            second = got[count + n // 2]
-            if n % 2:
-                second = pltpu.roll(second, 64, 1)
+            rows = [comb[1], comb_base[1], comb[2], comb_base[2]]
+            rows += [comb[0], comb_base[0], nothing, nothing]
+            got = folded(dot_nt(fz_ref[...], beside(jnp.concatenate(rows, 0))))
+            depth = LINE // CHUNKS
             at = pl.ds(pl.multiple_of(yh * depth, 8), depth)
-            for tile, part in enumerate((got[n], second)):
+            for tile, part in enumerate(lane_parts(got)):
                 for chunk in range(CHUNKS):
                     out_refs[chunk][tile, at, :] = part[chunk * depth : (chunk + 1) * depth]
 
@@ -800,7 +813,7 @@
             ks = kzs[pair : pair + 2]
             data = [
                 jnp.concatenate(
-                    [stacked(along_y(lines_ref, t, kz, LINE // CHUNKS)) for kz in ks], 1
+                    [stacked(along_y(lines_ref, t, kz)) for kz in ks], 1
                 )
                 for t in (0, 1)
             ]
@@ -958,7 +971,6 @@
     base_half = lax.dynamic_slice_in_dim(own_base, core * 16, 16, 1)
     back = [((s + 1) % seg_count, s) for s in range(seg_count)]
     around = [(2 * i, 2 * o) for i, o in back] + [(2 * o + 1, 2 * i + 1) for i, o in back]
-    base_next = lax.ppermute(base_half, "seg", back)
     state_next = lax.ppermute(own_state, ("seg", "comp"), around)
     sds = jax.ShapeDtypeStruct
     core_at = core.reshape(1)
@@ -967,7 +979,7 @@
         base_kernel,
         sds((SENT, ROWS, LANES), f32),
         [
-            pltpu.VMEM((1, HALF * LINE, LANES), f32),
+            pltpu.VMEM((HALF * HALF_LINE, LANES), f32),
             pltpu.VMEM(own_base.shape, f32),
             pltpu.VMEM(t["ahead"].shape, bf16),
             pltpu.SemaphoreType.DMA((PIECES + 1,)),
@@ -1034,6 +1046,9 @@
             room=12,
             in_smem=2,
         )
+        if chunk == 0:
+            base_half, near_part = lax.optimization_barrier((base_half, near_part))
+            base_next = lax.ppermute(base_half, "seg", back)
         near.append(near_part)
         far.append(lax.ppermute(far_part, "slab", swap))
     planes = sds((2, CHUNK * LANES, LANES), f32)

time: 71.9 us -> 70.1 us (0.975)
  Pallas kernels: 43 us -> 41.7 us
  starting transfers between devices: 12.4 us -> 11.5 us
    pallas_call x10, Pallas kernels: 43 us -> 41.7 us  [call(): pl.pallas_call(kernel, out_shape=outs, in_specs=[small if n < in_smem els...]
    ppermute x1, starting transfers between devices: 1.48 us -> 0.69 us  [body(): base_next = lax.ppermute(base_half, 'seg', back)]
  transfers between devices with their start and end apart: 8 -> 8, of which waited for: 4 -> 3; matrix products, arithmetic and copies ran while one was open for 0% -> 0% of each run, Pallas kernels for 48% -> 48%
where the time goes in v10:
time: 70.1 us; the launch traced here: 69.9 us
  Pallas kernels  41.7 us (59%)
  waiting for transfers between devices  14.7 us (21%)
  starting transfers between devices  11.5 us (16%)
  between operations  1.62 us (2%)
    pallas_call x10, Pallas kernels, call(): pl.pallas_call(kernel, out_shape=outs, in_specs=[small if n < in_smem els...  41.7 us
    ppermute x3, waiting for transfers between devices, body(): far.append(lax.ppermute(far_part, 'slab', swap))  14.6 us
    ppermute x3, starting transfers between devices, body(): far.append(lax.ppermute(far_part, 'slab', swap))  3.63 us
    ppermute x1, starting transfers between devices, body(): state_next = lax.ppermute(own_state, ('seg', 'comp'), around)  3.6 us
    ppermute x1, starting transfers between devices, body(): there_own = lax.ppermute(here_own, 'slab', swap)  3 us
  transfers between devices with their start and end apart: 8, of which 3 were waited for; matrix products, arithmetic and copies ran while one was open for 0% of the time, Pallas kernels for 48%

profile of v10, /device:TPU:0, one launch (start us, length us, event | category | flops | bytes accessed | tf_op | source)
XLA Modules:
  0.0 69.9 jit_solution(6620451826983654095)
XLA Ops:
  0.6 3.6 %shard_map.86.here_ref = f32[9,88,128]{2,1,0:T(8,128)} custom-call(s32[1]{0:T(128)} %bitcast.core_ref, f32[3,32,4096]{2,1,0:T(8,128)} %bitcast.7, bf16[736,256]{1,0:T(8,128)(2,1)} %constant.17.clone.ahead_hbm.ahead_ref), custom_call_target="tpu_custom_call" | custom-call | flops 1000 | bytes 1000 | tf_op jit(solution)/shard_map/pallas_call | solution.py:951
  4.3 3.0 %collective-permute-start = (f32[9,88,128]{2,1,0:T(8,128)}, f32[9,88,128]{2,1,0:T(8,128)}, u32[]{:S(2)}, u32[]{:S(2)}) collective-permute-start(f32[9,88,128]{2,1,0:T(8,128)} %shard_map.86.here_ref), channel_id=1, source_target_pairs={{0,2},{2,0},{1,3},{3,1},{4,6},{6,4},{5,7},{7,5},{8,10},{10,8},{9,1... | collective-permute-start | bytes 1216520 | tf_op jit(solution)/shard_map/ppermute | solution.py:992
  7.3 0.0 copy-start.1
  7.3 3.6 %collective-permute-start.6 = (f32[3,32,4096]{2,1,0:T(8,128)}, f32[3,32,4096]{2,1,0:T(8,128)}, u32[]{:S(2)}, u32[]{:S(2)}) collective-permute-start(f32[3,32,4096]{2,1,0:T(8,128)} %bitcast.3.state_hbm.state_ref), channel_id=1, source_target_pairs={{4,0},{8,4},{12,8},{0,12},{1,5},{5,9},{9,13},{13,1},{6,2},{10,6},{... | collective-permute-start | bytes 4718600 | tf_op jit(solution)/shard_map/ppermute | solution.py:974
  10.9 0.0 collective-permute-start.1
  10.9 0.0 copy-start
  10.9 7.9 %shard_map.87 = (f32[2,8,88,128]{3,2,1,0:T(8,128)}, f32[3,1024,128]{2,1,0:T(8,128)}, f32[3,1024,128]{2,1,0:T(8,128)}) custom-call(s32[1]{0:T(128)} %bitcast.core_ref, f32[3,32,4096]{2,1,0:T(8,128)} %bitcast.8, f32[3,32,4096]{2,1,0:T(8,128)} %bitcast.3.state_hbm.state_ref, bf16[736,256]{1,0:T(8,128)(2,1)} %constant.17.clone.ahead_hbm.ahead_ref), custom_call_target="tpu_custom_call" | custom-call | flops 1000 | bytes 1000 | tf_op jit(solution)/shard_map/pallas_call | solution.py:951
  18.8 0.0 copy-start.8
  19.5 0.0 copy-start.4
  19.5 0.0 collective-permute-done.there_ref
  19.5 0.6 collective-permute-start.2
  20.1 0.0 copy-done.1
  20.1 0.1 dynamic-slice_bitcast_fusion
  20.1 0.0 copy-done
  20.1 0.0 copy-done.8
  20.2 0.3 copy-done.4
  20.5 0.0 copy-start.3
  20.5 3.2 %shard_map.88.own_ref = f32[3,1536,128]{2,1,0:T(8,128)S(1)} custom-call(s32[1]{0:T(128)} %bitcast.core_ref, s32[3]{0:T(128)S(1)} %copy-done.8, f32[9,88,128]{2,1,0:T(8,128)S(1)} %copy-done.4, f32[9,88,128]{2,1,0:T(8,128)} %collective-permute-done.there_ref, bf16[3584,256]{1,0:T(8,128)(2,1)S(1)} %copy-done), custom_call_target="tpu_custom_call" | custom-call | flops 1000 | bytes 1000 | tf_op jit(solution)/shard_map/pallas_call | solution.py:951
  23.7 0.0 copy-start.2
  23.7 0.0 copy-start.7
  23.7 0.0 collective-permute-done.1.here_ref
  23.7 0.0 collective-permute-done.2.there_ref
  23.7 0.0 copy-done.3
  23.7 10.8 %shard_map.89 = (f32[2,1024,128]{2,1,0:T(8,128)S(1)}, f32[2,1024,128]{2,1,0:T(8,128)S(1)}, f32[2,1024,128]{2,1,0:T(8,128)S(1)}) custom-call(s32[1]{0:T(128)} %bitcast.core_ref, s32[3]{0:T(128)S(1)} %copy-done.8, s32[1]{0:T(128)S(6)} %copy.9.wave_ref, f32[3,32,4096]{2,1,0:T(8,128)S(1)} %bitcast.9, f32[3,32,4096]{2,1,0:T(8,128)} %bitcast.3.state_hbm.state_ref, ...), custom_call_target="tpu_custom_call" | custom-call | flops 1000 | bytes 1000 | tf_op jit(solution)/shard_map/pallas_call | solution.py:951
  34.5 0.0 copy-done.2
  34.5 0.0 copy-done.7
  34.5 0.0 copy-start.6
  34.5 3.1 %shard_map.90 = (f32[9,88,128]{2,1,0:T(8,128)S(1)}, f32[9,88,128]{2,1,0:T(8,128)S(1)}) custom-call(s32[1]{0:T(128)} %bitcast.core_ref, s32[3]{0:T(128)S(1)} %copy-done.8, f32[2,1024,128]{2,1,0:T(8,128)S(1)} %get-tuple-element.32.lines_ref, f32[2,8,88,128]{3,2,1,0:T(8,128)S(1)} %copy-done.7, bf16[736,256]{1,0:T(8,128)(2,1)S(1)} %copy-done.3, ...), custom_call_target="tpu_custom_call" | custom-call | flops 1000 | bytes 1000 | tf_op jit(solution)/shard_map/pallas_call | solution.py:951
  37.6 0.7 collective-permute-start.7
  38.3 1.5 %collective-permute-start.4 = (f32[9,88,128]{2,1,0:T(8,128)S(1)}, f32[9,88,128]{2,1,0:T(8,128)S(1)}, u32[]{:S(2)}, u32[]{:S(2)}) collective-permute-start(f32[9,88,128]{2,1,0:T(8,128)S(1)} %get-tuple-element.47), channel_id=1, source_target_pairs={{0,2},{2,0},{1,3},{3,1},{4,6},{6,4},{5,7},{7,5},{8,10},{10,8},{9,1... | collective-permute-start | bytes 1216520 | tf_op jit(solution)/shard_map/ppermute | solution.py:1053
  39.8 0.0 copy-done.6
  39.8 0.0 copy-start.5
  39.8 4.5 %shard_map.91 = (f32[9,88,128]{2,1,0:T(8,128)S(1)}, f32[9,88,128]{2,1,0:T(8,128)S(1)}) custom-call(s32[1]{0:T(128)} %bitcast.core_ref, s32[3]{0:T(128)S(1)} %copy-done.8, f32[2,1024,128]{2,1,0:T(8,128)S(1)} %get-tuple-element.37.lines_ref, f32[3,1024,128]{2,1,0:T(8,128)S(1)} %copy-done.6, bf16[736,256]{1,0:T(8,128)(2,1)S(1)} %copy-done.3, ...), custom_call_target="tpu_custom_call" | custom-call | flops 1000 | bytes 1000 | tf_op jit(solution)/shard_map/pallas_call | solution.py:951
  44.3 0.6 collective-permute-start.5
  44.9 0.0 copy-done.5
  44.9 3.2 %shard_map.92 = (f32[7,88,128]{2,1,0:T(8,128)S(1)}, f32[7,88,128]{2,1,0:T(8,128)S(1)}) custom-call(s32[1]{0:T(128)} %bitcast.core_ref, s32[3]{0:T(128)S(1)} %copy-done.8, f32[2,1024,128]{2,1,0:T(8,128)S(1)} %get-tuple-element.41.lines_ref, f32[3,1024,128]{2,1,0:T(8,128)S(1)} %copy-done.5, bf16[736,256]{1,0:T(8,128)(2,1)S(1)} %copy-done.3, ...), custom_call_target="tpu_custom_call" | custom-call | flops 1000 | bytes 1000 | tf_op jit(solution)/shard_map/pallas_call | solution.py:951
  48.1 1.5 %collective-permute-start.3 = (f32[7,88,128]{2,1,0:T(8,128)S(1)}, f32[7,88,128]{2,1,0:T(8,128)S(1)}, u32[]{:S(2)}, u32[]{:S(2)}) collective-permute-start(f32[7,88,128]{2,1,0:T(8,128)S(1)} %get-tuple-element.44), channel_id=1, source_target_pairs={{0,2},{2,0},{1,3},{3,1},{4,6},{6,4},{5,7},{7,5},{8,10},{10,8},{9,1... | collective-permute-start | bytes 946184 | tf_op jit(solution)/shard_map/ppermute | solution.py:1053
  49.6 0.9 %collective-permute-done.4.far_ref = f32[9,88,128]{2,1,0:T(8,128)S(1)} collective-permute-done((f32[9,88,128]{2,1,0:T(8,128)S(1)}, f32[9,88,128]{2,1,0:T(8,128)S(1)}, u32[]{:S(2)}, u32[]{:S(2)}) %collective-permute-start.4) | collective-permute-done | bytes 405536 | tf_op jit(solution)/shard_map/ppermute | solution.py:1053
  50.5 0.5 shard_map.93.planes_a
  51.0 8.2 %collective-permute-done.5.far_ref = f32[9,88,128]{2,1,0:T(8,128)S(1)} collective-permute-done((f32[9,88,128]{2,1,0:T(8,128)S(1)}, f32[9,88,128]{2,1,0:T(8,128)S(1)}, u32[]{:S(2)}, u32[]{:S(2)}) %collective-permute-start.5) | collective-permute-done | bytes 405536 | tf_op jit(solution)/shard_map/ppermute | solution.py:1053
  59.2 0.5 shard_map.94.planes_b
  59.7 5.5 %collective-permute-done.3.far_ref = f32[7,88,128]{2,1,0:T(8,128)S(1)} collective-permute-done((f32[7,88,128]{2,1,0:T(8,128)S(1)}, f32[7,88,128]{2,1,0:T(8,128)S(1)}, u32[]{:S(2)}, u32[]{:S(2)}) %collective-permute-start.3) | collective-permute-done | bytes 315424 | tf_op jit(solution)/shard_map/ppermute | solution.py:1053
  65.3 0.0 collective-permute-done.6.state_hbm
  65.3 0.0 collective-permute-done.7.base_hbm
  65.3 4.4 %shard_map.95 = (f32[3,16,4096]{2,1,0:T(8,128)}, f32[3,32,4096]{2,1,0:T(8,128)}) custom-call(f32[7,88,128]{2,1,0:T(8,128)S(1)} %get-tuple-element.43.near_ref, f32[7,88,128]{2,1,0:T(8,128)S(1)} %collective-permute-done.3.far_ref, f32[2,1024,128]{2,1,0:T(8,128)S(1)} %shard_map.93.planes_a, f32[2,1024,128]{2,1,0:T(8,128)S(1)} %shard_map.94.planes_b, ...), custom_call_target="tpu_custom_call" | custom-call | flops 1000 | bytes 1000 | tf_op jit(solution)/shard_map/pallas_call | solution.py:951
Async XLA Ops:
  4.3 15.2 %collective-permute-start = (f32[9,88,128]{2,1,0:T(8,128)}, f32[9,88,128]{2,1,0:T(8,128)}, u32[]{:S(2)}, u32[]{:S(2)}) collective-permute-start(f32[9,88,128]{2,1,0:T(8,128)} %shard_map.86.here_ref), channel_id=1, source_target_pairs={{0,2},{2,0},{1,3},{3,1},{4,6},{6,4},{5,7},{7,5},{8,10},{10,8},{9,1... | collective-permute-start | bytes 1216520 | tf_op jit(solution)/shard_map/ppermute | solution.py:992
  7.3 12.8 %copy-start.1 = (f32[1,3,32,4096]{3,2,1,0:T(8,128)S(1)}, f32[1,3,32,4096]{3,2,1,0:T(8,128)}, u32[]{:S(2)}) copy-start(f32[1,3,32,4096]{3,2,1,0:T(8,128)} %param.7) | copy-start | bytes 4718596
  7.3 58.0 %collective-permute-start.6 = (f32[3,32,4096]{2,1,0:T(8,128)}, f32[3,32,4096]{2,1,0:T(8,128)}, u32[]{:S(2)}, u32[]{:S(2)}) collective-permute-start(f32[3,32,4096]{2,1,0:T(8,128)} %bitcast.3.state_hbm.state_ref), channel_id=1, source_target_pairs={{4,0},{8,4},{12,8},{0,12},{1,5},{5,9},{9,13},{13,1},{6,2},{10,6},{... | collective-permute-start | bytes 4718600 | tf_op jit(solution)/shard_map/ppermute | solution.py:974
  10.9 12.8 %collective-permute-start.1 = (f32[9,88,128]{2,1,0:T(8,128)}, f32[9,88,128]{2,1,0:T(8,128)}, u32[]{:S(2)}, u32[]{:S(2)}) collective-permute-start(f32[9,88,128]{2,1,0:T(8,128)} %shard_map.86.here_ref), channel_id=1, source_target_pairs={{0,1},{1,0},{2,3},{3,2},{4,5},{5,4},{6,7},{7,6},{8,9},{9,8},{10,11... | collective-permute-start | bytes 1216520 | tf_op jit(solution)/shard_map/ppermute | solution.py:993
  10.9 9.3 %copy-start = (bf16[3584,256]{1,0:T(8,128)(2,1)S(1)}, bf16[3584,256]{1,0:T(8,128)(2,1)}, u32[]{:S(2)}) copy-start(bf16[3584,256]{1,0:T(8,128)(2,1)} %constant.18.clone.back_ref) | copy-start | bytes 5505028
  18.8 1.3 %copy-start.8 = (s32[3]{0:T(128)S(1)}, s32[3]{0:T(128)}, u32[]{:S(2)}) copy-start(s32[3]{0:T(128)} %cutoff_ref.9) | copy-start | bytes 40
  19.5 1.0 %copy-start.4 = (f32[9,88,128]{2,1,0:T(8,128)S(1)}, f32[9,88,128]{2,1,0:T(8,128)}, u32[]{:S(2)}) copy-start(f32[9,88,128]{2,1,0:T(8,128)} %shard_map.86.here_ref) | copy-start | bytes 1216516
  19.5 4.2 %collective-permute-start.2 = (f32[9,88,128]{2,1,0:T(8,128)}, f32[9,88,128]{2,1,0:T(8,128)S(1)}, u32[]{:S(2)}, u32[]{:S(2)}) collective-permute-start(f32[9,88,128]{2,1,0:T(8,128)} %collective-permute-done.there_ref), channel_id=1, source_target_pairs={{0,1},{1,0},{2,3},{3,2},{4,5},{5,4},{6,7},{7,6},{8,9},{9,8},{10,11... | collective-permute-start | bytes 1216520 | tf_op jit(solution)/shard_map/ppermute | solution.py:1017
  20.5 3.2 %copy-start.3 = (bf16[736,256]{1,0:T(8,128)(2,1)S(1)}, bf16[736,256]{1,0:T(8,128)(2,1)}, u32[]{:S(2)}) copy-start(bf16[736,256]{1,0:T(8,128)(2,1)} %constant.17.clone.ahead_hbm.ahead_ref) | copy-start | bytes 1130500
  23.7 10.8 %copy-start.2 = (bf16[3072,256]{1,0:T(8,128)(2,1)S(1)}, bf16[3072,256]{1,0:T(8,128)(2,1)}, u32[]{:S(2)}) copy-start(bf16[3072,256]{1,0:T(8,128)(2,1)} %constant.19.clone.along_ref) | copy-start | bytes 4718596
  23.7 10.8 %copy-start.7 = (f32[2,8,88,128]{3,2,1,0:T(8,128)S(1)}, f32[2,8,88,128]{3,2,1,0:T(8,128)}, u32[]{:S(2)}) copy-start(f32[2,8,88,128]{3,2,1,0:T(8,128)} %get-tuple-element.33.flux_ref) | copy-start | bytes 2162692
  34.5 5.3 %copy-start.6 = (f32[3,1024,128]{2,1,0:T(8,128)S(1)}, f32[3,1024,128]{2,1,0:T(8,128)}, u32[]{:S(2)}) copy-start(f32[3,1024,128]{2,1,0:T(8,128)} %get-tuple-element.38.flux_ref) | copy-start | bytes 4718596
  37.6 27.6 %collective-permute-start.7 = (f32[3,16,4096]{2,1,0:T(8,128)S(1)}, f32[3,16,4096]{2,1,0:T(8,128)S(1)}, u32[]{:S(2)}, u32[]{:S(2)}) collective-permute-start(f32[3,16,4096]{2,1,0:T(8,128)S(1)} %dynamic-slice_bitcast_fusion), channel_id=1, source_target_pairs={{4,0},{8,4},{12,8},{0,12},{5,1},{9,5},{13,9},{1,13},{6,2},{10,6},{... | collective-permute-start | bytes 2359304 | tf_op jit(solution)/shard_map/ppermute | solution.py:1051
  38.3 12.2 %collective-permute-start.4 = (f32[9,88,128]{2,1,0:T(8,128)S(1)}, f32[9,88,128]{2,1,0:T(8,128)S(1)}, u32[]{:S(2)}, u32[]{:S(2)}) collective-permute-start(f32[9,88,128]{2,1,0:T(8,128)S(1)} %get-tuple-element.47), channel_id=1, source_target_pairs={{0,2},{2,0},{1,3},{3,1},{4,6},{6,4},{5,7},{7,5},{8,10},{10,8},{9,1... | collective-permute-start | bytes 1216520 | tf_op jit(solution)/shard_map/ppermute | solution.py:1053
  39.8 5.1 %copy-start.5 = (f32[3,1024,128]{2,1,0:T(8,128)S(1)}, f32[3,1024,128]{2,1,0:T(8,128)}, u32[]{:S(2)}) copy-start(f32[3,1024,128]{2,1,0:T(8,128)} %get-tuple-element.42.flux_ref) | copy-start | bytes 4718596
  44.3 14.9 %collective-permute-start.5 = (f32[9,88,128]{2,1,0:T(8,128)S(1)}, f32[9,88,128]{2,1,0:T(8,128)S(1)}, u32[]{:S(2)}, u32[]{:S(2)}) collective-permute-start(f32[9,88,128]{2,1,0:T(8,128)S(1)} %get-tuple-element.50), channel_id=1, source_target_pairs={{0,2},{2,0},{1,3},{3,1},{4,6},{6,4},{5,7},{7,5},{8,10},{10,8},{9,1... | collective-permute-start | bytes 1216520 | tf_op jit(solution)/shard_map/ppermute | solution.py:1053
  48.1 17.2 %collective-permute-start.3 = (f32[7,88,128]{2,1,0:T(8,128)S(1)}, f32[7,88,128]{2,1,0:T(8,128)S(1)}, u32[]{:S(2)}, u32[]{:S(2)}) collective-permute-start(f32[7,88,128]{2,1,0:T(8,128)S(1)} %get-tuple-element.44), channel_id=1, source_target_pairs={{0,2},{2,0},{1,3},{3,1},{4,6},{6,4},{5,7},{7,5},{8,10},{10,8},{9,1... | collective-permute-start | bytes 946184 | tf_op jit(solution)/shard_map/ppermute | solution.py:1053

commit v11 on v10

--- a/solution.py
+++ b/solution.py
@@ -328,6 +328,17 @@
 
     out["iz"] = by_chunk(inverse)
     out["izr"] = by_chunk(turned)
+
+    def last_pair(table):
+        first, last = planes_of(CHUNKS - 1)
+        depth = 4 * CHUNK
+        wide = np.zeros((depth, 2 * N))
+        wide[: 4 * (last - first)] = table.reshape(NKZ, 4, 2 * N)[first:last].reshape(-1, 2 * N)
+        both = np.zeros((2, 2, 2 * depth, 4 * N), ml_dtypes.bfloat16)
+        both[0, 0] = both[1, 1] = right_table(wide, depth)
+        return both.reshape(2 * LANES, 256)
+
+    out["izc"] = np.concatenate([last_pair(inverse), last_pair(turned)], 0)
 
     def by_half(table):
         wide = np.zeros((2, HALF_KZ + 1, 4, 2 * N))
@@ -432,6 +443,7 @@
     gx = [out["gxh"].reshape(-1, 256), out["gxl"].reshape(-1, 256)]
     square = [out[name] for name in ("iy", "iyd", "izg", "izd", "iz", "izr")]
     merged["back"] = np.concatenate(square + gx, 0)
+    merged["last"] = out["izc"]
     merged["along"] = np.concatenate([out["fx"].reshape(-1, 256), out["ix"].reshape(-1, 256)], 0)
     return merged
 
@@ -690,10 +702,10 @@
 
 
 def gradient_planes(cutoff_ref, here_ref, there_ref, back_ref, planes, start):
-    cut_x, cut_y, cut_z = cutoff_ref[0], cutoff_ref[1], cutoff_ref[2]
+    cut_x, cut_y, cut_z = (cutoff_ref[i] for i in range(3))
     which = jnp.clip(cut_x - (KEEP - 3), 0, 3)
     keep_y = jnp.where(jnp.abs(ky_rows()) <= cut_y.astype(f32), 1.0, 0.0).astype(f32)
-    iy_ref, iyd_ref = (view(back_ref, n) for n in range(2))
+    tall_ref = view(back_ref, 0, 512)
     for d in range(3):
         planes[d, HALF_KZ * LANES :, :] = jnp.zeros((LANES, LANES), f32)
     for first in range(0, HALF_KZ, 4):
@@ -708,15 +720,16 @@
         low = back_ref[pl.ds(pl.multiple_of((10 + which) * 256, 256), 256), :]
         got = triple(jnp.concatenate(rows, 0), high, low)
         data = [stacked(padded(got[n * ROWS : (n + 1) * ROWS])) for n in range(len(kzs))]
-        for n, kz in enumerate(kzs):
-            even = lane_parts(folded(dot(iy_ref[...], data[n])))
-            planes[0, kz * LANES : (kz + 1) * LANES, :] = even[1]
-            planes[2, kz * LANES : (kz + 1) * LANES, :] = even[0]
         for n in range(0, len(kzs), 2):
-            both = jnp.concatenate([one[:, :LANES] for one in data[n : n + 2]], 1)
-            for k, part in enumerate(lane_parts(folded(dot(iyd_ref[...], both)))):
-                kz = kzs[n + k]
-                planes[1, kz * LANES : (kz + 1) * LANES, :] = part
+            pair = list(enumerate(kzs))[n : n + 2]
+            value = jnp.concatenate([data[k][:, :LANES] for k, _ in pair], 1)
+            slope = jnp.concatenate([data[k][:, LANES:] for k, _ in pair], 1)
+            both = dot(tall_ref[...], value)
+            parts = [lane_parts(folded(dot(tall_ref[:256, :], slope)))]
+            parts += [lane_parts(folded(both[256:])), lane_parts(folded(both[:256]))]
+            for d in range(3):
+                for k, (_, kz) in enumerate(pair):
+                    planes[d, kz * LANES : (kz + 1) * LANES, :] = parts[d][k]
 
 
 def half_kernel(core_ref, cutoff_ref, here_ref, there_ref, back_ref, planes):
@@ -786,7 +799,7 @@
 ):
     _, fy_ref, fyr_ref = ahead_tables(ahead_ref)
     core = core_ref[0]
-    cut_x, cut_y, cut_z = cutoff_ref[0], cutoff_ref[1], cutoff_ref[2]
+    cut_x, cut_y, cut_z = (cutoff_ref[i] for i in range(3))
     first, last = planes_of(chunk)
     extra = last - first
     ky = ky_rows()
@@ -879,9 +892,38 @@
     inverse_y(near_ref, far_ref, view(back_ref, 0), planes)
 
 
+def early_kernel(near_ref, far_ref, planes_a, back_ref, base_part, state_part, planes_b):
+    inverse_y(near_ref, far_ref, view(back_ref, 0), planes_b)
+    iz_ref, izr_ref = view(back_ref, 4), view(back_ref, 5)
+
+    def along_chunks(tile, yh):
+        at = pl.ds(yh, 4 * CHUNK, stride=HALF)
+        return padded(jnp.concatenate([ref[tile, at, :] for ref in (planes_a, planes_b)], 0)).T
+
+    many = HALF // PIECES
+    for piece in range(PIECES):
+        yhs = range(piece * many, (piece + 1) * many)
+        data = [along_chunks(0, yh) for yh in yhs]
+        rest = [along_chunks(1, yh)[:16] for yh in yhs]
+        turned = beside(jnp.concatenate([one[:48] for one in data], 0))
+        plain = beside(jnp.concatenate([one[48:] for one in data] + rest, 0))
+        turned = folded_lanes(dot(turned, izr_ref[...]))
+        plain = folded_lanes(dot(plain, iz_ref[...]))
+        for n, yh in enumerate(yhs):
+            at = slice(yh * LANES, (yh + 1) * LANES)
+            first = turned[48 * n : 48 * n + 48]
+            second = plain[80 * n : 80 * n + 80]
+            state_part[0, :, at] = first[:32]
+            state_part[1, :, at] = second[16:48]
+            state_part[2, :, at] = second[48:80]
+            base_part[0, :, at] = first[32:48]
+            base_part[1, :, at] = second[:16]
+            base_part[2, :, at] = plain[80 * many + 16 * n :][:16]
+
+
 def final_kernel(
-    near_ref, far_ref, planes_a, planes_b, state_hbm, base_hbm, back_ref, base_out, state_out,
-    planes_c, state_ref, base_ref, state_gap, base_gap, arrived, left,
+    near_ref, far_ref, base_part, state_part, state_hbm, base_hbm, back_ref, last_ref,
+    base_out, state_out, planes_c, state_ref, base_ref, state_gap, base_gap, arrived, left,
 ):
     wide = N * N // PIECES
     cuts = [pl.ds(n * wide, wide) for n in range(PIECES)]
@@ -902,38 +944,46 @@
     for piece in reads:
         for copy in piece:
             copy.start()
-    iy_ref, iz_ref, izr_ref = (view(back_ref, n) for n in (0, 4, 5))
-    inverse_y(near_ref, far_ref, iy_ref, planes_c)
-
-    def along_chunks(tile, yh):
-        parts = [
-            ref[tile, pl.ds(yh, 4 * CHUNK, stride=HALF), :]
-            for ref in (planes_a, planes_b, planes_c)
-        ]
-        return padded(jnp.concatenate(parts, 0)).T
+    inverse_y(near_ref, far_ref, view(back_ref, 0), planes_c)
+
+    def pair_of_lines(tile, yh):
+        rows = []
+        for n in range(2):
+            value = planes_c[tile, pl.ds(yh + n, 4 * CHUNK, stride=HALF), :]
+            high = value.astype(bf16).astype(f32)
+            rows += [high, value - high]
+        return jnp.concatenate(rows, 0).T
+
+    def table(n):
+        rows = last_ref[n * 256 : (n + 1) * 256, :].reshape(2, LANES, 256)
+        return jnp.concatenate([rows[0], rows[1]], 1)
 
     many = HALF // PIECES
     for piece in range(PIECES):
-        yhs = range(piece * many, (piece + 1) * many)
-        data = [along_chunks(0, yh) for yh in yhs]
-        rest = [along_chunks(1, yh)[:16] for yh in yhs]
-        turned = beside(jnp.concatenate([one[:48] for one in data], 0))
-        plain = beside(jnp.concatenate([one[48:] for one in data] + rest, 0))
-        turned = folded_lanes(dot(turned, izr_ref[...]))
-        plain = folded_lanes(dot(plain, iz_ref[...]))
+        yhs = range(piece * many, (piece + 1) * many, 2)
+        data = [pair_of_lines(0, yh) for yh in yhs]
+        rest = [pair_of_lines(1, yh)[:16] for yh in yhs]
+        turned = jnp.concatenate([one[:48] for one in data], 0).astype(bf16)
+        plain = jnp.concatenate([one[48:] for one in data] + rest, 0).astype(bf16)
+        turned = dot(turned, table(1))
+        plain = dot(plain, table(0))
+        turned = [folded_lanes(turned[:, :256]), folded_lanes(turned[:, 256:])]
+        plain = [folded_lanes(plain[:, :256]), folded_lanes(plain[:, 256:])]
         for copy in reads[piece]:
             copy.wait()
-        for n, yh in enumerate(yhs):
-            at = slice(yh * LANES, (yh + 1) * LANES)
-            first = turned[48 * n : 48 * n + 48]
-            second = plain[80 * n : 80 * n + 80]
-            third = plain[80 * many + 16 * n :][:16]
-            state_gap[0, :, at] = first[:32] - state_ref[0, :, at]
-            state_gap[1, :, at] = second[16:48] - state_ref[1, :, at]
-            state_gap[2, :, at] = second[48:80] - state_ref[2, :, at]
-            base_gap[0, :, at] = first[32:48] - base_ref[0, :, at]
-            base_gap[1, :, at] = second[:16] - base_ref[1, :, at]
-            base_gap[2, :, at] = third - base_ref[2, :, at]
+        for n, start in enumerate(yhs):
+            for k in range(2):
+                at = slice((start + k) * LANES, (start + k + 1) * LANES)
+                first = turned[k][48 * n : 48 * n + 48]
+                second = plain[k][80 * n : 80 * n + 80]
+                third = plain[k][40 * many + 16 * n :][:16]
+                states = [first[:32], second[16:48], second[48:80]]
+                bases = [first[32:48], second[:16], third]
+                for i in range(3):
+                    part = state_part[i, :, at] - state_ref[i, :, at]
+                    state_gap[i, :, at] = states[i] + part
+                    part = base_part[i, :, at] - base_ref[i, :, at]
+                    base_gap[i, :, at] = bases[i] + part
         for copy in writes[piece]:
             copy.start()
     for piece in writes:
@@ -1054,7 +1104,13 @@
     planes = sds((2, CHUNK * LANES, LANES), f32)
     planes_a = call(inverse_kernel, planes, [], [near[0], far[0], t["back"]], room=8)
     near[1], planes_a = lax.optimization_barrier((near[1], planes_a))
-    planes_b = call(inverse_kernel, planes, [], [near[1], far[1], t["back"]], room=8)
+    base_part, state_part = call(
+        early_kernel,
+        [sds(base_next.shape, f32), sds(state_next.shape, f32)],
+        [pltpu.VMEM(planes.shape, f32)],
+        [near[1], far[1], planes_a, t["back"]],
+        room=14,
+    )
     base_gap, state_gap = call(
         final_kernel,
         [sds(base_next.shape, f32), sds(state_next.shape, f32)],
@@ -1067,7 +1123,7 @@
             pltpu.SemaphoreType.DMA((2 * PIECES,)),
             pltpu.SemaphoreType.DMA((2 * PIECES,)),
         ],
-        [near[2], far[2], planes_a, planes_b, state_next, base_next, t["back"]],
+        [near[2], far[2], base_part, state_part, state_next, base_next, t["back"], t["last"]],
         room=16,
         in_hbm=(4, 5),
         out_hbm=True,

time: 70.1 us -> 69.3 us (0.989)
  waiting for transfers between devices: 14.7 us -> 13 us
  Pallas kernels: 41.7 us -> 42.5 us
    ppermute x3, waiting for transfers between devices: 14.6 us -> 13 us  [body(): far.append(lax.ppermute(far_part, 'slab', swap))]
    pallas_call x10, Pallas kernels: 41.7 us -> 42.5 us  [call(): pl.pallas_call(kernel, out_shape=outs, in_specs=[small if n < in_smem els...]
  transfers between devices with their start and end apart: 8 -> 8, of which waited for: 3 -> 3; matrix products, arithmetic and copies ran while one was open for 0% -> 0% of each run, Pallas kernels for 48% -> 51%
where the time goes in v11:
time: 69.3 us; the launch traced here: 69.1 us
  Pallas kernels  42.5 us (61%)
  waiting for transfers between devices  13 us (19%)
  starting transfers between devices  11.5 us (17%)
  between operations  1.64 us (2%)
    pallas_call x10, Pallas kernels, call(): pl.pallas_call(kernel, out_shape=outs, in_specs=[small if n < in_smem els...  42.5 us
    ppermute x3, waiting for transfers between devices, body(): far.append(lax.ppermute(far_part, 'slab', swap))  13 us
    ppermute x3, starting transfers between devices, body(): far.append(lax.ppermute(far_part, 'slab', swap))  3.63 us
    ppermute x1, starting transfers between devices, body(): state_next = lax.ppermute(own_state, ('seg', 'comp'), around)  3.6 us
    ppermute x1, starting transfers between devices, body(): there_own = lax.ppermute(here_own, 'slab', swap)  3 us
  transfers between devices with their start and end apart: 8, of which 3 were waited for; matrix products, arithmetic and copies ran while one was open for 0% of the time, Pallas kernels for 51%

profile of v11, /device:TPU:0, one launch (start us, length us, event | category | flops | bytes accessed | tf_op | source)
XLA Modules:
  0.0 69.1 jit_solution(10159875911720041839)
XLA Ops:
  0.6 3.6 %shard_map.95.here_ref = f32[9,88,128]{2,1,0:T(8,128)} custom-call(s32[1]{0:T(128)} %bitcast.core_ref, f32[3,32,4096]{2,1,0:T(8,128)} %bitcast.7, bf16[736,256]{1,0:T(8,128)(2,1)} %constant.19.clone.ahead_hbm.ahead_ref), custom_call_target="tpu_custom_call" | custom-call | flops 1000 | bytes 1000 | tf_op jit(solution)/shard_map/pallas_call | solution.py:1001
  4.2 3.0 %collective-permute-start = (f32[9,88,128]{2,1,0:T(8,128)}, f32[9,88,128]{2,1,0:T(8,128)}, u32[]{:S(2)}, u32[]{:S(2)}) collective-permute-start(f32[9,88,128]{2,1,0:T(8,128)} %shard_map.95.here_ref), channel_id=1, source_target_pairs={{0,2},{2,0},{1,3},{3,1},{4,6},{6,4},{5,7},{7,5},{8,10},{10,8},{9,1... | collective-permute-start | bytes 1216520 | tf_op jit(solution)/shard_map/ppermute | solution.py:1042
  7.3 0.0 copy-start.1
  7.3 3.6 %collective-permute-start.6 = (f32[3,32,4096]{2,1,0:T(8,128)}, f32[3,32,4096]{2,1,0:T(8,128)}, u32[]{:S(2)}, u32[]{:S(2)}) collective-permute-start(f32[3,32,4096]{2,1,0:T(8,128)} %bitcast.3.state_hbm.state_ref), channel_id=1, source_target_pairs={{4,0},{8,4},{12,8},{0,12},{1,5},{5,9},{9,13},{13,1},{6,2},{10,6},{... | collective-permute-start | bytes 4718600 | tf_op jit(solution)/shard_map/ppermute | solution.py:1024
  10.9 0.0 collective-permute-start.1
  10.9 0.0 copy-start
  10.9 7.9 %shard_map.96 = (f32[2,8,88,128]{3,2,1,0:T(8,128)}, f32[3,1024,128]{2,1,0:T(8,128)}, f32[3,1024,128]{2,1,0:T(8,128)}) custom-call(s32[1]{0:T(128)} %bitcast.core_ref, f32[3,32,4096]{2,1,0:T(8,128)} %bitcast.8, f32[3,32,4096]{2,1,0:T(8,128)} %bitcast.3.state_hbm.state_ref, bf16[736,256]{1,0:T(8,128)(2,1)} %constant.19.clone.ahead_hbm.ahead_ref), custom_call_target="tpu_custom_call" | custom-call | flops 1000 | bytes 1000 | tf_op jit(solution)/shard_map/pallas_call | solution.py:1001
  18.8 0.0 copy-start.9
  19.5 0.0 copy-start.4
  19.5 0.0 collective-permute-done.there_ref
  19.5 0.6 collective-permute-start.2
  20.1 0.0 copy-done.1
  20.1 0.1 dynamic-slice_bitcast_fusion
  20.1 0.0 copy-done
  20.1 0.0 copy-done.9
  20.1 0.3 copy-done.4
  20.5 0.0 copy-start.3
  20.5 3.3 %shard_map.97.own_ref = f32[3,1536,128]{2,1,0:T(8,128)S(1)} custom-call(s32[1]{0:T(128)} %bitcast.core_ref, s32[3]{0:T(128)S(1)} %copy-done.9, f32[9,88,128]{2,1,0:T(8,128)S(1)} %copy-done.4, f32[9,88,128]{2,1,0:T(8,128)} %collective-permute-done.there_ref, bf16[3584,256]{1,0:T(8,128)(2,1)S(1)} %copy-done), custom_call_target="tpu_custom_call" | custom-call | flops 1000 | bytes 1000 | tf_op jit(solution)/shard_map/pallas_call | solution.py:1001
  23.8 0.0 copy-start.2
  23.8 0.0 copy-start.7
  23.8 0.0 collective-permute-done.1.here_ref
  23.8 0.0 collective-permute-done.2.there_ref
  23.8 0.0 copy-done.3
  23.8 10.8 %shard_map.98 = (f32[2,1024,128]{2,1,0:T(8,128)S(1)}, f32[2,1024,128]{2,1,0:T(8,128)S(1)}, f32[2,1024,128]{2,1,0:T(8,128)S(1)}) custom-call(s32[1]{0:T(128)} %bitcast.core_ref, s32[3]{0:T(128)S(1)} %copy-done.9, s32[1]{0:T(128)S(6)} %copy.10.wave_ref, f32[3,32,4096]{2,1,0:T(8,128)S(1)} %bitcast.9, f32[3,32,4096]{2,1,0:T(8,128)} %bitcast.3.state_hbm.state_ref, ...), custom_call_target="tpu_custom_call" | custom-call | flops 1000 | bytes 1000 | tf_op jit(solution)/shard_map/pallas_call | solution.py:1001
  34.7 0.0 copy-done.2
  34.7 0.0 copy-done.7
  34.7 0.0 copy-start.6
  34.7 3.1 %shard_map.99 = (f32[9,88,128]{2,1,0:T(8,128)S(1)}, f32[9,88,128]{2,1,0:T(8,128)S(1)}) custom-call(s32[1]{0:T(128)} %bitcast.core_ref, s32[3]{0:T(128)S(1)} %copy-done.9, f32[2,1024,128]{2,1,0:T(8,128)S(1)} %get-tuple-element.34.lines_ref, f32[2,8,88,128]{3,2,1,0:T(8,128)S(1)} %copy-done.7, bf16[736,256]{1,0:T(8,128)(2,1)S(1)} %copy-done.3, ...), custom_call_target="tpu_custom_call" | custom-call | flops 1000 | bytes 1000 | tf_op jit(solution)/shard_map/pallas_call | solution.py:1001
  37.8 0.7 collective-permute-start.7
  38.5 1.5 %collective-permute-start.4 = (f32[9,88,128]{2,1,0:T(8,128)S(1)}, f32[9,88,128]{2,1,0:T(8,128)S(1)}, u32[]{:S(2)}, u32[]{:S(2)}) collective-permute-start(f32[9,88,128]{2,1,0:T(8,128)S(1)} %get-tuple-element.49), channel_id=1, source_target_pairs={{0,2},{2,0},{1,3},{3,1},{4,6},{6,4},{5,7},{7,5},{8,10},{10,8},{9,1... | collective-permute-start | bytes 1216520 | tf_op jit(solution)/shard_map/ppermute | solution.py:1103
  40.0 0.0 copy-done.6
  40.0 0.0 copy-start.5
  40.0 4.5 %shard_map.100 = (f32[9,88,128]{2,1,0:T(8,128)S(1)}, f32[9,88,128]{2,1,0:T(8,128)S(1)}) custom-call(s32[1]{0:T(128)} %bitcast.core_ref, s32[3]{0:T(128)S(1)} %copy-done.9, f32[2,1024,128]{2,1,0:T(8,128)S(1)} %get-tuple-element.39.lines_ref, f32[3,1024,128]{2,1,0:T(8,128)S(1)} %copy-done.6, bf16[736,256]{1,0:T(8,128)(2,1)S(1)} %copy-done.3, ...), custom_call_target="tpu_custom_call" | custom-call | flops 1000 | bytes 1000 | tf_op jit(solution)/shard_map/pallas_call | solution.py:1001
  44.5 0.6 collective-permute-start.5
  45.1 0.0 copy-done.5
  45.1 3.2 %shard_map.101 = (f32[7,88,128]{2,1,0:T(8,128)S(1)}, f32[7,88,128]{2,1,0:T(8,128)S(1)}) custom-call(s32[1]{0:T(128)} %bitcast.core_ref, s32[3]{0:T(128)S(1)} %copy-done.9, f32[2,1024,128]{2,1,0:T(8,128)S(1)} %get-tuple-element.43.lines_ref, f32[3,1024,128]{2,1,0:T(8,128)S(1)} %copy-done.5, bf16[736,256]{1,0:T(8,128)(2,1)S(1)} %copy-done.3, ...), custom_call_target="tpu_custom_call" | custom-call | flops 1000 | bytes 1000 | tf_op jit(solution)/shard_map/pallas_call | solution.py:1001
  48.3 1.5 %collective-permute-start.3 = (f32[7,88,128]{2,1,0:T(8,128)S(1)}, f32[7,88,128]{2,1,0:T(8,128)S(1)}, u32[]{:S(2)}, u32[]{:S(2)}) collective-permute-start(f32[7,88,128]{2,1,0:T(8,128)S(1)} %get-tuple-element.46), channel_id=1, source_target_pairs={{0,2},{2,0},{1,3},{3,1},{4,6},{6,4},{5,7},{7,5},{8,10},{10,8},{9,1... | collective-permute-start | bytes 946184 | tf_op jit(solution)/shard_map/ppermute | solution.py:1103
  49.8 0.9 %collective-permute-done.4.far_ref = f32[9,88,128]{2,1,0:T(8,128)S(1)} collective-permute-done((f32[9,88,128]{2,1,0:T(8,128)S(1)}, f32[9,88,128]{2,1,0:T(8,128)S(1)}, u32[]{:S(2)}, u32[]{:S(2)}) %collective-permute-start.4) | collective-permute-done | bytes 405536 | tf_op jit(solution)/shard_map/ppermute | solution.py:1103
  50.7 0.5 shard_map.102.planes_a
  51.2 0.0 copy-start.8
  51.2 8.2 %collective-permute-done.5.far_ref = f32[9,88,128]{2,1,0:T(8,128)S(1)} collective-permute-done((f32[9,88,128]{2,1,0:T(8,128)S(1)}, f32[9,88,128]{2,1,0:T(8,128)S(1)}, u32[]{:S(2)}, u32[]{:S(2)}) %collective-permute-start.5) | collective-permute-done | bytes 405536 | tf_op jit(solution)/shard_map/ppermute | solution.py:1103
  59.4 2.1 %shard_map.103 = (f32[3,16,4096]{2,1,0:T(8,128)S(1)}, f32[3,32,4096]{2,1,0:T(8,128)S(1)}) custom-call(f32[9,88,128]{2,1,0:T(8,128)S(1)} %get-tuple-element.50.near_ref, f32[9,88,128]{2,1,0:T(8,128)S(1)} %collective-permute-done.5.far_ref, f32[2,1024,128]{2,1,0:T(8,128)S(1)} %shard_map.102.planes_a, bf16[3584,256]{1,0:T(8,128)(2,1)S(1)} %copy-done), custom_call_target="tpu_custom_call" | custom-call | flops 1000 | bytes 1000 | tf_op jit(solution)/shard_map/pallas_call | solution.py:1001
  61.5 3.9 %collective-permute-done.3.far_ref = f32[7,88,128]{2,1,0:T(8,128)S(1)} collective-permute-done((f32[7,88,128]{2,1,0:T(8,128)S(1)}, f32[7,88,128]{2,1,0:T(8,128)S(1)}, u32[]{:S(2)}, u32[]{:S(2)}) %collective-permute-start.3) | collective-permute-done | bytes 315424 | tf_op jit(solution)/shard_map/ppermute | solution.py:1103
  65.5 0.0 collective-permute-done.6.state_hbm
  65.5 0.0 collective-permute-done.7.base_hbm
  65.5 0.0 copy-done.8
  65.5 3.5 %shard_map.104 = (f32[3,16,4096]{2,1,0:T(8,128)}, f32[3,32,4096]{2,1,0:T(8,128)}) custom-call(f32[7,88,128]{2,1,0:T(8,128)S(1)} %get-tuple-element.45.near_ref, f32[7,88,128]{2,1,0:T(8,128)S(1)} %collective-permute-done.3.far_ref, f32[3,16,4096]{2,1,0:T(8,128)S(1)} %get-tuple-element.53.base_part, f32[3,32,4096]{2,1,0:T(8,128)S(1)} %get-tuple-element.54.state_part, ...), custom_call_target="tpu_custom_call" | custom-call | flops 1000 | bytes 1000 | tf_op jit(solution)/shard_map/pallas_call | solution.py:1001
Async XLA Ops:
  4.2 15.2 %collective-permute-start = (f32[9,88,128]{2,1,0:T(8,128)}, f32[9,88,128]{2,1,0:T(8,128)}, u32[]{:S(2)}, u32[]{:S(2)}) collective-permute-start(f32[9,88,128]{2,1,0:T(8,128)} %shard_map.95.here_ref), channel_id=1, source_target_pairs={{0,2},{2,0},{1,3},{3,1},{4,6},{6,4},{5,7},{7,5},{8,10},{10,8},{9,1... | collective-permute-start | bytes 1216520 | tf_op jit(solution)/shard_map/ppermute | solution.py:1042
  7.3 12.8 %copy-start.1 = (f32[1,3,32,4096]{3,2,1,0:T(8,128)S(1)}, f32[1,3,32,4096]{3,2,1,0:T(8,128)}, u32[]{:S(2)}) copy-start(f32[1,3,32,4096]{3,2,1,0:T(8,128)} %param.8) | copy-start | bytes 4718596
  7.3 58.2 %collective-permute-start.6 = (f32[3,32,4096]{2,1,0:T(8,128)}, f32[3,32,4096]{2,1,0:T(8,128)}, u32[]{:S(2)}, u32[]{:S(2)}) collective-permute-start(f32[3,32,4096]{2,1,0:T(8,128)} %bitcast.3.state_hbm.state_ref), channel_id=1, source_target_pairs={{4,0},{8,4},{12,8},{0,12},{1,5},{5,9},{9,13},{13,1},{6,2},{10,6},{... | collective-permute-start | bytes 4718600 | tf_op jit(solution)/shard_map/ppermute | solution.py:1024
  10.9 12.9 %collective-permute-start.1 = (f32[9,88,128]{2,1,0:T(8,128)}, f32[9,88,128]{2,1,0:T(8,128)}, u32[]{:S(2)}, u32[]{:S(2)}) collective-permute-start(f32[9,88,128]{2,1,0:T(8,128)} %shard_map.95.here_ref), channel_id=1, source_target_pairs={{0,1},{1,0},{2,3},{3,2},{4,5},{5,4},{6,7},{7,6},{8,9},{9,8},{10,11... | collective-permute-start | bytes 1216520 | tf_op jit(solution)/shard_map/ppermute | solution.py:1043
  10.9 9.3 %copy-start = (bf16[3584,256]{1,0:T(8,128)(2,1)S(1)}, bf16[3584,256]{1,0:T(8,128)(2,1)}, u32[]{:S(2)}) copy-start(bf16[3584,256]{1,0:T(8,128)(2,1)} %constant.20.clone.back_ref) | copy-start | bytes 5505028
  18.8 1.3 %copy-start.9 = (s32[3]{0:T(128)S(1)}, s32[3]{0:T(128)}, u32[]{:S(2)}) copy-start(s32[3]{0:T(128)} %cutoff_ref.9) | copy-start | bytes 40
  19.5 1.0 %copy-start.4 = (f32[9,88,128]{2,1,0:T(8,128)S(1)}, f32[9,88,128]{2,1,0:T(8,128)}, u32[]{:S(2)}) copy-start(f32[9,88,128]{2,1,0:T(8,128)} %shard_map.95.here_ref) | copy-start | bytes 1216516
  19.5 4.3 %collective-permute-start.2 = (f32[9,88,128]{2,1,0:T(8,128)}, f32[9,88,128]{2,1,0:T(8,128)S(1)}, u32[]{:S(2)}, u32[]{:S(2)}) collective-permute-start(f32[9,88,128]{2,1,0:T(8,128)} %collective-permute-done.there_ref), channel_id=1, source_target_pairs={{0,1},{1,0},{2,3},{3,2},{4,5},{5,4},{6,7},{7,6},{8,9},{9,8},{10,11... | collective-permute-start | bytes 1216520 | tf_op jit(solution)/shard_map/ppermute | solution.py:1067
  20.5 3.3 %copy-start.3 = (bf16[736,256]{1,0:T(8,128)(2,1)S(1)}, bf16[736,256]{1,0:T(8,128)(2,1)}, u32[]{:S(2)}) copy-start(bf16[736,256]{1,0:T(8,128)(2,1)} %constant.19.clone.ahead_hbm.ahead_ref) | copy-start | bytes 1130500
  23.8 10.9 %copy-start.2 = (bf16[3072,256]{1,0:T(8,128)(2,1)S(1)}, bf16[3072,256]{1,0:T(8,128)(2,1)}, u32[]{:S(2)}) copy-start(bf16[3072,256]{1,0:T(8,128)(2,1)} %constant.22.clone.along_ref) | copy-start | bytes 4718596
  23.8 10.9 %copy-start.7 = (f32[2,8,88,128]{3,2,1,0:T(8,128)S(1)}, f32[2,8,88,128]{3,2,1,0:T(8,128)}, u32[]{:S(2)}) copy-start(f32[2,8,88,128]{3,2,1,0:T(8,128)} %get-tuple-element.35.flux_ref) | copy-start | bytes 2162692
  34.7 5.3 %copy-start.6 = (f32[3,1024,128]{2,1,0:T(8,128)S(1)}, f32[3,1024,128]{2,1,0:T(8,128)}, u32[]{:S(2)}) copy-start(f32[3,1024,128]{2,1,0:T(8,128)} %get-tuple-element.40.flux_ref) | copy-start | bytes 4718596
  37.8 27.6 %collective-permute-start.7 = (f32[3,16,4096]{2,1,0:T(8,128)S(1)}, f32[3,16,4096]{2,1,0:T(8,128)S(1)}, u32[]{:S(2)}, u32[]{:S(2)}) collective-permute-start(f32[3,16,4096]{2,1,0:T(8,128)S(1)} %dynamic-slice_bitcast_fusion), channel_id=1, source_target_pairs={{4,0},{8,4},{12,8},{0,12},{5,1},{9,5},{13,9},{1,13},{6,2},{10,6},{... | collective-permute-start | bytes 2359304 | tf_op jit(solution)/shard_map/ppermute | solution.py:1101
  38.5 12.2 %collective-permute-start.4 = (f32[9,88,128]{2,1,0:T(8,128)S(1)}, f32[9,88,128]{2,1,0:T(8,128)S(1)}, u32[]{:S(2)}, u32[]{:S(2)}) collective-permute-start(f32[9,88,128]{2,1,0:T(8,128)S(1)} %get-tuple-element.49), channel_id=1, source_target_pairs={{0,2},{2,0},{1,3},{3,1},{4,6},{6,4},{5,7},{7,5},{8,10},{10,8},{9,1... | collective-permute-start | bytes 1216520 | tf_op jit(solution)/shard_map/ppermute | solution.py:1103
  40.0 5.1 %copy-start.5 = (f32[3,1024,128]{2,1,0:T(8,128)S(1)}, f32[3,1024,128]{2,1,0:T(8,128)}, u32[]{:S(2)}) copy-start(f32[3,1024,128]{2,1,0:T(8,128)} %get-tuple-element.44.flux_ref) | copy-start | bytes 4718596
  44.5 14.9 %collective-permute-start.5 = (f32[9,88,128]{2,1,0:T(8,128)S(1)}, f32[9,88,128]{2,1,0:T(8,128)S(1)}, u32[]{:S(2)}, u32[]{:S(2)}) collective-permute-start(f32[9,88,128]{2,1,0:T(8,128)S(1)} %get-tuple-element.51), channel_id=1, source_target_pairs={{0,2},{2,0},{1,3},{3,1},{4,6},{6,4},{5,7},{7,5},{8,10},{10,8},{9,1... | collective-permute-start | bytes 1216520 | tf_op jit(solution)/shard_map/ppermute | solution.py:1103
  48.3 17.2 %collective-permute-start.3 = (f32[7,88,128]{2,1,0:T(8,128)S(1)}, f32[7,88,128]{2,1,0:T(8,128)S(1)}, u32[]{:S(2)}, u32[]{:S(2)}) collective-permute-start(f32[7,88,128]{2,1,0:T(8,128)S(1)} %get-tuple-element.46), channel_id=1, source_target_pairs={{0,2},{2,0},{1,3},{3,1},{4,6},{6,4},{5,7},{7,5},{8,10},{10,8},{9,1... | collective-permute-start | bytes 946184 | tf_op jit(solution)/shard_map/ppermute | solution.py:1103
  51.2 14.3 %copy-start.8 = (bf16[512,256]{1,0:T(8,128)(2,1)S(1)}, bf16[512,256]{1,0:T(8,128)(2,1)}, u32[]{:S(2)}) copy-start(bf16[512,256]{1,0:T(8,128)(2,1)} %constant.21.clone.last_ref) | copy-start | bytes 786436

commit v12 on v11

--- a/solution.py
+++ b/solution.py
@@ -702,10 +702,10 @@
 
 
 def gradient_planes(cutoff_ref, here_ref, there_ref, back_ref, planes, start):
-    cut_x, cut_y, cut_z = (cutoff_ref[i] for i in range(3))
+    cut_x, cut_y, cut_z = cutoff_ref[0], cutoff_ref[1], cutoff_ref[2]
     which = jnp.clip(cut_x - (KEEP - 3), 0, 3)
     keep_y = jnp.where(jnp.abs(ky_rows()) <= cut_y.astype(f32), 1.0, 0.0).astype(f32)
-    tall_ref = view(back_ref, 0, 512)
+    iy_ref, iyd_ref = (view(back_ref, n) for n in range(2))
     for d in range(3):
         planes[d, HALF_KZ * LANES :, :] = jnp.zeros((LANES, LANES), f32)
     for first in range(0, HALF_KZ, 4):
@@ -720,16 +720,15 @@
         low = back_ref[pl.ds(pl.multiple_of((10 + which) * 256, 256), 256), :]
         got = triple(jnp.concatenate(rows, 0), high, low)
         data = [stacked(padded(got[n * ROWS : (n + 1) * ROWS])) for n in range(len(kzs))]
+        for n, kz in enumerate(kzs):
+            even = lane_parts(folded(dot(iy_ref[...], data[n])))
+            planes[0, kz * LANES : (kz + 1) * LANES, :] = even[1]
+            planes[2, kz * LANES : (kz + 1) * LANES, :] = even[0]
         for n in range(0, len(kzs), 2):
-            pair = list(enumerate(kzs))[n : n + 2]
-            value = jnp.concatenate([data[k][:, :LANES] for k, _ in pair], 1)
-            slope = jnp.concatenate([data[k][:, LANES:] for k, _ in pair], 1)
-            both = dot(tall_ref[...], value)
-            parts = [lane_parts(folded(dot(tall_ref[:256, :], slope)))]
-            parts += [lane_parts(folded(both[256:])), lane_parts(folded(both[:256]))]
-            for d in range(3):
-                for k, (_, kz) in enumerate(pair):
-                    planes[d, kz * LANES : (kz + 1) * LANES, :] = parts[d][k]
+            both = jnp.concatenate([one[:, :LANES] for one in data[n : n + 2]], 1)
+            for k, part in enumerate(lane_parts(folded(dot(iyd_ref[...], both)))):
+                kz = kzs[n + k]
+                planes[1, kz * LANES : (kz + 1) * LANES, :] = part
 
 
 def half_kernel(core_ref, cutoff_ref, here_ref, there_ref, back_ref, planes):

time: 69.3 us -> 69.1 us (level)
  no operation moved by 1% of the time
where the time goes in v12:
time: 69.1 us; the launch traced here: 68.9 us
  Pallas kernels  42.3 us (61%)
  waiting for transfers between devices  13 us (19%)
  starting transfers between devices  11.5 us (17%)
  between operations  1.63 us (2%)
    pallas_call x10, Pallas kernels, call(): pl.pallas_call(kernel, out_shape=outs, in_specs=[small if n < in_smem els...  42.3 us
    ppermute x3, waiting for transfers between devices, body(): far.append(lax.ppermute(far_part, 'slab', swap))  13 us
    ppermute x3, starting transfers between devices, body(): far.append(lax.ppermute(far_part, 'slab', swap))  3.62 us
    ppermute x1, starting transfers between devices, body(): state_next = lax.ppermute(own_state, ('seg', 'comp'), around)  3.6 us
    ppermute x1, starting transfers between devices, body(): there_own = lax.ppermute(here_own, 'slab', swap)  3 us
  transfers between devices with their start and end apart: 8, of which 3 were waited for; matrix products, arithmetic and copies ran while one was open for 0% of the time, Pallas kernels for 51%

profile of v12, /device:TPU:0, one launch (start us, length us, event | category | flops | bytes accessed | tf_op | source)
XLA Modules:
  0.0 68.9 jit_solution(16401932305943211937)
XLA Ops:
  0.6 3.6 %shard_map.95.here_ref = f32[9,88,128]{2,1,0:T(8,128)} custom-call(s32[1]{0:T(128)} %bitcast.core_ref, f32[3,32,4096]{2,1,0:T(8,128)} %bitcast.7, bf16[736,256]{1,0:T(8,128)(2,1)} %constant.19.clone.ahead_hbm.ahead_ref), custom_call_target="tpu_custom_call" | custom-call | flops 1000 | bytes 1000 | tf_op jit(solution)/shard_map/pallas_call | solution.py:1000
  4.2 3.0 %collective-permute-start = (f32[9,88,128]{2,1,0:T(8,128)}, f32[9,88,128]{2,1,0:T(8,128)}, u32[]{:S(2)}, u32[]{:S(2)}) collective-permute-start(f32[9,88,128]{2,1,0:T(8,128)} %shard_map.95.here_ref), channel_id=1, source_target_pairs={{0,2},{2,0},{1,3},{3,1},{4,6},{6,4},{5,7},{7,5},{8,10},{10,8},{9,1... | collective-permute-start | bytes 1216520 | tf_op jit(solution)/shard_map/ppermute | solution.py:1041
  7.3 0.0 copy-start.1
  7.3 3.6 %collective-permute-start.6 = (f32[3,32,4096]{2,1,0:T(8,128)}, f32[3,32,4096]{2,1,0:T(8,128)}, u32[]{:S(2)}, u32[]{:S(2)}) collective-permute-start(f32[3,32,4096]{2,1,0:T(8,128)} %bitcast.3.state_hbm.state_ref), channel_id=1, source_target_pairs={{4,0},{8,4},{12,8},{0,12},{1,5},{5,9},{9,13},{13,1},{6,2},{10,6},{... | collective-permute-start | bytes 4718600 | tf_op jit(solution)/shard_map/ppermute | solution.py:1023
  10.9 0.0 collective-permute-start.1
  10.9 0.0 copy-start
  10.9 7.9 %shard_map.96 = (f32[2,8,88,128]{3,2,1,0:T(8,128)}, f32[3,1024,128]{2,1,0:T(8,128)}, f32[3,1024,128]{2,1,0:T(8,128)}) custom-call(s32[1]{0:T(128)} %bitcast.core_ref, f32[3,32,4096]{2,1,0:T(8,128)} %bitcast.8, f32[3,32,4096]{2,1,0:T(8,128)} %bitcast.3.state_hbm.state_ref, bf16[736,256]{1,0:T(8,128)(2,1)} %constant.19.clone.ahead_hbm.ahead_ref), custom_call_target="tpu_custom_call" | custom-call | flops 1000 | bytes 1000 | tf_op jit(solution)/shard_map/pallas_call | solution.py:1000
  18.8 0.0 copy-start.9
  19.5 0.0 copy-start.4
  19.5 0.0 collective-permute-done.there_ref
  19.5 0.6 collective-permute-start.2
  20.1 0.0 copy-done.1
  20.1 0.1 dynamic-slice_bitcast_fusion
  20.1 0.0 copy-done
  20.1 0.0 copy-done.9
  20.1 0.3 copy-done.4
  20.5 0.0 copy-start.3
  20.5 3.2 %shard_map.97.own_ref = f32[3,1536,128]{2,1,0:T(8,128)S(1)} custom-call(s32[1]{0:T(128)} %bitcast.core_ref, s32[3]{0:T(128)S(1)} %copy-done.9, f32[9,88,128]{2,1,0:T(8,128)S(1)} %copy-done.4, f32[9,88,128]{2,1,0:T(8,128)} %collective-permute-done.there_ref, bf16[3584,256]{1,0:T(8,128)(2,1)S(1)} %copy-done), custom_call_target="tpu_custom_call" | custom-call | flops 1000 | bytes 1000 | tf_op jit(solution)/shard_map/pallas_call | solution.py:1000
  23.7 0.0 copy-start.2
  23.7 0.0 copy-start.7
  23.7 0.0 collective-permute-done.1.here_ref
  23.7 0.0 collective-permute-done.2.there_ref
  23.7 0.0 copy-done.3
  23.7 10.8 %shard_map.98 = (f32[2,1024,128]{2,1,0:T(8,128)S(1)}, f32[2,1024,128]{2,1,0:T(8,128)S(1)}, f32[2,1024,128]{2,1,0:T(8,128)S(1)}) custom-call(s32[1]{0:T(128)} %bitcast.core_ref, s32[3]{0:T(128)S(1)} %copy-done.9, s32[1]{0:T(128)S(6)} %copy.10.wave_ref, f32[3,32,4096]{2,1,0:T(8,128)S(1)} %bitcast.9, f32[3,32,4096]{2,1,0:T(8,128)} %bitcast.3.state_hbm.state_ref, ...), custom_call_target="tpu_custom_call" | custom-call | flops 1000 | bytes 1000 | tf_op jit(solution)/shard_map/pallas_call | solution.py:1000
  34.5 0.0 copy-done.2
  34.5 0.0 copy-done.7
  34.5 0.0 copy-start.6
  34.5 3.1 %shard_map.99 = (f32[9,88,128]{2,1,0:T(8,128)S(1)}, f32[9,88,128]{2,1,0:T(8,128)S(1)}) custom-call(s32[1]{0:T(128)} %bitcast.core_ref, s32[3]{0:T(128)S(1)} %copy-done.9, f32[2,1024,128]{2,1,0:T(8,128)S(1)} %get-tuple-element.34.lines_ref, f32[2,8,88,128]{3,2,1,0:T(8,128)S(1)} %copy-done.7, bf16[736,256]{1,0:T(8,128)(2,1)S(1)} %copy-done.3, ...), custom_call_target="tpu_custom_call" | custom-call | flops 1000 | bytes 1000 | tf_op jit(solution)/shard_map/pallas_call | solution.py:1000
  37.6 0.7 collective-permute-start.7
  38.3 1.5 %collective-permute-start.4 = (f32[9,88,128]{2,1,0:T(8,128)S(1)}, f32[9,88,128]{2,1,0:T(8,128)S(1)}, u32[]{:S(2)}, u32[]{:S(2)}) collective-permute-start(f32[9,88,128]{2,1,0:T(8,128)S(1)} %get-tuple-element.49), channel_id=1, source_target_pairs={{0,2},{2,0},{1,3},{3,1},{4,6},{6,4},{5,7},{7,5},{8,10},{10,8},{9,1... | collective-permute-start | bytes 1216520 | tf_op jit(solution)/shard_map/ppermute | solution.py:1102
  39.8 0.0 copy-done.6
  39.8 0.0 copy-start.5
  39.8 4.5 %shard_map.100 = (f32[9,88,128]{2,1,0:T(8,128)S(1)}, f32[9,88,128]{2,1,0:T(8,128)S(1)}) custom-call(s32[1]{0:T(128)} %bitcast.core_ref, s32[3]{0:T(128)S(1)} %copy-done.9, f32[2,1024,128]{2,1,0:T(8,128)S(1)} %get-tuple-element.39.lines_ref, f32[3,1024,128]{2,1,0:T(8,128)S(1)} %copy-done.6, bf16[736,256]{1,0:T(8,128)(2,1)S(1)} %copy-done.3, ...), custom_call_target="tpu_custom_call" | custom-call | flops 1000 | bytes 1000 | tf_op jit(solution)/shard_map/pallas_call | solution.py:1000
  44.3 0.6 collective-permute-start.5
  44.9 0.0 copy-done.5
  44.9 3.2 %shard_map.101 = (f32[7,88,128]{2,1,0:T(8,128)S(1)}, f32[7,88,128]{2,1,0:T(8,128)S(1)}) custom-call(s32[1]{0:T(128)} %bitcast.core_ref, s32[3]{0:T(128)S(1)} %copy-done.9, f32[2,1024,128]{2,1,0:T(8,128)S(1)} %get-tuple-element.43.lines_ref, f32[3,1024,128]{2,1,0:T(8,128)S(1)} %copy-done.5, bf16[736,256]{1,0:T(8,128)(2,1)S(1)} %copy-done.3, ...), custom_call_target="tpu_custom_call" | custom-call | flops 1000 | bytes 1000 | tf_op jit(solution)/shard_map/pallas_call | solution.py:1000
  48.1 1.5 %collective-permute-start.3 = (f32[7,88,128]{2,1,0:T(8,128)S(1)}, f32[7,88,128]{2,1,0:T(8,128)S(1)}, u32[]{:S(2)}, u32[]{:S(2)}) collective-permute-start(f32[7,88,128]{2,1,0:T(8,128)S(1)} %get-tuple-element.46), channel_id=1, source_target_pairs={{0,2},{2,0},{1,3},{3,1},{4,6},{6,4},{5,7},{7,5},{8,10},{10,8},{9,1... | collective-permute-start | bytes 946184 | tf_op jit(solution)/shard_map/ppermute | solution.py:1102
  49.6 0.9 %collective-permute-done.4.far_ref = f32[9,88,128]{2,1,0:T(8,128)S(1)} collective-permute-done((f32[9,88,128]{2,1,0:T(8,128)S(1)}, f32[9,88,128]{2,1,0:T(8,128)S(1)}, u32[]{:S(2)}, u32[]{:S(2)}) %collective-permute-start.4) | collective-permute-done | bytes 405536 | tf_op jit(solution)/shard_map/ppermute | solution.py:1102
  50.5 0.5 shard_map.102.planes_a
  51.0 0.0 copy-start.8
  51.0 8.2 %collective-permute-done.5.far_ref = f32[9,88,128]{2,1,0:T(8,128)S(1)} collective-permute-done((f32[9,88,128]{2,1,0:T(8,128)S(1)}, f32[9,88,128]{2,1,0:T(8,128)S(1)}, u32[]{:S(2)}, u32[]{:S(2)}) %collective-permute-start.5) | collective-permute-done | bytes 405536 | tf_op jit(solution)/shard_map/ppermute | solution.py:1102
  59.2 2.1 %shard_map.103 = (f32[3,16,4096]{2,1,0:T(8,128)S(1)}, f32[3,32,4096]{2,1,0:T(8,128)S(1)}) custom-call(f32[9,88,128]{2,1,0:T(8,128)S(1)} %get-tuple-element.50.near_ref, f32[9,88,128]{2,1,0:T(8,128)S(1)} %collective-permute-done.5.far_ref, f32[2,1024,128]{2,1,0:T(8,128)S(1)} %shard_map.102.planes_a, bf16[3584,256]{1,0:T(8,128)(2,1)S(1)} %copy-done), custom_call_target="tpu_custom_call" | custom-call | flops 1000 | bytes 1000 | tf_op jit(solution)/shard_map/pallas_call | solution.py:1000
  61.3 3.9 %collective-permute-done.3.far_ref = f32[7,88,128]{2,1,0:T(8,128)S(1)} collective-permute-done((f32[7,88,128]{2,1,0:T(8,128)S(1)}, f32[7,88,128]{2,1,0:T(8,128)S(1)}, u32[]{:S(2)}, u32[]{:S(2)}) %collective-permute-start.3) | collective-permute-done | bytes 315424 | tf_op jit(solution)/shard_map/ppermute | solution.py:1102
  65.3 0.0 collective-permute-done.6.state_hbm
  65.3 0.0 collective-permute-done.7.base_hbm
  65.3 0.0 copy-done.8
  65.3 3.5 %shard_map.104 = (f32[3,16,4096]{2,1,0:T(8,128)}, f32[3,32,4096]{2,1,0:T(8,128)}) custom-call(f32[7,88,128]{2,1,0:T(8,128)S(1)} %get-tuple-element.45.near_ref, f32[7,88,128]{2,1,0:T(8,128)S(1)} %collective-permute-done.3.far_ref, f32[3,16,4096]{2,1,0:T(8,128)S(1)} %get-tuple-element.53.base_part, f32[3,32,4096]{2,1,0:T(8,128)S(1)} %get-tuple-element.54.state_part, ...), custom_call_target="tpu_custom_call" | custom-call | flops 1000 | bytes 1000 | tf_op jit(solution)/shard_map/pallas_call | solution.py:1000
Async XLA Ops:
  4.2 15.2 %collective-permute-start = (f32[9,88,128]{2,1,0:T(8,128)}, f32[9,88,128]{2,1,0:T(8,128)}, u32[]{:S(2)}, u32[]{:S(2)}) collective-permute-start(f32[9,88,128]{2,1,0:T(8,128)} %shard_map.95.here_ref), channel_id=1, source_target_pairs={{0,2},{2,0},{1,3},{3,1},{4,6},{6,4},{5,7},{7,5},{8,10},{10,8},{9,1... | collective-permute-start | bytes 1216520 | tf_op jit(solution)/shard_map/ppermute | solution.py:1041
  7.3 12.8 %copy-start.1 = (f32[1,3,32,4096]{3,2,1,0:T(8,128)S(1)}, f32[1,3,32,4096]{3,2,1,0:T(8,128)}, u32[]{:S(2)}) copy-start(f32[1,3,32,4096]{3,2,1,0:T(8,128)} %param.8) | copy-start | bytes 4718596
  7.3 58.0 %collective-permute-start.6 = (f32[3,32,4096]{2,1,0:T(8,128)}, f32[3,32,4096]{2,1,0:T(8,128)}, u32[]{:S(2)}, u32[]{:S(2)}) collective-permute-start(f32[3,32,4096]{2,1,0:T(8,128)} %bitcast.3.state_hbm.state_ref), channel_id=1, source_target_pairs={{4,0},{8,4},{12,8},{0,12},{1,5},{5,9},{9,13},{13,1},{6,2},{10,6},{... | collective-permute-start | bytes 4718600 | tf_op jit(solution)/shard_map/ppermute | solution.py:1023
  10.9 12.8 %collective-permute-start.1 = (f32[9,88,128]{2,1,0:T(8,128)}, f32[9,88,128]{2,1,0:T(8,128)}, u32[]{:S(2)}, u32[]{:S(2)}) collective-permute-start(f32[9,88,128]{2,1,0:T(8,128)} %shard_map.95.here_ref), channel_id=1, source_target_pairs={{0,1},{1,0},{2,3},{3,2},{4,5},{5,4},{6,7},{7,6},{8,9},{9,8},{10,11... | collective-permute-start | bytes 1216520 | tf_op jit(solution)/shard_map/ppermute | solution.py:1042
  10.9 9.3 %copy-start = (bf16[3584,256]{1,0:T(8,128)(2,1)S(1)}, bf16[3584,256]{1,0:T(8,128)(2,1)}, u32[]{:S(2)}) copy-start(bf16[3584,256]{1,0:T(8,128)(2,1)} %constant.20.clone.back_ref) | copy-start | bytes 5505028
  18.8 1.3 %copy-start.9 = (s32[3]{0:T(128)S(1)}, s32[3]{0:T(128)}, u32[]{:S(2)}) copy-start(s32[3]{0:T(128)} %cutoff_ref.9) | copy-start | bytes 40
  19.5 1.0 %copy-start.4 = (f32[9,88,128]{2,1,0:T(8,128)S(1)}, f32[9,88,128]{2,1,0:T(8,128)}, u32[]{:S(2)}) copy-start(f32[9,88,128]{2,1,0:T(8,128)} %shard_map.95.here_ref) | copy-start | bytes 1216516
  19.5 4.2 %collective-permute-start.2 = (f32[9,88,128]{2,1,0:T(8,128)}, f32[9,88,128]{2,1,0:T(8,128)S(1)}, u32[]{:S(2)}, u32[]{:S(2)}) collective-permute-start(f32[9,88,128]{2,1,0:T(8,128)} %collective-permute-done.there_ref), channel_id=1, source_target_pairs={{0,1},{1,0},{2,3},{3,2},{4,5},{5,4},{6,7},{7,6},{8,9},{9,8},{10,11... | collective-permute-start | bytes 1216520 | tf_op jit(solution)/shard_map/ppermute | solution.py:1066
  20.5 3.2 %copy-start.3 = (bf16[736,256]{1,0:T(8,128)(2,1)S(1)}, bf16[736,256]{1,0:T(8,128)(2,1)}, u32[]{:S(2)}) copy-start(bf16[736,256]{1,0:T(8,128)(2,1)} %constant.19.clone.ahead_hbm.ahead_ref) | copy-start | bytes 1130500
  23.7 10.8 %copy-start.2 = (bf16[3072,256]{1,0:T(8,128)(2,1)S(1)}, bf16[3072,256]{1,0:T(8,128)(2,1)}, u32[]{:S(2)}) copy-start(bf16[3072,256]{1,0:T(8,128)(2,1)} %constant.22.clone.along_ref) | copy-start | bytes 4718596
  23.7 10.8 %copy-start.7 = (f32[2,8,88,128]{3,2,1,0:T(8,128)S(1)}, f32[2,8,88,128]{3,2,1,0:T(8,128)}, u32[]{:S(2)}) copy-start(f32[2,8,88,128]{3,2,1,0:T(8,128)} %get-tuple-element.35.flux_ref) | copy-start | bytes 2162692
  34.5 5.3 %copy-start.6 = (f32[3,1024,128]{2,1,0:T(8,128)S(1)}, f32[3,1024,128]{2,1,0:T(8,128)}, u32[]{:S(2)}) copy-start(f32[3,1024,128]{2,1,0:T(8,128)} %get-tuple-element.40.flux_ref) | copy-start | bytes 4718596
  37.6 27.6 %collective-permute-start.7 = (f32[3,16,4096]{2,1,0:T(8,128)S(1)}, f32[3,16,4096]{2,1,0:T(8,128)S(1)}, u32[]{:S(2)}, u32[]{:S(2)}) collective-permute-start(f32[3,16,4096]{2,1,0:T(8,128)S(1)} %dynamic-slice_bitcast_fusion), channel_id=1, source_target_pairs={{4,0},{8,4},{12,8},{0,12},{5,1},{9,5},{13,9},{1,13},{6,2},{10,6},{... | collective-permute-start | bytes 2359304 | tf_op jit(solution)/shard_map/ppermute | solution.py:1100
  38.3 12.2 %collective-permute-start.4 = (f32[9,88,128]{2,1,0:T(8,128)S(1)}, f32[9,88,128]{2,1,0:T(8,128)S(1)}, u32[]{:S(2)}, u32[]{:S(2)}) collective-permute-start(f32[9,88,128]{2,1,0:T(8,128)S(1)} %get-tuple-element.49), channel_id=1, source_target_pairs={{0,2},{2,0},{1,3},{3,1},{4,6},{6,4},{5,7},{7,5},{8,10},{10,8},{9,1... | collective-permute-start | bytes 1216520 | tf_op jit(solution)/shard_map/ppermute | solution.py:1102
  39.8 5.1 %copy-start.5 = (f32[3,1024,128]{2,1,0:T(8,128)S(1)}, f32[3,1024,128]{2,1,0:T(8,128)}, u32[]{:S(2)}) copy-start(f32[3,1024,128]{2,1,0:T(8,128)} %get-tuple-element.44.flux_ref) | copy-start | bytes 4718596
  44.3 14.9 %collective-permute-start.5 = (f32[9,88,128]{2,1,0:T(8,128)S(1)}, f32[9,88,128]{2,1,0:T(8,128)S(1)}, u32[]{:S(2)}, u32[]{:S(2)}) collective-permute-start(f32[9,88,128]{2,1,0:T(8,128)S(1)} %get-tuple-element.51), channel_id=1, source_target_pairs={{0,2},{2,0},{1,3},{3,1},{4,6},{6,4},{5,7},{7,5},{8,10},{10,8},{9,1... | collective-permute-start | bytes 1216520 | tf_op jit(solution)/shard_map/ppermute | solution.py:1102
  48.1 17.2 %collective-permute-start.3 = (f32[7,88,128]{2,1,0:T(8,128)S(1)}, f32[7,88,128]{2,1,0:T(8,128)S(1)}, u32[]{:S(2)}, u32[]{:S(2)}) collective-permute-start(f32[7,88,128]{2,1,0:T(8,128)S(1)} %get-tuple-element.46), channel_id=1, source_target_pairs={{0,2},{2,0},{1,3},{3,1},{4,6},{6,4},{5,7},{7,5},{8,10},{10,8},{9,1... | collective-permute-start | bytes 946184 | tf_op jit(solution)/shard_map/ppermute | solution.py:1102
  51.0 14.3 %copy-start.8 = (bf16[512,256]{1,0:T(8,128)(2,1)S(1)}, bf16[512,256]{1,0:T(8,128)(2,1)}, u32[]{:S(2)}) copy-start(bf16[512,256]{1,0:T(8,128)(2,1)} %constant.21.clone.last_ref) | copy-start | bytes 786436
